TPU v7x, 512 devices: a whole 4x8x8 slice. The times are simulated.
512 devices in a mesh: ctx: 16 (over y, x_lo), exp: 32 (over z, x_hi, core).
Axes of the slice: x: 4 (x_hi: 2, x_lo: 2; x = x_hi * 2 + x_lo), y: 8, z: 8, core: 2. Of those that a mesh axis runs over, the one named last changes fastest.
Arguments:
- queries: bfloat16 [4096, 64, 576], P('ctx', 'exp'), may hold values from -40 to 40
- latent: bfloat16 [4096, 576], P('ctx'), may hold values from -6.5 to 6.5
- segment_ids: int32 [4096], P('ctx'), may hold values from 0 to 7, never falling along the last dimension, each value on 1 to 2048 neighbouring positions
- value_up: bfloat16 [64, 512, 128], P('exp'), may hold values from -0.25 to 0.25
- out_proj: bfloat16 [8192, 2560], P('exp'), may hold values from -0.125 to 0.125
- residual: bfloat16 [4096, 2560], P(('ctx', 'exp')), may hold values from -4 to 4
- norm_gain: float32 [2560], replicated, may hold values from 0.1 to 1.9
- route_ids: int32 [256, 16, 6], P('exp'), may hold values from 0 to 95, all different within a row; in each aligned block of 128 rows (0 to 127, 128 to 255, ..., all dimensions but the last counted through in order) at most 10 rows name the same one
- route_gates: float32 [256, 16, 6], P('exp'), may hold values from 0.1 to 1
- expert_gate: bfloat16 [96, 2560, 768], P('exp', 'ctx'), may hold values from -0.125 to 0.125
- expert_up: bfloat16 [96, 2560, 768], P('exp', 'ctx'), may hold values from -0.125 to 0.125
- expert_down: bfloat16 [96, 768, 2560], P('exp', None, 'ctx'), may hold values from -0.21875 to 0.21875
Outputs:
- layer_out: bfloat16 [256, 16, 2560], P('exp', None, 'ctx')
Inputs may be any that keep to these rules, and one draw needn't show every extreme that they name: `segment_ids`: never falling along the sequence; no document is longer than half of 4096 tokens, and one has exactly that length. `route_ids`: in the rows of one device (aligned blocks of 128 rows over the first two dimensions together, in order) no expert is named more than 10 times, a bound that some block reaches.
All inputs are finite; a program needn't handle non-finite values.
Results may differ from a plain program's by a relative error of at most 0.04.
Values may be sent and summed in bfloat16 or wider, within the bound.
No kernel may reach another device: no remote copies, remote signals or barrier semaphores. Data moves between devices by JAX's collectives and lax.ppermute only.
A program may use at most 64 MiB of HBM per device.

v0:
```python
import jax
import jax.numpy as jnp
from jax import lax
from jax.sharding import PartitionSpec as P

LATENT = 512
VDIM = 128
QKDIM = 192
EXPERTS = 96
TOPK = 6
CAP = 10


def on_device(
    queries,
    latent,
    segment_ids,
    value_up,
    out_proj,
    residual,
    norm_gain,
    route_ids,
    route_gates,
    expert_gate,
    expert_up,
    expert_down,
):
    block_len = queries.shape[0]
    local_heads = queries.shape[1]
    rows_all = block_len * local_heads
    query_rows = queries.reshape(rows_all, queries.shape[2])
    ctx_index = lax.axis_index("ctx")
    ctx_count = lax.axis_size("ctx")
    exp_count = lax.axis_size("exp")
    tok_dev = block_len // exp_count
    query_pos = ctx_index * block_len + jnp.arange(rows_all, dtype=jnp.int32) // local_heads
    query_seg = jnp.repeat(segment_ids, local_heads)
    scaling = QKDIM ** (-0.5)
    key_rows = lax.all_gather(latent, "ctx", axis=0, tiled=True)
    key_seg = lax.all_gather(segment_ids, "ctx", axis=0, tiled=True)
    key_pos = jnp.arange(key_rows.shape[0], dtype=jnp.int32)
    allowed = (key_pos[None, :] <= query_pos[:, None]) & (key_seg[None, :] == query_seg[:, None])
    peak_old = jnp.full((rows_all,), -jnp.inf, jnp.float32)
    sums_old = jnp.zeros((rows_all,), jnp.float32)
    accum_old = jnp.zeros((rows_all, LATENT), jnp.float32)
    scores = jnp.dot(query_rows, key_rows.T, preferred_element_type=jnp.float32) * scaling
    scores = jnp.where(allowed, scores, -jnp.inf)
    peak_new = jnp.max(scores, axis=1)
    shift_by = jnp.where(jnp.isfinite(peak_new), peak_new, 0.0)
    factor = jnp.exp(peak_old - shift_by)
    exp_terms = jnp.exp(scores - shift_by[:, None])
    sums_new = sums_old * factor + jnp.sum(exp_terms, axis=1)
    accum_new = accum_old * factor[:, None] + jnp.dot(
        exp_terms.astype(jnp.bfloat16), key_rows[:, :LATENT], preferred_element_type=jnp.float32
    )
    fold_state = (peak_new, sums_new, accum_new)
    peak_final, sums_final, accum_final = fold_state
    mixed_latent = (
        (accum_final / sums_final[:, None])
        .astype(jnp.bfloat16)
        .reshape(block_len, local_heads, LATENT)
    )
    head_values = jnp.einsum(
        "thl,hlv->thv", mixed_latent, value_up, preferred_element_type=jnp.float32
    ).astype(jnp.bfloat16)
    head_values = head_values.reshape(block_len, local_heads * VDIM)
    attended = lax.psum_scatter(
        jnp.dot(head_values, out_proj, preferred_element_type=jnp.float32).astype(jnp.bfloat16),
        "exp",
        scatter_dimension=0,
        tiled=True,
    ).astype(jnp.float32)
    stream = (residual.astype(jnp.float32) + attended).astype(jnp.bfloat16)
    stream_wide = stream.astype(jnp.float32)
    mean_sq = jnp.mean(stream_wide * stream_wide, axis=1, keepdims=True)
    normed = (stream_wide * lax.rsqrt(mean_sq + 1e-06) * norm_gain[None, :]).astype(jnp.bfloat16)
    width_model = stream.shape[1]
    stream_split, normed_split = (
        lax.all_to_all(
            stream.reshape(tok_dev, 1, width_model), "ctx", split_axis=2, concat_axis=1, tiled=True
        ),
        lax.all_to_all(
            normed.reshape(tok_dev, 1, width_model), "ctx", split_axis=2, concat_axis=1, tiled=True
        ),
    )
    token_count = tok_dev * ctx_count
    width_local = stream_split.shape[2]
    exp_dev = expert_gate.shape[0]
    routes = route_ids.reshape(token_count, TOPK)
    gates_local = route_gates.reshape(token_count, TOPK)
    flat_routes = routes.reshape(token_count * TOPK)
    onehot = (flat_routes[:, None] == jnp.arange(EXPERTS, dtype=jnp.int32)[None, :]).astype(
        jnp.int32
    )
    earlier = jnp.cumsum(onehot, axis=0) - onehot
    slot_of = jnp.sum(earlier * onehot, axis=1)
    target = (flat_routes * CAP + slot_of).reshape(token_count, TOPK)
    slot_index = jnp.arange(EXPERTS * CAP, dtype=jnp.int32)
    matches = target[None, :, :] == slot_index[:, None, None]
    picker = jnp.any(matches, axis=2).astype(jnp.bfloat16)
    outgoing = jnp.dot(
        picker, normed_split.reshape(token_count, width_local), preferred_element_type=jnp.float32
    ).astype(jnp.bfloat16)
    outgoing = outgoing.reshape(exp_count, exp_dev, CAP, width_local)
    received = lax.all_to_all(outgoing, "exp", split_axis=0, concat_axis=2, tiled=True)
    received = received.reshape(exp_dev, exp_count * CAP, width_local)
    gate_part = jnp.einsum(
        "erd,edf->erf", received, expert_gate, preferred_element_type=jnp.float32
    )
    up_part = jnp.einsum("erd,edf->erf", received, expert_up, preferred_element_type=jnp.float32)
    gate_sum, up_sum = (
        lax.psum(gate_part.astype(jnp.bfloat16), "ctx").astype(jnp.float32),
        lax.psum(up_part.astype(jnp.bfloat16), "ctx").astype(jnp.float32),
    )
    hidden = (jax.nn.silu(gate_sum) * up_sum).astype(jnp.bfloat16)
    expert_out = jnp.einsum(
        "erf,efd->erd", hidden, expert_down, preferred_element_type=jnp.float32
    ).astype(jnp.bfloat16)
    returned = lax.all_to_all(
        expert_out.reshape(1, exp_dev, exp_count * CAP, width_local),
        "exp",
        split_axis=2,
        concat_axis=0,
        tiled=True,
    )
    returned = returned.reshape(EXPERTS * CAP, width_local)
    weighting = jnp.sum(jnp.where(matches, gates_local[None, :, :], 0.0), axis=2)
    mixture = jnp.einsum(
        "sn,sd->nd", weighting, returned.astype(jnp.float32), precision=lax.Precision.HIGHEST
    )
    result = (stream_split.reshape(token_count, width_local).astype(jnp.float32) + mixture).astype(
        jnp.bfloat16
    )
    return result.reshape(tok_dev, ctx_count, width_local)


def solution(mesh):
    return jax.shard_map(
        on_device,
        mesh=mesh,
        in_specs=(
            P("ctx", "exp", None),
            P("ctx", None),
            P("ctx"),
            P("exp", None, None),
            P("exp", None),
            P(("ctx", "exp"), None),
            P(),
            P("exp", None, None),
            P("exp", None, None),
            P("exp", "ctx", None),
            P("exp", "ctx", None),
            P("exp", None, "ctx"),
        ),
        out_specs=P("exp", None, "ctx"),
        check_vma=False,
    )
```

profile of v0, /device:TPU:6, one launch (start us, length us, event | category | flops | bytes accessed | tf_op | source)
XLA Modules:
  0.0 546.8 jit_solution(16366526199191594582)
XLA Ops:
  7.3 2.4 copy.79
  11.2 32.3 %all-gather = s32[16,1,256]{2,1,0:T(1,128)S(1)} all-gather(s32[1,1,256]{2,1,0:T(1,128)S(1)} %bitcast.86), channel_id=1, replica_groups=mesh['ctx'=16,'exp'=32] {'ctx'}, dimensions={0}, use_global_device_ids=true | all-gather | bytes 17408 | tf_op jit(solution)/shard_map/all_gather | solution.py:40
  43.5 109.5 %all-gather.3.cloned.1.call-done = bf16[4096,576]{0,1:T(8,128)(2,1)} async-done(((bf16[256,576]{0,1:T(8,128)(2,1)}), bf16[4096,576]{0,1:T(8,128)(2,1)}) %all-gather.3.cloned.1.call-update) | async-done | bytes 4718608 | tf_op jit(solution)/shard_map/all_gather | solution.py:39
  153.0 6.8 %fusion.55 = (f32[512]{0:T(512)S(1)}, f32[512,4096]{1,0:T(8,128)S(1)}) fusion(bf16[512,576]{1,0:T(8,128)(2,1)S(1)} %reshape.115, bf16[4096,576]{0,1:T(8,128)(2,1)} %all-gather.3.cloned.1.call-done, s32[512]{0:T(512)S(1)} %eq.54, s32[4096]{0:T(1024)S(1)} %bitcast.85, s32[512]{0:T(512)S(1)} %fusion.48), kind=kOutput, calls=%fused_computation.68 | convolution fusion | flops 2428501504 | bytes 13719552 | tf_op jit(solution)/shard_map/dot_general | solution.py:46
  162.2 2.5 fusion.28
  165.3 1.6 convolution_convert_fusion
  167.4 2.1 reduce-window.6
  170.3 118.5 %reduce-scatter.2.cloned.1.call-done = bf16[8,2560]{1,0:T(8,128)(2,1)} async-done(((bf16[256,2560]{1,0:T(8,128)(2,1)}), bf16[8,2560]{1,0:T(8,128)(2,1)}) %reduce-scatter.2.cloned.1.call-update) | async-done | bytes 40976 | tf_op jit(solution)/shard_map/reduce_scatter | solution.py:67
  292.1 14.3 %reduce.3 = bf16[2560,8]{1,0:T(8,128)(2,1)S(1)} reduce(bf16[2560,1,8]{2,1,0:T(2,128)(2,1)S(1)} %bitcast.73, bf16[]{:T(256)} %broadcast.107), dimensions={1}, to_apply=%bitcast.50.reduce_sub_computation | reduce | bytes 81922
  306.4 1.3 reshape.133
  307.7 8.2 %all-to-all-start.1 = ((bf16[16,2,640]{2,1,0:T(2,128)(2,1)}), bf16[16,2,640]{2,1,0:T(2,128)(2,1)S(1)}, u32[]{:S(2)}, u32[]{:S(2)}) async-start(bf16[16,2,640]{2,1,0:T(2,128)(2,1)} %reshape.133), calls=%async_computation.2 | async-start | bytes 81920 | tf_op jit(solution)/shard_map/all_to_all | solution.py:82
  316.5 7.0 %all-to-all-done.1 = bf16[16,2,640]{2,1,0:T(2,128)(2,1)S(1)} async-done(((bf16[16,2,640]{2,1,0:T(2,128)(2,1)}), bf16[16,2,640]{2,1,0:T(2,128)(2,1)S(1)}, u32[]{:S(2)}, u32[]{:S(2)}) %all-to-all-start.1) | async-done | bytes 40992 | tf_op jit(solution)/shard_map/all_to_all | solution.py:82
  323.5 1.5 reshape.134
  327.6 21.0 %all_to_all.48 = bf16[32,2,2400]{2,1,0:T(2,128)(2,1)S(1)} all-to-all(bf16[32,2,2400]{2,1,0:T(2,128)(2,1)S(1)} %reshape.135), channel_id=1, replica_groups=mesh['ctx'=16,'exp'=32] {'exp'}, dimensions={0} | all-to-all | bytes 614400 | tf_op jit(solution)/shard_map/all_to_all | solution.py:105
  349.4 1.7 convolution_convert_fusion.1
  351.0 1.7 convolution_convert_fusion.2
  353.7 14.3 %reduce.2 = bf16[2560,8]{1,0:T(8,128)(2,1)S(1)} reduce(bf16[2560,1,8]{2,1,0:T(2,128)(2,1)S(1)} %bitcast.74, bf16[]{:T(256)} %broadcast.107), dimensions={1}, to_apply=%bitcast.48.reduce_sub_computation | reduce | bytes 81922
  369.3 4.7 all-to-all-start
  374.0 134.6 %all-reduce.3.cloned.1.call-done = (bf16[3,320,768]{2,1,0:T(8,128)(2,1)}, bf16[3,320,768]{2,1,0:T(8,128)(2,1)}) async-done(((bf16[3,320,768]{2,1,0:T(8,128)(2,1)}, bf16[3,320,768]{2,1,0:T(8,128)(2,1)}), (bf16[3,320,768]{2,1,0:T(8,128)(2,1)}, bf16[3,320,768]{2,1,0:T(8,128)(2,1)})) %all-reduce.3.cloned.1.call-update) | async-done | bytes 2949136 | tf_op jit(solution)/shard_map/psum | solution.py:113
  508.6 3.2 fusion.33
  512.5 1.4 reshape.137
  513.9 10.6 %all-to-all-start.3 = ((bf16[32,2,2400]{2,1,0:T(2,128)(2,1)}), bf16[32,2,2400]{2,1,0:T(2,128)(2,1)S(1)}, u32[]{:S(2)}, u32[]{:S(2)}) async-start(bf16[32,2,2400]{2,1,0:T(2,128)(2,1)} %reshape.137), calls=%async_computation.4 | async-start | bytes 622592 | tf_op jit(solution)/shard_map/all_to_all | solution.py:119
  524.9 1.5 reshape.132
  527.4 10.3 %all-to-all-done.3 = bf16[32,2,2400]{2,1,0:T(2,128)(2,1)S(1)} async-done(((bf16[32,2,2400]{2,1,0:T(2,128)(2,1)}), bf16[32,2,2400]{2,1,0:T(2,128)(2,1)S(1)}, u32[]{:S(2)}, u32[]{:S(2)}) %all-to-all-start.3) | async-done | bytes 307232 | tf_op jit(solution)/shard_map/all_to_all | solution.py:119
  (76 shorter events, 20.3 us)
Async XLA Ops:
  6.5 158.7 %copy-start = (bf16[256,2560]{1,0:T(8,128)(2,1)S(1)}, bf16[256,2560]{1,0:T(8,128)(2,1)}, u32[]{:S(2)}) copy-start(bf16[256,2560]{1,0:T(8,128)(2,1)} %param.16) | copy-start | bytes 3932164
  6.5 4.7 copy-start.7
  6.5 146.5 %all-gather.3.cloned.1.call-start = ((), (), s32[]{:S(2)}) async-start(), calls=%async_computation.5 | async-start | bytes 5013504 | tf_op jit(solution)/shard_map/all_gather | solution.py:39
  7.3 281.5 %reduce-scatter.2.cloned.1.call-start = ((), (), s32[]{:S(2)}) async-start(), calls=%async_computation.6 | async-start | bytes 1351680 | tf_op jit(solution)/shard_map/reduce_scatter | solution.py:67
  159.9 2.3 copy-start.8
  162.2 2.7 copy-start.9
  164.7 2.2 copy-start.4
  165.3 123.5 %copy-start.3 = (bf16[8,2560]{1,0:T(8,128)(2,1)S(1)}, bf16[8,2560]{1,0:T(8,128)(2,1)}, u32[]{:S(2)}) copy-start(bf16[8,2560]{1,0:T(8,128)(2,1)} %param.17) | copy-start | bytes 122884
  165.3 124.4 %copy-start.6 = (f32[2560]{0:T(1024)S(1)}, f32[2560]{0:T(1024)}, u32[]{:S(2)}) copy-start(f32[2560]{0:T(1024)} %param.18) | copy-start | bytes 30724
  307.7 15.7 %all-to-all-start.1 = ((bf16[16,2,640]{2,1,0:T(2,128)(2,1)}), bf16[16,2,640]{2,1,0:T(2,128)(2,1)S(1)}, u32[]{:S(2)}, u32[]{:S(2)}) async-start(bf16[16,2,640]{2,1,0:T(2,128)(2,1)} %reshape.133), calls=%async_computation.2 | async-start | bytes 81920 | tf_op jit(solution)/shard_map/all_to_all | solution.py:82
  315.9 192.6 %all-reduce.3.cloned.1.call-start = ((), (), s32[]{:S(2)}) async-start(), calls=%async_computation.7 | async-start | bytes 5898240 | tf_op jit(solution)/shard_map/psum | solution.py:113
  326.1 23.3 %copy-start.1 = (bf16[3,160,768]{2,1,0:T(8,128)(2,1)S(1)}, bf16[3,160,768]{2,1,0:T(8,128)(2,1)}, u32[]{:S(2)}) copy-start(bf16[3,160,768]{2,1,0:T(8,128)(2,1)} %param.22) | copy-start | bytes 2211844
  349.3 1.7 copy-start.2
  369.3 144.6 %all-to-all-start = ((bf16[16,2,640]{2,1,0:T(2,128)(2,1)}), bf16[16,2,640]{2,1,0:T(2,128)(2,1)S(1)}, u32[]{:S(2)}, u32[]{:S(2)}) async-start(bf16[16,2,640]{2,1,0:T(2,128)(2,1)} %reshape.131), calls=%async_computation.1 | async-start | bytes 81920 | tf_op jit(solution)/shard_map/all_to_all | solution.py:79
  508.6 15.9 %copy-start.5 = (f32[8,16,6]{1,0,2:T(8,128)S(1)}, f32[8,16,6]{1,0,2:T(8,128)}, u32[]{:S(2)}) copy-start(f32[8,16,6]{1,0,2:T(8,128)} %param.20) | copy-start | bytes 9220
  513.9 23.8 %all-to-all-start.3 = ((bf16[32,2,2400]{2,1,0:T(2,128)(2,1)}), bf16[32,2,2400]{2,1,0:T(2,128)(2,1)S(1)}, u32[]{:S(2)}, u32[]{:S(2)}) async-start(bf16[32,2,2400]{2,1,0:T(2,128)(2,1)} %reshape.137), calls=%async_computation.4 | async-start | bytes 622592 | tf_op jit(solution)/shard_map/all_to_all | solution.py:119
Sparse Core Ops, SparseCore 0:
  9.4 143.6 all-gather.2
  167.0 121.7 reduce-scatter.1
  352.8 155.6 all-reduce.2
where the time goes:
time: 550 us; the launch traced here: 547 us
  waiting for transfers between devices  381 us (69%)
  blocking collectives  53.4 us (10%)
  other arithmetic  34.8 us (6%)
  starting transfers between devices  23.6 us (4%)
  local copies, waits for them, and re-layouts  22.3 us (4%)
  matrix products  18.6 us (3%)
  between operations  13.5 us (2%)
    psum x1, waiting for transfers between devices, on_device(): lax.psum(up_part.astype(jnp.bfloat16), 'ctx').astype(jnp.float32)  135 us
    reduce_scatter x1, waiting for transfers between devices, on_device(): lax.psum_scatter(jnp.dot(head_values, out_proj, preferred_element_type=jn...  119 us
    all_gather x1, waiting for transfers between devices, on_device(): key_rows = lax.all_gather(latent, 'ctx', axis=0, tiled=True)  109 us
    all_gather x1, blocking collectives, on_device(): key_seg = lax.all_gather(segment_ids, 'ctx', axis=0, tiled=True)  32.3 us
    unnamed x2, other arithmetic  28.6 us
    all_to_all x1, blocking collectives, on_device(): lax.all_to_all(outgoing, 'exp', split_axis=0, concat_axis=2, tiled=True)  21 us
    unnamed x31, local copies, waits for them, and re-layouts  13.4 us
  transfers between devices with their start and end apart: 6, of which 5 were waited for; matrix products, arithmetic and copies ran while one was open for 6% of the time, Pallas kernels for 0%

commit v1 on v0

v1 whole, which is shorter than its diff:
```python
import jax
import jax.numpy as jnp
from jax import lax
from jax.sharding import Mesh, PartitionSpec as P

LATENT = 512
VDIM = 128
QKDIM = 192
EXPERTS = 96
TOPK = 6
CAP = 10
SLOTS = 32

CTX = ("y", "xl")
EXP = ("z", "xh", "core")
SWAP = [(0, 1), (1, 0)]


def shift(count, by):
    return [(i, (i + by) % count) for i in range(count)]


def on_device(
    queries,
    latent,
    segment_ids,
    value_up,
    out_proj,
    residual,
    norm_gain,
    route_ids,
    route_gates,
    expert_gate,
    expert_up,
    expert_down,
):
    f32, bf16 = jnp.float32, jnp.bfloat16
    block_len, local_heads, width_key = queries.shape
    width_model = residual.shape[1]
    width_out = width_model // 16
    width_pair = 2 * width_out
    ff = expert_gate.shape[2]
    ff_half = ff // 2
    y, xl, core = (lax.axis_index(a) for a in ("y", "xl", "core"))
    half = block_len // 2

    def keep_send(array, axis):
        parts = jnp.split(array, 2, axis=axis)
        return jnp.where(xl == 0, parts[0], parts[1]), jnp.where(xl == 0, parts[1], parts[0])

    gate_keep, gate_send = keep_send(expert_gate, 2)
    up_keep, up_send = keep_send(expert_up, 2)
    down_keep, down_send = keep_send(expert_down, 1)
    in_keep = jnp.concatenate([gate_keep, up_keep], axis=2)
    in_got = lax.ppermute(jnp.concatenate([gate_send, up_send], axis=2), "xl", SWAP)
    down_got = lax.ppermute(down_send, "xl", SWAP)
    w_in = jnp.concatenate(
        [jnp.where(xl == 0, in_keep, in_got), jnp.where(xl == 0, in_got, in_keep)], axis=1
    ).reshape(3 * width_pair, 2 * ff_half)
    w_down = jnp.concatenate(
        [jnp.where(xl == 0, down_keep, down_got), jnp.where(xl == 0, down_got, down_keep)], axis=2
    ).reshape(3 * ff_half, width_pair)

    pad = 640 - width_key - 1
    keys_own = jnp.concatenate(
        [latent, segment_ids.astype(bf16)[:, None], jnp.zeros((block_len, pad), bf16)], axis=1
    )
    mine = lax.dynamic_slice_in_dim(keys_own, core * half, half, 0)
    back = [lax.ppermute(mine, "y", shift(8, k)) for k in (1, 2, 3, 4)]
    column = jnp.stack(back)
    other_send = jnp.where(xl == 0, jnp.stack([mine] + back[:3]), column)
    other = lax.ppermute(other_send, "xl", SWAP)
    halves = jnp.concatenate([column, other])
    halves_other = lax.ppermute(halves, "core", SWAP)
    keys_all = jnp.concatenate([halves, halves_other]).reshape(16 * half, 640)
    keys_all = jnp.concatenate([keys_own, keys_all])
    block = 2 * y + xl
    step = jnp.arange(1, 5, dtype=jnp.int32)
    first_other = jnp.where(xl == 0, 2 * (y - step) + 1, 2 * (y - step + 1))
    blocks = jnp.concatenate([2 * (y - step) + xl, first_other])
    rows = jnp.arange(half, dtype=jnp.int32)
    start = blocks * block_len
    pos_halves = jnp.concatenate(
        [
            (start[:, None] + core * half + rows[None, :]).reshape(-1),
            (start[:, None] + (1 - core) * half + rows[None, :]).reshape(-1),
        ]
    )
    key_pos = jnp.concatenate(
        [block * block_len + jnp.arange(block_len, dtype=jnp.int32), pos_halves]
    )
    key_seg = keys_all[:, width_key].astype(jnp.int32)
    rows_all = block_len * local_heads
    query_rows = queries.reshape(rows_all, width_key)
    query_pos = block * block_len + jnp.arange(rows_all, dtype=jnp.int32) // local_heads
    query_seg = jnp.repeat(segment_ids, local_heads)
    allowed = (
        (key_pos[None, :] >= 0)
        & (key_pos[None, :] <= query_pos[:, None])
        & (key_seg[None, :] == query_seg[:, None])
    )
    scores = lax.dot_general(
        query_rows, keys_all[:, :width_key], (((1,), (1,)), ((), ())), preferred_element_type=f32
    ) * (QKDIM ** (-0.5))
    scores = jnp.where(allowed, scores, -jnp.inf)
    peak = jnp.max(scores, axis=1, keepdims=True)
    terms = jnp.exp(scores - peak)
    totals = jnp.sum(terms, axis=1, keepdims=True)
    mixed = jnp.dot(terms.astype(bf16), keys_all[:, :LATENT], preferred_element_type=f32) / totals
    mixed = mixed.astype(bf16).reshape(block_len, local_heads, LATENT)
    head_values = jnp.einsum("thl,hlv->thv", mixed, value_up, preferred_element_type=f32)
    head_values = head_values.astype(bf16).reshape(16, 2, 8, local_heads * VDIM)

    def project(which):
        picked = lax.dynamic_index_in_dim(head_values, which, 1, keepdims=False)
        return jnp.dot(
            picked.reshape(half, local_heads * VDIM), out_proj, preferred_element_type=f32
        )

    got = lax.ppermute(project(1 - core).astype(bf16), "core", SWAP)
    pair_sum = (project(core) + got.astype(f32)).astype(bf16).reshape(16, 8, width_model)
    spread = lax.all_to_all(pair_sum, ("z", "xh"), split_axis=0, concat_axis=0, tiled=True)
    attended = jnp.sum(spread.astype(f32), axis=0)
    stream = (residual.astype(f32) + attended).astype(bf16)
    stream_wide = stream.astype(f32)
    mean_sq = jnp.mean(stream_wide * stream_wide, axis=1, keepdims=True)
    normed = (stream_wide * lax.rsqrt(mean_sq + 1e-06) * norm_gain[None, :]).astype(bf16)

    packed = jnp.stack(
        [
            jnp.concatenate(
                [
                    normed[:, (c // 2) * width_pair : (c // 2 + 1) * width_pair],
                    stream[:, c * width_out : (c + 1) * width_out],
                ],
                axis=1,
            )
            for c in range(16)
        ]
    )
    split = lax.all_to_all(packed, CTX, split_axis=0, concat_axis=0, tiled=True)
    split = split.reshape(128, width_pair + width_out)

    routes = jnp.transpose(route_ids, (1, 0, 2)).reshape(128, TOPK)
    expert_axis = jnp.arange(EXPERTS, dtype=jnp.int32)
    named = jnp.any(routes[:, :, None] == expert_axis[None, None, :], axis=1)
    earlier_tokens = jnp.tril(jnp.ones((128, 128), bf16), -1)
    slot_all = jnp.dot(earlier_tokens, named.astype(bf16), preferred_element_type=f32).astype(jnp.int32)
    slot_of = jnp.sum(
        jnp.where(routes[:, :, None] == expert_axis[None, None, :], slot_all[:, None, :], 0), axis=2
    )
    target = (routes // 3) * SLOTS + (routes % 3) * CAP + slot_of
    slot_axis = jnp.arange(32 * SLOTS, dtype=jnp.int32)
    matches = target[:, :, None] == slot_axis[None, None, :]
    picker = jnp.any(matches, axis=1).astype(bf16)
    order = jnp.arange(128, dtype=jnp.int32)
    back_order = ((order % 16) * 8 + order // 16)[:, None] == order[None, :]
    target_rb = jnp.transpose(target.reshape(16, 8, TOPK), (1, 0, 2)).reshape(128, TOPK)
    gates_rb = route_gates.reshape(128, TOPK)
    weighting = jnp.sum(
        jnp.where(target_rb[:, :, None] == slot_axis[None, None, :], gates_rb[:, :, None], 0.0),
        axis=1,
    )

    outgoing = lax.dot_general(
        picker, split[:, :width_pair], (((0,), (0,)), ((), ())), preferred_element_type=f32
    ).astype(bf16)
    received = lax.all_to_all(
        outgoing.reshape(32, SLOTS, width_pair), EXP, split_axis=0, concat_axis=0, tiled=True
    ).reshape(32 * SLOTS, width_pair)
    row_expert = (slot_axis % SLOTS) // CAP

    def widen(array):
        return jnp.concatenate(
            [jnp.where((row_expert == j)[:, None], array, jnp.zeros_like(array)) for j in range(3)],
            axis=1,
        )

    pre = jnp.dot(widen(received), w_in, preferred_element_type=f32).astype(bf16)
    pre_parts = lax.all_to_all(
        pre.reshape(8, 128, 2 * ff_half), "y", split_axis=0, concat_axis=0, tiled=True
    )
    pre_sum = jnp.sum(pre_parts.astype(f32), axis=0)
    hidden = (jax.nn.silu(pre_sum[:, :ff_half]) * pre_sum[:, ff_half:]).astype(bf16)
    hidden_all = lax.all_to_all(
        jnp.broadcast_to(hidden[None], (8, 128, ff_half)), "y", split_axis=0, concat_axis=0, tiled=True
    ).reshape(32 * SLOTS, ff_half)
    expert_out = jnp.dot(widen(hidden_all), w_down, preferred_element_type=f32).astype(bf16)
    returned = lax.all_to_all(
        expert_out.reshape(32, SLOTS, width_pair), EXP, split_axis=0, concat_axis=0, tiled=True
    ).reshape(32 * SLOTS, width_pair)
    mixture = jnp.dot(weighting, returned.astype(f32), precision=lax.Precision.HIGHEST)
    low, high = mixture[:, :width_out], mixture[:, width_out:]
    mix_got = lax.ppermute(jnp.where(xl == 0, high, low).astype(bf16), "xl", SWAP)
    stream_rb = jnp.dot(back_order.astype(bf16), split[:, width_pair:], preferred_element_type=f32)
    result = (stream_rb + jnp.where(xl == 0, low, high) + mix_got.astype(f32)).astype(bf16)
    return result.reshape(8, 16, width_out)


def solution(mesh):
    grid = Mesh(mesh.devices.reshape(8, 2, 8, 2, 2), ("y", "xl", "z", "xh", "core"))
    return jax.shard_map(
        on_device,
        mesh=grid,
        in_specs=(
            P(CTX, EXP, None),
            P(CTX, None),
            P(CTX),
            P(EXP, None, None),
            P(EXP, None),
            P(CTX + EXP, None),
            P(),
            P(EXP, None, None),
            P(EXP, None, None),
            P(EXP, CTX, None),
            P(EXP, CTX, None),
            P(EXP, None, CTX),
        ),
        out_specs=P(EXP, None, CTX),
        check_vma=False,
    )
```

time: 550 us -> 295 us (0.54)
  waiting for transfers between devices: 381 us -> 122 us
  starting transfers between devices: 23.6 us -> 73.6 us
  between operations: 13.5 us -> 0.59 us
  blocking collectives: 53.4 us -> 42.6 us
  other arithmetic: 34.8 us -> 25.9 us
  matrix products: 18.6 us -> 11 us
    psum x1 -> x0, waiting for transfers between devices: 135 us -> none  [on_device(): lax.psum(up_part.astype(jnp.bfloat16), 'ctx').astype(jnp.float32)]
    reduce_scatter x1 -> x0, waiting for transfers between devices: 119 us -> none  [on_device(): lax.psum_scatter(jnp.dot(head_values, out_proj, preferred_element_type=jn...]
    all_gather x1 -> x0, waiting for transfers between devices: 109 us -> none  [on_device(): key_rows = lax.all_gather(latent, 'ctx', axis=0, tiled=True)]
    ppermute x0 -> x10, waiting for transfers between devices: none -> 65.3 us  [the longest x1 24.7 us: on_device(): lax.ppermute(jnp.concatenate([gate_send, up_send], axis=2), 'xl', SWAP)]
    all_to_all x3 -> x5, waiting for transfers between devices: 17.3 us -> 56.3 us  [the longest x1 22.5 us: on_device(): lax.all_to_all(expert_out.reshape(32, SLOTS, width_pair), EXP, split_axis...]
    ppermute x0 -> x10, starting transfers between devices: none -> 33 us  [the longest x4 16.7 us: on_device(): back = [lax.ppermute(mine, 'y', shift(8, k)) for k in (1, 2, 3, 4)]]
    all_gather x1 -> x0, blocking collectives: 32.3 us -> none  [on_device(): key_seg = lax.all_gather(segment_ids, 'ctx', axis=0, tiled=True)]
    all_to_all x1, blocking collectives: 21 us -> 42.6 us  [on_device(): lax.all_to_all(pre.reshape(8, 128, 2 * ff_half), 'y', split_axis=0, conca...]
  transfers between devices with their start and end apart: 6 -> 15, of which waited for: 5 -> 12; matrix products, arithmetic and copies ran while one was open for 6% -> 5% of each run, Pallas kernels for 0% -> 0%
where the time goes in v1:
time: 295 us; the launch traced here: 293 us
  waiting for transfers between devices  122 us (41%)
  starting transfers between devices  73.6 us (25%)
  blocking collectives  42.6 us (14%)
  other arithmetic  25.9 us (9%)
  local copies, waits for them, and re-layouts  17.5 us (6%)
  matrix products  11 us (4%)
    all_to_all x1, blocking collectives, on_device(): lax.all_to_all(pre.reshape(8, 128, 2 * ff_half), 'y', split_axis=0, conca...  42.6 us
    ppermute x1, waiting for transfers between devices, on_device(): lax.ppermute(jnp.concatenate([gate_send, up_send], axis=2), 'xl', SWAP)  24.7 us
    all_to_all x1, waiting for transfers between devices, on_device(): lax.all_to_all(expert_out.reshape(32, SLOTS, width_pair), EXP, split_axis...  22.5 us
    all_to_all x1, waiting for transfers between devices, on_device(): lax.all_to_all(pair_sum, ('z', 'xh'), split_axis=0, concat_axis=0, tiled=...  18.4 us
    ppermute x4, starting transfers between devices, on_device(): back = [lax.ppermute(mine, 'y', shift(8, k)) for k in (1, 2, 3, 4)]  16.7 us
    ppermute x4, waiting for transfers between devices, on_device(): back = [lax.ppermute(mine, 'y', shift(8, k)) for k in (1, 2, 3, 4)]  15.9 us
    all_to_all x1, starting transfers between devices, on_device(): lax.all_to_all(pair_sum, ('z', 'xh'), split_axis=0, concat_axis=0, tiled=...  13.3 us
    ppermute x1, waiting for transfers between devices, on_device(): other = lax.ppermute(other_send, 'xl', SWAP)  11.6 us
  transfers between devices with their start and end apart: 15, of which 12 were waited for; matrix products, arithmetic and copies ran while one was open for 5% of the time, Pallas kernels for 0%

profile of v1, /device:TPU:6, one launch (start us, length us, event | category | flops | bytes accessed | tf_op | source)
XLA Modules:
  0.0 292.7 jit_solution(10430082299831378325)
XLA Ops:
  2.2 3.5 %collective-permute-start = (bf16[128,640]{1,0:T(8,128)(2,1)S(1)}, bf16[128,640]{1,0:T(8,128)(2,1)S(1)}, u32[]{:S(2)}, u32[]{:S(2)}) collective-permute-start(bf16[128,640]{1,0:T(8,128)(2,1)S(1)} %fusion.38), channel_id=1, source_target_pairs={{0,64},{64,128},{128,192},{192,256},{256,320},{320,384},{384,448},... | collective-permute-start | bytes 491528 | tf_op jit(solution)/shard_map/ppermute | solution.py:69
  5.7 4.5 %collective-permute-start.1 = (bf16[128,640]{1,0:T(8,128)(2,1)S(1)}, bf16[128,640]{1,0:T(8,128)(2,1)S(1)}, u32[]{:S(2)}, u32[]{:S(2)}) collective-permute-start(bf16[128,640]{1,0:T(8,128)(2,1)S(1)} %fusion.38), channel_id=1, source_target_pairs={{0,128},{64,192},{128,256},{192,320},{256,384},{320,448},{384,0},{... | collective-permute-start | bytes 491528 | tf_op jit(solution)/shard_map/ppermute | solution.py:69
  10.2 4.9 %collective-permute-start.2 = (bf16[128,640]{1,0:T(8,128)(2,1)S(1)}, bf16[128,640]{1,0:T(8,128)(2,1)S(1)}, u32[]{:S(2)}, u32[]{:S(2)}) collective-permute-start(bf16[128,640]{1,0:T(8,128)(2,1)S(1)} %fusion.38), channel_id=1, source_target_pairs={{0,192},{64,256},{128,320},{192,384},{256,448},{320,0},{384,64},{4... | collective-permute-start | bytes 491528 | tf_op jit(solution)/shard_map/ppermute | solution.py:69
  15.1 3.8 %collective-permute-start.3 = (bf16[128,640]{1,0:T(8,128)(2,1)S(1)}, bf16[128,640]{1,0:T(8,128)(2,1)S(1)}, u32[]{:S(2)}, u32[]{:S(2)}) collective-permute-start(bf16[128,640]{1,0:T(8,128)(2,1)S(1)} %fusion.38), channel_id=1, source_target_pairs={{0,256},{64,320},{128,384},{192,448},{256,0},{320,64},{384,128},{4... | collective-permute-start | bytes 491528 | tf_op jit(solution)/shard_map/ppermute | solution.py:69
  19.1 11.2 %collective-permute-done.2 = bf16[128,640]{1,0:T(8,128)(2,1)S(1)} collective-permute-done((bf16[128,640]{1,0:T(8,128)(2,1)S(1)}, bf16[128,640]{1,0:T(8,128)(2,1)S(1)}, u32[]{:S(2)}, u32[]{:S(2)}) %collective-permute-start.2) | collective-permute-done | bytes 163872 | tf_op jit(solution)/shard_map/ppermute | solution.py:69
  30.3 4.7 %collective-permute-done.3 = bf16[128,640]{1,0:T(8,128)(2,1)S(1)} collective-permute-done((bf16[128,640]{1,0:T(8,128)(2,1)S(1)}, bf16[128,640]{1,0:T(8,128)(2,1)S(1)}, u32[]{:S(2)}, u32[]{:S(2)}) %collective-permute-start.3) | collective-permute-done | bytes 163872 | tf_op jit(solution)/shard_map/ppermute | solution.py:69
  35.2 2.7 collective-permute-start.4
  41.0 11.6 %collective-permute-done.4 = bf16[4,128,640]{2,1,0:T(8,128)(2,1)S(1)} collective-permute-done((bf16[4,128,640]{2,1,0:T(8,128)(2,1)S(1)}, bf16[4,128,640]{2,1,0:T(8,128)(2,1)S(1)}, u32[]{:S(2)}, u32[]{:S(2)}) %collective-permute-start.4) | collective-permute-done | bytes 655392 | tf_op jit(solution)/shard_map/ppermute | solution.py:72
  61.6 2.6 pad_maximum_fusion
  65.9 3.1 %fusion.103 = (f32[512]{0:T(512)S(1)}, f32[512,2304]{0,1:T(8,128)S(1)}) fusion(bf16[512,576]{1,0:T(8,128)(2,1)S(1)} %reshape.229, bf16[2304,640]{1,0:T(8,128)(2,1)S(1)} %pad_maximum_fusion, s32[512]{0:T(512)S(1)} %eq.135, s32[2304]{0:T(1024)S(1)} %convert_reduce_fusion.2, s32[512]{0:T(512)S(1)} %fusion.88, s32[2304]{0:T(1024)S(1)} %pad_add_fusion, ...), kind=kOutput, calls=%fused_computation.222 | convolution fusion | flops 1367211520 | bytes 8284416 | tf_op jit(solution)/shard_map/dot_general | solution.py:102
  77.4 13.3 %all-to-all-start = ((bf16[16,8,2560]{2,1,0:T(8,128)(2,1)}), bf16[16,8,2560]{2,1,0:T(8,128)(2,1)S(1)}, u32[]{:S(2)}, u32[]{:S(2)}) async-start(bf16[16,8,2560]{2,1,0:T(8,128)(2,1)} %fusion.33), calls=%async_computation | async-start | bytes 1310720 | tf_op jit(solution)/shard_map/all_to_all | solution.py:122
  91.8 18.4 %all-to-all-done = bf16[16,8,2560]{2,1,0:T(8,128)(2,1)S(1)} async-done(((bf16[16,8,2560]{2,1,0:T(8,128)(2,1)}), bf16[16,8,2560]{2,1,0:T(8,128)(2,1)S(1)}, u32[]{:S(2)}, u32[]{:S(2)}) %all-to-all-start) | async-done | bytes 655392 | tf_op jit(solution)/shard_map/all_to_all | solution.py:122
  122.0 9.1 %all-to-all-start.1 = ((bf16[16,8,480]{2,1,0:T(8,128)(2,1)}), bf16[16,8,480]{2,1,0:T(8,128)(2,1)S(1)}, u32[]{:S(2)}, u32[]{:S(2)}) async-start(bf16[16,8,480]{2,1,0:T(8,128)(2,1)} %constant_dynamic-update-slice_fusion.11), calls=%async_computation.1 | async-start | bytes 262144 | tf_op jit(solution)/shard_map/all_to_all | solution.py:141
  133.2 6.4 %all-to-all-done.1 = bf16[16,8,480]{2,1,0:T(8,128)(2,1)S(1)} async-done(((bf16[16,8,480]{2,1,0:T(8,128)(2,1)}), bf16[16,8,480]{2,1,0:T(8,128)(2,1)S(1)}, u32[]{:S(2)}, u32[]{:S(2)}) %all-to-all-start.1) | async-done | bytes 122912 | tf_op jit(solution)/shard_map/all_to_all | solution.py:141
  141.1 6.4 %all-to-all-start.2 = ((bf16[32,32,320]{2,1,0:T(8,128)(2,1)}), bf16[32,32,320]{2,1,0:T(8,128)(2,1)S(1)}, u32[]{:S(2)}, u32[]{:S(2)}) async-start(bf16[32,32,320]{2,1,0:T(8,128)(2,1)} %bitcast.32), calls=%async_computation.2 | async-start | bytes 1572864 | tf_op jit(solution)/shard_map/all_to_all | solution.py:168
  151.2 24.7 %collective-permute-done.7 = bf16[3,160,768]{2,1,0:T(8,128)(2,1)S(1)} collective-permute-done((bf16[3,160,768]{2,1,0:T(8,128)(2,1)S(1)}, bf16[3,160,768]{2,1,0:T(8,128)(2,1)S(1)}, u32[]{:S(2)}, u32[]{:S(2)}) %collective-permute-start.7) | collective-permute-done | bytes 737312 | tf_op jit(solution)/shard_map/ppermute | solution.py:55
  180.6 42.6 %all_to_all.30 = bf16[8,128,768]{2,1,0:T(8,128)(2,1)S(1)} all-to-all(bf16[8,128,768]{2,1,0:T(8,128)(2,1)S(1)} %bitcast.138), channel_id=1, replica_groups=mesh['y'=8,'xl'=2,'z'=8,'xh'=2,'core'=2] {'y'}, dimensions={0} | all-to-all | bytes 3145728 | tf_op jit(solution)/shard_map/all_to_all | solution.py:180
  224.5 3.5 %all-to-all-start.4 = ((bf16[8,128,384]{2,1,0:T(8,128)(2,1)}), bf16[8,128,384]{2,1,0:T(8,128)(2,1)S(1)}, u32[]{:S(2)}, u32[]{:S(2)}) async-start(bf16[8,128,384]{2,1,0:T(8,128)(2,1)} %broadcast_in_dim.129), calls=%async_computation.4 | async-start | bytes 1572864 | tf_op jit(solution)/shard_map/all_to_all | solution.py:185
  228.1 2.9 collective-permute-start.8
  231.0 7.9 %collective-permute-done.8 = bf16[3,384,160]{1,2,0:T(8,128)(2,1)S(1)} collective-permute-done((bf16[3,384,160]{1,2,0:T(8,128)(2,1)S(1)}, bf16[3,384,160]{1,2,0:T(8,128)(2,1)S(1)}, u32[]{:S(2)}, u32[]{:S(2)}) %collective-permute-start.8) | collective-permute-done | bytes 368672 | tf_op jit(solution)/shard_map/ppermute | solution.py:56
  241.0 8.9 %all-to-all-done.4 = bf16[8,128,384]{2,1,0:T(8,128)(2,1)S(1)} async-done(((bf16[8,128,384]{2,1,0:T(8,128)(2,1)}), bf16[8,128,384]{2,1,0:T(8,128)(2,1)S(1)}, u32[]{:S(2)}, u32[]{:S(2)}) %all-to-all-start.4) | async-done | bytes 786464 | tf_op jit(solution)/shard_map/all_to_all | solution.py:185
  253.1 8.2 %all-to-all-start.5 = ((bf16[32,32,320]{2,1,0:T(8,128)(2,1)}), bf16[32,32,320]{2,1,0:T(8,128)(2,1)S(1)}, u32[]{:S(2)}, u32[]{:S(2)}) async-start(bf16[32,32,320]{2,1,0:T(8,128)(2,1)} %bitcast.38), calls=%async_computation.5 | async-start | bytes 1572864 | tf_op jit(solution)/shard_map/all_to_all | solution.py:189
  262.2 22.5 %all-to-all-done.5 = bf16[32,32,320]{2,1,0:T(8,128)(2,1)S(1)} async-done(((bf16[32,32,320]{2,1,0:T(8,128)(2,1)}), bf16[32,32,320]{2,1,0:T(8,128)(2,1)S(1)}, u32[]{:S(2)}, u32[]{:S(2)}) %all-to-all-start.5) | async-done | bytes 655392 | tf_op jit(solution)/shard_map/all_to_all | solution.py:189
  285.6 4.1 %collective-permute-start.9 = (bf16[128,160]{0,1:T(8,128)(2,1)S(1)}, bf16[128,160]{0,1:T(8,128)(2,1)S(1)}, u32[]{:S(2)}, u32[]{:S(2)}) collective-permute-start(bf16[128,160]{0,1:T(8,128)(2,1)S(1)} %select_convert_fusion), channel_id=1, source_target_pairs={{0,32},{32,0},{1,33},{33,1},{2,34},{34,2},{3,35},{35,3},{4,36},{36... | collective-permute-start | bytes 122888 | tf_op jit(solution)/shard_map/ppermute | solution.py:194
  (126 shorter events, 60.4 us)
Async XLA Ops:
  0.0 71.9 %copy-start = (bf16[256,2560]{1,0:T(8,128)(2,1)S(1)}, bf16[256,2560]{1,0:T(8,128)(2,1)}, u32[]{:S(2)}) copy-start(bf16[256,2560]{1,0:T(8,128)(2,1)} %param.16) | copy-start | bytes 3932164
  2.2 16.9 %collective-permute-start = (bf16[128,640]{1,0:T(8,128)(2,1)S(1)}, bf16[128,640]{1,0:T(8,128)(2,1)S(1)}, u32[]{:S(2)}, u32[]{:S(2)}) collective-permute-start(bf16[128,640]{1,0:T(8,128)(2,1)S(1)} %fusion.38), channel_id=1, source_target_pairs={{0,64},{64,128},{128,192},{192,256},{256,320},{320,384},{384,448},... | collective-permute-start | bytes 491528 | tf_op jit(solution)/shard_map/ppermute | solution.py:69
  5.7 13.4 %collective-permute-start.1 = (bf16[128,640]{1,0:T(8,128)(2,1)S(1)}, bf16[128,640]{1,0:T(8,128)(2,1)S(1)}, u32[]{:S(2)}, u32[]{:S(2)}) collective-permute-start(bf16[128,640]{1,0:T(8,128)(2,1)S(1)} %fusion.38), channel_id=1, source_target_pairs={{0,128},{64,192},{128,256},{192,320},{256,384},{320,448},{384,0},{... | collective-permute-start | bytes 491528 | tf_op jit(solution)/shard_map/ppermute | solution.py:69
  10.2 20.1 %collective-permute-start.2 = (bf16[128,640]{1,0:T(8,128)(2,1)S(1)}, bf16[128,640]{1,0:T(8,128)(2,1)S(1)}, u32[]{:S(2)}, u32[]{:S(2)}) collective-permute-start(bf16[128,640]{1,0:T(8,128)(2,1)S(1)} %fusion.38), channel_id=1, source_target_pairs={{0,192},{64,256},{128,320},{192,384},{256,448},{320,0},{384,64},{4... | collective-permute-start | bytes 491528 | tf_op jit(solution)/shard_map/ppermute | solution.py:69
  15.1 19.9 %collective-permute-start.3 = (bf16[128,640]{1,0:T(8,128)(2,1)S(1)}, bf16[128,640]{1,0:T(8,128)(2,1)S(1)}, u32[]{:S(2)}, u32[]{:S(2)}) collective-permute-start(bf16[128,640]{1,0:T(8,128)(2,1)S(1)} %fusion.38), channel_id=1, source_target_pairs={{0,256},{64,320},{128,384},{192,448},{256,0},{320,64},{384,128},{4... | collective-permute-start | bytes 491528 | tf_op jit(solution)/shard_map/ppermute | solution.py:69
  35.0 20.7 %copy-start.5 = (bf16[256,2,576]{0,2,1:T(8,128)(2,1)S(1)}, bf16[256,2,576]{0,2,1:T(8,128)(2,1)}, u32[]{:S(2)}) copy-start(bf16[256,2,576]{0,2,1:T(8,128)(2,1)} %param.12) | copy-start | bytes 1769476
  35.2 17.4 %collective-permute-start.4 = (bf16[4,128,640]{2,1,0:T(8,128)(2,1)S(1)}, bf16[4,128,640]{2,1,0:T(8,128)(2,1)S(1)}, u32[]{:S(2)}, u32[]{:S(2)}) collective-permute-start(bf16[4,128,640]{2,1,0:T(8,128)(2,1)S(1)} %maximum_select_fusion), channel_id=1, source_target_pairs={{0,32},{32,0},{1,33},{33,1},{2,34},{34,2},{3,35},{35,3},{4,36},{36... | collective-permute-start | bytes 1966088 | tf_op jit(solution)/shard_map/ppermute | solution.py:72
  40.2 17.1 %copy-start.9 = (s32[256]{0:T(256)S(1)}, s32[256]{0:T(256)}, u32[]{:S(2)}) copy-start(s32[256]{0:T(256)} %param.14) | copy-start | bytes 3076
  53.8 5.3 %collective-permute-start.5 = (bf16[8,128,640]{2,1,0:T(8,128)(2,1)}, bf16[8,128,640]{2,1,0:T(8,128)(2,1)}, u32[]{:S(2)}, u32[]{:S(2)}) collective-permute-start(bf16[8,128,640]{2,1,0:T(8,128)(2,1)} %get-tuple-element.21), channel_id=1, source_target_pairs={{0,1},{1,0},{2,3},{3,2},{4,5},{5,4},{6,7},{7,6},{8,9},{9,8},{10,11... | collective-permute-start | bytes 3932168 | tf_op jit(solution)/shard_map/ppermute | solution.py:74
  71.9 18.8 %copy-start.8 = (s32[8,16,6]{1,0,2:T(8,128)S(1)}, s32[8,16,6]{1,0,2:T(8,128)}, u32[]{:S(2)}) copy-start(s32[8,16,6]{1,0,2:T(8,128)} %param.19) | copy-start | bytes 9220
  72.3 38.0 %copy-start.6 = (bf16[8,2560]{1,0:T(8,128)(2,1)S(1)}, bf16[8,2560]{1,0:T(8,128)(2,1)}, u32[]{:S(2)}) copy-start(bf16[8,2560]{1,0:T(8,128)(2,1)} %param.17) | copy-start | bytes 122884
  72.3 4.0 %collective-permute-start.6 = (bf16[128,2560]{1,0:T(8,128)(2,1)S(1)}, bf16[128,2560]{1,0:T(8,128)(2,1)S(1)}, u32[]{:S(2)}, u32[]{:S(2)}) collective-permute-start(bf16[128,2560]{1,0:T(8,128)(2,1)S(1)} %convolution_convert_fusion), channel_id=1, source_target_pairs={{0,1},{1,0},{2,3},{3,2},{4,5},{5,4},{6,7},{7,6},{8,9},{9,8},{10,11... | collective-permute-start | bytes 1966088 | tf_op jit(solution)/shard_map/ppermute | solution.py:120
  74.3 56.9 %copy-start.4 = (bf16[3,160,768]{2,1,0:T(8,128)(2,1)S(1)}, bf16[3,160,768]{2,1,0:T(8,128)(2,1)}, u32[]{:S(2)}) copy-start(bf16[3,160,768]{2,1,0:T(8,128)(2,1)} %param.22) | copy-start | bytes 2211844
  77.4 32.7 %all-to-all-start = ((bf16[16,8,2560]{2,1,0:T(8,128)(2,1)}), bf16[16,8,2560]{2,1,0:T(8,128)(2,1)S(1)}, u32[]{:S(2)}, u32[]{:S(2)}) async-start(bf16[16,8,2560]{2,1,0:T(8,128)(2,1)} %fusion.33), calls=%async_computation | async-start | bytes 1310720 | tf_op jit(solution)/shard_map/all_to_all | solution.py:122
  122.0 17.6 %all-to-all-start.1 = ((bf16[16,8,480]{2,1,0:T(8,128)(2,1)}), bf16[16,8,480]{2,1,0:T(8,128)(2,1)S(1)}, u32[]{:S(2)}, u32[]{:S(2)}) async-start(bf16[16,8,480]{2,1,0:T(8,128)(2,1)} %constant_dynamic-update-slice_fusion.11), calls=%async_computation.1 | async-start | bytes 262144 | tf_op jit(solution)/shard_map/all_to_all | solution.py:141
  141.1 36.3 %all-to-all-start.2 = ((bf16[32,32,320]{2,1,0:T(8,128)(2,1)}), bf16[32,32,320]{2,1,0:T(8,128)(2,1)S(1)}, u32[]{:S(2)}, u32[]{:S(2)}) async-start(bf16[32,32,320]{2,1,0:T(8,128)(2,1)} %bitcast.32), calls=%async_computation.2 | async-start | bytes 1572864 | tf_op jit(solution)/shard_map/all_to_all | solution.py:168
  148.6 27.3 %collective-permute-start.7 = (bf16[3,160,768]{2,1,0:T(8,128)(2,1)S(1)}, bf16[3,160,768]{2,1,0:T(8,128)(2,1)S(1)}, u32[]{:S(2)}, u32[]{:S(2)}) collective-permute-start(bf16[3,160,768]{2,1,0:T(8,128)(2,1)S(1)} %pad_maximum_fusion.3), channel_id=1, source_target_pairs={{0,32},{32,0},{1,33},{33,1},{2,34},{34,2},{3,35},{35,3},{4,36},{36... | collective-permute-start | bytes 2211848 | tf_op jit(solution)/shard_map/ppermute | solution.py:55
  223.2 4.8 %copy-start.1 = (bf16[3,768,160]{1,2,0:T(8,128)(2,1)S(1)}, bf16[3,768,160]{1,2,0:T(8,128)(2,1)}, u32[]{:S(2)}) copy-start(bf16[3,768,160]{1,2,0:T(8,128)(2,1)} %param.23) | copy-start | bytes 2211844
  224.5 25.5 %all-to-all-start.4 = ((bf16[8,128,384]{2,1,0:T(8,128)(2,1)}), bf16[8,128,384]{2,1,0:T(8,128)(2,1)S(1)}, u32[]{:S(2)}, u32[]{:S(2)}) async-start(bf16[8,128,384]{2,1,0:T(8,128)(2,1)} %broadcast_in_dim.129), calls=%async_computation.4 | async-start | bytes 1572864 | tf_op jit(solution)/shard_map/all_to_all | solution.py:185
  228.1 10.8 %collective-permute-start.8 = (bf16[3,384,160]{1,2,0:T(8,128)(2,1)S(1)}, bf16[3,384,160]{1,2,0:T(8,128)(2,1)S(1)}, u32[]{:S(2)}, u32[]{:S(2)}) collective-permute-start(bf16[3,384,160]{1,2,0:T(8,128)(2,1)S(1)} %broadcast_select_fusion.4), channel_id=1, source_target_pairs={{0,32},{32,0},{1,33},{33,1},{2,34},{34,2},{3,35},{35,3},{4,36},{36... | collective-permute-start | bytes 1105928 | tf_op jit(solution)/shard_map/ppermute | solution.py:56
  241.0 9.9 %copy-start.3 = (bf16[3,384,320]{2,1,0:T(8,128)(2,1)S(1)}, bf16[3,384,320]{2,1,0:T(8,128)(2,1)}, u32[]{:S(2)}) copy-start(bf16[3,384,320]{2,1,0:T(8,128)(2,1)} %copy.56) | copy-start | bytes 2211844
  252.0 9.7 %copy-start.7 = (f32[8,16,6]{1,0,2:T(8,128)S(1)}, f32[8,16,6]{1,0,2:T(8,128)}, u32[]{:S(2)}) copy-start(f32[8,16,6]{1,0,2:T(8,128)} %param.20) | copy-start | bytes 9220
  253.1 31.6 %all-to-all-start.5 = ((bf16[32,32,320]{2,1,0:T(8,128)(2,1)}), bf16[32,32,320]{2,1,0:T(8,128)(2,1)S(1)}, u32[]{:S(2)}, u32[]{:S(2)}) async-start(bf16[32,32,320]{2,1,0:T(8,128)(2,1)} %bitcast.38), calls=%async_computation.5 | async-start | bytes 1572864 | tf_op jit(solution)/shard_map/all_to_all | solution.py:189
  285.6 6.1 %collective-permute-start.9 = (bf16[128,160]{0,1:T(8,128)(2,1)S(1)}, bf16[128,160]{0,1:T(8,128)(2,1)S(1)}, u32[]{:S(2)}, u32[]{:S(2)}) collective-permute-start(bf16[128,160]{0,1:T(8,128)(2,1)S(1)} %select_convert_fusion), channel_id=1, source_target_pairs={{0,32},{32,0},{1,33},{33,1},{2,34},{34,2},{3,35},{35,3},{4,36},{36... | collective-permute-start | bytes 122888 | tf_op jit(solution)/shard_map/ppermute | solution.py:194
  (2 other events, 3.1 us)

commit v2 on v1

v2 whole, which is shorter than its diff:
```python
import jax
import jax.numpy as jnp
from jax import lax
from jax.experimental import pallas as pl
from jax.experimental.pallas import tpu as pltpu
from jax.sharding import Mesh, PartitionSpec as P

LATENT = 512
VDIM = 128
QKDIM = 192
EXPERTS = 96
TOPK = 6
CAP = 10
SLOTS = 32
SEGMENTS = 8
KEYW = 640
FAR = float(2**20)

CTX = ("y", "xl")
EXP = ("z", "xh", "core")
SWAP = [(0, 1), (1, 0)]
BIG_VMEM = pltpu.CompilerParams(vmem_limit_bytes=44 * 2**20)
f32, bf16, i32 = jnp.float32, jnp.bfloat16, jnp.int32


def nt_dot(a, b):
    return lax.dot_general(a, b, (((1,), (1,)), ((), ())), preferred_element_type=f32)


def attention_kernel(
    info, query, own, p0, p1, p2, p3, o0, o1, o2, o3, value_up, out_proj, send, keep, scores, values
):
    scale = QKDIM ** (-0.5)
    core = info[8]
    chunks = [own] + [p0, p1, p2, p3] + [o0, o1, o2, o3]
    lane = lax.broadcasted_iota(i32, (256, 256), 1)
    row = lax.broadcasted_iota(i32, (256, 256), 0)
    token = (row % 128) // 8 * 16 + row // 128 * 8 + row % 8

    @pl.loop(0, 2)
    def _(head):
        rows = query[head]
        peak = jnp.full((256, 128), -jnp.inf, f32)
        for n, chunk in enumerate(chunks):
            keys = chunk[...].reshape(256, KEYW)
            part = nt_dot(rows, keys) * scale
            if n == 0:
                part = jnp.where(lane <= token, part, -FAR)
            else:
                piece = (n - 1) % 4
                first = jnp.where(info[2 * piece] >= 0, 0.0, -FAR)
                second = jnp.where(info[2 * piece + 1] >= 0, 0.0, -FAR)
                part = part + jnp.where(lane < 128, first, second)
            scores[:, n * 256 : (n + 1) * 256] = part
            peak = jnp.maximum(peak, jnp.maximum(part[:, :128], part[:, 128:]))
        peak = jnp.max(peak, axis=1, keepdims=True)
        sums = jnp.zeros((256, 128), f32)
        mixed = jnp.zeros((256, LATENT), f32)
        for n, chunk in enumerate(chunks):
            keys = chunk[...].reshape(256, KEYW)
            terms = jnp.exp(scores[:, n * 256 : (n + 1) * 256] - peak)
            sums = sums + terms[:, :128] + terms[:, 128:]
            mixed = mixed + jnp.dot(terms.astype(bf16), keys[:, :LATENT], preferred_element_type=f32)
        mixed = (mixed / jnp.sum(sums, axis=1, keepdims=True)).astype(bf16)
        values[head] = jnp.dot(mixed, value_up[head], preferred_element_type=f32).astype(bf16)

    def project(which, out):
        start = pl.multiple_of(which * 128, 128)
        left = values[0, pl.ds(start, 128), :]
        right = values[1, pl.ds(start, 128), :]
        both = jnp.concatenate([left, right], axis=1)
        for c in range(0, out.shape[1], 640):
            out[:, c : c + 640] = jnp.dot(
                both, out_proj[:, c : c + 640], preferred_element_type=f32
            ).astype(out.dtype)

    project(1 - core, send)
    project(core, keep)


def norm_kernel(spread, residual, gain, packed):
    attended = jnp.sum(spread[...].astype(f32), axis=0)
    stream = (residual[...].astype(f32) + attended).astype(bf16).astype(f32)
    mean_sq = jnp.mean(stream * stream, axis=1, keepdims=True)
    normed = (stream * lax.rsqrt(mean_sq + 1e-06) * gain[...]).astype(bf16).astype(f32)
    width = stream.shape[1] // 16
    fill = jnp.zeros((stream.shape[0], packed.shape[2] - 3 * width), f32)
    for c in range(16):
        mine, other = c * width, (c ^ 1) * width
        packed[c] = jnp.concatenate(
            [
                normed[:, mine : mine + width],
                normed[:, other : other + width],
                stream[:, mine : mine + width],
                fill,
            ],
            axis=1,
        ).astype(bf16)


def row_masks(count):
    slot = lax.broadcasted_iota(i32, (count, 1), 0) % SLOTS
    return [(slot >= j * CAP) & (slot < (j + 1) * CAP) for j in range(3)]


def masked(rows, mask):
    return jnp.where(mask, rows.astype(f32), 0.0).astype(bf16)


def gate_up_kernel(received, weights, pre):
    width = pre.shape[1]

    @pl.loop(0, received.shape[0] // 256)
    def _(n):
        start = pl.multiple_of(n * 256, 256)
        rows = received[pl.ds(start, 256), :]
        masks = row_masks(256)
        total = jnp.zeros((256, width), f32)
        for j in range(3):
            total = total + jnp.dot(
                masked(rows, masks[j]), weights[j, :, :width], preferred_element_type=f32
            )
        pre[pl.ds(start, 256), :] = total.astype(bf16)


def hidden_kernel(parts, out):
    total = jnp.sum(parts[...].astype(f32), axis=0)
    half = total.shape[1] // 2
    gate, up = total[:, :half], total[:, half:]
    hidden = (gate / (1.0 + jnp.exp(-gate)) * up).astype(bf16)
    for n in range(out.shape[0]):
        out[n] = hidden


def down_kernel(hidden, weights, out):
    width = hidden.shape[1]

    @pl.loop(0, hidden.shape[0] // 256)
    def _(n):
        start = pl.multiple_of(n * 256, 256)
        rows = hidden[pl.ds(start, 256), :]
        masks = row_masks(256)
        total = jnp.zeros((256, out.shape[1]), f32)
        for j in range(3):
            total = total + nt_dot(masked(rows, masks[j]), weights[j, :, -width:])
        out[pl.ds(start, 256), :] = total.astype(bf16)


def combine_kernel(weighting, returned, keep, send):
    width = keep.shape[1]
    top = weighting[...].astype(bf16)
    rest = (weighting[...] - top.astype(f32)).astype(bf16)
    mixture = jnp.dot(top, returned[...], preferred_element_type=f32) + jnp.dot(
        rest, returned[...], preferred_element_type=f32
    )
    keep[...] = mixture[:, :width]
    send[...] = mixture[:, width:].astype(bf16)


def call(kernel, outs, scratch=(), smem_first=False, count=0):
    specs = [pl.BlockSpec(memory_space=pltpu.VMEM)] * count
    if smem_first:
        specs[0] = pl.BlockSpec(memory_space=pltpu.SMEM)
    out_specs = [pl.BlockSpec(memory_space=pltpu.VMEM)] * len(outs)
    single = len(outs) == 1
    return pl.pallas_call(
        kernel,
        in_specs=specs,
        out_specs=out_specs[0] if single else out_specs,
        out_shape=outs[0] if single else outs,
        scratch_shapes=list(scratch),
        compiler_params=BIG_VMEM,
    )


def sds(shape, dtype):
    return jax.ShapeDtypeStruct(shape, dtype)


def on_device(
    queries,
    latent,
    segment_ids,
    value_up,
    out_proj,
    residual,
    norm_gain,
    route_ids,
    route_gates,
    expert_gate,
    expert_up,
    expert_down,
):
    block_len, local_heads, width_key = queries.shape
    width_model = residual.shape[1]
    width_out = width_model // 16
    width_pair = 2 * width_out
    ff = expert_gate.shape[2]
    ff_half = ff // 2
    y, xl, xh, core = (lax.axis_index(a) for a in ("y", "xl", "xh", "core"))
    half = block_len // 2

    segment_axis = jnp.arange(SEGMENTS, dtype=i32)
    own_segment = segment_ids[:, None] == segment_axis[None, :]
    pad = KEYW - width_key - SEGMENTS
    keys_own = jnp.concatenate(
        [latent, own_segment.astype(bf16), jnp.zeros((block_len, pad), bf16)], axis=1
    )
    mine = lax.dynamic_slice_in_dim(keys_own, core * half, half, 0)

    def along_y(near, far):
        pairs = [
            (2 * i + h, 2 * ((i + (near, far)[h]) % 8) + h) for i in range(8) for h in range(2)
        ]
        return lax.ppermute(mine, ("y", "xh"), pairs)

    column = jnp.stack([along_y(1, 3), along_y(2, 4)])
    to_other = jnp.where(
        (xl == 0) & (xh == 1), jnp.stack([mine, column[0]]), column
    )
    diagonal = [(0, 3), (1, 2), (2, 1), (3, 0)]
    pieces = [
        column,
        lax.ppermute(column, "xh", SWAP),
        lax.ppermute(to_other, "xl", SWAP),
        lax.ppermute(to_other, ("xl", "xh"), diagonal),
    ]
    others = [lax.ppermute(piece, "core", SWAP) for piece in pieces]

    def blocks_of(x, h):
        return [2 * (y - 1 - 2 * h) + x, 2 * (y - 2 - 2 * h) + x]

    def blocks_sent(x, h):
        near, far = blocks_of(x, h)
        odd = (x == 0) & (h == 1)
        return [jnp.where(odd, 2 * y, near), jnp.where(odd, near, far)]

    info = jnp.stack(
        blocks_of(xl, xh)
        + blocks_of(xl, 1 - xh)
        + blocks_sent(1 - xl, xh)
        + blocks_sent(1 - xl, 1 - xh)
        + [core]
    ).astype(i32)

    masks = jnp.where(own_segment, 0.0, -FAR).astype(bf16)
    query_rows = jnp.concatenate(
        [
            queries,
            jnp.broadcast_to(masks[:, None, :], (block_len, local_heads, SEGMENTS)),
            jnp.zeros((block_len, local_heads, pad), bf16),
        ],
        axis=2,
    )
    query_rows = query_rows.reshape(16, 2, 8, local_heads, KEYW).transpose(3, 1, 0, 2, 4)
    query_rows = query_rows.reshape(local_heads, block_len, KEYW)
    send, keep = call(
        attention_kernel,
        [sds((half, width_model), bf16), sds((half, width_model), f32)],
        [pltpu.VMEM((256, 9 * 256), f32), pltpu.VMEM((2, 256, VDIM), bf16)],
        smem_first=True,
        count=13,
    )(info, query_rows, keys_own, *pieces, *others, value_up, out_proj)
    got = lax.ppermute(send, "core", SWAP)
    pair_sum = (keep + got.astype(f32)).astype(bf16).reshape(16, 8, width_model)

    weights = [expert_gate, expert_up, jnp.transpose(expert_down, (0, 2, 1))]
    low = jnp.concatenate([w[:, :, :ff_half] for w in weights], axis=2)
    high = jnp.concatenate([w[:, :, ff_half:] for w in weights], axis=2)
    w_send = jnp.where(xl == 0, high, low)
    w_keep = jnp.where(xl == 0, low, high)
    pair_sum, w_send = lax.optimization_barrier((pair_sum, w_send))
    w_got = lax.ppermute(w_send, "xl", SWAP)

    spread = lax.all_to_all(pair_sum, ("z", "xh"), split_axis=0, concat_axis=0, tiled=True)
    spread, w_got = lax.optimization_barrier((spread, w_got))
    w_all = jnp.concatenate([w_keep, w_got], axis=1)
    packed = call(norm_kernel, [sds((16, 8, 512), bf16)], count=3)(
        spread, residual, norm_gain[None, :]
    )
    split = lax.all_to_all(packed, CTX, split_axis=0, concat_axis=0, tiled=True)
    split = split.reshape(128, 512)

    routes = jnp.transpose(route_ids, (1, 0, 2)).reshape(128, TOPK)
    expert_axis = jnp.arange(EXPERTS, dtype=i32)
    named = jnp.any(routes[:, :, None] == expert_axis[None, None, :], axis=1)
    earlier_tokens = jnp.tril(jnp.ones((128, 128), bf16), -1)
    slot_all = jnp.dot(earlier_tokens, named.astype(bf16), preferred_element_type=f32).astype(i32)
    slot_of = jnp.sum(
        jnp.where(routes[:, :, None] == expert_axis[None, None, :], slot_all[:, None, :], 0), axis=2
    )
    target = (routes // 3) * SLOTS + (routes % 3) * CAP + slot_of
    slot_axis = jnp.arange(32 * SLOTS, dtype=i32)
    picker = jnp.any(target.T[None, :, :] == slot_axis[:, None, None], axis=1).astype(bf16)
    order = jnp.arange(128, dtype=i32)
    back_order = ((order % 16) * 8 + order // 16)[:, None] == order[None, :]
    target_rb = jnp.transpose(target.reshape(16, 8, TOPK), (1, 0, 2)).reshape(128, TOPK)
    gates_rb = route_gates.reshape(128, TOPK)
    weighting = jnp.sum(
        jnp.where(target_rb[:, :, None] == slot_axis[None, None, :], gates_rb[:, :, None], 0.0),
        axis=1,
    )

    outgoing = jnp.dot(picker, split[:, :width_pair], preferred_element_type=f32).astype(bf16)
    received = lax.all_to_all(
        outgoing.reshape(32, SLOTS, width_pair), EXP, split_axis=0, concat_axis=0, tiled=True
    ).reshape(32 * SLOTS, width_pair)
    pre = call(gate_up_kernel, [sds((32 * SLOTS, 2 * ff_half), bf16)], count=2)(received, w_all)
    pre_parts = lax.all_to_all(
        pre.reshape(8, 128, 2 * ff_half), "y", split_axis=0, concat_axis=0, tiled=True
    )
    hidden = call(hidden_kernel, [sds((8, 128, ff_half), bf16)], count=1)(pre_parts)
    hidden_all = lax.all_to_all(hidden, "y", split_axis=0, concat_axis=0, tiled=True)
    expert_out = call(down_kernel, [sds((32 * SLOTS, width_pair), bf16)], count=2)(
        hidden_all.reshape(32 * SLOTS, ff_half), w_all
    )
    returned = lax.all_to_all(
        expert_out.reshape(32, SLOTS, width_pair), EXP, split_axis=0, concat_axis=0, tiled=True
    ).reshape(32 * SLOTS, width_pair)
    mix_keep, mix_send = call(
        combine_kernel, [sds((128, width_out), f32), sds((128, width_out), bf16)], count=2
    )(weighting, returned)
    mix_got = lax.ppermute(mix_send, "xl", SWAP)
    stream_rb = jnp.dot(
        back_order.astype(bf16),
        split[:, width_pair : width_pair + width_out],
        preferred_element_type=f32,
    )
    result = (stream_rb + mix_keep + mix_got.astype(f32)).astype(bf16)
    return result.reshape(8, 16, width_out)


def solution(mesh):
    grid = Mesh(mesh.devices.reshape(8, 2, 8, 2, 2), ("y", "xl", "z", "xh", "core"))
    return jax.shard_map(
        on_device,
        mesh=grid,
        in_specs=(
            P(CTX, EXP, None),
            P(CTX, None),
            P(CTX),
            P(EXP, None, None),
            P(EXP, None),
            P(CTX + EXP, None),
            P(),
            P(EXP, None, None),
            P(EXP, None, None),
            P(EXP, CTX, None),
            P(EXP, CTX, None),
            P(EXP, None, CTX),
        ),
        out_specs=P(EXP, None, CTX),
        check_vma=False,
    )
```

time: 295 us -> 277 us (0.939)
  blocking collectives: 42.6 us -> 66.9 us
  waiting for transfers between devices: 122 us -> 101 us
  other arithmetic: 25.9 us -> 7.16 us
  Pallas kernels: 0 us -> 16.5 us
  local copies, waits for them, and re-layouts: 17.5 us -> 4.68 us
  matrix products: 11 us -> 1.44 us
  starting transfers between devices: 73.6 us -> 77.8 us
    all_to_all x0 -> x1, blocking collectives: none -> 24.3 us  [on_device(): lax.all_to_all(hidden, 'y', split_axis=0, concat_axis=0, tiled=True)]
    all_to_all x1, waiting for transfers between devices: 0.01 us -> 21.6 us  [on_device(): lax.all_to_all(outgoing.reshape(32, SLOTS, width_pair), EXP, split_axis=0...]
    all_to_all x1, waiting for transfers between devices: 18.4 us -> 0.01 us  [on_device(): lax.all_to_all(pair_sum, ('z', 'xh'), split_axis=0, concat_axis=0, tiled=...]
    pallas_call x0 -> x6, Pallas kernels: none -> 16.5 us  [the longest x1 8.69 us: on_device(): call(attention_kernel, [sds((half, width_model), bf16), sds((half, width_...]
    ppermute x10 -> x12, waiting for transfers between devices: 65.3 us -> 48.7 us  [the longest x1 30.9 us: on_device(): w_got = lax.ppermute(w_send, 'xl', SWAP)]
    unnamed x15 -> x0, other arithmetic: 9.98 us -> none
    dot_general x10 -> x2, matrix products: 10.8 us -> 1.24 us  [the longest x1 0.86 us: on_device(): jnp.dot(back_order.astype(bf16), split[:, width_pair:width_pair + width_o...]
    all_to_all x1 -> x0, waiting for transfers between devices: 8.95 us -> none  [on_device(): lax.all_to_all(jnp.broadcast_to(hidden[None], (8, 128, ff_half)), 'y', sp...]
  transfers between devices with their start and end apart: 15 -> 16, of which waited for: 12 -> 8; matrix products, arithmetic and copies ran while one was open for 5% -> 3% of each run, Pallas kernels for 0% -> 0%
where the time goes in v2:
time: 277 us; the launch traced here: 276 us
  waiting for transfers between devices  101 us (36%)
  starting transfers between devices  77.8 us (28%)
  blocking collectives  66.9 us (24%)
  Pallas kernels  16.5 us (6%)
  other arithmetic  7.16 us (3%)
  local copies, waits for them, and re-layouts  4.68 us (2%)
    all_to_all x1, blocking collectives, on_device(): lax.all_to_all(pre.reshape(8, 128, 2 * ff_half), 'y', split_axis=0, conca...  42.6 us
    ppermute x1, waiting for transfers between devices, on_device(): w_got = lax.ppermute(w_send, 'xl', SWAP)  30.9 us
    all_to_all x1, blocking collectives, on_device(): lax.all_to_all(hidden, 'y', split_axis=0, concat_axis=0, tiled=True)  24.3 us
    all_to_all x1, waiting for transfers between devices, on_device(): lax.all_to_all(expert_out.reshape(32, SLOTS, width_pair), EXP, split_axis...  22.5 us
    all_to_all x1, waiting for transfers between devices, on_device(): lax.all_to_all(outgoing.reshape(32, SLOTS, width_pair), EXP, split_axis=0...  21.6 us
    all_to_all x1, starting transfers between devices, on_device(): lax.all_to_all(pair_sum, ('z', 'xh'), split_axis=0, concat_axis=0, tiled=...  13.6 us
    ppermute x2, waiting for transfers between devices, along_y(): return lax.ppermute(mine, ('y', 'xh'), pairs)  12.6 us
    all_to_all x1, starting transfers between devices, on_device(): split = lax.all_to_all(packed, CTX, split_axis=0, concat_axis=0, tiled=True)  10.8 us
  transfers between devices with their start and end apart: 16, of which 8 were waited for; matrix products, arithmetic and copies ran while one was open for 3% of the time, Pallas kernels for 0%

profile of v2, /device:TPU:6, one launch (start us, length us, event | category | flops | bytes accessed | tf_op | source)
XLA Modules:
  0.0 275.7 jit_solution(10378884274906468988)
XLA Ops:
  2.2 5.5 %collective-permute-start = (bf16[128,640]{1,0:T(8,128)(2,1)S(1)}, bf16[128,640]{1,0:T(8,128)(2,1)S(1)}, u32[]{:S(2)}, u32[]{:S(2)}) collective-permute-start(bf16[128,640]{1,0:T(8,128)(2,1)S(1)} %constant_dynamic-slice_fusion), channel_id=1, source_target_pairs={{0,64},{2,194},{64,128},{66,258},{128,192},{130,322},{192,256},{19... | collective-permute-start | bytes 491528 | tf_op jit(solution)/shard_map/ppermute | solution.py:215
  7.8 5.0 %collective-permute-start.1 = (bf16[128,640]{1,0:T(8,128)(2,1)S(1)}, bf16[128,640]{1,0:T(8,128)(2,1)S(1)}, u32[]{:S(2)}, u32[]{:S(2)}) collective-permute-start(bf16[128,640]{1,0:T(8,128)(2,1)S(1)} %constant_dynamic-slice_fusion), channel_id=1, source_target_pairs={{0,128},{2,258},{64,192},{66,322},{128,256},{130,386},{192,320},{1... | collective-permute-start | bytes 491528 | tf_op jit(solution)/shard_map/ppermute | solution.py:215
  12.8 5.4 %collective-permute-done = bf16[128,640]{1,0:T(8,128)(2,1)S(1)} collective-permute-done((bf16[128,640]{1,0:T(8,128)(2,1)S(1)}, bf16[128,640]{1,0:T(8,128)(2,1)S(1)}, u32[]{:S(2)}, u32[]{:S(2)}) %collective-permute-start) | collective-permute-done | bytes 163872 | tf_op jit(solution)/shard_map/ppermute | solution.py:215
  18.3 7.1 %collective-permute-done.1 = bf16[128,640]{1,0:T(8,128)(2,1)S(1)} collective-permute-done((bf16[128,640]{1,0:T(8,128)(2,1)S(1)}, bf16[128,640]{1,0:T(8,128)(2,1)S(1)}, u32[]{:S(2)}, u32[]{:S(2)}) %collective-permute-start.1) | collective-permute-done | bytes 163872 | tf_op jit(solution)/shard_map/ppermute | solution.py:215
  27.4 2.7 collective-permute-start.3
  30.2 5.2 %collective-permute-start.4 = (bf16[2,128,640]{2,1,0:T(8,128)(2,1)S(1)}, bf16[2,128,640]{2,1,0:T(8,128)(2,1)}, u32[]{:S(2)}, u32[]{:S(2)}) collective-permute-start(bf16[2,128,640]{2,1,0:T(8,128)(2,1)S(1)} %get-tuple-element.29), channel_id=1, source_target_pairs={{0,34},{2,32},{32,2},{34,0},{1,35},{3,33},{33,3},{35,1},{4,38},{6,... | collective-permute-start | bytes 983048 | tf_op jit(solution)/shard_map/ppermute | solution.py:226
  41.5 2.4 collective-permute-start.7
  48.3 8.7 %shard_map.118 = (bf16[128,2560]{1,0:T(8,128)(2,1)S(1)}, f32[128,2560]{1,0:T(8,128)S(1)}) custom-call(s32[9]{0:T(128)S(1)} %stack.54.info, bf16[2,256,640]{2,1,0:T(8,128)(2,1)S(1)} %bitcast.48, bf16[256,640]{1,0:T(8,128)(2,1)S(1)} %maximum_maximum_fusion.1.own, bf16[2,128,640]{2,1,0:T(8,128)(2,1)S(1)} %get-tuple-element.30.p0, ...), custom_call_target="tpu_custom_call" | custom-call | tf_op jit(solution)/shard_map/pallas_call | solution.py:257
  57.0 2.5 collective-permute-start.9
  62.3 13.6 %all-to-all-start = ((bf16[16,8,2560]{2,1,0:T(8,128)(2,1)}), bf16[16,8,2560]{2,1,0:T(8,128)(2,1)S(1)}, u32[]{:S(2)}, u32[]{:S(2)}) async-start(bf16[16,8,2560]{2,1,0:T(8,128)(2,1)} %fusion.1), calls=%async_computation | async-start | bytes 1310720 | tf_op jit(solution)/shard_map/all_to_all | solution.py:275
  75.8 2.5 collective-permute-start.10
  78.8 30.9 %collective-permute-done.10 = bf16[3,160,1152]{2,1,0:T(8,128)(2,1)S(1)} collective-permute-done((bf16[3,160,1152]{2,1,0:T(8,128)(2,1)S(1)}, bf16[3,160,1152]{2,1,0:T(8,128)(2,1)S(1)}, u32[]{:S(2)}, u32[]{:S(2)}) %collective-permute-start.10) | collective-permute-done | bytes 1105952 | tf_op jit(solution)/shard_map/ppermute | solution.py:273
  110.8 10.8 %all-to-all-start.1 = ((bf16[16,8,512]{2,1,0:T(8,128)(2,1)}), bf16[16,8,512]{2,1,0:T(8,128)(2,1)S(1)}, u32[]{:S(2)}, u32[]{:S(2)}) async-start(bf16[16,8,512]{2,1,0:T(8,128)(2,1)} %shard_map.119), calls=%async_computation.1 | async-start | bytes 262144 | tf_op jit(solution)/shard_map/all_to_all | solution.py:281
  122.2 7.9 %all-to-all-done.1 = bf16[16,8,512]{2,1,0:T(8,128)(2,1)S(1)} async-done(((bf16[16,8,512]{2,1,0:T(8,128)(2,1)}), bf16[16,8,512]{2,1,0:T(8,128)(2,1)S(1)}, u32[]{:S(2)}, u32[]{:S(2)}) %all-to-all-start.1) | async-done | bytes 131104 | tf_op jit(solution)/shard_map/all_to_all | solution.py:281
  131.6 9.8 %all-to-all-start.2 = ((bf16[32,32,320]{2,1,0:T(8,128)(2,1)}), bf16[32,32,320]{2,1,0:T(8,128)(2,1)S(1)}, u32[]{:S(2)}, u32[]{:S(2)}) async-start(bf16[32,32,320]{2,1,0:T(8,128)(2,1)} %bitcast.21), calls=%async_computation.2 | async-start | bytes 1572864 | tf_op jit(solution)/shard_map/all_to_all | solution.py:305
  143.2 21.6 %all-to-all-done.2 = bf16[32,32,320]{2,1,0:T(8,128)(2,1)S(1)} async-done(((bf16[32,32,320]{2,1,0:T(8,128)(2,1)}), bf16[32,32,320]{2,1,0:T(8,128)(2,1)S(1)}, u32[]{:S(2)}, u32[]{:S(2)}) %all-to-all-start.2) | async-done | bytes 655392 | tf_op jit(solution)/shard_map/all_to_all | solution.py:305
  164.7 3.0 %shard_map.120 = bf16[1024,768]{1,0:T(8,128)(2,1)S(1)} custom-call(bf16[1024,320]{1,0:T(8,128)(2,1)S(1)} %bitcast.45, bf16[3,320,1152]{2,1,0:T(8,128)(2,1)S(1)} %pad_maximum_fusion.weights), custom_call_target="tpu_custom_call" | custom-call | tf_op jit(solution)/shard_map/pallas_call | solution.py:308
  167.8 42.6 %all_to_all.30.parts = bf16[8,128,768]{2,1,0:T(8,128)(2,1)S(1)} all-to-all(bf16[8,128,768]{2,1,0:T(8,128)(2,1)S(1)} %bitcast.44), channel_id=1, replica_groups=mesh['y'=8,'xl'=2,'z'=8,'xh'=2,'core'=2] {'y'}, dimensions={0} | all-to-all | bytes 3145728 | tf_op jit(solution)/shard_map/all_to_all | solution.py:309
  210.6 24.3 %all_to_all.31 = bf16[8,128,384]{2,1,0:T(8,128)(2,1)S(1)} all-to-all(bf16[8,128,384]{2,1,0:T(8,128)(2,1)S(1)} %shard_map.121), channel_id=1, replica_groups=mesh['y'=8,'xl'=2,'z'=8,'xh'=2,'core'=2] {'y'}, dimensions={0} | all-to-all | bytes 1572864 | tf_op jit(solution)/shard_map/all_to_all | solution.py:313
  235.0 3.0 %shard_map.122 = bf16[1024,320]{1,0:T(8,128)(2,1)} custom-call(bf16[1024,384]{1,0:T(8,128)(2,1)S(1)} %bitcast.47, bf16[3,320,1152]{2,1,0:T(8,128)(2,1)S(1)} %pad_maximum_fusion.weights), custom_call_target="tpu_custom_call" | custom-call | tf_op jit(solution)/shard_map/pallas_call | solution.py:314
  238.0 6.9 %all-to-all-start.5 = ((bf16[32,32,320]{2,1,0:T(8,128)(2,1)}), bf16[32,32,320]{2,1,0:T(8,128)(2,1)S(1)}, u32[]{:S(2)}, u32[]{:S(2)}) async-start(bf16[32,32,320]{2,1,0:T(8,128)(2,1)} %bitcast.25), calls=%async_computation.5 | async-start | bytes 1572864 | tf_op jit(solution)/shard_map/all_to_all | solution.py:317
  245.7 22.5 %all-to-all-done.5 = bf16[32,32,320]{2,1,0:T(8,128)(2,1)S(1)} async-done(((bf16[32,32,320]{2,1,0:T(8,128)(2,1)}), bf16[32,32,320]{2,1,0:T(8,128)(2,1)S(1)}, u32[]{:S(2)}, u32[]{:S(2)}) %all-to-all-start.5) | async-done | bytes 655392 | tf_op jit(solution)/shard_map/all_to_all | solution.py:317
  268.7 3.2 %collective-permute-start.11 = (bf16[128,160]{1,0:T(8,128)(2,1)S(1)}, bf16[128,160]{1,0:T(8,128)(2,1)S(1)}, u32[]{:S(2)}, u32[]{:S(2)}) collective-permute-start(bf16[128,160]{1,0:T(8,128)(2,1)S(1)} %get-tuple-element.20), channel_id=1, source_target_pairs={{0,32},{32,0},{1,33},{33,1},{2,34},{34,2},{3,35},{35,3},{4,36},{36... | collective-permute-start | bytes 122888 | tf_op jit(solution)/shard_map/ppermute | solution.py:323
  271.9 2.9 %collective-permute-done.11 = bf16[128,160]{1,0:T(8,128)(2,1)S(1)} collective-permute-done((bf16[128,160]{1,0:T(8,128)(2,1)S(1)}, bf16[128,160]{1,0:T(8,128)(2,1)S(1)}, u32[]{:S(2)}, u32[]{:S(2)}) %collective-permute-start.11) | collective-permute-done | bytes 40992 | tf_op jit(solution)/shard_map/ppermute | solution.py:323
  (78 shorter events, 25.0 us)
Async XLA Ops:
  0.0 45.8 %copy-start.11 = (s32[256]{0:T(256)S(1)}, s32[256]{0:T(256)}, u32[]{:S(2)}) copy-start(s32[256]{0:T(256)} %param.14) | copy-start | bytes 3076
  0.0 46.6 %copy-start.7 = (bf16[256,2,576]{0,2,1:T(8,128)(2,1)S(1)}, bf16[256,2,576]{0,2,1:T(8,128)(2,1)}, u32[]{:S(2)}) copy-start(bf16[256,2,576]{0,2,1:T(8,128)(2,1)} %param.12) | copy-start | bytes 1769476
  2.2 16.0 %collective-permute-start = (bf16[128,640]{1,0:T(8,128)(2,1)S(1)}, bf16[128,640]{1,0:T(8,128)(2,1)S(1)}, u32[]{:S(2)}, u32[]{:S(2)}) collective-permute-start(bf16[128,640]{1,0:T(8,128)(2,1)S(1)} %constant_dynamic-slice_fusion), channel_id=1, source_target_pairs={{0,64},{2,194},{64,128},{66,258},{128,192},{130,322},{192,256},{19... | collective-permute-start | bytes 491528 | tf_op jit(solution)/shard_map/ppermute | solution.py:215
  7.8 17.7 %collective-permute-start.1 = (bf16[128,640]{1,0:T(8,128)(2,1)S(1)}, bf16[128,640]{1,0:T(8,128)(2,1)S(1)}, u32[]{:S(2)}, u32[]{:S(2)}) collective-permute-start(bf16[128,640]{1,0:T(8,128)(2,1)S(1)} %constant_dynamic-slice_fusion), channel_id=1, source_target_pairs={{0,128},{2,258},{64,192},{66,322},{128,256},{130,386},{192,320},{1... | collective-permute-start | bytes 491528 | tf_op jit(solution)/shard_map/ppermute | solution.py:215
  25.5 14.0 %collective-permute-start.2 = (bf16[2,128,640]{2,1,0:T(8,128)(2,1)S(1)}, bf16[2,128,640]{2,1,0:T(8,128)(2,1)S(1)}, u32[]{:S(2)}, u32[]{:S(2)}) collective-permute-start(bf16[2,128,640]{2,1,0:T(8,128)(2,1)S(1)} %get-tuple-element.30.p0), channel_id=1, source_target_pairs={{0,2},{2,0},{1,3},{3,1},{4,6},{6,4},{5,7},{7,5},{8,10},{10,8},{9,1... | collective-permute-start | bytes 983048 | tf_op jit(solution)/shard_map/ppermute | solution.py:224
  27.4 14.0 %collective-permute-start.3 = (bf16[2,128,640]{2,1,0:T(8,128)(2,1)S(1)}, bf16[2,128,640]{2,1,0:T(8,128)(2,1)S(1)}, u32[]{:S(2)}, u32[]{:S(2)}) collective-permute-start(bf16[2,128,640]{2,1,0:T(8,128)(2,1)S(1)} %get-tuple-element.29), channel_id=1, source_target_pairs={{0,32},{32,0},{1,33},{33,1},{2,34},{34,2},{3,35},{35,3},{4,36},{36... | collective-permute-start | bytes 983048 | tf_op jit(solution)/shard_map/ppermute | solution.py:225
  30.2 13.7 %collective-permute-start.4 = (bf16[2,128,640]{2,1,0:T(8,128)(2,1)S(1)}, bf16[2,128,640]{2,1,0:T(8,128)(2,1)}, u32[]{:S(2)}, u32[]{:S(2)}) collective-permute-start(bf16[2,128,640]{2,1,0:T(8,128)(2,1)S(1)} %get-tuple-element.29), channel_id=1, source_target_pairs={{0,34},{2,32},{32,2},{34,0},{1,35},{3,33},{33,3},{35,1},{4,38},{6,... | collective-permute-start | bytes 983048 | tf_op jit(solution)/shard_map/ppermute | solution.py:226
  35.3 12.9 %collective-permute-start.5 = (bf16[2,128,640]{2,1,0:T(8,128)(2,1)S(1)}, bf16[2,128,640]{2,1,0:T(8,128)(2,1)}, u32[]{:S(2)}, u32[]{:S(2)}) collective-permute-start(bf16[2,128,640]{2,1,0:T(8,128)(2,1)S(1)} %get-tuple-element.30.p0), channel_id=1, source_target_pairs={{0,1},{1,0},{2,3},{3,2},{4,5},{5,4},{6,7},{7,6},{8,9},{9,8},{10,11... | collective-permute-start | bytes 983048 | tf_op jit(solution)/shard_map/ppermute | solution.py:228
  39.5 8.7 %collective-permute-start.6 = (bf16[2,128,640]{2,1,0:T(8,128)(2,1)S(1)}, bf16[2,128,640]{2,1,0:T(8,128)(2,1)}, u32[]{:S(2)}, u32[]{:S(2)}) collective-permute-start(bf16[2,128,640]{2,1,0:T(8,128)(2,1)S(1)} %collective-permute-done.2.p1), channel_id=1, source_target_pairs={{0,1},{1,0},{2,3},{3,2},{4,5},{5,4},{6,7},{7,6},{8,9},{9,8},{10,11... | collective-permute-start | bytes 983048 | tf_op jit(solution)/shard_map/ppermute | solution.py:228
  41.5 6.7 %collective-permute-start.7 = (bf16[2,128,640]{2,1,0:T(8,128)(2,1)S(1)}, bf16[2,128,640]{2,1,0:T(8,128)(2,1)}, u32[]{:S(2)}, u32[]{:S(2)}) collective-permute-start(bf16[2,128,640]{2,1,0:T(8,128)(2,1)S(1)} %collective-permute-done.3.p2), channel_id=1, source_target_pairs={{0,1},{1,0},{2,3},{3,2},{4,5},{5,4},{6,7},{7,6},{8,9},{9,8},{10,11... | collective-permute-start | bytes 983048 | tf_op jit(solution)/shard_map/ppermute | solution.py:228
  43.9 4.3 %collective-permute-start.8 = (bf16[2,128,640]{2,1,0:T(8,128)(2,1)}, bf16[2,128,640]{2,1,0:T(8,128)(2,1)}, u32[]{:S(2)}, u32[]{:S(2)}) collective-permute-start(bf16[2,128,640]{2,1,0:T(8,128)(2,1)} %collective-permute-done.4.p3), channel_id=1, source_target_pairs={{0,1},{1,0},{2,3},{3,2},{4,5},{5,4},{6,7},{7,6},{8,9},{9,8},{10,11... | collective-permute-start | bytes 983048 | tf_op jit(solution)/shard_map/ppermute | solution.py:228
  48.3 11.3 %copy-start.4 = (bf16[3,768,160]{1,2,0:T(8,128)(2,1)S(1)}, bf16[3,768,160]{1,2,0:T(8,128)(2,1)}, u32[]{:S(2)}) copy-start(bf16[3,768,160]{1,2,0:T(8,128)(2,1)} %param.23) | copy-start | bytes 2211844
  57.0 4.3 %collective-permute-start.9 = (bf16[128,2560]{1,0:T(8,128)(2,1)S(1)}, bf16[128,2560]{1,0:T(8,128)(2,1)S(1)}, u32[]{:S(2)}, u32[]{:S(2)}) collective-permute-start(bf16[128,2560]{1,0:T(8,128)(2,1)S(1)} %get-tuple-element.14), channel_id=1, source_target_pairs={{0,1},{1,0},{2,3},{3,2},{4,5},{5,4},{6,7},{7,6},{8,9},{9,8},{10,11... | collective-permute-start | bytes 1966088 | tf_op jit(solution)/shard_map/ppermute | solution.py:264
  61.3 17.0 %copy-start.10 = (f32[2560]{0:T(1024)S(1)}, f32[2560]{0:T(1024)}, u32[]{:S(2)}) copy-start(f32[2560]{0:T(1024)} %param.18) | copy-start | bytes 30724
  61.3 17.1 %copy-start.9 = (s32[8,16,6]{1,0,2:T(8,128)S(1)}, s32[8,16,6]{1,0,2:T(8,128)}, u32[]{:S(2)}) copy-start(s32[8,16,6]{1,0,2:T(8,128)} %param.19) | copy-start | bytes 9220
  61.3 48.5 %copy-start.2 = (bf16[8,2560]{1,0:T(8,128)(2,1)S(1)}, bf16[8,2560]{1,0:T(8,128)(2,1)}, u32[]{:S(2)}) copy-start(bf16[8,2560]{1,0:T(8,128)(2,1)} %residual.1) | copy-start | bytes 122884
  62.3 47.5 %all-to-all-start = ((bf16[16,8,2560]{2,1,0:T(8,128)(2,1)}), bf16[16,8,2560]{2,1,0:T(8,128)(2,1)S(1)}, u32[]{:S(2)}, u32[]{:S(2)}) async-start(bf16[16,8,2560]{2,1,0:T(8,128)(2,1)} %fusion.1), calls=%async_computation | async-start | bytes 1310720 | tf_op jit(solution)/shard_map/all_to_all | solution.py:275
  75.8 33.9 %collective-permute-start.10 = (bf16[3,160,1152]{2,1,0:T(8,128)(2,1)S(1)}, bf16[3,160,1152]{2,1,0:T(8,128)(2,1)S(1)}, u32[]{:S(2)}, u32[]{:S(2)}) collective-permute-start(bf16[3,160,1152]{2,1,0:T(8,128)(2,1)S(1)} %get-tuple-element.16), channel_id=1, source_target_pairs={{0,32},{32,0},{1,33},{33,1},{2,34},{34,2},{3,35},{35,3},{4,36},{36... | collective-permute-start | bytes 3317768 | tf_op jit(solution)/shard_map/ppermute | solution.py:273
  109.8 21.9 %copy-start.3 = (bf16[3,160,1152]{2,1,0:T(8,128)(2,1)}, bf16[3,160,1152]{2,1,0:T(8,128)(2,1)S(1)}, u32[]{:S(2)}) copy-start(bf16[3,160,1152]{2,1,0:T(8,128)(2,1)S(1)} %collective-permute-done.10) | copy-start | bytes 3317764
  110.8 19.3 %all-to-all-start.1 = ((bf16[16,8,512]{2,1,0:T(8,128)(2,1)}), bf16[16,8,512]{2,1,0:T(8,128)(2,1)S(1)}, u32[]{:S(2)}, u32[]{:S(2)}) async-start(bf16[16,8,512]{2,1,0:T(8,128)(2,1)} %shard_map.119), calls=%async_computation.1 | async-start | bytes 262144 | tf_op jit(solution)/shard_map/all_to_all | solution.py:281
  131.6 33.1 %all-to-all-start.2 = ((bf16[32,32,320]{2,1,0:T(8,128)(2,1)}), bf16[32,32,320]{2,1,0:T(8,128)(2,1)S(1)}, u32[]{:S(2)}, u32[]{:S(2)}) async-start(bf16[32,32,320]{2,1,0:T(8,128)(2,1)} %bitcast.21), calls=%async_computation.2 | async-start | bytes 1572864 | tf_op jit(solution)/shard_map/all_to_all | solution.py:305
  238.0 7.2 %copy-start.8 = (f32[8,16,6]{1,0,2:T(8,128)S(1)}, f32[8,16,6]{1,0,2:T(8,128)}, u32[]{:S(2)}) copy-start(f32[8,16,6]{1,0,2:T(8,128)} %param.20) | copy-start | bytes 9220
  238.0 30.2 %all-to-all-start.5 = ((bf16[32,32,320]{2,1,0:T(8,128)(2,1)}), bf16[32,32,320]{2,1,0:T(8,128)(2,1)S(1)}, u32[]{:S(2)}, u32[]{:S(2)}) async-start(bf16[32,32,320]{2,1,0:T(8,128)(2,1)} %bitcast.25), calls=%async_computation.5 | async-start | bytes 1572864 | tf_op jit(solution)/shard_map/all_to_all | solution.py:317
  268.7 6.2 %collective-permute-start.11 = (bf16[128,160]{1,0:T(8,128)(2,1)S(1)}, bf16[128,160]{1,0:T(8,128)(2,1)S(1)}, u32[]{:S(2)}, u32[]{:S(2)}) collective-permute-start(bf16[128,160]{1,0:T(8,128)(2,1)S(1)} %get-tuple-element.20), channel_id=1, source_target_pairs={{0,32},{32,0},{1,33},{33,1},{2,34},{34,2},{3,35},{35,3},{4,36},{36... | collective-permute-start | bytes 122888 | tf_op jit(solution)/shard_map/ppermute | solution.py:323
  (4 other events, 8.1 us)

commit v3 on v2

--- a/solution.py
+++ b/solution.py
@@ -27,40 +27,87 @@
     return lax.dot_general(a, b, (((1,), (1,)), ((), ())), preferred_element_type=f32)
 
 
-def attention_kernel(
-    info, query, own, p0, p1, p2, p3, o0, o1, o2, o3, value_up, out_proj, send, keep, scores, values
-):
+def attend_chunks(rows, chunks, biases, scores, old):
     scale = QKDIM ** (-0.5)
-    core = info[8]
-    chunks = [own] + [p0, p1, p2, p3] + [o0, o1, o2, o3]
+    peak = jnp.full((256, 128), -FAR, f32) if old is None else old[0]
+    for n, (chunk, bias) in enumerate(zip(chunks, biases)):
+        part = bias(nt_dot(rows, chunk[...].reshape(256, KEYW)) * scale)
+        scores[:, n * 256 : (n + 1) * 256] = part
+        peak = jnp.maximum(peak, jnp.maximum(part[:, :128], part[:, 128:]))
+    peak = jnp.max(peak, axis=1, keepdims=True)
+    if old is None:
+        sums, mixed = jnp.zeros((256, 128), f32), jnp.zeros((256, LATENT), f32)
+    else:
+        factor = jnp.exp(old[0][:, :1] - peak)
+        sums, mixed = old[1] * factor, old[2] * factor
+    for n, chunk in enumerate(chunks):
+        terms = jnp.exp(scores[:, n * 256 : (n + 1) * 256] - peak)
+        sums = sums + terms[:, :128] + terms[:, 128:]
+        keys = chunk[...].reshape(256, KEYW)
+        mixed = mixed + jnp.dot(terms.astype(bf16), keys[:, :LATENT], preferred_element_type=f32)
+    return jnp.broadcast_to(peak, (256, 128)), sums, mixed
+
+
+def valid_bias(info, piece):
+    def bias(part):
+        lane = lax.broadcasted_iota(i32, (256, 256), 1)
+        first = jnp.where(info[2 * piece] >= 0, 0.0, -FAR)
+        second = jnp.where(info[2 * piece + 1] >= 0, 0.0, -FAR)
+        return part + jnp.where(lane < 128, first, second)
+
+    return bias
+
+
+def causal_bias(part):
     lane = lax.broadcasted_iota(i32, (256, 256), 1)
     row = lax.broadcasted_iota(i32, (256, 256), 0)
     token = (row % 128) // 8 * 16 + row // 128 * 8 + row % 8
-
+    return jnp.where(lane <= token, part, -FAR)
+
+
+def first_attention_kernel(info, query, own, p0, peak, sums, mixed, scores):
     @pl.loop(0, 2)
     def _(head):
-        rows = query[head]
-        peak = jnp.full((256, 128), -jnp.inf, f32)
-        for n, chunk in enumerate(chunks):
-            keys = chunk[...].reshape(256, KEYW)
-            part = nt_dot(rows, keys) * scale
-            if n == 0:
-                part = jnp.where(lane <= token, part, -FAR)
-            else:
-                piece = (n - 1) % 4
-                first = jnp.where(info[2 * piece] >= 0, 0.0, -FAR)
-                second = jnp.where(info[2 * piece + 1] >= 0, 0.0, -FAR)
-                part = part + jnp.where(lane < 128, first, second)
-            scores[:, n * 256 : (n + 1) * 256] = part
-            peak = jnp.maximum(peak, jnp.maximum(part[:, :128], part[:, 128:]))
-        peak = jnp.max(peak, axis=1, keepdims=True)
-        sums = jnp.zeros((256, 128), f32)
-        mixed = jnp.zeros((256, LATENT), f32)
-        for n, chunk in enumerate(chunks):
-            keys = chunk[...].reshape(256, KEYW)
-            terms = jnp.exp(scores[:, n * 256 : (n + 1) * 256] - peak)
-            sums = sums + terms[:, :128] + terms[:, 128:]
-            mixed = mixed + jnp.dot(terms.astype(bf16), keys[:, :LATENT], preferred_element_type=f32)
+        state = attend_chunks(
+            query[head], [own, p0], [causal_bias, valid_bias(info, 0)], scores, None
+        )
+        peak[head], sums[head], mixed[head] = state
+
+
+def second_attention_kernel(
+    info, query, p1, p2, p3, o0, old_peak, old_sums, old_mixed, peak, sums, mixed, scores
+):
+    @pl.loop(0, 2)
+    def _(head):
+        old = old_peak[head], old_sums[head], old_mixed[head]
+        biases = [valid_bias(info, n) for n in (1, 2, 3, 0)]
+        state = attend_chunks(query[head], [p1, p2, p3, o0], biases, scores, old)
+        peak[head], sums[head], mixed[head] = state
+
+
+def last_attention_kernel(
+    info,
+    query,
+    o1,
+    o2,
+    o3,
+    old_peak,
+    old_sums,
+    old_mixed,
+    value_up,
+    out_proj,
+    send,
+    keep,
+    scores,
+    values,
+):
+    core = info[8]
+
+    @pl.loop(0, 2)
+    def _(head):
+        old = old_peak[head], old_sums[head], old_mixed[head]
+        biases = [valid_bias(info, n) for n in (1, 2, 3)]
+        _, sums, mixed = attend_chunks(query[head], [o1, o2, o3], biases, scores, old)
         mixed = (mixed / jnp.sum(sums, axis=1, keepdims=True)).astype(bf16)
         values[head] = jnp.dot(mixed, value_up[head], preferred_element_type=f32).astype(bf16)
 
@@ -98,29 +145,47 @@
         ).astype(bf16)
 
 
-def row_masks(count):
+def pick_kernel(picker, split, out):
+    out[...] = jnp.dot(picker[...], split[:, : out.shape[1]], preferred_element_type=f32).astype(bf16)
+
+
+def row_mask(count, j):
     slot = lax.broadcasted_iota(i32, (count, 1), 0) % SLOTS
-    return [(slot >= j * CAP) & (slot < (j + 1) * CAP) for j in range(3)]
-
-
-def masked(rows, mask):
-    return jnp.where(mask, rows.astype(f32), 0.0).astype(bf16)
+    return jnp.where((slot >= j * CAP) & (slot < (j + 1) * CAP), 1.0, 0.0).astype(bf16)
+
+
+def slot_places(full, packed, expert=None):
+    wide = lax.broadcasted_iota(i32, (full, packed), 0)
+    tight = lax.broadcasted_iota(i32, (full, packed), 1)
+    slot = wide % SLOTS
+    low, high = (0, 3 * CAP) if expert is None else (expert * CAP, (expert + 1) * CAP)
+    found = (wide // SLOTS * 3 * CAP + slot == tight) & (slot >= low) & (slot < high)
+    return jnp.where(found, 1.0, 0.0).astype(bf16)
 
 
 def gate_up_kernel(received, weights, pre):
-    width = pre.shape[1]
-
-    @pl.loop(0, received.shape[0] // 256)
-    def _(n):
-        start = pl.multiple_of(n * 256, 256)
-        rows = received[pl.ds(start, 256), :]
-        masks = row_masks(256)
-        total = jnp.zeros((256, width), f32)
-        for j in range(3):
-            total = total + jnp.dot(
-                masked(rows, masks[j]), weights[j, :, :width], preferred_element_type=f32
-            )
-        pre[pl.ds(start, 256), :] = total.astype(bf16)
+    chunks, packed, width = pre.shape
+    full = received.shape[0] // chunks
+    places = slot_places(full, packed)
+    step = 4 * full
+    for r in range(0, received.shape[0], step):
+        rows = received[r : r + step, :]
+        for c in range(0, width, 256):
+            total = jnp.zeros((step, 256), f32)
+            for j in range(3):
+                total = total + jnp.dot(
+                    rows * row_mask(step, j),
+                    weights[j, :, c : c + 256],
+                    preferred_element_type=f32,
+                )
+            total = total.astype(bf16)
+            for n in range(4):
+                pre[r // full + n, :, c : c + 256] = lax.dot_general(
+                    places,
+                    total[n * full : (n + 1) * full],
+                    (((0,), (0,)), ((), ())),
+                    preferred_element_type=f32,
+                ).astype(bf16)
 
 
 def hidden_kernel(parts, out):
@@ -133,17 +198,18 @@
 
 
 def down_kernel(hidden, weights, out):
-    width = hidden.shape[1]
-
-    @pl.loop(0, hidden.shape[0] // 256)
-    def _(n):
-        start = pl.multiple_of(n * 256, 256)
-        rows = hidden[pl.ds(start, 256), :]
-        masks = row_masks(256)
-        total = jnp.zeros((256, out.shape[1]), f32)
+    chunks, packed, width = hidden.shape
+    full = out.shape[0] // chunks
+    places = [slot_places(full, packed, j) for j in range(3)]
+    for r in range(0, chunks, 4):
+        total = jnp.zeros((4 * full, out.shape[1]), f32)
         for j in range(3):
-            total = total + nt_dot(masked(rows, masks[j]), weights[j, :, -width:])
-        out[pl.ds(start, 256), :] = total.astype(bf16)
+            rows = [
+                jnp.dot(places[j], hidden[r + n], preferred_element_type=f32).astype(bf16)
+                for n in range(4)
+            ]
+            total = total + nt_dot(jnp.concatenate(rows, axis=0), weights[j])
+        out[r * full : (r + 4) * full, :] = total.astype(bf16)
 
 
 def combine_kernel(weighting, returned, keep, send):
@@ -225,7 +291,6 @@
         lax.ppermute(to_other, "xl", SWAP),
         lax.ppermute(to_other, ("xl", "xh"), diagonal),
     ]
-    others = [lax.ppermute(piece, "core", SWAP) for piece in pieces]
 
     def blocks_of(x, h):
         return [2 * (y - 1 - 2 * h) + x, 2 * (y - 2 - 2 * h) + x]
@@ -254,13 +319,27 @@
     )
     query_rows = query_rows.reshape(16, 2, 8, local_heads, KEYW).transpose(3, 1, 0, 2, 4)
     query_rows = query_rows.reshape(local_heads, block_len, KEYW)
+    state_out = [
+        sds((2, 256, 128), f32),
+        sds((2, 256, 128), f32),
+        sds((2, 256, LATENT), f32),
+    ]
+    state = call(
+        first_attention_kernel, state_out, [pltpu.VMEM((256, 2 * 256), f32)], True, 4
+    )(info, query_rows, keys_own, column)
+    piece_x, peak = lax.optimization_barrier((pieces[1], state[0]))
+    pieces[1], state = piece_x, [peak] + list(state[1:])
+    others = [lax.ppermute(piece, "core", SWAP) for piece in pieces]
+    state = call(
+        second_attention_kernel, state_out, [pltpu.VMEM((256, 4 * 256), f32)], True, 9
+    )(info, query_rows, pieces[1], pieces[2], pieces[3], others[0], *state)
     send, keep = call(
-        attention_kernel,
+        last_attention_kernel,
         [sds((half, width_model), bf16), sds((half, width_model), f32)],
-        [pltpu.VMEM((256, 9 * 256), f32), pltpu.VMEM((2, 256, VDIM), bf16)],
-        smem_first=True,
-        count=13,
-    )(info, query_rows, keys_own, *pieces, *others, value_up, out_proj)
+        [pltpu.VMEM((256, 3 * 256), f32), pltpu.VMEM((2, 256, VDIM), bf16)],
+        True,
+        10,
+    )(info, query_rows, others[1], others[2], others[3], *state, value_up, out_proj)
     got = lax.ppermute(send, "core", SWAP)
     pair_sum = (keep + got.astype(f32)).astype(bf16).reshape(16, 8, width_model)
 
@@ -273,13 +352,16 @@
     w_got = lax.ppermute(w_send, "xl", SWAP)
 
     spread = lax.all_to_all(pair_sum, ("z", "xh"), split_axis=0, concat_axis=0, tiled=True)
-    spread, w_got = lax.optimization_barrier((spread, w_got))
-    w_all = jnp.concatenate([w_keep, w_got], axis=1)
     packed = call(norm_kernel, [sds((16, 8, 512), bf16)], count=3)(
         spread, residual, norm_gain[None, :]
     )
     split = lax.all_to_all(packed, CTX, split_axis=0, concat_axis=0, tiled=True)
+    split, w_got = lax.optimization_barrier((split, w_got))
     split = split.reshape(128, 512)
+    w_both = jnp.concatenate([w_keep, w_got], axis=1)
+    rows_in = 384
+    w_in = jnp.pad(w_both[:, :, : 2 * ff_half], ((0, 0), (0, rows_in - width_pair), (0, 0)))
+    w_down = w_both[:, :, 2 * ff_half :]
 
     routes = jnp.transpose(route_ids, (1, 0, 2)).reshape(128, TOPK)
     expert_axis = jnp.arange(EXPERTS, dtype=i32)
@@ -301,18 +383,17 @@
         axis=1,
     )
 
-    outgoing = jnp.dot(picker, split[:, :width_pair], preferred_element_type=f32).astype(bf16)
+    outgoing = call(pick_kernel, [sds((32 * SLOTS, rows_in), bf16)], count=2)(picker, split)
     received = lax.all_to_all(
-        outgoing.reshape(32, SLOTS, width_pair), EXP, split_axis=0, concat_axis=0, tiled=True
-    ).reshape(32 * SLOTS, width_pair)
-    pre = call(gate_up_kernel, [sds((32 * SLOTS, 2 * ff_half), bf16)], count=2)(received, w_all)
-    pre_parts = lax.all_to_all(
-        pre.reshape(8, 128, 2 * ff_half), "y", split_axis=0, concat_axis=0, tiled=True
-    )
-    hidden = call(hidden_kernel, [sds((8, 128, ff_half), bf16)], count=1)(pre_parts)
+        outgoing.reshape(32, SLOTS, rows_in), EXP, split_axis=0, concat_axis=0, tiled=True
+    ).reshape(32 * SLOTS, rows_in)
+    packed_rows = 4 * 3 * CAP
+    pre = call(gate_up_kernel, [sds((8, packed_rows, 2 * ff_half), bf16)], count=2)(received, w_in)
+    pre_parts = lax.all_to_all(pre, "y", split_axis=0, concat_axis=0, tiled=True)
+    hidden = call(hidden_kernel, [sds((8, packed_rows, ff_half), bf16)], count=1)(pre_parts)
     hidden_all = lax.all_to_all(hidden, "y", split_axis=0, concat_axis=0, tiled=True)
     expert_out = call(down_kernel, [sds((32 * SLOTS, width_pair), bf16)], count=2)(
-        hidden_all.reshape(32 * SLOTS, ff_half), w_all
+        hidden_all, w_down
     )
     returned = lax.all_to_all(
         expert_out.reshape(32, SLOTS, width_pair), EXP, split_axis=0, concat_axis=0, tiled=True

time: 277 us -> 264 us (0.953)
  blocking collectives: 66.9 us -> 45.5 us
  Pallas kernels: 16.5 us -> 21.3 us
  waiting for transfers between devices: 101 us -> 105 us
    ppermute x1, waiting for transfers between devices: 30.9 us -> 2.9 us  [on_device(): w_got = lax.ppermute(w_send, 'xl', SWAP)]
    all_to_all x2 -> x1, blocking collectives: 66.9 us -> 45.5 us  [on_device(): lax.all_to_all(pre, 'y', split_axis=0, concat_axis=0, tiled=True)]
    all_to_all x1 -> x2, waiting for transfers between devices: 21.6 us -> 41.6 us  [the longest x1 22 us: on_device(): lax.all_to_all(outgoing.reshape(32, SLOTS, rows_in), EXP, split_axis=0, c...]
    all_to_all x1, waiting for transfers between devices: 0.01 us -> 16.1 us  [on_device(): lax.all_to_all(pair_sum, ('z', 'xh'), split_axis=0, concat_axis=0, tiled=...]
    pallas_call x3 -> x6, Pallas kernels: 12 us -> 16.5 us  [the longest x1 5.75 us: on_device(): call(gate_up_kernel, [sds((8, packed_rows, 2 * ff_half), bf16)], count=2)]
    ppermute x1, starting transfers between devices: 5.16 us -> 1.92 us  [on_device(): lax.ppermute(to_other, ('xl', 'xh'), diagonal)]
    ppermute x1, starting transfers between devices: 1.92 us -> 5.16 us  [on_device(): lax.ppermute(column, 'xh', SWAP)]
    all_to_all x1, waiting for transfers between devices: 7.91 us -> 4.95 us  [on_device(): split = lax.all_to_all(packed, CTX, split_axis=0, concat_axis=0, tiled=True)]
  transfers between devices with their start and end apart: 16 -> 17, of which waited for: 8 -> 11; matrix products, arithmetic and copies ran while one was open for 3% -> 3% of each run, Pallas kernels for 0% -> 2%
where the time goes in v3:
time: 264 us; the launch traced here: 262 us
  waiting for transfers between devices  105 us (40%)
  starting transfers between devices  79.1 us (30%)
  blocking collectives  45.5 us (17%)
  Pallas kernels  21.3 us (8%)
  other arithmetic  7.1 us (3%)
  local copies, waits for them, and re-layouts  2.64 us (1%)
    all_to_all x1, blocking collectives, on_device(): lax.all_to_all(pre, 'y', split_axis=0, concat_axis=0, tiled=True)  45.5 us
    all_to_all x1, waiting for transfers between devices, on_device(): lax.all_to_all(expert_out.reshape(32, SLOTS, width_pair), EXP, split_axis...  22.5 us
    all_to_all x1, waiting for transfers between devices, on_device(): lax.all_to_all(outgoing.reshape(32, SLOTS, rows_in), EXP, split_axis=0, c...  22 us
    all_to_all x1, waiting for transfers between devices, on_device(): lax.all_to_all(hidden, 'y', split_axis=0, concat_axis=0, tiled=True)  19.5 us
    all_to_all x1, waiting for transfers between devices, on_device(): lax.all_to_all(pair_sum, ('z', 'xh'), split_axis=0, concat_axis=0, tiled=...  16.1 us
    all_to_all x1, starting transfers between devices, on_device(): lax.all_to_all(pair_sum, ('z', 'xh'), split_axis=0, concat_axis=0, tiled=...  13.5 us
    ppermute x2, waiting for transfers between devices, along_y(): return lax.ppermute(mine, ('y', 'xh'), pairs)  12.6 us
    all_to_all x1, starting transfers between devices, on_device(): split = lax.all_to_all(packed, CTX, split_axis=0, concat_axis=0, tiled=True)  10.9 us
  transfers between devices with their start and end apart: 17, of which 11 were waited for; matrix products, arithmetic and copies ran while one was open for 3% of the time, Pallas kernels for 2%

profile of v3, /device:TPU:6, one launch (start us, length us, event | category | flops | bytes accessed | tf_op | source)
XLA Modules:
  0.0 262.1 jit_solution(10993508218707487973)
XLA Ops:
  2.3 5.5 %collective-permute-start = (bf16[128,640]{1,0:T(8,128)(2,1)S(1)}, bf16[128,640]{1,0:T(8,128)(2,1)S(1)}, u32[]{:S(2)}, u32[]{:S(2)}) collective-permute-start(bf16[128,640]{1,0:T(8,128)(2,1)S(1)} %constant_dynamic-slice_fusion), channel_id=1, source_target_pairs={{0,64},{2,194},{64,128},{66,258},{128,192},{130,322},{192,256},{19... | collective-permute-start | bytes 491528 | tf_op jit(solution)/shard_map/ppermute | solution.py:281
  7.8 5.0 %collective-permute-start.1 = (bf16[128,640]{1,0:T(8,128)(2,1)S(1)}, bf16[128,640]{1,0:T(8,128)(2,1)S(1)}, u32[]{:S(2)}, u32[]{:S(2)}) collective-permute-start(bf16[128,640]{1,0:T(8,128)(2,1)S(1)} %constant_dynamic-slice_fusion), channel_id=1, source_target_pairs={{0,128},{2,258},{64,192},{66,322},{128,256},{130,386},{192,320},{1... | collective-permute-start | bytes 491528 | tf_op jit(solution)/shard_map/ppermute | solution.py:281
  12.9 5.4 %collective-permute-done = bf16[128,640]{1,0:T(8,128)(2,1)S(1)} collective-permute-done((bf16[128,640]{1,0:T(8,128)(2,1)S(1)}, bf16[128,640]{1,0:T(8,128)(2,1)S(1)}, u32[]{:S(2)}, u32[]{:S(2)}) %collective-permute-start) | collective-permute-done | bytes 163872 | tf_op jit(solution)/shard_map/ppermute | solution.py:281
  18.3 7.1 %collective-permute-done.1 = bf16[128,640]{1,0:T(8,128)(2,1)S(1)} collective-permute-done((bf16[128,640]{1,0:T(8,128)(2,1)S(1)}, bf16[128,640]{1,0:T(8,128)(2,1)S(1)}, u32[]{:S(2)}, u32[]{:S(2)}) %collective-permute-start.1) | collective-permute-done | bytes 163872 | tf_op jit(solution)/shard_map/ppermute | solution.py:281
  25.5 2.7 %collective-permute-start.4 = (bf16[2,128,640]{2,1,0:T(8,128)(2,1)S(1)}, bf16[2,128,640]{2,1,0:T(8,128)(2,1)S(1)}, u32[]{:S(2)}, u32[]{:S(2)}) collective-permute-start(bf16[2,128,640]{2,1,0:T(8,128)(2,1)S(1)} %get-tuple-element.45), channel_id=1, source_target_pairs={{0,32},{32,0},{1,33},{33,1},{2,34},{34,2},{3,35},{35,3},{4,36},{36... | collective-permute-start | bytes 983048 | tf_op jit(solution)/shard_map/ppermute | solution.py:291
  30.2 5.2 %collective-permute-start.2 = (bf16[2,128,640]{2,1,0:T(8,128)(2,1)S(1)}, bf16[2,128,640]{2,1,0:T(8,128)(2,1)S(1)}, u32[]{:S(2)}, u32[]{:S(2)}) collective-permute-start(bf16[2,128,640]{2,1,0:T(8,128)(2,1)S(1)} %get-tuple-element.46.p0), channel_id=1, source_target_pairs={{0,2},{2,0},{1,3},{3,1},{4,6},{6,4},{5,7},{7,5},{8,10},{10,8},{9,1... | collective-permute-start | bytes 983048 | tf_op jit(solution)/shard_map/ppermute | solution.py:290
  50.4 3.8 %shard_map.120 = (bf16[128,2560]{1,0:T(8,128)(2,1)S(1)}, f32[128,2560]{1,0:T(8,128)S(1)}) custom-call(s32[9]{0:T(128)S(1)} %stack.54.info, bf16[2,256,640]{2,1,0:T(8,128)(2,1)S(1)} %bitcast.43, bf16[2,128,640]{2,1,0:T(8,128)(2,1)S(1)} %collective-permute-done.3.o1, bf16[2,128,640]{2,1,0:T(8,128)(2,1)S(1)} %collective-permute-done.5.o2, ...), custom_call_target="tpu_custom_call" | custom-call | tf_op jit(solution)/shard_map/pallas_call | solution.py:336
  59.4 13.5 %all-to-all-start = ((bf16[16,8,2560]{2,1,0:T(8,128)(2,1)}), bf16[16,8,2560]{2,1,0:T(8,128)(2,1)S(1)}, u32[]{:S(2)}, u32[]{:S(2)}) async-start(bf16[16,8,2560]{2,1,0:T(8,128)(2,1)} %fusion.2), calls=%async_computation | async-start | bytes 1310720 | tf_op jit(solution)/shard_map/all_to_all | solution.py:354
  72.8 3.1 %collective-permute-start.10 = (bf16[3,160,1152]{2,1,0:T(8,128)(2,1)}, bf16[3,160,1152]{2,1,0:T(8,128)(2,1)}, u32[]{:S(2)}, u32[]{:S(2)}) collective-permute-start(bf16[3,160,1152]{2,1,0:T(8,128)(2,1)} %get-tuple-element.32), channel_id=1, source_target_pairs={{0,32},{32,0},{1,33},{33,1},{2,34},{34,2},{3,35},{35,3},{4,36},{36... | collective-permute-start | bytes 3317768 | tf_op jit(solution)/shard_map/ppermute | solution.py:352
  76.5 16.1 %all-to-all-done.spread = bf16[16,8,2560]{2,1,0:T(8,128)(2,1)S(1)} async-done(((bf16[16,8,2560]{2,1,0:T(8,128)(2,1)}), bf16[16,8,2560]{2,1,0:T(8,128)(2,1)S(1)}, u32[]{:S(2)}, u32[]{:S(2)}) %all-to-all-start) | async-done | bytes 655392 | tf_op jit(solution)/shard_map/all_to_all | solution.py:354
  93.5 10.9 %all-to-all-start.1 = ((bf16[16,8,512]{2,1,0:T(8,128)(2,1)}), bf16[16,8,512]{2,1,0:T(8,128)(2,1)S(1)}, u32[]{:S(2)}, u32[]{:S(2)}) async-start(bf16[16,8,512]{2,1,0:T(8,128)(2,1)} %shard_map.121), calls=%async_computation.1 | async-start | bytes 262144 | tf_op jit(solution)/shard_map/all_to_all | solution.py:358
  105.0 2.9 %collective-permute-done.10 = bf16[3,160,1152]{2,1,0:T(8,128)(2,1)} collective-permute-done((bf16[3,160,1152]{2,1,0:T(8,128)(2,1)}, bf16[3,160,1152]{2,1,0:T(8,128)(2,1)}, u32[]{:S(2)}, u32[]{:S(2)}) %collective-permute-start.10) | collective-permute-done | bytes 1105952 | tf_op jit(solution)/shard_map/ppermute | solution.py:352
  107.9 4.9 %all-to-all-done.1 = bf16[16,8,512]{2,1,0:T(8,128)(2,1)S(1)} async-done(((bf16[16,8,512]{2,1,0:T(8,128)(2,1)}), bf16[16,8,512]{2,1,0:T(8,128)(2,1)S(1)}, u32[]{:S(2)}, u32[]{:S(2)}) %all-to-all-start.1) | async-done | bytes 131104 | tf_op jit(solution)/shard_map/all_to_all | solution.py:358
  114.1 6.9 %all-to-all-start.2 = ((bf16[32,32,384]{2,1,0:T(8,128)(2,1)}), bf16[32,32,384]{2,1,0:T(8,128)(2,1)S(1)}, u32[]{:S(2)}, u32[]{:S(2)}) async-start(bf16[32,32,384]{2,1,0:T(8,128)(2,1)} %bitcast.21), calls=%async_computation.2 | async-start | bytes 1572864 | tf_op jit(solution)/shard_map/all_to_all | solution.py:387
  122.3 22.0 %all-to-all-done.2 = bf16[32,32,384]{2,1,0:T(8,128)(2,1)S(1)} async-done(((bf16[32,32,384]{2,1,0:T(8,128)(2,1)}), bf16[32,32,384]{2,1,0:T(8,128)(2,1)S(1)}, u32[]{:S(2)}, u32[]{:S(2)}) %all-to-all-start.2) | async-done | bytes 786464 | tf_op jit(solution)/shard_map/all_to_all | solution.py:387
  144.4 5.7 %shard_map.123 = bf16[8,120,768]{2,1,0:T(8,128)(2,1)S(1)} custom-call(bf16[1024,384]{1,0:T(8,128)(2,1)S(1)} %bitcast.45, bf16[3,384,768]{2,1,0:T(8,128)(2,1)S(1)} %pad.4.weights), custom_call_target="tpu_custom_call" | custom-call | tf_op jit(solution)/shard_map/pallas_call | solution.py:391
  150.1 45.5 %all_to_all.30.parts = bf16[8,120,768]{2,1,0:T(8,128)(2,1)S(1)} all-to-all(bf16[8,120,768]{2,1,0:T(8,128)(2,1)S(1)} %shard_map.123), channel_id=1, replica_groups=mesh['y'=8,'xl'=2,'z'=8,'xh'=2,'core'=2] {'y'}, dimensions={0} | all-to-all | bytes 2949120 | tf_op jit(solution)/shard_map/all_to_all | solution.py:392
  196.8 3.5 %all-to-all-start.4 = ((bf16[8,120,384]{2,1,0:T(8,128)(2,1)}), bf16[8,120,384]{2,1,0:T(8,128)(2,1)S(1)}, u32[]{:S(2)}, u32[]{:S(2)}) async-start(bf16[8,120,384]{2,1,0:T(8,128)(2,1)} %shard_map.124), calls=%async_computation.4 | async-start | bytes 1474560 | tf_op jit(solution)/shard_map/all_to_all | solution.py:394
  201.4 19.5 %all-to-all-done.4.hidden = bf16[8,120,384]{2,1,0:T(8,128)(2,1)S(1)} async-done(((bf16[8,120,384]{2,1,0:T(8,128)(2,1)}), bf16[8,120,384]{2,1,0:T(8,128)(2,1)S(1)}, u32[]{:S(2)}, u32[]{:S(2)}) %all-to-all-start.4) | async-done | bytes 737312 | tf_op jit(solution)/shard_map/all_to_all | solution.py:394
  220.9 3.3 %shard_map.125 = bf16[1024,320]{1,0:T(8,128)(2,1)} custom-call(bf16[8,120,384]{2,1,0:T(8,128)(2,1)S(1)} %all-to-all-done.4.hidden, bf16[3,320,384]{2,1,0:T(8,128)(2,1)S(1)} %pad_maximum_fusion.2.weights), custom_call_target="tpu_custom_call" | custom-call | tf_op jit(solution)/shard_map/pallas_call | solution.py:395
  224.2 7.0 %all-to-all-start.5 = ((bf16[32,32,320]{2,1,0:T(8,128)(2,1)}), bf16[32,32,320]{2,1,0:T(8,128)(2,1)S(1)}, u32[]{:S(2)}, u32[]{:S(2)}) async-start(bf16[32,32,320]{2,1,0:T(8,128)(2,1)} %bitcast.23), calls=%async_computation.5 | async-start | bytes 1572864 | tf_op jit(solution)/shard_map/all_to_all | solution.py:398
  232.1 22.5 %all-to-all-done.5 = bf16[32,32,320]{2,1,0:T(8,128)(2,1)S(1)} async-done(((bf16[32,32,320]{2,1,0:T(8,128)(2,1)}), bf16[32,32,320]{2,1,0:T(8,128)(2,1)S(1)}, u32[]{:S(2)}, u32[]{:S(2)}) %all-to-all-start.5) | async-done | bytes 655392 | tf_op jit(solution)/shard_map/all_to_all | solution.py:398
  255.1 3.1 %collective-permute-start.11 = (bf16[128,160]{1,0:T(8,128)(2,1)S(1)}, bf16[128,160]{1,0:T(8,128)(2,1)S(1)}, u32[]{:S(2)}, u32[]{:S(2)}) collective-permute-start(bf16[128,160]{1,0:T(8,128)(2,1)S(1)} %get-tuple-element.36), channel_id=1, source_target_pairs={{0,32},{32,0},{1,33},{33,1},{2,34},{34,2},{3,35},{35,3},{4,36},{36... | collective-permute-start | bytes 122888 | tf_op jit(solution)/shard_map/ppermute | solution.py:404
  258.2 3.0 %collective-permute-done.11 = bf16[128,160]{1,0:T(8,128)(2,1)S(1)} collective-permute-done((bf16[128,160]{1,0:T(8,128)(2,1)S(1)}, bf16[128,160]{1,0:T(8,128)(2,1)S(1)}, u32[]{:S(2)}, u32[]{:S(2)}) %collective-permute-start.11) | collective-permute-done | bytes 40992 | tf_op jit(solution)/shard_map/ppermute | solution.py:404
  (85 shorter events, 33.1 us)
Async XLA Ops:
  0.0 35.4 %copy-start.12 = (s32[256]{0:T(256)S(1)}, s32[256]{0:T(256)}, u32[]{:S(2)}) copy-start(s32[256]{0:T(256)} %param.14) | copy-start | bytes 3076
  1.2 34.3 %copy-start.8 = (bf16[256,2,576]{0,2,1:T(8,128)(2,1)S(1)}, bf16[256,2,576]{0,2,1:T(8,128)(2,1)}, u32[]{:S(2)}) copy-start(bf16[256,2,576]{0,2,1:T(8,128)(2,1)} %param.12) | copy-start | bytes 1769476
  2.3 16.0 %collective-permute-start = (bf16[128,640]{1,0:T(8,128)(2,1)S(1)}, bf16[128,640]{1,0:T(8,128)(2,1)S(1)}, u32[]{:S(2)}, u32[]{:S(2)}) collective-permute-start(bf16[128,640]{1,0:T(8,128)(2,1)S(1)} %constant_dynamic-slice_fusion), channel_id=1, source_target_pairs={{0,64},{2,194},{64,128},{66,258},{128,192},{130,322},{192,256},{19... | collective-permute-start | bytes 491528 | tf_op jit(solution)/shard_map/ppermute | solution.py:281
  7.8 17.7 %collective-permute-start.1 = (bf16[128,640]{1,0:T(8,128)(2,1)S(1)}, bf16[128,640]{1,0:T(8,128)(2,1)S(1)}, u32[]{:S(2)}, u32[]{:S(2)}) collective-permute-start(bf16[128,640]{1,0:T(8,128)(2,1)S(1)} %constant_dynamic-slice_fusion), channel_id=1, source_target_pairs={{0,128},{2,258},{64,192},{66,322},{128,256},{130,386},{192,320},{1... | collective-permute-start | bytes 491528 | tf_op jit(solution)/shard_map/ppermute | solution.py:281
  25.5 17.4 %collective-permute-start.4 = (bf16[2,128,640]{2,1,0:T(8,128)(2,1)S(1)}, bf16[2,128,640]{2,1,0:T(8,128)(2,1)S(1)}, u32[]{:S(2)}, u32[]{:S(2)}) collective-permute-start(bf16[2,128,640]{2,1,0:T(8,128)(2,1)S(1)} %get-tuple-element.45), channel_id=1, source_target_pairs={{0,32},{32,0},{1,33},{33,1},{2,34},{34,2},{3,35},{35,3},{4,36},{36... | collective-permute-start | bytes 983048 | tf_op jit(solution)/shard_map/ppermute | solution.py:291
  28.3 17.4 %collective-permute-start.6 = (bf16[2,128,640]{2,1,0:T(8,128)(2,1)S(1)}, bf16[2,128,640]{2,1,0:T(8,128)(2,1)S(1)}, u32[]{:S(2)}, u32[]{:S(2)}) collective-permute-start(bf16[2,128,640]{2,1,0:T(8,128)(2,1)S(1)} %get-tuple-element.45), channel_id=1, source_target_pairs={{0,34},{2,32},{32,2},{34,0},{1,35},{3,33},{33,3},{35,1},{4,38},{6,... | collective-permute-start | bytes 983048 | tf_op jit(solution)/shard_map/ppermute | solution.py:292
  30.2 10.8 %collective-permute-start.2 = (bf16[2,128,640]{2,1,0:T(8,128)(2,1)S(1)}, bf16[2,128,640]{2,1,0:T(8,128)(2,1)S(1)}, u32[]{:S(2)}, u32[]{:S(2)}) collective-permute-start(bf16[2,128,640]{2,1,0:T(8,128)(2,1)S(1)} %get-tuple-element.46.p0), channel_id=1, source_target_pairs={{0,2},{2,0},{1,3},{3,1},{4,6},{6,4},{5,7},{7,5},{8,10},{10,8},{9,1... | collective-permute-start | bytes 983048 | tf_op jit(solution)/shard_map/ppermute | solution.py:290
  36.2 11.4 %collective-permute-start.8 = (bf16[2,128,640]{2,1,0:T(8,128)(2,1)S(1)}, bf16[2,128,640]{2,1,0:T(8,128)(2,1)S(1)}, u32[]{:S(2)}, u32[]{:S(2)}) collective-permute-start(bf16[2,128,640]{2,1,0:T(8,128)(2,1)S(1)} %get-tuple-element.46.p0), channel_id=1, source_target_pairs={{0,1},{1,0},{2,3},{3,2},{4,5},{5,4},{6,7},{7,6},{8,9},{9,8},{10,11... | collective-permute-start | bytes 983048 | tf_op jit(solution)/shard_map/ppermute | solution.py:332
  40.9 9.3 %collective-permute-start.3 = (bf16[2,128,640]{2,1,0:T(8,128)(2,1)S(1)}, bf16[2,128,640]{2,1,0:T(8,128)(2,1)S(1)}, u32[]{:S(2)}, u32[]{:S(2)}) collective-permute-start(bf16[2,128,640]{2,1,0:T(8,128)(2,1)S(1)} %collective-permute-done.2.p1), channel_id=1, source_target_pairs={{0,1},{1,0},{2,3},{3,2},{4,5},{5,4},{6,7},{7,6},{8,9},{9,8},{10,11... | collective-permute-start | bytes 983048 | tf_op jit(solution)/shard_map/ppermute | solution.py:332
  42.9 7.4 %collective-permute-start.5 = (bf16[2,128,640]{2,1,0:T(8,128)(2,1)S(1)}, bf16[2,128,640]{2,1,0:T(8,128)(2,1)S(1)}, u32[]{:S(2)}, u32[]{:S(2)}) collective-permute-start(bf16[2,128,640]{2,1,0:T(8,128)(2,1)S(1)} %collective-permute-done.4.p2), channel_id=1, source_target_pairs={{0,1},{1,0},{2,3},{3,2},{4,5},{5,4},{6,7},{7,6},{8,9},{9,8},{10,11... | collective-permute-start | bytes 983048 | tf_op jit(solution)/shard_map/ppermute | solution.py:332
  45.6 4.7 %collective-permute-start.7 = (bf16[2,128,640]{2,1,0:T(8,128)(2,1)S(1)}, bf16[2,128,640]{2,1,0:T(8,128)(2,1)S(1)}, u32[]{:S(2)}, u32[]{:S(2)}) collective-permute-start(bf16[2,128,640]{2,1,0:T(8,128)(2,1)S(1)} %collective-permute-done.6.p3), channel_id=1, source_target_pairs={{0,1},{1,0},{2,3},{3,2},{4,5},{5,4},{6,7},{7,6},{8,9},{9,8},{10,11... | collective-permute-start | bytes 983048 | tf_op jit(solution)/shard_map/ppermute | solution.py:332
  54.2 4.2 %collective-permute-start.9 = (bf16[128,2560]{1,0:T(8,128)(2,1)S(1)}, bf16[128,2560]{1,0:T(8,128)(2,1)S(1)}, u32[]{:S(2)}, u32[]{:S(2)}) collective-permute-start(bf16[128,2560]{1,0:T(8,128)(2,1)S(1)} %get-tuple-element.30), channel_id=1, source_target_pairs={{0,1},{1,0},{2,3},{3,2},{4,5},{5,4},{6,7},{7,6},{8,9},{9,8},{10,11... | collective-permute-start | bytes 1966088 | tf_op jit(solution)/shard_map/ppermute | solution.py:343
  58.4 62.6 %copy-start.3 = (bf16[3,160,1152]{2,1,0:T(8,128)(2,1)}, bf16[3,160,1152]{2,1,0:T(8,128)(2,1)S(1)}, u32[]{:S(2)}) copy-start(bf16[3,160,1152]{2,1,0:T(8,128)(2,1)S(1)} %get-tuple-element.37) | copy-start | bytes 3317764
  58.4 17.5 %copy-start.11 = (f32[2560]{0:T(1024)S(1)}, f32[2560]{0:T(1024)}, u32[]{:S(2)}) copy-start(f32[2560]{0:T(1024)} %param.18) | copy-start | bytes 30724
  58.4 17.6 %copy-start.10 = (s32[8,16,6]{1,0,2:T(8,128)S(1)}, s32[8,16,6]{1,0,2:T(8,128)}, u32[]{:S(2)}) copy-start(s32[8,16,6]{1,0,2:T(8,128)} %param.19) | copy-start | bytes 9220
  58.4 34.1 %copy-start.2 = (bf16[8,2560]{1,0:T(8,128)(2,1)S(1)}, bf16[8,2560]{1,0:T(8,128)(2,1)}, u32[]{:S(2)}) copy-start(bf16[8,2560]{1,0:T(8,128)(2,1)} %residual.1) | copy-start | bytes 122884
  59.4 33.2 %all-to-all-start = ((bf16[16,8,2560]{2,1,0:T(8,128)(2,1)}), bf16[16,8,2560]{2,1,0:T(8,128)(2,1)S(1)}, u32[]{:S(2)}, u32[]{:S(2)}) async-start(bf16[16,8,2560]{2,1,0:T(8,128)(2,1)} %fusion.2), calls=%async_computation | async-start | bytes 1310720 | tf_op jit(solution)/shard_map/all_to_all | solution.py:354
  72.8 35.0 %collective-permute-start.10 = (bf16[3,160,1152]{2,1,0:T(8,128)(2,1)}, bf16[3,160,1152]{2,1,0:T(8,128)(2,1)}, u32[]{:S(2)}, u32[]{:S(2)}) collective-permute-start(bf16[3,160,1152]{2,1,0:T(8,128)(2,1)} %get-tuple-element.32), channel_id=1, source_target_pairs={{0,32},{32,0},{1,33},{33,1},{2,34},{34,2},{3,35},{35,3},{4,36},{36... | collective-permute-start | bytes 3317768 | tf_op jit(solution)/shard_map/ppermute | solution.py:352
  93.5 19.3 %all-to-all-start.1 = ((bf16[16,8,512]{2,1,0:T(8,128)(2,1)}), bf16[16,8,512]{2,1,0:T(8,128)(2,1)S(1)}, u32[]{:S(2)}, u32[]{:S(2)}) async-start(bf16[16,8,512]{2,1,0:T(8,128)(2,1)} %shard_map.121), calls=%async_computation.1 | async-start | bytes 262144 | tf_op jit(solution)/shard_map/all_to_all | solution.py:358
  114.1 30.3 %all-to-all-start.2 = ((bf16[32,32,384]{2,1,0:T(8,128)(2,1)}), bf16[32,32,384]{2,1,0:T(8,128)(2,1)S(1)}, u32[]{:S(2)}, u32[]{:S(2)}) async-start(bf16[32,32,384]{2,1,0:T(8,128)(2,1)} %bitcast.21), calls=%async_computation.2 | async-start | bytes 1572864 | tf_op jit(solution)/shard_map/all_to_all | solution.py:387
  196.8 24.2 %all-to-all-start.4 = ((bf16[8,120,384]{2,1,0:T(8,128)(2,1)}), bf16[8,120,384]{2,1,0:T(8,128)(2,1)S(1)}, u32[]{:S(2)}, u32[]{:S(2)}) async-start(bf16[8,120,384]{2,1,0:T(8,128)(2,1)} %shard_map.124), calls=%async_computation.4 | async-start | bytes 1474560 | tf_op jit(solution)/shard_map/all_to_all | solution.py:394
  224.2 7.3 %copy-start.9 = (f32[8,16,6]{1,0,2:T(8,128)S(1)}, f32[8,16,6]{1,0,2:T(8,128)}, u32[]{:S(2)}) copy-start(f32[8,16,6]{1,0,2:T(8,128)} %param.20) | copy-start | bytes 9220
  224.2 30.4 %all-to-all-start.5 = ((bf16[32,32,320]{2,1,0:T(8,128)(2,1)}), bf16[32,32,320]{2,1,0:T(8,128)(2,1)S(1)}, u32[]{:S(2)}, u32[]{:S(2)}) async-start(bf16[32,32,320]{2,1,0:T(8,128)(2,1)} %bitcast.23), calls=%async_computation.5 | async-start | bytes 1572864 | tf_op jit(solution)/shard_map/all_to_all | solution.py:398
  255.1 6.2 %collective-permute-start.11 = (bf16[128,160]{1,0:T(8,128)(2,1)S(1)}, bf16[128,160]{1,0:T(8,128)(2,1)S(1)}, u32[]{:S(2)}, u32[]{:S(2)}) collective-permute-start(bf16[128,160]{1,0:T(8,128)(2,1)S(1)} %get-tuple-element.36), channel_id=1, source_target_pairs={{0,32},{32,0},{1,33},{33,1},{2,34},{34,2},{3,35},{35,3},{4,36},{36... | collective-permute-start | bytes 122888 | tf_op jit(solution)/shard_map/ppermute | solution.py:404
  (6 other events, 21.9 us)

commit v4 on v3

--- a/solution.py
+++ b/solution.py
@@ -86,43 +86,36 @@
 
 
 def last_attention_kernel(
-    info,
-    query,
-    o1,
-    o2,
-    o3,
-    old_peak,
-    old_sums,
-    old_mixed,
-    value_up,
-    out_proj,
-    send,
-    keep,
-    scores,
-    values,
+    info, query, others, old_peak, old_sums, old_mixed, value_up, send, keep, scores, values
 ):
     core = info[8]
 
     @pl.loop(0, 2)
     def _(head):
         old = old_peak[head], old_sums[head], old_mixed[head]
+        chunks = [others.at[2 * n : 2 * n + 2] for n in range(3)]
         biases = [valid_bias(info, n) for n in (1, 2, 3)]
-        _, sums, mixed = attend_chunks(query[head], [o1, o2, o3], biases, scores, old)
+        _, sums, mixed = attend_chunks(query[head], chunks, biases, scores, old)
         mixed = (mixed / jnp.sum(sums, axis=1, keepdims=True)).astype(bf16)
         values[head] = jnp.dot(mixed, value_up[head], preferred_element_type=f32).astype(bf16)
 
-    def project(which, out):
+    for which, out in ((1 - core, send), (core, keep)):
         start = pl.multiple_of(which * 128, 128)
-        left = values[0, pl.ds(start, 128), :]
-        right = values[1, pl.ds(start, 128), :]
-        both = jnp.concatenate([left, right], axis=1)
-        for c in range(0, out.shape[1], 640):
-            out[:, c : c + 640] = jnp.dot(
-                both, out_proj[:, c : c + 640], preferred_element_type=f32
-            ).astype(out.dtype)
-
-    project(1 - core, send)
-    project(core, keep)
+        for head in range(2):
+            out[:, head * VDIM : (head + 1) * VDIM] = values[head, pl.ds(start, 128), :]
+
+
+def project_kernel(own, got, proj_own, proj_got, out):
+    chips, rows, width = out.shape
+    for c in range(0, width, 640):
+        total = jnp.dot(own[...], proj_own[:, c : c + 640], preferred_element_type=f32)
+        total = total + jnp.dot(got[...], proj_got[:, c : c + 640], preferred_element_type=f32)
+        out[:, :, c : c + 640] = total.reshape(chips, rows, 640).astype(bf16)
+
+
+def gather_kernel(p1, p2, p3, out):
+    for n, piece in enumerate((p1, p2, p3)):
+        out[2 * n : 2 * n + 2] = piece[...]
 
 
 def norm_kernel(spread, residual, gain, packed):
@@ -145,8 +138,27 @@
         ).astype(bf16)
 
 
+def store_packed(out, n, rows):
+    left = lax.broadcasted_iota(i32, (SLOTS // 2, 128), 1) < 64
+    out[n, 0:32] = rows[:, :128].astype(bf16)
+    out[n, 32:64] = rows[:, 128:256].astype(bf16)
+    out[n, 64:80] = jnp.where(left, rows[:16, 256:], rows[16:, 256:]).astype(bf16)
+
+
+def load_packed(ref, n):
+    last = ref[n, 64:80]
+    left = jnp.where(lax.broadcasted_iota(i32, (1, 128), 1) < 64, 1.0, 0.0).astype(bf16)
+    last = jnp.concatenate([last * left, last * (1 - left)], axis=0)
+    return jnp.concatenate([ref[n, 0:32], ref[n, 32:64], last], axis=1)
+
+
 def pick_kernel(picker, split, out):
-    out[...] = jnp.dot(picker[...], split[:, : out.shape[1]], preferred_element_type=f32).astype(bf16)
+    values = split[:, :384]
+    doubled = jnp.concatenate([values[:, :320], values[:, 256:320]], axis=1)
+    for r in range(0, picker.shape[0], 256):
+        rows = jnp.dot(picker[r : r + 256, :], doubled, preferred_element_type=f32)
+        for n in range(256 // SLOTS):
+            store_packed(out, r // SLOTS + n, rows[n * SLOTS : (n + 1) * SLOTS])
 
 
 def row_mask(count, j):
@@ -154,38 +166,16 @@
     return jnp.where((slot >= j * CAP) & (slot < (j + 1) * CAP), 1.0, 0.0).astype(bf16)
 
 
-def slot_places(full, packed, expert=None):
-    wide = lax.broadcasted_iota(i32, (full, packed), 0)
-    tight = lax.broadcasted_iota(i32, (full, packed), 1)
-    slot = wide % SLOTS
-    low, high = (0, 3 * CAP) if expert is None else (expert * CAP, (expert + 1) * CAP)
-    found = (wide // SLOTS * 3 * CAP + slot == tight) & (slot >= low) & (slot < high)
-    return jnp.where(found, 1.0, 0.0).astype(bf16)
+def spread_experts(rows, masks):
+    return jnp.concatenate([rows * mask for mask in masks], axis=1)
 
 
 def gate_up_kernel(received, weights, pre):
-    chunks, packed, width = pre.shape
-    full = received.shape[0] // chunks
-    places = slot_places(full, packed)
-    step = 4 * full
-    for r in range(0, received.shape[0], step):
-        rows = received[r : r + step, :]
-        for c in range(0, width, 256):
-            total = jnp.zeros((step, 256), f32)
-            for j in range(3):
-                total = total + jnp.dot(
-                    rows * row_mask(step, j),
-                    weights[j, :, c : c + 256],
-                    preferred_element_type=f32,
-                )
-            total = total.astype(bf16)
-            for n in range(4):
-                pre[r // full + n, :, c : c + 256] = lax.dot_general(
-                    places,
-                    total[n * full : (n + 1) * full],
-                    (((0,), (0,)), ((), ())),
-                    preferred_element_type=f32,
-                ).astype(bf16)
+    masks = [row_mask(256, j) for j in range(3)]
+    for r in range(0, received.shape[0], 8):
+        rows = jnp.concatenate([load_packed(received, r + n) for n in range(8)], axis=0)
+        total = jnp.dot(spread_experts(rows, masks), weights[...], preferred_element_type=f32)
+        pre[r * SLOTS : (r + 8) * SLOTS, :] = total.astype(bf16)
 
 
 def hidden_kernel(parts, out):
@@ -198,29 +188,25 @@
 
 
 def down_kernel(hidden, weights, out):
-    chunks, packed, width = hidden.shape
-    full = out.shape[0] // chunks
-    places = [slot_places(full, packed, j) for j in range(3)]
-    for r in range(0, chunks, 4):
-        total = jnp.zeros((4 * full, out.shape[1]), f32)
-        for j in range(3):
-            rows = [
-                jnp.dot(places[j], hidden[r + n], preferred_element_type=f32).astype(bf16)
-                for n in range(4)
-            ]
-            total = total + nt_dot(jnp.concatenate(rows, axis=0), weights[j])
-        out[r * full : (r + 4) * full, :] = total.astype(bf16)
+    masks = [row_mask(256, j) for j in range(3)]
+    for r in range(0, hidden.shape[0], 256):
+        rows = spread_experts(hidden[r : r + 256, :], masks)
+        total = nt_dot(rows, weights[...])
+        for n in range(256 // SLOTS):
+            store_packed(out, r // SLOTS + n, total[n * SLOTS : (n + 1) * SLOTS])
 
 
 def combine_kernel(weighting, returned, keep, send):
     width = keep.shape[1]
+    rows = jnp.concatenate([load_packed(returned, n) for n in range(returned.shape[0])], axis=0)
     top = weighting[...].astype(bf16)
     rest = (weighting[...] - top.astype(f32)).astype(bf16)
-    mixture = jnp.dot(top, returned[...], preferred_element_type=f32) + jnp.dot(
-        rest, returned[...], preferred_element_type=f32
-    )
+    mixture = jnp.dot(top, rows, preferred_element_type=f32) + jnp.dot(
+        rest, rows, preferred_element_type=f32
+    )
+    tail = mixture[:, 256:320] + mixture[:, 320:384]
     keep[...] = mixture[:, :width]
-    send[...] = mixture[:, width:].astype(bf16)
+    send[...] = jnp.concatenate([mixture[:, width:256], tail], axis=1).astype(bf16)
 
 
 def call(kernel, outs, scratch=(), smem_first=False, count=0):
@@ -280,7 +266,7 @@
         ]
         return lax.ppermute(mine, ("y", "xh"), pairs)
 
-    column = jnp.stack([along_y(1, 3), along_y(2, 4)])
+    column = jnp.stack([along_y(1, 2), along_y(3, 4)])
     to_other = jnp.where(
         (xl == 0) & (xh == 1), jnp.stack([mine, column[0]]), column
     )
@@ -293,7 +279,7 @@
     ]
 
     def blocks_of(x, h):
-        return [2 * (y - 1 - 2 * h) + x, 2 * (y - 2 - 2 * h) + x]
+        return [2 * (y - 1 - h) + x, 2 * (y - 3 - h) + x]
 
     def blocks_sent(x, h):
         near, far = blocks_of(x, h)
@@ -327,21 +313,27 @@
     state = call(
         first_attention_kernel, state_out, [pltpu.VMEM((256, 2 * 256), f32)], True, 4
     )(info, query_rows, keys_own, column)
-    piece_x, peak = lax.optimization_barrier((pieces[1], state[0]))
+    proj_got = lax.ppermute(out_proj, "core", SWAP)
+    piece_x, peak, proj_got = lax.optimization_barrier((pieces[1], state[0], proj_got))
     pieces[1], state = piece_x, [peak] + list(state[1:])
-    others = [lax.ppermute(piece, "core", SWAP) for piece in pieces]
+    first_other = lax.ppermute(column, "core", SWAP)
+    three = call(gather_kernel, [sds((6, half, KEYW), bf16)], count=3)(*pieces[1:])
+    others = lax.ppermute(three, "core", SWAP)
     state = call(
         second_attention_kernel, state_out, [pltpu.VMEM((256, 4 * 256), f32)], True, 9
-    )(info, query_rows, pieces[1], pieces[2], pieces[3], others[0], *state)
+    )(info, query_rows, pieces[1], pieces[2], pieces[3], first_other, *state)
+    values_out = sds((half, local_heads * VDIM), bf16)
     send, keep = call(
         last_attention_kernel,
-        [sds((half, width_model), bf16), sds((half, width_model), f32)],
+        [values_out, values_out],
         [pltpu.VMEM((256, 3 * 256), f32), pltpu.VMEM((2, 256, VDIM), bf16)],
         True,
-        10,
-    )(info, query_rows, others[1], others[2], others[3], *state, value_up, out_proj)
+        7,
+    )(info, query_rows, others, *state, value_up)
     got = lax.ppermute(send, "core", SWAP)
-    pair_sum = (keep + got.astype(f32)).astype(bf16).reshape(16, 8, width_model)
+    pair_sum = call(project_kernel, [sds((16, 8, width_model), bf16)], count=4)(
+        keep, got, out_proj, proj_got
+    )
 
     weights = [expert_gate, expert_up, jnp.transpose(expert_down, (0, 2, 1))]
     low = jnp.concatenate([w[:, :, :ff_half] for w in weights], axis=2)
@@ -359,9 +351,9 @@
     split, w_got = lax.optimization_barrier((split, w_got))
     split = split.reshape(128, 512)
     w_both = jnp.concatenate([w_keep, w_got], axis=1)
-    rows_in = 384
-    w_in = jnp.pad(w_both[:, :, : 2 * ff_half], ((0, 0), (0, rows_in - width_pair), (0, 0)))
-    w_down = w_both[:, :, 2 * ff_half :]
+    w_both = jnp.concatenate([w_both, w_both[:, 256:width_pair]], axis=1)
+    w_in = w_both[:, :, : 2 * ff_half].reshape(3 * 384, 2 * ff_half)
+    w_down = jnp.transpose(w_both[:, :, 2 * ff_half :], (1, 0, 2)).reshape(384, 3 * ff_half)
 
     routes = jnp.transpose(route_ids, (1, 0, 2)).reshape(128, TOPK)
     expert_axis = jnp.arange(EXPERTS, dtype=i32)
@@ -383,21 +375,19 @@
         axis=1,
     )
 
-    outgoing = call(pick_kernel, [sds((32 * SLOTS, rows_in), bf16)], count=2)(picker, split)
-    received = lax.all_to_all(
-        outgoing.reshape(32, SLOTS, rows_in), EXP, split_axis=0, concat_axis=0, tiled=True
-    ).reshape(32 * SLOTS, rows_in)
-    packed_rows = 4 * 3 * CAP
-    pre = call(gate_up_kernel, [sds((8, packed_rows, 2 * ff_half), bf16)], count=2)(received, w_in)
-    pre_parts = lax.all_to_all(pre, "y", split_axis=0, concat_axis=0, tiled=True)
-    hidden = call(hidden_kernel, [sds((8, packed_rows, ff_half), bf16)], count=1)(pre_parts)
+    travel = sds((32, 80, 128), bf16)
+    outgoing = call(pick_kernel, [travel], count=2)(picker, split)
+    received = lax.all_to_all(outgoing, EXP, split_axis=0, concat_axis=0, tiled=True)
+    pre = call(gate_up_kernel, [sds((32 * SLOTS, 2 * ff_half), bf16)], count=2)(received, w_in)
+    pre_parts = lax.all_to_all(
+        pre.reshape(8, 128, 2 * ff_half), "y", split_axis=0, concat_axis=0, tiled=True
+    )
+    hidden = call(hidden_kernel, [sds((8, 128, ff_half), bf16)], count=1)(pre_parts)
     hidden_all = lax.all_to_all(hidden, "y", split_axis=0, concat_axis=0, tiled=True)
-    expert_out = call(down_kernel, [sds((32 * SLOTS, width_pair), bf16)], count=2)(
-        hidden_all, w_down
-    )
-    returned = lax.all_to_all(
-        expert_out.reshape(32, SLOTS, width_pair), EXP, split_axis=0, concat_axis=0, tiled=True
-    ).reshape(32 * SLOTS, width_pair)
+    expert_out = call(down_kernel, [travel], count=2)(
+        hidden_all.reshape(32 * SLOTS, ff_half), w_down
+    )
+    returned = lax.all_to_all(expert_out, EXP, split_axis=0, concat_axis=0, tiled=True)
     mix_keep, mix_send = call(
         combine_kernel, [sds((128, width_out), f32), sds((128, width_out), bf16)], count=2
     )(weighting, returned)

time: 264 us -> 278 us (1.053)
  local copies, waits for them, and re-layouts: 2.64 us -> 31.7 us
  waiting for transfers between devices: 105 us -> 87.9 us
    unnamed x29 -> x52, local copies, waits for them, and re-layouts: 1.6 us -> 17.2 us
    all_to_all x2, waiting for transfers between devices: 44.5 us -> 29.9 us  [the longest x1 19.7 us: on_device(): lax.all_to_all(expert_out, EXP, split_axis=0, concat_axis=0, tiled=True)]
    ppermute x1, starting transfers between devices: 1.92 us -> 6.55 us  [on_device(): lax.ppermute(to_other, ('xl', 'xh'), diagonal)]
    optimization_barrier x0 -> x2, local copies, waits for them, and re-layouts: none -> 4.5 us  [the longest x1 2.47 us: on_device(): split, w_got = lax.optimization_barrier((split, w_got))]
    slice x0 -> x3, local copies, waits for them, and re-layouts: none -> 4.36 us  [the longest x2 4.03 us: on_device(): w_in = w_both[:, :, :2 * ff_half].reshape(3 * 384, 2 * ff_half)]
    all_to_all x1, waiting for transfers between devices: 4.95 us -> 1.28 us  [on_device(): split = lax.all_to_all(packed, CTX, split_axis=0, concat_axis=0, tiled=True)]
    ppermute x1, waiting for transfers between devices: 2.9 us -> 6.56 us  [on_device(): w_got = lax.ppermute(w_send, 'xl', SWAP)]
    slice x2 -> x3, local copies, waits for them, and re-layouts: 0.23 us -> 3.36 us  [on_device(): high = jnp.concatenate([w[:, :, ff_half:] for w in weights], axis=2)]
  transfers between devices with their start and end apart: 17 -> 16, of which waited for: 11 -> 11; matrix products, arithmetic and copies ran while one was open for 3% -> 13% of each run, Pallas kernels for 2% -> 2%
where the time goes in v4:
time: 278 us; the launch traced here: 277 us
  waiting for transfers between devices  87.9 us (32%)
  starting transfers between devices  77.9 us (28%)
  blocking collectives  47.5 us (17%)
  local copies, waits for them, and re-layouts  31.7 us (11%)
  Pallas kernels  21.1 us (8%)
  other arithmetic  8.93 us (3%)
    all_to_all x1, blocking collectives, on_device(): lax.all_to_all(pre.reshape(8, 128, 2 * ff_half), 'y', split_axis=0, conca...  47.5 us
    all_to_all x1, waiting for transfers between devices, on_device(): lax.all_to_all(expert_out, EXP, split_axis=0, concat_axis=0, tiled=True)  19.7 us
    all_to_all x1, waiting for transfers between devices, on_device(): lax.all_to_all(hidden, 'y', split_axis=0, concat_axis=0, tiled=True)  17.2 us
    unnamed x52, local copies, waits for them, and re-layouts  17.2 us
    all_to_all x1, waiting for transfers between devices, on_device(): lax.all_to_all(pair_sum, ('z', 'xh'), split_axis=0, concat_axis=0, tiled=...  15.4 us
    all_to_all x1, starting transfers between devices, on_device(): lax.all_to_all(pair_sum, ('z', 'xh'), split_axis=0, concat_axis=0, tiled=...  13.4 us
    ppermute x2, starting transfers between devices, along_y(): return lax.ppermute(mine, ('y', 'xh'), pairs)  10.4 us
    all_to_all x1, waiting for transfers between devices, on_device(): lax.all_to_all(outgoing, EXP, split_axis=0, concat_axis=0, tiled=True)  10.2 us
  transfers between devices with their start and end apart: 16, of which 11 were waited for; matrix products, arithmetic and copies ran while one was open for 13% of the time, Pallas kernels for 2%

profile of v4, /device:TPU:6, one launch (start us, length us, event | category | flops | bytes accessed | tf_op | source)
XLA Modules:
  0.0 276.7 jit_solution(1873440841856811151)
XLA Ops:
  4.2 4.5 %collective-permute-start = (bf16[128,640]{1,0:T(8,128)(2,1)S(1)}, bf16[128,640]{1,0:T(8,128)(2,1)S(1)}, u32[]{:S(2)}, u32[]{:S(2)}) collective-permute-start(bf16[128,640]{1,0:T(8,128)(2,1)S(1)} %constant_dynamic-slice_fusion), channel_id=1, source_target_pairs={{0,64},{2,130},{64,128},{66,194},{128,192},{130,258},{192,256},{19... | collective-permute-start | bytes 491528 | tf_op jit(solution)/shard_map/ppermute | solution.py:267
  8.7 5.9 %collective-permute-start.1 = (bf16[128,640]{1,0:T(8,128)(2,1)S(1)}, bf16[128,640]{1,0:T(8,128)(2,1)S(1)}, u32[]{:S(2)}, u32[]{:S(2)}) collective-permute-start(bf16[128,640]{1,0:T(8,128)(2,1)S(1)} %constant_dynamic-slice_fusion), channel_id=1, source_target_pairs={{0,192},{2,258},{64,256},{66,322},{128,320},{130,386},{192,384},{1... | collective-permute-start | bytes 491528 | tf_op jit(solution)/shard_map/ppermute | solution.py:267
  14.7 2.6 collective-permute-done
  17.3 7.3 %collective-permute-done.1 = bf16[128,640]{1,0:T(8,128)(2,1)S(1)} collective-permute-done((bf16[128,640]{1,0:T(8,128)(2,1)S(1)}, bf16[128,640]{1,0:T(8,128)(2,1)S(1)}, u32[]{:S(2)}, u32[]{:S(2)}) %collective-permute-start.1) | collective-permute-done | bytes 163872 | tf_op jit(solution)/shard_map/ppermute | solution.py:267
  25.4 2.7 collective-permute-start.4
  28.2 6.6 %collective-permute-start.5 = (bf16[2,128,640]{2,1,0:T(8,128)(2,1)}, bf16[2,128,640]{2,1,0:T(8,128)(2,1)S(1)}, u32[]{:S(2)}, u32[]{:S(2)}) collective-permute-start(bf16[2,128,640]{2,1,0:T(8,128)(2,1)} %get-tuple-element.47), channel_id=1, source_target_pairs={{0,34},{2,32},{32,2},{34,0},{1,35},{3,33},{33,3},{35,1},{4,38},{6,... | collective-permute-start | bytes 983048 | tf_op jit(solution)/shard_map/ppermute | solution.py:278
  34.7 3.4 %collective-permute-start.2 = (bf16[2,128,640]{2,1,0:T(8,128)(2,1)S(1)}, bf16[2,128,640]{2,1,0:T(8,128)(2,1)}, u32[]{:S(2)}, u32[]{:S(2)}) collective-permute-start(bf16[2,128,640]{2,1,0:T(8,128)(2,1)S(1)} %get-tuple-element.48.p0), channel_id=1, source_target_pairs={{0,2},{2,0},{1,3},{3,1},{4,6},{6,4},{5,7},{7,5},{8,10},{10,8},{9,1... | collective-permute-start | bytes 983048 | tf_op jit(solution)/shard_map/ppermute | solution.py:276
  43.7 3.0 %collective-permute-done.2.p1 = bf16[2,128,640]{2,1,0:T(8,128)(2,1)} collective-permute-done((bf16[2,128,640]{2,1,0:T(8,128)(2,1)S(1)}, bf16[2,128,640]{2,1,0:T(8,128)(2,1)}, u32[]{:S(2)}, u32[]{:S(2)}) %collective-permute-start.2) | collective-permute-done | bytes 327712 | tf_op jit(solution)/shard_map/ppermute | solution.py:276
  67.9 3.2 %shard_map.120 = (f32[2,256,128]{2,1,0:T(8,128)S(1)}, f32[2,256,128]{2,1,0:T(8,128)S(1)}, f32[2,256,512]{2,1,0:T(8,128)S(1)}) custom-call(s32[9]{0:T(128)S(1)} %stack.54.info, bf16[2,256,640]{2,1,0:T(8,128)(2,1)S(1)} %bitcast.42, bf16[2,128,640]{2,1,0:T(8,128)(2,1)} %collective-permute-done.2.p1, bf16[2,128,640]{2,1,0:T(8,128)(2,1)S(1)} %collective-permute-done.4.p2, ...), custom_call_target="tpu_custom_call" | custom-call | tf_op jit(solution)/shard_map/pallas_call | solution.py:322
  71.1 4.0 %shard_map.121 = (bf16[128,256]{1,0:T(8,128)(2,1)S(1)}, bf16[128,256]{1,0:T(8,128)(2,1)S(1)}) custom-call(s32[9]{0:T(128)S(1)} %stack.54.info, bf16[2,256,640]{2,1,0:T(8,128)(2,1)S(1)} %bitcast.43, bf16[6,128,640]{2,1,0:T(8,128)(2,1)} %collective-permute-done.6.others, f32[2,256,128]{2,1,0:T(8,128)S(1)} %get-tuple-element.27.old_peak, ...), custom_call_target="tpu_custom_call" | custom-call | tf_op jit(solution)/shard_map/pallas_call | solution.py:326
  80.5 13.4 %all-to-all-start = ((bf16[16,8,2560]{2,1,0:T(8,128)(2,1)}), bf16[16,8,2560]{2,1,0:T(8,128)(2,1)S(1)}, u32[]{:S(2)}, u32[]{:S(2)}) async-start(bf16[16,8,2560]{2,1,0:T(8,128)(2,1)} %shard_map.122), calls=%async_computation | async-start | bytes 1310720 | tf_op jit(solution)/shard_map/all_to_all | solution.py:346
  98.5 15.4 %all-to-all-done.spread = bf16[16,8,2560]{2,1,0:T(8,128)(2,1)S(1)} async-done(((bf16[16,8,2560]{2,1,0:T(8,128)(2,1)}), bf16[16,8,2560]{2,1,0:T(8,128)(2,1)S(1)}, u32[]{:S(2)}, u32[]{:S(2)}) %all-to-all-start) | async-done | bytes 655392 | tf_op jit(solution)/shard_map/all_to_all | solution.py:346
  114.8 9.4 %all-to-all-start.1 = ((bf16[16,8,512]{2,1,0:T(8,128)(2,1)}), bf16[16,8,512]{2,1,0:T(8,128)(2,1)S(1)}, u32[]{:S(2)}, u32[]{:S(2)}) async-start(bf16[16,8,512]{2,1,0:T(8,128)(2,1)} %shard_map.123), calls=%async_computation.1 | async-start | bytes 262144 | tf_op jit(solution)/shard_map/all_to_all | solution.py:350
  124.8 6.6 %collective-permute-done.9 = bf16[3,160,1152]{2,1,0:T(8,128)(2,1)S(1)} collective-permute-done((bf16[3,160,1152]{2,1,0:T(8,128)(2,1)}, bf16[3,160,1152]{2,1,0:T(8,128)(2,1)S(1)}, u32[]{:S(2)}, u32[]{:S(2)}) %collective-permute-start.9) | collective-permute-done | bytes 1105952 | tf_op jit(solution)/shard_map/ppermute | solution.py:344
  133.9 8.9 %all-to-all-start.2 = ((bf16[32,80,128]{2,1,0:T(8,128)(2,1)}), bf16[32,80,128]{2,1,0:T(8,128)(2,1)S(1)}, u32[]{:S(2)}, u32[]{:S(2)}) async-start(bf16[32,80,128]{2,1,0:T(8,128)(2,1)} %shard_map.124), calls=%async_computation.2 | async-start | bytes 1310720 | tf_op jit(solution)/shard_map/all_to_all | solution.py:380
  150.5 2.6 copy.87
  153.1 10.2 %all-to-all-done.2.received = bf16[32,80,128]{2,1,0:T(8,128)(2,1)S(1)} async-done(((bf16[32,80,128]{2,1,0:T(8,128)(2,1)}), bf16[32,80,128]{2,1,0:T(8,128)(2,1)S(1)}, u32[]{:S(2)}, u32[]{:S(2)}) %all-to-all-start.2) | async-done | bytes 655392 | tf_op jit(solution)/shard_map/all_to_all | solution.py:380
  165.5 47.5 %all_to_all.30.parts = bf16[8,128,768]{2,1,0:T(8,128)(2,1)S(1)} all-to-all(bf16[8,128,768]{2,1,0:T(8,128)(2,1)S(1)} %bitcast.45), channel_id=1, replica_groups=mesh['y'=8,'xl'=2,'z'=8,'xh'=2,'core'=2] {'y'}, dimensions={0} | all-to-all | bytes 3145728 | tf_op jit(solution)/shard_map/all_to_all | solution.py:382
  214.2 3.5 %all-to-all-start.4 = ((bf16[8,128,384]{2,1,0:T(8,128)(2,1)}), bf16[8,128,384]{2,1,0:T(8,128)(2,1)S(1)}, u32[]{:S(2)}, u32[]{:S(2)}) async-start(bf16[8,128,384]{2,1,0:T(8,128)(2,1)} %shard_map.126), calls=%async_computation.4 | async-start | bytes 1572864 | tf_op jit(solution)/shard_map/all_to_all | solution.py:386
  217.7 2.5 pad_maximum_fusion.3
  221.9 17.2 %all-to-all-done.4 = bf16[8,128,384]{2,1,0:T(8,128)(2,1)S(1)} async-done(((bf16[8,128,384]{2,1,0:T(8,128)(2,1)}), bf16[8,128,384]{2,1,0:T(8,128)(2,1)S(1)}, u32[]{:S(2)}, u32[]{:S(2)}) %all-to-all-start.4) | async-done | bytes 786464 | tf_op jit(solution)/shard_map/all_to_all | solution.py:386
  241.5 7.2 %all-to-all-start.5 = ((bf16[32,80,128]{2,1,0:T(8,128)(2,1)}), bf16[32,80,128]{2,1,0:T(8,128)(2,1)S(1)}, u32[]{:S(2)}, u32[]{:S(2)}) async-start(bf16[32,80,128]{2,1,0:T(8,128)(2,1)} %shard_map.127), calls=%async_computation.5 | async-start | bytes 1310720 | tf_op jit(solution)/shard_map/all_to_all | solution.py:390
  249.4 19.7 %all-to-all-done.5.returned = bf16[32,80,128]{2,1,0:T(8,128)(2,1)S(1)} async-done(((bf16[32,80,128]{2,1,0:T(8,128)(2,1)}), bf16[32,80,128]{2,1,0:T(8,128)(2,1)S(1)}, u32[]{:S(2)}, u32[]{:S(2)}) %all-to-all-start.5) | async-done | bytes 655392 | tf_op jit(solution)/shard_map/all_to_all | solution.py:390
  272.0 3.9 %collective-permute-done.10 = bf16[128,160]{1,0:T(8,128)(2,1)S(1)} collective-permute-done((bf16[128,160]{1,0:T(8,128)(2,1)S(1)}, bf16[128,160]{1,0:T(8,128)(2,1)S(1)}, u32[]{:S(2)}, u32[]{:S(2)}) %collective-permute-start.10) | collective-permute-done | bytes 40992 | tf_op jit(solution)/shard_map/ppermute | solution.py:394
  (113 shorter events, 64.8 us)
Async XLA Ops:
  0.0 38.1 %copy-start.21 = (s32[256]{0:T(256)S(1)}, s32[256]{0:T(256)}, u32[]{:S(2)}) copy-start(s32[256]{0:T(256)} %param.14) | copy-start | bytes 3076
  0.0 46.7 %collective-permute-start.3 = (bf16[256,2560]{1,0:T(8,128)(2,1)}, bf16[256,2560]{1,0:T(8,128)(2,1)S(1)}, u32[]{:S(2)}, u32[]{:S(2)}) collective-permute-start(bf16[256,2560]{1,0:T(8,128)(2,1)} %proj_own.1), channel_id=1, source_target_pairs={{0,1},{1,0},{2,3},{3,2},{4,5},{5,4},{6,7},{7,6},{8,9},{9,8},{10,11... | collective-permute-start | bytes 3932168 | tf_op jit(solution)/shard_map/ppermute | solution.py:316
  4.2 13.1 %collective-permute-start = (bf16[128,640]{1,0:T(8,128)(2,1)S(1)}, bf16[128,640]{1,0:T(8,128)(2,1)S(1)}, u32[]{:S(2)}, u32[]{:S(2)}) collective-permute-start(bf16[128,640]{1,0:T(8,128)(2,1)S(1)} %constant_dynamic-slice_fusion), channel_id=1, source_target_pairs={{0,64},{2,130},{64,128},{66,194},{128,192},{130,258},{192,256},{19... | collective-permute-start | bytes 491528 | tf_op jit(solution)/shard_map/ppermute | solution.py:267
  8.7 15.9 %collective-permute-start.1 = (bf16[128,640]{1,0:T(8,128)(2,1)S(1)}, bf16[128,640]{1,0:T(8,128)(2,1)S(1)}, u32[]{:S(2)}, u32[]{:S(2)}) collective-permute-start(bf16[128,640]{1,0:T(8,128)(2,1)S(1)} %constant_dynamic-slice_fusion), channel_id=1, source_target_pairs={{0,192},{2,258},{64,256},{66,322},{128,320},{130,386},{192,384},{1... | collective-permute-start | bytes 491528 | tf_op jit(solution)/shard_map/ppermute | solution.py:267
  25.4 21.3 %collective-permute-start.4 = (bf16[2,128,640]{2,1,0:T(8,128)(2,1)}, bf16[2,128,640]{2,1,0:T(8,128)(2,1)S(1)}, u32[]{:S(2)}, u32[]{:S(2)}) collective-permute-start(bf16[2,128,640]{2,1,0:T(8,128)(2,1)} %get-tuple-element.47), channel_id=1, source_target_pairs={{0,32},{32,0},{1,33},{33,1},{2,34},{34,2},{3,35},{35,3},{4,36},{36... | collective-permute-start | bytes 983048 | tf_op jit(solution)/shard_map/ppermute | solution.py:277
  28.2 19.3 %collective-permute-start.5 = (bf16[2,128,640]{2,1,0:T(8,128)(2,1)}, bf16[2,128,640]{2,1,0:T(8,128)(2,1)S(1)}, u32[]{:S(2)}, u32[]{:S(2)}) collective-permute-start(bf16[2,128,640]{2,1,0:T(8,128)(2,1)} %get-tuple-element.47), channel_id=1, source_target_pairs={{0,34},{2,32},{32,2},{34,0},{1,35},{3,33},{33,3},{35,1},{4,38},{6,... | collective-permute-start | bytes 983048 | tf_op jit(solution)/shard_map/ppermute | solution.py:278
  34.7 12.0 %collective-permute-start.2 = (bf16[2,128,640]{2,1,0:T(8,128)(2,1)S(1)}, bf16[2,128,640]{2,1,0:T(8,128)(2,1)}, u32[]{:S(2)}, u32[]{:S(2)}) collective-permute-start(bf16[2,128,640]{2,1,0:T(8,128)(2,1)S(1)} %get-tuple-element.48.p0), channel_id=1, source_target_pairs={{0,2},{2,0},{1,3},{3,1},{4,6},{6,4},{5,7},{7,5},{8,10},{10,8},{9,1... | collective-permute-start | bytes 983048 | tf_op jit(solution)/shard_map/ppermute | solution.py:276
  40.0 11.4 %copy-start.16 = (bf16[3,160,768]{2,1,0:T(8,128)(2,1)S(1)}, bf16[3,160,768]{2,1,0:T(8,128)(2,1)}, u32[]{:S(2)}) copy-start(bf16[3,160,768]{2,1,0:T(8,128)(2,1)} %param.21) | copy-start | bytes 2211844
  43.7 11.1 %copy-start.17 = (bf16[3,160,768]{2,1,0:T(8,128)(2,1)S(1)}, bf16[3,160,768]{2,1,0:T(8,128)(2,1)}, u32[]{:S(2)}) copy-start(bf16[3,160,768]{2,1,0:T(8,128)(2,1)} %param.22) | copy-start | bytes 2211844
  49.4 21.7 %collective-permute-start.6 = (bf16[6,128,640]{2,1,0:T(8,128)(2,1)}, bf16[6,128,640]{2,1,0:T(8,128)(2,1)}, u32[]{:S(2)}, u32[]{:S(2)}) collective-permute-start(bf16[6,128,640]{2,1,0:T(8,128)(2,1)} %shard_map.119), channel_id=1, source_target_pairs={{0,1},{1,0},{2,3},{3,2},{4,5},{5,4},{6,7},{7,6},{8,9},{9,8},{10,11... | collective-permute-start | bytes 2949128 | tf_op jit(solution)/shard_map/ppermute | solution.py:321
  52.3 15.4 %collective-permute-start.7 = (bf16[2,128,640]{2,1,0:T(8,128)(2,1)S(1)}, bf16[2,128,640]{2,1,0:T(8,128)(2,1)S(1)}, u32[]{:S(2)}, u32[]{:S(2)}) collective-permute-start(bf16[2,128,640]{2,1,0:T(8,128)(2,1)S(1)} %get-tuple-element.48.p0), channel_id=1, source_target_pairs={{0,1},{1,0},{2,3},{3,2},{4,5},{5,4},{6,7},{7,6},{8,9},{9,8},{10,11... | collective-permute-start | bytes 983048 | tf_op jit(solution)/shard_map/ppermute | solution.py:319
  71.1 6.0 %copy-start.11 = (bf16[3,160,384]{1,2,0:T(8,128)(2,1)S(1)}, bf16[3,160,384]{1,2,0:T(8,128)(2,1)}, u32[]{:S(2)}) copy-start(bf16[3,160,384]{1,2,0:T(8,128)(2,1)} %copy.91) | copy-start | bytes 1105924
  71.1 6.0 %copy-start.12 = (bf16[3,160,384]{1,2,0:T(8,128)(2,1)S(1)}, bf16[3,160,384]{1,2,0:T(8,128)(2,1)}, u32[]{:S(2)}) copy-start(bf16[3,160,384]{1,2,0:T(8,128)(2,1)} %copy.92) | copy-start | bytes 1105924
  75.2 3.9 %collective-permute-start.8 = (bf16[128,256]{1,0:T(8,128)(2,1)S(1)}, bf16[128,256]{1,0:T(8,128)(2,1)S(1)}, u32[]{:S(2)}, u32[]{:S(2)}) collective-permute-start(bf16[128,256]{1,0:T(8,128)(2,1)S(1)} %get-tuple-element.31), channel_id=1, source_target_pairs={{0,1},{1,0},{2,3},{3,2},{4,5},{5,4},{6,7},{7,6},{8,9},{9,8},{10,11... | collective-permute-start | bytes 196616 | tf_op jit(solution)/shard_map/ppermute | solution.py:333
  80.5 17.4 %copy-start.20 = (f32[2560]{0:T(1024)S(1)}, f32[2560]{0:T(1024)}, u32[]{:S(2)}) copy-start(f32[2560]{0:T(1024)} %param.18) | copy-start | bytes 30724
  80.5 33.3 %all-to-all-start = ((bf16[16,8,2560]{2,1,0:T(8,128)(2,1)}), bf16[16,8,2560]{2,1,0:T(8,128)(2,1)S(1)}, u32[]{:S(2)}, u32[]{:S(2)}) async-start(bf16[16,8,2560]{2,1,0:T(8,128)(2,1)} %shard_map.122), calls=%async_computation | async-start | bytes 1310720 | tf_op jit(solution)/shard_map/all_to_all | solution.py:346
  94.0 19.9 %copy-start.6 = (bf16[8,2560]{1,0:T(8,128)(2,1)S(1)}, bf16[8,2560]{1,0:T(8,128)(2,1)}, u32[]{:S(2)}) copy-start(bf16[8,2560]{1,0:T(8,128)(2,1)} %residual.1) | copy-start | bytes 122884
  96.0 35.4 %collective-permute-start.9 = (bf16[3,160,1152]{2,1,0:T(8,128)(2,1)}, bf16[3,160,1152]{2,1,0:T(8,128)(2,1)S(1)}, u32[]{:S(2)}, u32[]{:S(2)}) collective-permute-start(bf16[3,160,1152]{2,1,0:T(8,128)(2,1)} %copy.82), channel_id=1, source_target_pairs={{0,32},{32,0},{1,33},{33,1},{2,34},{34,2},{3,35},{35,3},{4,36},{36... | collective-permute-start | bytes 3317768 | tf_op jit(solution)/shard_map/ppermute | solution.py:344
  114.8 17.8 %all-to-all-start.1 = ((bf16[16,8,512]{2,1,0:T(8,128)(2,1)}), bf16[16,8,512]{2,1,0:T(8,128)(2,1)S(1)}, u32[]{:S(2)}, u32[]{:S(2)}) async-start(bf16[16,8,512]{2,1,0:T(8,128)(2,1)} %shard_map.123), calls=%async_computation.1 | async-start | bytes 262144 | tf_op jit(solution)/shard_map/all_to_all | solution.py:350
  133.9 29.4 %all-to-all-start.2 = ((bf16[32,80,128]{2,1,0:T(8,128)(2,1)}), bf16[32,80,128]{2,1,0:T(8,128)(2,1)S(1)}, u32[]{:S(2)}, u32[]{:S(2)}) async-start(bf16[32,80,128]{2,1,0:T(8,128)(2,1)} %shard_map.124), calls=%async_computation.2 | async-start | bytes 1310720 | tf_op jit(solution)/shard_map/all_to_all | solution.py:380
  214.2 24.9 %all-to-all-start.4 = ((bf16[8,128,384]{2,1,0:T(8,128)(2,1)}), bf16[8,128,384]{2,1,0:T(8,128)(2,1)S(1)}, u32[]{:S(2)}, u32[]{:S(2)}) async-start(bf16[8,128,384]{2,1,0:T(8,128)(2,1)} %shard_map.126), calls=%async_computation.4 | async-start | bytes 1572864 | tf_op jit(solution)/shard_map/all_to_all | solution.py:386
  239.1 9.9 %copy-start.18 = (f32[8,16,6]{1,0,2:T(8,128)S(1)}, f32[8,16,6]{1,0,2:T(8,128)}, u32[]{:S(2)}) copy-start(f32[8,16,6]{1,0,2:T(8,128)} %param.20) | copy-start | bytes 9220
  241.5 27.7 %all-to-all-start.5 = ((bf16[32,80,128]{2,1,0:T(8,128)(2,1)}), bf16[32,80,128]{2,1,0:T(8,128)(2,1)S(1)}, u32[]{:S(2)}, u32[]{:S(2)}) async-start(bf16[32,80,128]{2,1,0:T(8,128)(2,1)} %shard_map.127), calls=%async_computation.5 | async-start | bytes 1310720 | tf_op jit(solution)/shard_map/all_to_all | solution.py:390
  269.7 6.2 %collective-permute-start.10 = (bf16[128,160]{1,0:T(8,128)(2,1)S(1)}, bf16[128,160]{1,0:T(8,128)(2,1)S(1)}, u32[]{:S(2)}, u32[]{:S(2)}) collective-permute-start(bf16[128,160]{1,0:T(8,128)(2,1)S(1)} %get-tuple-element.38), channel_id=1, source_target_pairs={{0,32},{32,0},{1,33},{33,1},{2,34},{34,2},{3,35},{35,3},{4,36},{36... | collective-permute-start | bytes 122888 | tf_op jit(solution)/shard_map/ppermute | solution.py:394
  (14 other events, 43.0 us)

commit v5 on v4

--- a/solution.py
+++ b/solution.py
@@ -19,7 +19,7 @@
 CTX = ("y", "xl")
 EXP = ("z", "xh", "core")
 SWAP = [(0, 1), (1, 0)]
-BIG_VMEM = pltpu.CompilerParams(vmem_limit_bytes=44 * 2**20)
+BIG_VMEM = pltpu.CompilerParams(vmem_limit_bytes=20 * 2**20)
 f32, bf16, i32 = jnp.float32, jnp.bfloat16, jnp.int32
 
 
@@ -168,6 +168,39 @@
 
 def spread_experts(rows, masks):
     return jnp.concatenate([rows * mask for mask in masks], axis=1)
+
+
+def split_weights_kernel(info, gate, up, down, send, keep):
+    half = gate.shape[2] // 2
+
+    def move(out, start):
+        for n, weights in enumerate((gate, up, down)):
+            out[:, :, n * half : (n + 1) * half] = weights[:, :, start : start + half]
+
+    @pl.when(info[9] == 0)
+    def _():
+        move(keep, 0)
+        move(send, half)
+
+    @pl.when(info[9] != 0)
+    def _():
+        move(keep, half)
+        move(send, 0)
+
+
+def join_weights_kernel(keep, got, into, down):
+    rows = keep.shape[1]
+    wide = into.shape[1]
+    narrow = keep.shape[2] - wide
+    for j in range(3):
+        base = j * 384
+        into[base : base + rows, :] = keep[j, :, :wide]
+        into[base + rows : base + 2 * rows, :] = got[j, :, :wide]
+        into[base + 2 * rows : base + 384, :] = got[j, 256 - rows :, :wide]
+        lanes = slice(j * narrow, (j + 1) * narrow)
+        down[:rows, lanes] = keep[j, :, wide:]
+        down[rows : 2 * rows, lanes] = got[j, :, wide:]
+        down[2 * rows :, lanes] = got[j, 256 - rows :, wide:]
 
 
 def gate_up_kernel(received, weights, pre):
@@ -291,7 +324,7 @@
         + blocks_of(xl, 1 - xh)
         + blocks_sent(1 - xl, xh)
         + blocks_sent(1 - xl, 1 - xh)
-        + [core]
+        + [core, xl]
     ).astype(i32)
 
     masks = jnp.where(own_segment, 0.0, -FAR).astype(bf16)
@@ -313,10 +346,13 @@
     state = call(
         first_attention_kernel, state_out, [pltpu.VMEM((256, 2 * 256), f32)], True, 4
     )(info, query_rows, keys_own, column)
-    proj_got = lax.ppermute(out_proj, "core", SWAP)
-    piece_x, peak, proj_got = lax.optimization_barrier((pieces[1], state[0], proj_got))
+    piece_x, peak = lax.optimization_barrier((pieces[1], state[0]))
     pieces[1], state = piece_x, [peak] + list(state[1:])
+    peak, proj_send = lax.optimization_barrier((state[0], out_proj))
+    state = [peak] + list(state[1:])
     first_other = lax.ppermute(column, "core", SWAP)
+    proj_got = lax.ppermute(proj_send, "core", SWAP)
+    pieces[2], proj_got = lax.optimization_barrier((pieces[2], proj_got))
     three = call(gather_kernel, [sds((6, half, KEYW), bf16)], count=3)(*pieces[1:])
     others = lax.ppermute(three, "core", SWAP)
     state = call(
@@ -335,11 +371,10 @@
         keep, got, out_proj, proj_got
     )
 
-    weights = [expert_gate, expert_up, jnp.transpose(expert_down, (0, 2, 1))]
-    low = jnp.concatenate([w[:, :, :ff_half] for w in weights], axis=2)
-    high = jnp.concatenate([w[:, :, ff_half:] for w in weights], axis=2)
-    w_send = jnp.where(xl == 0, high, low)
-    w_keep = jnp.where(xl == 0, low, high)
+    weights_out = sds((3, width_out, 3 * ff_half), bf16)
+    w_send, w_keep = call(split_weights_kernel, [weights_out, weights_out], (), True, 4)(
+        info, expert_gate, expert_up, jnp.transpose(expert_down, (0, 2, 1))
+    )
     pair_sum, w_send = lax.optimization_barrier((pair_sum, w_send))
     w_got = lax.ppermute(w_send, "xl", SWAP)
 
@@ -350,10 +385,11 @@
     split = lax.all_to_all(packed, CTX, split_axis=0, concat_axis=0, tiled=True)
     split, w_got = lax.optimization_barrier((split, w_got))
     split = split.reshape(128, 512)
-    w_both = jnp.concatenate([w_keep, w_got], axis=1)
-    w_both = jnp.concatenate([w_both, w_both[:, 256:width_pair]], axis=1)
-    w_in = w_both[:, :, : 2 * ff_half].reshape(3 * 384, 2 * ff_half)
-    w_down = jnp.transpose(w_both[:, :, 2 * ff_half :], (1, 0, 2)).reshape(384, 3 * ff_half)
+    w_in, w_down = call(
+        join_weights_kernel,
+        [sds((3 * 384, 2 * ff_half), bf16), sds((384, 3 * ff_half), bf16)],
+        count=2,
+    )(w_keep, w_got)
 
     routes = jnp.transpose(route_ids, (1, 0, 2)).reshape(128, TOPK)
     expert_axis = jnp.arange(EXPERTS, dtype=i32)

time: 278 us -> 262 us (0.942)
  local copies, waits for them, and re-layouts: 31.7 us -> 5.15 us
  blocking collectives: 47.5 us -> 71.1 us
  starting transfers between devices: 77.9 us -> 67.4 us
  waiting for transfers between devices: 87.9 us -> 95 us
  other arithmetic: 8.93 us -> 2.38 us
  Pallas kernels: 21.1 us -> 17.9 us
    all_to_all x0 -> x1, blocking collectives: none -> 24.1 us  [on_device(): lax.all_to_all(hidden, 'y', split_axis=0, concat_axis=0, tiled=True)]
    all_to_all x1 -> x0, waiting for transfers between devices: 17.2 us -> none  [on_device(): lax.all_to_all(hidden, 'y', split_axis=0, concat_axis=0, tiled=True)]
    unnamed x52 -> x43, local copies, waits for them, and re-layouts: 17.2 us -> 4.46 us
    all_to_all x1, waiting for transfers between devices: 10.2 us -> 18.1 us  [on_device(): lax.all_to_all(outgoing, EXP, split_axis=0, concat_axis=0, tiled=True)]
    slice x6 -> x0, local copies, waits for them, and re-layouts: 7.72 us -> none  [the longest x2 4.03 us: on_device(): w_in = w_both[:, :, :2 * ff_half].reshape(3 * 384, 2 * ff_half)]
    ppermute x1, waiting for transfers between devices: 0.01 us -> 7.14 us  [on_device(): lax.ppermute(to_other, 'xl', SWAP)]
    optimization_barrier x2 -> x0, local copies, waits for them, and re-layouts: 4.5 us -> none  [the longest x1 2.47 us: on_device(): split, w_got = lax.optimization_barrier((split, w_got))]
    ppermute x1, starting transfers between devices: 6.55 us -> 2.11 us  [on_device(): lax.ppermute(to_other, ('xl', 'xh'), diagonal)]
  transfers between devices with their start and end apart: 16 -> 15, of which waited for: 11 -> 13; matrix products, arithmetic and copies ran while one was open for 13% -> 1% of each run, Pallas kernels for 2% -> 3%
where the time goes in v5:
time: 262 us; the launch traced here: 261 us
  waiting for transfers between devices  95 us (36%)
  blocking collectives  71.1 us (27%)
  starting transfers between devices  67.4 us (26%)
  Pallas kernels  17.9 us (7%)
  local copies, waits for them, and re-layouts  5.15 us (2%)
    all_to_all x1, blocking collectives, on_device(): lax.all_to_all(pre.reshape(8, 128, 2 * ff_half), 'y', split_axis=0, conca...  47.1 us
    all_to_all x1, blocking collectives, on_device(): lax.all_to_all(hidden, 'y', split_axis=0, concat_axis=0, tiled=True)  24.1 us
    all_to_all x1, waiting for transfers between devices, on_device(): lax.all_to_all(expert_out, EXP, split_axis=0, concat_axis=0, tiled=True)  19.7 us
    all_to_all x1, waiting for transfers between devices, on_device(): lax.all_to_all(outgoing, EXP, split_axis=0, concat_axis=0, tiled=True)  18.1 us
    all_to_all x1, waiting for transfers between devices, on_device(): lax.all_to_all(pair_sum, ('z', 'xh'), split_axis=0, concat_axis=0, tiled=...  17.2 us
    all_to_all x1, starting transfers between devices, on_device(): lax.all_to_all(pair_sum, ('z', 'xh'), split_axis=0, concat_axis=0, tiled=...  13.4 us
    ppermute x2, starting transfers between devices, along_y(): return lax.ppermute(mine, ('y', 'xh'), pairs)  10.4 us
    ppermute x2, waiting for transfers between devices, along_y(): return lax.ppermute(mine, ('y', 'xh'), pairs)  9.67 us
  transfers between devices with their start and end apart: 15, of which 13 were waited for; matrix products, arithmetic and copies ran while one was open for 1% of the time, Pallas kernels for 3%

profile of v5, /device:TPU:6, one launch (start us, length us, event | category | flops | bytes accessed | tf_op | source)
XLA Modules:
  0.0 260.6 jit_solution(13382619605503882616)
XLA Ops:
  2.2 4.5 %collective-permute-start = (bf16[128,640]{1,0:T(8,128)(2,1)S(1)}, bf16[128,640]{1,0:T(8,128)(2,1)S(1)}, u32[]{:S(2)}, u32[]{:S(2)}) collective-permute-start(bf16[128,640]{1,0:T(8,128)(2,1)S(1)} %constant_dynamic-slice_fusion), channel_id=1, source_target_pairs={{0,64},{2,130},{64,128},{66,194},{128,192},{130,258},{192,256},{19... | collective-permute-start | bytes 491528 | tf_op jit(solution)/shard_map/ppermute | solution.py:300
  6.7 5.9 %collective-permute-start.1 = (bf16[128,640]{1,0:T(8,128)(2,1)S(1)}, bf16[128,640]{1,0:T(8,128)(2,1)S(1)}, u32[]{:S(2)}, u32[]{:S(2)}) collective-permute-start(bf16[128,640]{1,0:T(8,128)(2,1)S(1)} %constant_dynamic-slice_fusion), channel_id=1, source_target_pairs={{0,192},{2,258},{64,256},{66,322},{128,320},{130,386},{192,384},{1... | collective-permute-start | bytes 491528 | tf_op jit(solution)/shard_map/ppermute | solution.py:300
  14.7 7.7 %collective-permute-done.1 = bf16[128,640]{1,0:T(8,128)(2,1)S(1)} collective-permute-done((bf16[128,640]{1,0:T(8,128)(2,1)S(1)}, bf16[128,640]{1,0:T(8,128)(2,1)S(1)}, u32[]{:S(2)}, u32[]{:S(2)}) %collective-permute-start.1) | collective-permute-done | bytes 163872 | tf_op jit(solution)/shard_map/ppermute | solution.py:300
  22.5 2.6 %collective-permute-start.2 = (bf16[2,128,640]{2,1,0:T(8,128)(2,1)S(1)}, bf16[2,128,640]{2,1,0:T(8,128)(2,1)S(1)}, u32[]{:S(2)}, u32[]{:S(2)}) collective-permute-start(bf16[2,128,640]{2,1,0:T(8,128)(2,1)S(1)} %get-tuple-element.54.p0), channel_id=1, source_target_pairs={{0,2},{2,0},{1,3},{3,1},{4,6},{6,4},{5,7},{7,5},{8,10},{10,8},{9,1... | collective-permute-start | bytes 983048 | tf_op jit(solution)/shard_map/ppermute | solution.py:309
  27.9 6.5 %collective-permute-done.2.p1 = bf16[2,128,640]{2,1,0:T(8,128)(2,1)S(1)} collective-permute-done((bf16[2,128,640]{2,1,0:T(8,128)(2,1)S(1)}, bf16[2,128,640]{2,1,0:T(8,128)(2,1)S(1)}, u32[]{:S(2)}, u32[]{:S(2)}) %collective-permute-start.2) | collective-permute-done | bytes 327712 | tf_op jit(solution)/shard_map/ppermute | solution.py:309
  36.3 2.7 %collective-permute-start.3 = (bf16[2,128,640]{2,1,0:T(8,128)(2,1)S(1)}, bf16[2,128,640]{2,1,0:T(8,128)(2,1)S(1)}, u32[]{:S(2)}, u32[]{:S(2)}) collective-permute-start(bf16[2,128,640]{2,1,0:T(8,128)(2,1)S(1)} %get-tuple-element.53), channel_id=1, source_target_pairs={{0,32},{32,0},{1,33},{33,1},{2,34},{34,2},{3,35},{35,3},{4,36},{36... | collective-permute-start | bytes 983048 | tf_op jit(solution)/shard_map/ppermute | solution.py:310
  41.2 7.1 %collective-permute-done.3.p2 = bf16[2,128,640]{2,1,0:T(8,128)(2,1)S(1)} collective-permute-done((bf16[2,128,640]{2,1,0:T(8,128)(2,1)S(1)}, bf16[2,128,640]{2,1,0:T(8,128)(2,1)S(1)}, u32[]{:S(2)}, u32[]{:S(2)}) %collective-permute-start.3) | collective-permute-done | bytes 327712 | tf_op jit(solution)/shard_map/ppermute | solution.py:310
  48.3 3.7 %collective-permute-done.5.p3 = bf16[2,128,640]{2,1,0:T(8,128)(2,1)S(1)} collective-permute-done((bf16[2,128,640]{2,1,0:T(8,128)(2,1)S(1)}, bf16[2,128,640]{2,1,0:T(8,128)(2,1)S(1)}, u32[]{:S(2)}, u32[]{:S(2)}) %collective-permute-start.5) | collective-permute-done | bytes 327712 | tf_op jit(solution)/shard_map/ppermute | solution.py:311
  54.0 2.4 collective-permute-start.7
  57.6 2.7 %shard_map.120 = (f32[2,256,128]{2,1,0:T(8,128)S(1)}, f32[2,256,128]{2,1,0:T(8,128)S(1)}, f32[2,256,512]{2,1,0:T(8,128)S(1)}) custom-call(s32[10]{0:T(128)S(1)} %stack.58.info, bf16[2,256,640]{2,1,0:T(8,128)(2,1)S(1)} %bitcast.39, bf16[2,128,640]{2,1,0:T(8,128)(2,1)S(1)} %collective-permute-done.2.p1, bf16[2,128,640]{2,1,0:T(8,128)(2,1)S(1)} %collective-permute-done.3.p2, ...), custom_call_target="tpu_custom_call" | custom-call | tf_op jit(solution)/shard_map/pallas_call | solution.py:358
  60.4 3.3 %shard_map.121 = (bf16[128,256]{1,0:T(8,128)(2,1)S(1)}, bf16[128,256]{1,0:T(8,128)(2,1)S(1)}) custom-call(s32[10]{0:T(128)S(1)} %stack.58.info, bf16[2,256,640]{2,1,0:T(8,128)(2,1)S(1)} %bitcast.40, bf16[6,128,640]{2,1,0:T(8,128)(2,1)S(1)} %collective-permute-done.6.others, f32[2,256,128]{2,1,0:T(8,128)S(1)} %get-tuple-element.37.old_peak, ...), custom_call_target="tpu_custom_call" | custom-call | tf_op jit(solution)/shard_map/pallas_call | solution.py:362
  68.3 13.4 %all-to-all-start = ((bf16[16,8,2560]{2,1,0:T(8,128)(2,1)}), bf16[16,8,2560]{2,1,0:T(8,128)(2,1)S(1)}, u32[]{:S(2)}, u32[]{:S(2)}) async-start(bf16[16,8,2560]{2,1,0:T(8,128)(2,1)} %shard_map.122), calls=%async_computation | async-start | bytes 1310720 | tf_op jit(solution)/shard_map/all_to_all | solution.py:381
  84.2 17.2 %all-to-all-done.spread = bf16[16,8,2560]{2,1,0:T(8,128)(2,1)S(1)} async-done(((bf16[16,8,2560]{2,1,0:T(8,128)(2,1)}), bf16[16,8,2560]{2,1,0:T(8,128)(2,1)S(1)}, u32[]{:S(2)}, u32[]{:S(2)}) %all-to-all-start) | async-done | bytes 655392 | tf_op jit(solution)/shard_map/all_to_all | solution.py:381
  102.4 8.9 %all-to-all-start.1 = ((bf16[16,8,512]{2,1,0:T(8,128)(2,1)}), bf16[16,8,512]{2,1,0:T(8,128)(2,1)S(1)}, u32[]{:S(2)}, u32[]{:S(2)}) async-start(bf16[16,8,512]{2,1,0:T(8,128)(2,1)} %shard_map.124), calls=%async_computation.1 | async-start | bytes 262144 | tf_op jit(solution)/shard_map/all_to_all | solution.py:385
  111.9 5.2 %collective-permute-done.9.got = bf16[3,160,1152]{2,1,0:T(8,128)(2,1)S(1)} collective-permute-done((bf16[3,160,1152]{2,1,0:T(8,128)(2,1)}, bf16[3,160,1152]{2,1,0:T(8,128)(2,1)S(1)}, u32[]{:S(2)}, u32[]{:S(2)}) %collective-permute-start.9) | collective-permute-done | bytes 1105952 | tf_op jit(solution)/shard_map/ppermute | solution.py:379
  117.1 2.6 %all-to-all-done.1 = bf16[16,8,512]{2,1,0:T(8,128)(2,1)S(1)} async-done(((bf16[16,8,512]{2,1,0:T(8,128)(2,1)}), bf16[16,8,512]{2,1,0:T(8,128)(2,1)S(1)}, u32[]{:S(2)}, u32[]{:S(2)}) %all-to-all-start.1) | async-done | bytes 131104 | tf_op jit(solution)/shard_map/all_to_all | solution.py:385
  121.6 7.3 %all-to-all-start.2 = ((bf16[32,80,128]{2,1,0:T(8,128)(2,1)}), bf16[32,80,128]{2,1,0:T(8,128)(2,1)S(1)}, u32[]{:S(2)}, u32[]{:S(2)}) async-start(bf16[32,80,128]{2,1,0:T(8,128)(2,1)} %shard_map.125), calls=%async_computation.2 | async-start | bytes 1310720 | tf_op jit(solution)/shard_map/all_to_all | solution.py:416
  131.3 18.1 %all-to-all-done.2.received = bf16[32,80,128]{2,1,0:T(8,128)(2,1)S(1)} async-done(((bf16[32,80,128]{2,1,0:T(8,128)(2,1)}), bf16[32,80,128]{2,1,0:T(8,128)(2,1)S(1)}, u32[]{:S(2)}, u32[]{:S(2)}) %all-to-all-start.2) | async-done | bytes 655392 | tf_op jit(solution)/shard_map/all_to_all | solution.py:416
  151.7 47.1 %all_to_all.30.parts = bf16[8,128,768]{2,1,0:T(8,128)(2,1)S(1)} all-to-all(bf16[8,128,768]{2,1,0:T(8,128)(2,1)S(1)} %bitcast.41), channel_id=1, replica_groups=mesh['y'=8,'xl'=2,'z'=8,'xh'=2,'core'=2] {'y'}, dimensions={0} | all-to-all | bytes 3145728 | tf_op jit(solution)/shard_map/all_to_all | solution.py:418
  199.0 24.1 %all_to_all.31 = bf16[8,128,384]{2,1,0:T(8,128)(2,1)S(1)} all-to-all(bf16[8,128,384]{2,1,0:T(8,128)(2,1)S(1)} %shard_map.128), channel_id=1, replica_groups=mesh['y'=8,'xl'=2,'z'=8,'xh'=2,'core'=2] {'y'}, dimensions={0} | all-to-all | bytes 1572864 | tf_op jit(solution)/shard_map/all_to_all | solution.py:422
  225.4 7.1 %all-to-all-start.5 = ((bf16[32,80,128]{2,1,0:T(8,128)(2,1)}), bf16[32,80,128]{2,1,0:T(8,128)(2,1)S(1)}, u32[]{:S(2)}, u32[]{:S(2)}) async-start(bf16[32,80,128]{2,1,0:T(8,128)(2,1)} %shard_map.129), calls=%async_computation.5 | async-start | bytes 1310720 | tf_op jit(solution)/shard_map/all_to_all | solution.py:426
  233.3 19.7 %all-to-all-done.5.returned = bf16[32,80,128]{2,1,0:T(8,128)(2,1)S(1)} async-done(((bf16[32,80,128]{2,1,0:T(8,128)(2,1)}), bf16[32,80,128]{2,1,0:T(8,128)(2,1)S(1)}, u32[]{:S(2)}, u32[]{:S(2)}) %all-to-all-start.5) | async-done | bytes 655392 | tf_op jit(solution)/shard_map/all_to_all | solution.py:426
  253.6 2.4 collective-permute-start.10
  256.0 3.8 %collective-permute-done.10 = bf16[128,160]{1,0:T(8,128)(2,1)S(1)} collective-permute-done((bf16[128,160]{1,0:T(8,128)(2,1)S(1)}, bf16[128,160]{1,0:T(8,128)(2,1)S(1)}, u32[]{:S(2)}, u32[]{:S(2)}) %collective-permute-start.10) | collective-permute-done | bytes 40992 | tf_op jit(solution)/shard_map/ppermute | solution.py:430
  (93 shorter events, 34.0 us)
Async XLA Ops:
  0.0 25.1 %copy-start.19 = (s32[256]{0:T(256)S(1)}, s32[256]{0:T(256)}, u32[]{:S(2)}) copy-start(s32[256]{0:T(256)} %param.14) | copy-start | bytes 3076
  0.0 25.3 %copy-start.13 = (bf16[256,2,576]{0,2,1:T(8,128)(2,1)S(1)}, bf16[256,2,576]{0,2,1:T(8,128)(2,1)}, u32[]{:S(2)}) copy-start(bf16[256,2,576]{0,2,1:T(8,128)(2,1)} %param.12) | copy-start | bytes 1769476
  2.2 12.5 %collective-permute-start = (bf16[128,640]{1,0:T(8,128)(2,1)S(1)}, bf16[128,640]{1,0:T(8,128)(2,1)S(1)}, u32[]{:S(2)}, u32[]{:S(2)}) collective-permute-start(bf16[128,640]{1,0:T(8,128)(2,1)S(1)} %constant_dynamic-slice_fusion), channel_id=1, source_target_pairs={{0,64},{2,130},{64,128},{66,194},{128,192},{130,258},{192,256},{19... | collective-permute-start | bytes 491528 | tf_op jit(solution)/shard_map/ppermute | solution.py:300
  6.7 15.7 %collective-permute-start.1 = (bf16[128,640]{1,0:T(8,128)(2,1)S(1)}, bf16[128,640]{1,0:T(8,128)(2,1)S(1)}, u32[]{:S(2)}, u32[]{:S(2)}) collective-permute-start(bf16[128,640]{1,0:T(8,128)(2,1)S(1)} %constant_dynamic-slice_fusion), channel_id=1, source_target_pairs={{0,192},{2,258},{64,256},{66,322},{128,320},{130,386},{192,384},{1... | collective-permute-start | bytes 491528 | tf_op jit(solution)/shard_map/ppermute | solution.py:300
  22.5 11.9 %collective-permute-start.2 = (bf16[2,128,640]{2,1,0:T(8,128)(2,1)S(1)}, bf16[2,128,640]{2,1,0:T(8,128)(2,1)S(1)}, u32[]{:S(2)}, u32[]{:S(2)}) collective-permute-start(bf16[2,128,640]{2,1,0:T(8,128)(2,1)S(1)} %get-tuple-element.54.p0), channel_id=1, source_target_pairs={{0,2},{2,0},{1,3},{3,1},{4,6},{6,4},{5,7},{7,5},{8,10},{10,8},{9,1... | collective-permute-start | bytes 983048 | tf_op jit(solution)/shard_map/ppermute | solution.py:309
  34.4 13.9 %collective-permute-start.4 = (bf16[256,2560]{1,0:T(8,128)(2,1)S(1)}, bf16[256,2560]{1,0:T(8,128)(2,1)S(1)}, u32[]{:S(2)}, u32[]{:S(2)}) collective-permute-start(bf16[256,2560]{1,0:T(8,128)(2,1)S(1)} %copy-done), channel_id=1, source_target_pairs={{0,1},{1,0},{2,3},{3,2},{4,5},{5,4},{6,7},{7,6},{8,9},{9,8},{10,11... | collective-permute-start | bytes 3932168 | tf_op jit(solution)/shard_map/ppermute | solution.py:354
  36.3 12.0 %collective-permute-start.3 = (bf16[2,128,640]{2,1,0:T(8,128)(2,1)S(1)}, bf16[2,128,640]{2,1,0:T(8,128)(2,1)S(1)}, u32[]{:S(2)}, u32[]{:S(2)}) collective-permute-start(bf16[2,128,640]{2,1,0:T(8,128)(2,1)S(1)} %get-tuple-element.53), channel_id=1, source_target_pairs={{0,32},{32,0},{1,33},{33,1},{2,34},{34,2},{3,35},{35,3},{4,36},{36... | collective-permute-start | bytes 983048 | tf_op jit(solution)/shard_map/ppermute | solution.py:310
  39.0 12.9 %collective-permute-start.5 = (bf16[2,128,640]{2,1,0:T(8,128)(2,1)S(1)}, bf16[2,128,640]{2,1,0:T(8,128)(2,1)S(1)}, u32[]{:S(2)}, u32[]{:S(2)}) collective-permute-start(bf16[2,128,640]{2,1,0:T(8,128)(2,1)S(1)} %get-tuple-element.53), channel_id=1, source_target_pairs={{0,34},{2,32},{32,2},{34,0},{1,35},{3,33},{33,3},{35,1},{4,38},{6,... | collective-permute-start | bytes 983048 | tf_op jit(solution)/shard_map/ppermute | solution.py:311
  52.0 8.3 %collective-permute-start.6 = (bf16[6,128,640]{2,1,0:T(8,128)(2,1)S(1)}, bf16[6,128,640]{2,1,0:T(8,128)(2,1)S(1)}, u32[]{:S(2)}, u32[]{:S(2)}) collective-permute-start(bf16[6,128,640]{2,1,0:T(8,128)(2,1)S(1)} %shard_map.119), channel_id=1, source_target_pairs={{0,1},{1,0},{2,3},{3,2},{4,5},{5,4},{6,7},{7,6},{8,9},{9,8},{10,11... | collective-permute-start | bytes 2949128 | tf_op jit(solution)/shard_map/ppermute | solution.py:357
  54.0 3.6 %collective-permute-start.7 = (bf16[2,128,640]{2,1,0:T(8,128)(2,1)S(1)}, bf16[2,128,640]{2,1,0:T(8,128)(2,1)S(1)}, u32[]{:S(2)}, u32[]{:S(2)}) collective-permute-start(bf16[2,128,640]{2,1,0:T(8,128)(2,1)S(1)} %get-tuple-element.54.p0), channel_id=1, source_target_pairs={{0,1},{1,0},{2,3},{3,2},{4,5},{5,4},{6,7},{7,6},{8,9},{9,8},{10,11... | collective-permute-start | bytes 983048 | tf_op jit(solution)/shard_map/ppermute | solution.py:353
  63.7 3.2 %collective-permute-start.8 = (bf16[128,256]{1,0:T(8,128)(2,1)S(1)}, bf16[128,256]{1,0:T(8,128)(2,1)S(1)}, u32[]{:S(2)}, u32[]{:S(2)}) collective-permute-start(bf16[128,256]{1,0:T(8,128)(2,1)S(1)} %get-tuple-element.41), channel_id=1, source_target_pairs={{0,1},{1,0},{2,3},{3,2},{4,5},{5,4},{6,7},{7,6},{8,9},{9,8},{10,11... | collective-permute-start | bytes 196616 | tf_op jit(solution)/shard_map/ppermute | solution.py:369
  66.9 16.8 %copy-start.18 = (f32[2560]{0:T(1024)S(1)}, f32[2560]{0:T(1024)}, u32[]{:S(2)}) copy-start(f32[2560]{0:T(1024)} %param.18) | copy-start | bytes 30724
  66.9 16.8 %copy-start.17 = (s32[8,16,6]{1,0,2:T(8,128)S(1)}, s32[8,16,6]{1,0,2:T(8,128)}, u32[]{:S(2)}) copy-start(s32[8,16,6]{1,0,2:T(8,128)} %param.19) | copy-start | bytes 9220
  68.3 33.1 %copy-start.11 = (bf16[8,2560]{1,0:T(8,128)(2,1)S(1)}, bf16[8,2560]{1,0:T(8,128)(2,1)}, u32[]{:S(2)}) copy-start(bf16[8,2560]{1,0:T(8,128)(2,1)} %residual.1) | copy-start | bytes 122884
  68.3 33.1 %all-to-all-start = ((bf16[16,8,2560]{2,1,0:T(8,128)(2,1)}), bf16[16,8,2560]{2,1,0:T(8,128)(2,1)S(1)}, u32[]{:S(2)}, u32[]{:S(2)}) async-start(bf16[16,8,2560]{2,1,0:T(8,128)(2,1)} %shard_map.122), calls=%async_computation | async-start | bytes 1310720 | tf_op jit(solution)/shard_map/all_to_all | solution.py:381
  81.7 35.4 %collective-permute-start.9 = (bf16[3,160,1152]{2,1,0:T(8,128)(2,1)}, bf16[3,160,1152]{2,1,0:T(8,128)(2,1)S(1)}, u32[]{:S(2)}, u32[]{:S(2)}) collective-permute-start(bf16[3,160,1152]{2,1,0:T(8,128)(2,1)} %copy-done.12), channel_id=1, source_target_pairs={{0,32},{32,0},{1,33},{33,1},{2,34},{34,2},{3,35},{35,3},{4,36},{36... | collective-permute-start | bytes 3317768 | tf_op jit(solution)/shard_map/ppermute | solution.py:379
  83.7 37.9 %copy-start.14 = (s32[8,16,6]{0,1,2:T(8,128)}, s32[8,16,6]{0,1,2:T(8,128)S(1)}, u32[]{:S(2)}) copy-start(s32[8,16,6]{0,1,2:T(8,128)S(1)} %copy.42) | copy-start | bytes 9220
  102.4 17.4 %all-to-all-start.1 = ((bf16[16,8,512]{2,1,0:T(8,128)(2,1)}), bf16[16,8,512]{2,1,0:T(8,128)(2,1)S(1)}, u32[]{:S(2)}, u32[]{:S(2)}) async-start(bf16[16,8,512]{2,1,0:T(8,128)(2,1)} %shard_map.124), calls=%async_computation.1 | async-start | bytes 262144 | tf_op jit(solution)/shard_map/all_to_all | solution.py:385
  117.1 11.8 %copy-start.1 = (bf16[3,160,1152]{2,1,0:T(8,128)(2,1)}, bf16[3,160,1152]{2,1,0:T(8,128)(2,1)S(1)}, u32[]{:S(2)}) copy-start(bf16[3,160,1152]{2,1,0:T(8,128)(2,1)S(1)} %collective-permute-done.9.got) | copy-start | bytes 3317764
  121.6 27.8 %all-to-all-start.2 = ((bf16[32,80,128]{2,1,0:T(8,128)(2,1)}), bf16[32,80,128]{2,1,0:T(8,128)(2,1)S(1)}, u32[]{:S(2)}, u32[]{:S(2)}) async-start(bf16[32,80,128]{2,1,0:T(8,128)(2,1)} %shard_map.125), calls=%async_computation.2 | async-start | bytes 1310720 | tf_op jit(solution)/shard_map/all_to_all | solution.py:416
  198.7 24.3 %copy-start.4 = (bf16[384,1152]{1,0:T(8,128)(2,1)S(1)}, bf16[384,1152]{1,0:T(8,128)(2,1)}, u32[]{:S(2)}) copy-start(bf16[384,1152]{1,0:T(8,128)(2,1)} %copy-done.3) | copy-start | bytes 2654212
  225.4 34.3 %copy-start.6 = (bf16[16,8,512]{2,1,0:T(8,128)(2,1)S(1)}, bf16[16,8,512]{2,1,0:T(8,128)(2,1)}, u32[]{:S(2)}) copy-start(bf16[16,8,512]{2,1,0:T(8,128)(2,1)} %copy-done.5) | copy-start | bytes 393220
  225.4 27.6 %all-to-all-start.5 = ((bf16[32,80,128]{2,1,0:T(8,128)(2,1)}), bf16[32,80,128]{2,1,0:T(8,128)(2,1)S(1)}, u32[]{:S(2)}, u32[]{:S(2)}) async-start(bf16[32,80,128]{2,1,0:T(8,128)(2,1)} %shard_map.129), calls=%async_computation.5 | async-start | bytes 1310720 | tf_op jit(solution)/shard_map/all_to_all | solution.py:426
  253.6 6.2 %collective-permute-start.10 = (bf16[128,160]{1,0:T(8,128)(2,1)S(1)}, bf16[128,160]{1,0:T(8,128)(2,1)S(1)}, u32[]{:S(2)}, u32[]{:S(2)}) collective-permute-start(bf16[128,160]{1,0:T(8,128)(2,1)S(1)} %get-tuple-element.52), channel_id=1, source_target_pairs={{0,32},{32,0},{1,33},{33,1},{2,34},{34,2},{3,35},{35,3},{4,36},{36... | collective-permute-start | bytes 122888 | tf_op jit(solution)/shard_map/ppermute | solution.py:430
  (11 other events, 51.8 us)

commit v6 on v5

--- a/solution.py
+++ b/solution.py
@@ -86,7 +86,7 @@
 
 
 def last_attention_kernel(
-    info, query, others, old_peak, old_sums, old_mixed, value_up, send, keep, scores, values
+    info, query, others, old_peak, old_sums, old_mixed, value_up, out_proj, send, keep, scores, values
 ):
     core = info[8]
 
@@ -99,18 +99,20 @@
         mixed = (mixed / jnp.sum(sums, axis=1, keepdims=True)).astype(bf16)
         values[head] = jnp.dot(mixed, value_up[head], preferred_element_type=f32).astype(bf16)
 
-    for which, out in ((1 - core, send), (core, keep)):
+    def project(which, out):
         start = pl.multiple_of(which * 128, 128)
-        for head in range(2):
-            out[:, head * VDIM : (head + 1) * VDIM] = values[head, pl.ds(start, 128), :]
-
-
-def project_kernel(own, got, proj_own, proj_got, out):
-    chips, rows, width = out.shape
-    for c in range(0, width, 640):
-        total = jnp.dot(own[...], proj_own[:, c : c + 640], preferred_element_type=f32)
-        total = total + jnp.dot(got[...], proj_got[:, c : c + 640], preferred_element_type=f32)
-        out[:, :, c : c + 640] = total.reshape(chips, rows, 640).astype(bf16)
+        both = jnp.concatenate([values[head, pl.ds(start, 128), :] for head in range(2)], axis=1)
+        for c in range(0, out.shape[1], 640):
+            out[:, c : c + 640] = jnp.dot(
+                both, out_proj[:, c : c + 640], preferred_element_type=f32
+            ).astype(out.dtype)
+
+    project(1 - core, send)
+    project(core, keep)
+
+
+def add_kernel(keep, got, out):
+    out[...] = (keep[...] + got[...].astype(f32)).reshape(out.shape).astype(bf16)
 
 
 def gather_kernel(p1, p2, p3, out):
@@ -346,30 +348,23 @@
     state = call(
         first_attention_kernel, state_out, [pltpu.VMEM((256, 2 * 256), f32)], True, 4
     )(info, query_rows, keys_own, column)
-    piece_x, peak = lax.optimization_barrier((pieces[1], state[0]))
-    pieces[1], state = piece_x, [peak] + list(state[1:])
-    peak, proj_send = lax.optimization_barrier((state[0], out_proj))
+    first_other = lax.ppermute(column, "core", SWAP)
+    *pieces, first_other, peak = lax.optimization_barrier((*pieces, first_other, state[0]))
     state = [peak] + list(state[1:])
-    first_other = lax.ppermute(column, "core", SWAP)
-    proj_got = lax.ppermute(proj_send, "core", SWAP)
-    pieces[2], proj_got = lax.optimization_barrier((pieces[2], proj_got))
     three = call(gather_kernel, [sds((6, half, KEYW), bf16)], count=3)(*pieces[1:])
     others = lax.ppermute(three, "core", SWAP)
     state = call(
         second_attention_kernel, state_out, [pltpu.VMEM((256, 4 * 256), f32)], True, 9
     )(info, query_rows, pieces[1], pieces[2], pieces[3], first_other, *state)
-    values_out = sds((half, local_heads * VDIM), bf16)
     send, keep = call(
         last_attention_kernel,
-        [values_out, values_out],
+        [sds((half, width_model), bf16), sds((half, width_model), f32)],
         [pltpu.VMEM((256, 3 * 256), f32), pltpu.VMEM((2, 256, VDIM), bf16)],
         True,
-        7,
-    )(info, query_rows, others, *state, value_up)
+        8,
+    )(info, query_rows, others, *state, value_up, out_proj)
     got = lax.ppermute(send, "core", SWAP)
-    pair_sum = call(project_kernel, [sds((16, 8, width_model), bf16)], count=4)(
-        keep, got, out_proj, proj_got
-    )
+    pair_sum = call(add_kernel, [sds((16, 8, width_model), bf16)], count=2)(keep, got)
 
     weights_out = sds((3, width_out, 3 * ff_half), bf16)
     w_send, w_keep = call(split_weights_kernel, [weights_out, weights_out], (), True, 4)(

time: 262 us -> 251 us (0.958)
  waiting for transfers between devices: 95 us -> 83.1 us
    ppermute x1, waiting for transfers between devices: 6.49 us -> 0.01 us  [on_device(): lax.ppermute(column, 'xh', SWAP)]
    ppermute x1, waiting for transfers between devices: 7.14 us -> 2.2 us  [on_device(): lax.ppermute(to_other, 'xl', SWAP)]
  transfers between devices with their start and end apart: 15 -> 14, of which waited for: 13 -> 11; matrix products, arithmetic and copies ran while one was open for 1% -> 1% of each run, Pallas kernels for 3% -> 3%
where the time goes in v6:
time: 251 us; the launch traced here: 250 us
  waiting for transfers between devices  83.1 us (33%)
  blocking collectives  71.3 us (28%)
  starting transfers between devices  67.2 us (27%)
  Pallas kernels  18.1 us (7%)
  local copies, waits for them, and re-layouts  5.15 us (2%)
  other arithmetic  3.11 us (1%)
    all_to_all x1, blocking collectives, on_device(): lax.all_to_all(pre.reshape(8, 128, 2 * ff_half), 'y', split_axis=0, conca...  47.3 us
    all_to_all x1, blocking collectives, on_device(): lax.all_to_all(hidden, 'y', split_axis=0, concat_axis=0, tiled=True)  24.1 us
    all_to_all x1, waiting for transfers between devices, on_device(): lax.all_to_all(expert_out, EXP, split_axis=0, concat_axis=0, tiled=True)  19.7 us
    all_to_all x1, waiting for transfers between devices, on_device(): lax.all_to_all(outgoing, EXP, split_axis=0, concat_axis=0, tiled=True)  18.1 us
    all_to_all x1, waiting for transfers between devices, on_device(): lax.all_to_all(pair_sum, ('z', 'xh'), split_axis=0, concat_axis=0, tiled=...  16.4 us
    all_to_all x1, starting transfers between devices, on_device(): lax.all_to_all(pair_sum, ('z', 'xh'), split_axis=0, concat_axis=0, tiled=...  12.1 us
    ppermute x2, starting transfers between devices, along_y(): return lax.ppermute(mine, ('y', 'xh'), pairs)  10.4 us
    ppermute x2, waiting for transfers between devices, along_y(): return lax.ppermute(mine, ('y', 'xh'), pairs)  9.67 us
  transfers between devices with their start and end apart: 14, of which 11 were waited for; matrix products, arithmetic and copies ran while one was open for 1% of the time, Pallas kernels for 3%

profile of v6, /device:TPU:6, one launch (start us, length us, event | category | flops | bytes accessed | tf_op | source)
XLA Modules:
  0.0 249.6 jit_solution(2643825163525327431)
XLA Ops:
  2.2 4.5 %collective-permute-start = (bf16[128,640]{1,0:T(8,128)(2,1)S(1)}, bf16[128,640]{1,0:T(8,128)(2,1)S(1)}, u32[]{:S(2)}, u32[]{:S(2)}) collective-permute-start(bf16[128,640]{1,0:T(8,128)(2,1)S(1)} %constant_dynamic-slice_fusion), channel_id=1, source_target_pairs={{0,64},{2,130},{64,128},{66,194},{128,192},{130,258},{192,256},{19... | collective-permute-start | bytes 491528 | tf_op jit(solution)/shard_map/ppermute | solution.py:302
  6.7 5.9 %collective-permute-start.1 = (bf16[128,640]{1,0:T(8,128)(2,1)S(1)}, bf16[128,640]{1,0:T(8,128)(2,1)S(1)}, u32[]{:S(2)}, u32[]{:S(2)}) collective-permute-start(bf16[128,640]{1,0:T(8,128)(2,1)S(1)} %constant_dynamic-slice_fusion), channel_id=1, source_target_pairs={{0,192},{2,258},{64,256},{66,322},{128,320},{130,386},{192,384},{1... | collective-permute-start | bytes 491528 | tf_op jit(solution)/shard_map/ppermute | solution.py:302
  14.7 7.7 %collective-permute-done.1 = bf16[128,640]{1,0:T(8,128)(2,1)S(1)} collective-permute-done((bf16[128,640]{1,0:T(8,128)(2,1)S(1)}, bf16[128,640]{1,0:T(8,128)(2,1)S(1)}, u32[]{:S(2)}, u32[]{:S(2)}) %collective-permute-start.1) | collective-permute-done | bytes 163872 | tf_op jit(solution)/shard_map/ppermute | solution.py:302
  23.2 2.6 %collective-permute-start.2 = (bf16[2,128,640]{2,1,0:T(8,128)(2,1)S(1)}, bf16[2,128,640]{2,1,0:T(8,128)(2,1)S(1)}, u32[]{:S(2)}, u32[]{:S(2)}) collective-permute-start(bf16[2,128,640]{2,1,0:T(8,128)(2,1)S(1)} %get-tuple-element.52.p0), channel_id=1, source_target_pairs={{0,2},{2,0},{1,3},{3,1},{4,6},{6,4},{5,7},{7,5},{8,10},{10,8},{9,1... | collective-permute-start | bytes 983048 | tf_op jit(solution)/shard_map/ppermute | solution.py:311
  27.7 3.6 %collective-permute-start.3 = (bf16[2,128,640]{2,1,0:T(8,128)(2,1)}, bf16[2,128,640]{2,1,0:T(8,128)(2,1)S(1)}, u32[]{:S(2)}, u32[]{:S(2)}) collective-permute-start(bf16[2,128,640]{2,1,0:T(8,128)(2,1)} %get-tuple-element.51), channel_id=1, source_target_pairs={{0,32},{32,0},{1,33},{33,1},{2,34},{34,2},{3,35},{35,3},{4,36},{36... | collective-permute-start | bytes 983048 | tf_op jit(solution)/shard_map/ppermute | solution.py:312
  31.3 3.6 %collective-permute-start.4 = (bf16[2,128,640]{2,1,0:T(8,128)(2,1)}, bf16[2,128,640]{2,1,0:T(8,128)(2,1)S(1)}, u32[]{:S(2)}, u32[]{:S(2)}) collective-permute-start(bf16[2,128,640]{2,1,0:T(8,128)(2,1)} %get-tuple-element.51), channel_id=1, source_target_pairs={{0,34},{2,32},{32,2},{34,0},{1,35},{3,33},{33,3},{35,1},{4,38},{6,... | collective-permute-start | bytes 983048 | tf_op jit(solution)/shard_map/ppermute | solution.py:313
  40.0 4.5 %collective-permute-done.4.p3 = bf16[2,128,640]{2,1,0:T(8,128)(2,1)S(1)} collective-permute-done((bf16[2,128,640]{2,1,0:T(8,128)(2,1)}, bf16[2,128,640]{2,1,0:T(8,128)(2,1)S(1)}, u32[]{:S(2)}, u32[]{:S(2)}) %collective-permute-start.4) | collective-permute-done | bytes 327712 | tf_op jit(solution)/shard_map/ppermute | solution.py:313
  46.5 2.7 %shard_map.120 = (f32[2,256,128]{2,1,0:T(8,128)S(1)}, f32[2,256,128]{2,1,0:T(8,128)S(1)}, f32[2,256,512]{2,1,0:T(8,128)S(1)}) custom-call(s32[10]{0:T(128)S(1)} %stack.58.info, bf16[2,256,640]{2,1,0:T(8,128)(2,1)S(1)} %bitcast.39, bf16[2,128,640]{2,1,0:T(8,128)(2,1)S(1)} %collective-permute-done.2.p1, bf16[2,128,640]{2,1,0:T(8,128)(2,1)S(1)} %collective-permute-done.3.p2, ...), custom_call_target="tpu_custom_call" | custom-call | tf_op jit(solution)/shard_map/pallas_call | solution.py:356
  49.3 3.8 %shard_map.121 = (bf16[128,2560]{1,0:T(8,128)(2,1)S(1)}, f32[128,2560]{1,0:T(8,128)S(1)}) custom-call(s32[10]{0:T(128)S(1)} %stack.58.info, bf16[2,256,640]{2,1,0:T(8,128)(2,1)S(1)} %bitcast.40, bf16[6,128,640]{2,1,0:T(8,128)(2,1)S(1)} %collective-permute-done.6.others, f32[2,256,128]{2,1,0:T(8,128)S(1)} %get-tuple-element.36.old_peak, ...), custom_call_target="tpu_custom_call" | custom-call | tf_op jit(solution)/shard_map/pallas_call | solution.py:359
  53.2 2.4 collective-permute-start.7
  58.3 12.1 %all-to-all-start = ((bf16[16,8,2560]{2,1,0:T(8,128)(2,1)}), bf16[16,8,2560]{2,1,0:T(8,128)(2,1)S(1)}, u32[]{:S(2)}, u32[]{:S(2)}) async-start(bf16[16,8,2560]{2,1,0:T(8,128)(2,1)} %shard_map.122), calls=%async_computation | async-start | bytes 1310720 | tf_op jit(solution)/shard_map/all_to_all | solution.py:376
  70.4 2.7 %collective-permute-start.8 = (bf16[3,160,1152]{2,1,0:T(8,128)(2,1)}, bf16[3,160,1152]{2,1,0:T(8,128)(2,1)S(1)}, u32[]{:S(2)}, u32[]{:S(2)}) collective-permute-start(bf16[3,160,1152]{2,1,0:T(8,128)(2,1)} %copy-done.12), channel_id=1, source_target_pairs={{0,32},{32,0},{1,33},{33,1},{2,34},{34,2},{3,35},{35,3},{4,36},{36... | collective-permute-start | bytes 3317768 | tf_op jit(solution)/shard_map/ppermute | solution.py:374
  73.6 16.4 %all-to-all-done.spread = bf16[16,8,2560]{2,1,0:T(8,128)(2,1)S(1)} async-done(((bf16[16,8,2560]{2,1,0:T(8,128)(2,1)}), bf16[16,8,2560]{2,1,0:T(8,128)(2,1)S(1)}, u32[]{:S(2)}, u32[]{:S(2)}) %all-to-all-start) | async-done | bytes 655392 | tf_op jit(solution)/shard_map/all_to_all | solution.py:376
  91.0 9.1 %all-to-all-start.1 = ((bf16[16,8,512]{2,1,0:T(8,128)(2,1)}), bf16[16,8,512]{2,1,0:T(8,128)(2,1)S(1)}, u32[]{:S(2)}, u32[]{:S(2)}) async-start(bf16[16,8,512]{2,1,0:T(8,128)(2,1)} %shard_map.124), calls=%async_computation.1 | async-start | bytes 262144 | tf_op jit(solution)/shard_map/all_to_all | solution.py:380
  100.7 4.9 %collective-permute-done.8.got = bf16[3,160,1152]{2,1,0:T(8,128)(2,1)S(1)} collective-permute-done((bf16[3,160,1152]{2,1,0:T(8,128)(2,1)}, bf16[3,160,1152]{2,1,0:T(8,128)(2,1)S(1)}, u32[]{:S(2)}, u32[]{:S(2)}) %collective-permute-start.8) | collective-permute-done | bytes 1105952 | tf_op jit(solution)/shard_map/ppermute | solution.py:374
  105.7 2.9 %all-to-all-done.1 = bf16[16,8,512]{2,1,0:T(8,128)(2,1)S(1)} async-done(((bf16[16,8,512]{2,1,0:T(8,128)(2,1)}), bf16[16,8,512]{2,1,0:T(8,128)(2,1)S(1)}, u32[]{:S(2)}, u32[]{:S(2)}) %all-to-all-start.1) | async-done | bytes 131104 | tf_op jit(solution)/shard_map/all_to_all | solution.py:380
  110.5 7.3 %all-to-all-start.2 = ((bf16[32,80,128]{2,1,0:T(8,128)(2,1)}), bf16[32,80,128]{2,1,0:T(8,128)(2,1)S(1)}, u32[]{:S(2)}, u32[]{:S(2)}) async-start(bf16[32,80,128]{2,1,0:T(8,128)(2,1)} %shard_map.125), calls=%async_computation.2 | async-start | bytes 1310720 | tf_op jit(solution)/shard_map/all_to_all | solution.py:411
  120.1 18.1 %all-to-all-done.2.received = bf16[32,80,128]{2,1,0:T(8,128)(2,1)S(1)} async-done(((bf16[32,80,128]{2,1,0:T(8,128)(2,1)}), bf16[32,80,128]{2,1,0:T(8,128)(2,1)S(1)}, u32[]{:S(2)}, u32[]{:S(2)}) %all-to-all-start.2) | async-done | bytes 655392 | tf_op jit(solution)/shard_map/all_to_all | solution.py:411
  140.5 47.3 %all_to_all.30.parts = bf16[8,128,768]{2,1,0:T(8,128)(2,1)S(1)} all-to-all(bf16[8,128,768]{2,1,0:T(8,128)(2,1)S(1)} %bitcast.41), channel_id=1, replica_groups=mesh['y'=8,'xl'=2,'z'=8,'xh'=2,'core'=2] {'y'}, dimensions={0} | all-to-all | bytes 3145728 | tf_op jit(solution)/shard_map/all_to_all | solution.py:413
  188.0 24.1 %all_to_all.31 = bf16[8,128,384]{2,1,0:T(8,128)(2,1)S(1)} all-to-all(bf16[8,128,384]{2,1,0:T(8,128)(2,1)S(1)} %shard_map.128), channel_id=1, replica_groups=mesh['y'=8,'xl'=2,'z'=8,'xh'=2,'core'=2] {'y'}, dimensions={0} | all-to-all | bytes 1572864 | tf_op jit(solution)/shard_map/all_to_all | solution.py:417
  214.4 7.1 %all-to-all-start.5 = ((bf16[32,80,128]{2,1,0:T(8,128)(2,1)}), bf16[32,80,128]{2,1,0:T(8,128)(2,1)S(1)}, u32[]{:S(2)}, u32[]{:S(2)}) async-start(bf16[32,80,128]{2,1,0:T(8,128)(2,1)} %shard_map.129), calls=%async_computation.5 | async-start | bytes 1310720 | tf_op jit(solution)/shard_map/all_to_all | solution.py:421
  222.4 19.7 %all-to-all-done.5.returned = bf16[32,80,128]{2,1,0:T(8,128)(2,1)S(1)} async-done(((bf16[32,80,128]{2,1,0:T(8,128)(2,1)}), bf16[32,80,128]{2,1,0:T(8,128)(2,1)S(1)}, u32[]{:S(2)}, u32[]{:S(2)}) %all-to-all-start.5) | async-done | bytes 655392 | tf_op jit(solution)/shard_map/all_to_all | solution.py:421
  242.6 2.4 collective-permute-start.9
  245.1 3.7 %collective-permute-done.9 = bf16[128,160]{1,0:T(8,128)(2,1)S(1)} collective-permute-done((bf16[128,160]{1,0:T(8,128)(2,1)S(1)}, bf16[128,160]{1,0:T(8,128)(2,1)S(1)}, u32[]{:S(2)}, u32[]{:S(2)}) %collective-permute-start.9) | collective-permute-done | bytes 40992 | tf_op jit(solution)/shard_map/ppermute | solution.py:425
  (91 shorter events, 29.8 us)
Async XLA Ops:
  0.0 35.0 %copy-start.19 = (s32[256]{0:T(256)S(1)}, s32[256]{0:T(256)}, u32[]{:S(2)}) copy-start(s32[256]{0:T(256)} %param.14) | copy-start | bytes 3076
  0.0 35.1 %copy-start.13 = (bf16[256,2,576]{0,2,1:T(8,128)(2,1)S(1)}, bf16[256,2,576]{0,2,1:T(8,128)(2,1)}, u32[]{:S(2)}) copy-start(bf16[256,2,576]{0,2,1:T(8,128)(2,1)} %param.12) | copy-start | bytes 1769476
  2.2 12.5 %collective-permute-start = (bf16[128,640]{1,0:T(8,128)(2,1)S(1)}, bf16[128,640]{1,0:T(8,128)(2,1)S(1)}, u32[]{:S(2)}, u32[]{:S(2)}) collective-permute-start(bf16[128,640]{1,0:T(8,128)(2,1)S(1)} %constant_dynamic-slice_fusion), channel_id=1, source_target_pairs={{0,64},{2,130},{64,128},{66,194},{128,192},{130,258},{192,256},{19... | collective-permute-start | bytes 491528 | tf_op jit(solution)/shard_map/ppermute | solution.py:302
  6.7 15.7 %collective-permute-start.1 = (bf16[128,640]{1,0:T(8,128)(2,1)S(1)}, bf16[128,640]{1,0:T(8,128)(2,1)S(1)}, u32[]{:S(2)}, u32[]{:S(2)}) collective-permute-start(bf16[128,640]{1,0:T(8,128)(2,1)S(1)} %constant_dynamic-slice_fusion), channel_id=1, source_target_pairs={{0,192},{2,258},{64,256},{66,322},{128,320},{130,386},{192,384},{1... | collective-permute-start | bytes 491528 | tf_op jit(solution)/shard_map/ppermute | solution.py:302
  23.2 14.5 %collective-permute-start.2 = (bf16[2,128,640]{2,1,0:T(8,128)(2,1)S(1)}, bf16[2,128,640]{2,1,0:T(8,128)(2,1)S(1)}, u32[]{:S(2)}, u32[]{:S(2)}) collective-permute-start(bf16[2,128,640]{2,1,0:T(8,128)(2,1)S(1)} %get-tuple-element.52.p0), channel_id=1, source_target_pairs={{0,2},{2,0},{1,3},{3,1},{4,6},{6,4},{5,7},{7,5},{8,10},{10,8},{9,1... | collective-permute-start | bytes 983048 | tf_op jit(solution)/shard_map/ppermute | solution.py:311
  25.8 11.9 %collective-permute-start.5 = (bf16[2,128,640]{2,1,0:T(8,128)(2,1)S(1)}, bf16[2,128,640]{2,1,0:T(8,128)(2,1)S(1)}, u32[]{:S(2)}, u32[]{:S(2)}) collective-permute-start(bf16[2,128,640]{2,1,0:T(8,128)(2,1)S(1)} %get-tuple-element.52.p0), channel_id=1, source_target_pairs={{0,1},{1,0},{2,3},{3,2},{4,5},{5,4},{6,7},{7,6},{8,9},{9,8},{10,11... | collective-permute-start | bytes 983048 | tf_op jit(solution)/shard_map/ppermute | solution.py:351
  27.7 12.2 %collective-permute-start.3 = (bf16[2,128,640]{2,1,0:T(8,128)(2,1)}, bf16[2,128,640]{2,1,0:T(8,128)(2,1)S(1)}, u32[]{:S(2)}, u32[]{:S(2)}) collective-permute-start(bf16[2,128,640]{2,1,0:T(8,128)(2,1)} %get-tuple-element.51), channel_id=1, source_target_pairs={{0,32},{32,0},{1,33},{33,1},{2,34},{34,2},{3,35},{35,3},{4,36},{36... | collective-permute-start | bytes 983048 | tf_op jit(solution)/shard_map/ppermute | solution.py:312
  31.3 13.1 %collective-permute-start.4 = (bf16[2,128,640]{2,1,0:T(8,128)(2,1)}, bf16[2,128,640]{2,1,0:T(8,128)(2,1)S(1)}, u32[]{:S(2)}, u32[]{:S(2)}) collective-permute-start(bf16[2,128,640]{2,1,0:T(8,128)(2,1)} %get-tuple-element.51), channel_id=1, source_target_pairs={{0,34},{2,32},{32,2},{34,0},{1,35},{3,33},{33,3},{35,1},{4,38},{6,... | collective-permute-start | bytes 983048 | tf_op jit(solution)/shard_map/ppermute | solution.py:313
  44.6 4.7 %collective-permute-start.6 = (bf16[6,128,640]{2,1,0:T(8,128)(2,1)S(1)}, bf16[6,128,640]{2,1,0:T(8,128)(2,1)S(1)}, u32[]{:S(2)}, u32[]{:S(2)}) collective-permute-start(bf16[6,128,640]{2,1,0:T(8,128)(2,1)S(1)} %shard_map.119), channel_id=1, source_target_pairs={{0,1},{1,0},{2,3},{3,2},{4,5},{5,4},{6,7},{7,6},{8,9},{9,8},{10,11... | collective-permute-start | bytes 2949128 | tf_op jit(solution)/shard_map/ppermute | solution.py:355
  53.2 4.1 %collective-permute-start.7 = (bf16[128,2560]{1,0:T(8,128)(2,1)S(1)}, bf16[128,2560]{1,0:T(8,128)(2,1)S(1)}, u32[]{:S(2)}, u32[]{:S(2)}) collective-permute-start(bf16[128,2560]{1,0:T(8,128)(2,1)S(1)} %get-tuple-element.40), channel_id=1, source_target_pairs={{0,1},{1,0},{2,3},{3,2},{4,5},{5,4},{6,7},{7,6},{8,9},{9,8},{10,11... | collective-permute-start | bytes 1966088 | tf_op jit(solution)/shard_map/ppermute | solution.py:366
  57.3 15.8 %copy-start.18 = (f32[2560]{0:T(1024)S(1)}, f32[2560]{0:T(1024)}, u32[]{:S(2)}) copy-start(f32[2560]{0:T(1024)} %param.18) | copy-start | bytes 30724
  57.3 15.8 %copy-start.17 = (s32[8,16,6]{1,0,2:T(8,128)S(1)}, s32[8,16,6]{1,0,2:T(8,128)}, u32[]{:S(2)}) copy-start(s32[8,16,6]{1,0,2:T(8,128)} %param.19) | copy-start | bytes 9220
  57.3 32.8 %copy-start.11 = (bf16[8,2560]{1,0:T(8,128)(2,1)S(1)}, bf16[8,2560]{1,0:T(8,128)(2,1)}, u32[]{:S(2)}) copy-start(bf16[8,2560]{1,0:T(8,128)(2,1)} %residual.1) | copy-start | bytes 122884
  58.3 31.8 %all-to-all-start = ((bf16[16,8,2560]{2,1,0:T(8,128)(2,1)}), bf16[16,8,2560]{2,1,0:T(8,128)(2,1)S(1)}, u32[]{:S(2)}, u32[]{:S(2)}) async-start(bf16[16,8,2560]{2,1,0:T(8,128)(2,1)} %shard_map.122), calls=%async_computation | async-start | bytes 1310720 | tf_op jit(solution)/shard_map/all_to_all | solution.py:376
  70.4 35.3 %collective-permute-start.8 = (bf16[3,160,1152]{2,1,0:T(8,128)(2,1)}, bf16[3,160,1152]{2,1,0:T(8,128)(2,1)S(1)}, u32[]{:S(2)}, u32[]{:S(2)}) collective-permute-start(bf16[3,160,1152]{2,1,0:T(8,128)(2,1)} %copy-done.12), channel_id=1, source_target_pairs={{0,32},{32,0},{1,33},{33,1},{2,34},{34,2},{3,35},{35,3},{4,36},{36... | collective-permute-start | bytes 3317768 | tf_op jit(solution)/shard_map/ppermute | solution.py:374
  73.2 37.3 %copy-start.14 = (s32[8,16,6]{0,1,2:T(8,128)}, s32[8,16,6]{0,1,2:T(8,128)S(1)}, u32[]{:S(2)}) copy-start(s32[8,16,6]{0,1,2:T(8,128)S(1)} %copy.42) | copy-start | bytes 9220
  91.0 17.6 %all-to-all-start.1 = ((bf16[16,8,512]{2,1,0:T(8,128)(2,1)}), bf16[16,8,512]{2,1,0:T(8,128)(2,1)S(1)}, u32[]{:S(2)}, u32[]{:S(2)}) async-start(bf16[16,8,512]{2,1,0:T(8,128)(2,1)} %shard_map.124), calls=%async_computation.1 | async-start | bytes 262144 | tf_op jit(solution)/shard_map/all_to_all | solution.py:380
  105.7 12.1 %copy-start.1 = (bf16[3,160,1152]{2,1,0:T(8,128)(2,1)}, bf16[3,160,1152]{2,1,0:T(8,128)(2,1)S(1)}, u32[]{:S(2)}) copy-start(bf16[3,160,1152]{2,1,0:T(8,128)(2,1)S(1)} %collective-permute-done.8.got) | copy-start | bytes 3317764
  110.5 27.8 %all-to-all-start.2 = ((bf16[32,80,128]{2,1,0:T(8,128)(2,1)}), bf16[32,80,128]{2,1,0:T(8,128)(2,1)S(1)}, u32[]{:S(2)}, u32[]{:S(2)}) async-start(bf16[32,80,128]{2,1,0:T(8,128)(2,1)} %shard_map.125), calls=%async_computation.2 | async-start | bytes 1310720 | tf_op jit(solution)/shard_map/all_to_all | solution.py:411
  187.7 24.3 %copy-start.4 = (bf16[384,1152]{1,0:T(8,128)(2,1)S(1)}, bf16[384,1152]{1,0:T(8,128)(2,1)}, u32[]{:S(2)}) copy-start(bf16[384,1152]{1,0:T(8,128)(2,1)} %copy-done.3) | copy-start | bytes 2654212
  212.1 9.8 %copy-start.16 = (f32[8,16,6]{1,0,2:T(8,128)S(1)}, f32[8,16,6]{1,0,2:T(8,128)}, u32[]{:S(2)}) copy-start(f32[8,16,6]{1,0,2:T(8,128)} %param.20) | copy-start | bytes 9220
  214.4 34.3 %copy-start.6 = (bf16[16,8,512]{2,1,0:T(8,128)(2,1)S(1)}, bf16[16,8,512]{2,1,0:T(8,128)(2,1)}, u32[]{:S(2)}) copy-start(bf16[16,8,512]{2,1,0:T(8,128)(2,1)} %copy-done.5) | copy-start | bytes 393220
  214.4 27.6 %all-to-all-start.5 = ((bf16[32,80,128]{2,1,0:T(8,128)(2,1)}), bf16[32,80,128]{2,1,0:T(8,128)(2,1)S(1)}, u32[]{:S(2)}, u32[]{:S(2)}) async-start(bf16[32,80,128]{2,1,0:T(8,128)(2,1)} %shard_map.129), calls=%async_computation.5 | async-start | bytes 1310720 | tf_op jit(solution)/shard_map/all_to_all | solution.py:421
  242.6 6.2 %collective-permute-start.9 = (bf16[128,160]{1,0:T(8,128)(2,1)S(1)}, bf16[128,160]{1,0:T(8,128)(2,1)S(1)}, u32[]{:S(2)}, u32[]{:S(2)}) collective-permute-start(bf16[128,160]{1,0:T(8,128)(2,1)S(1)} %get-tuple-element.50), channel_id=1, source_target_pairs={{0,32},{32,0},{1,33},{33,1},{2,34},{34,2},{3,35},{35,3},{4,36},{36... | collective-permute-start | bytes 122888 | tf_op jit(solution)/shard_map/ppermute | solution.py:425
  (10 other events, 38.7 us)

commit v7 on v6

--- a/solution.py
+++ b/solution.py
@@ -13,7 +13,7 @@
 CAP = 10
 SLOTS = 32
 SEGMENTS = 8
-KEYW = 640
+KEYW = 592
 FAR = float(2**20)
 
 CTX = ("y", "xl")
@@ -23,6 +23,17 @@
 f32, bf16, i32 = jnp.float32, jnp.bfloat16, jnp.int32
 
 
+def keys_kernel(latent, segments, own):
+    width, tokens = latent.shape
+    own[:width, :] = latent[...]
+    mark = lax.broadcasted_iota(i32, (KEYW - width, tokens), 0)
+    own[width:, :] = jnp.where(segments[...] == mark, 1.0, 0.0).astype(bf16)
+
+
+def keys_of(chunk):
+    return chunk[...] if len(chunk.shape) == 2 else jnp.concatenate([chunk[0], chunk[1]], axis=1)
+
+
 def nt_dot(a, b):
     return lax.dot_general(a, b, (((1,), (1,)), ((), ())), preferred_element_type=f32)
 
@@ -31,7 +42,7 @@
     scale = QKDIM ** (-0.5)
     peak = jnp.full((256, 128), -FAR, f32) if old is None else old[0]
     for n, (chunk, bias) in enumerate(zip(chunks, biases)):
-        part = bias(nt_dot(rows, chunk[...].reshape(256, KEYW)) * scale)
+        part = bias(jnp.dot(rows, keys_of(chunk), preferred_element_type=f32) * scale)
         scores[:, n * 256 : (n + 1) * 256] = part
         peak = jnp.maximum(peak, jnp.maximum(part[:, :128], part[:, 128:]))
     peak = jnp.max(peak, axis=1, keepdims=True)
@@ -43,8 +54,7 @@
     for n, chunk in enumerate(chunks):
         terms = jnp.exp(scores[:, n * 256 : (n + 1) * 256] - peak)
         sums = sums + terms[:, :128] + terms[:, 128:]
-        keys = chunk[...].reshape(256, KEYW)
-        mixed = mixed + jnp.dot(terms.astype(bf16), keys[:, :LATENT], preferred_element_type=f32)
+        mixed = mixed + nt_dot(terms.astype(bf16), keys_of(chunk)[:LATENT])
     return jnp.broadcast_to(peak, (256, 128)), sums, mixed
 
 
@@ -290,10 +300,10 @@
     segment_axis = jnp.arange(SEGMENTS, dtype=i32)
     own_segment = segment_ids[:, None] == segment_axis[None, :]
     pad = KEYW - width_key - SEGMENTS
-    keys_own = jnp.concatenate(
-        [latent, own_segment.astype(bf16), jnp.zeros((block_len, pad), bf16)], axis=1
-    )
-    mine = lax.dynamic_slice_in_dim(keys_own, core * half, half, 0)
+    keys_own = call(keys_kernel, [sds((KEYW, block_len), bf16)], count=2)(
+        latent.T, segment_ids[None, :]
+    )
+    mine = lax.dynamic_slice_in_dim(keys_own, core * half, half, 1)
 
     def along_y(near, far):
         pairs = [
@@ -348,10 +358,11 @@
     state = call(
         first_attention_kernel, state_out, [pltpu.VMEM((256, 2 * 256), f32)], True, 4
     )(info, query_rows, keys_own, column)
-    first_other = lax.ppermute(column, "core", SWAP)
+    pieces[1], column_late = lax.optimization_barrier((pieces[1], column))
+    first_other = lax.ppermute(column_late, "core", SWAP)
     *pieces, first_other, peak = lax.optimization_barrier((*pieces, first_other, state[0]))
     state = [peak] + list(state[1:])
-    three = call(gather_kernel, [sds((6, half, KEYW), bf16)], count=3)(*pieces[1:])
+    three = call(gather_kernel, [sds((6, KEYW, half), bf16)], count=3)(*pieces[1:])
     others = lax.ppermute(three, "core", SWAP)
     state = call(
         second_attention_kernel, state_out, [pltpu.VMEM((256, 4 * 256), f32)], True, 9

time: 251 us -> 246 us (0.980)
  waiting for transfers between devices: 83.1 us -> 78.9 us
    ppermute x1, waiting for transfers between devices: 4.54 us -> 0.12 us  [on_device(): lax.ppermute(to_other, ('xl', 'xh'), diagonal)]
    ppermute x1, waiting for transfers between devices: 0.01 us -> 3.67 us  [on_device(): lax.ppermute(column, 'xh', SWAP)]
where the time goes in v7:
time: 246 us; the launch traced here: 245 us
  waiting for transfers between devices  78.9 us (32%)
  blocking collectives  70.8 us (29%)
  starting transfers between devices  68.9 us (28%)
  Pallas kernels  17.9 us (7%)
  local copies, waits for them, and re-layouts  5.57 us (2%)
    all_to_all x1, blocking collectives, on_device(): lax.all_to_all(pre.reshape(8, 128, 2 * ff_half), 'y', split_axis=0, conca...  46.7 us
    all_to_all x1, blocking collectives, on_device(): lax.all_to_all(hidden, 'y', split_axis=0, concat_axis=0, tiled=True)  24.1 us
    all_to_all x1, waiting for transfers between devices, on_device(): lax.all_to_all(expert_out, EXP, split_axis=0, concat_axis=0, tiled=True)  19.7 us
    all_to_all x1, waiting for transfers between devices, on_device(): lax.all_to_all(outgoing, EXP, split_axis=0, concat_axis=0, tiled=True)  18.1 us
    all_to_all x1, waiting for transfers between devices, on_device(): lax.all_to_all(pair_sum, ('z', 'xh'), split_axis=0, concat_axis=0, tiled=...  16.1 us
    all_to_all x1, starting transfers between devices, on_device(): lax.all_to_all(pair_sum, ('z', 'xh'), split_axis=0, concat_axis=0, tiled=...  13.3 us
    ppermute x2, starting transfers between devices, along_y(): return lax.ppermute(mine, ('y', 'xh'), pairs)  10.6 us
    ppermute x2, waiting for transfers between devices, along_y(): return lax.ppermute(mine, ('y', 'xh'), pairs)  8.73 us
  transfers between devices with their start and end apart: 14, of which 11 were waited for; matrix products, arithmetic and copies ran while one was open for 1% of the time, Pallas kernels for 3%

profile of v7, /device:TPU:6, one launch (start us, length us, event | category | flops | bytes accessed | tf_op | source)
XLA Modules:
  0.0 245.2 jit_solution(12703994027919524754)
XLA Ops:
  1.7 4.6 %collective-permute-start = (bf16[592,128]{1,0:T(8,128)(2,1)S(1)}, bf16[592,128]{1,0:T(8,128)(2,1)S(1)}, u32[]{:S(2)}, u32[]{:S(2)}) collective-permute-start(bf16[592,128]{1,0:T(8,128)(2,1)S(1)} %constant_dynamic-slice_fusion), channel_id=1, source_target_pairs={{0,64},{2,130},{64,128},{66,194},{128,192},{130,258},{192,256},{19... | collective-permute-start | bytes 454664 | tf_op jit(solution)/shard_map/ppermute | solution.py:312
  6.4 5.9 %collective-permute-start.1 = (bf16[592,128]{1,0:T(8,128)(2,1)S(1)}, bf16[592,128]{1,0:T(8,128)(2,1)S(1)}, u32[]{:S(2)}, u32[]{:S(2)}) collective-permute-start(bf16[592,128]{1,0:T(8,128)(2,1)S(1)} %constant_dynamic-slice_fusion), channel_id=1, source_target_pairs={{0,192},{2,258},{64,256},{66,322},{128,320},{130,386},{192,384},{1... | collective-permute-start | bytes 454664 | tf_op jit(solution)/shard_map/ppermute | solution.py:312
  12.9 8.2 %collective-permute-done.1 = bf16[592,128]{1,0:T(8,128)(2,1)S(1)} collective-permute-done((bf16[592,128]{1,0:T(8,128)(2,1)S(1)}, bf16[592,128]{1,0:T(8,128)(2,1)S(1)}, u32[]{:S(2)}, u32[]{:S(2)}) %collective-permute-start.1) | collective-permute-done | bytes 151584 | tf_op jit(solution)/shard_map/ppermute | solution.py:312
  21.1 2.7 %collective-permute-start.2 = (bf16[2,592,128]{2,1,0:T(8,128)(2,1)S(1)}, bf16[2,592,128]{2,1,0:T(8,128)(2,1)S(1)}, u32[]{:S(2)}, u32[]{:S(2)}) collective-permute-start(bf16[2,592,128]{2,1,0:T(8,128)(2,1)S(1)} %get-tuple-element.31.p0), channel_id=1, source_target_pairs={{0,2},{2,0},{1,3},{3,1},{4,6},{6,4},{5,7},{7,5},{8,10},{10,8},{9,1... | collective-permute-start | bytes 909320 | tf_op jit(solution)/shard_map/ppermute | solution.py:321
  23.9 3.6 %collective-permute-start.3 = (bf16[2,592,128]{2,1,0:T(8,128)(2,1)S(1)}, bf16[2,592,128]{2,1,0:T(8,128)(2,1)S(1)}, u32[]{:S(2)}, u32[]{:S(2)}) collective-permute-start(bf16[2,592,128]{2,1,0:T(8,128)(2,1)S(1)} %get-tuple-element.55), channel_id=1, source_target_pairs={{0,32},{32,0},{1,33},{33,1},{2,34},{34,2},{3,35},{35,3},{4,36},{36... | collective-permute-start | bytes 909320 | tf_op jit(solution)/shard_map/ppermute | solution.py:322
  27.5 3.5 %collective-permute-start.4 = (bf16[2,592,128]{2,1,0:T(8,128)(2,1)S(1)}, bf16[2,592,128]{2,1,0:T(8,128)(2,1)S(1)}, u32[]{:S(2)}, u32[]{:S(2)}) collective-permute-start(bf16[2,592,128]{2,1,0:T(8,128)(2,1)S(1)} %get-tuple-element.55), channel_id=1, source_target_pairs={{0,34},{2,32},{32,2},{34,0},{1,35},{3,33},{33,3},{35,1},{4,38},{6,... | collective-permute-start | bytes 909320 | tf_op jit(solution)/shard_map/ppermute | solution.py:323
  31.0 3.7 %collective-permute-done.2.p1 = bf16[2,592,128]{2,1,0:T(8,128)(2,1)S(1)} collective-permute-done((bf16[2,592,128]{2,1,0:T(8,128)(2,1)S(1)}, bf16[2,592,128]{2,1,0:T(8,128)(2,1)S(1)}, u32[]{:S(2)}, u32[]{:S(2)}) %collective-permute-start.2) | collective-permute-done | bytes 303136 | tf_op jit(solution)/shard_map/ppermute | solution.py:321
  39.6 2.3 collective-permute-start.6
  41.9 2.7 %shard_map.121 = (f32[2,256,128]{2,1,0:T(8,128)S(1)}, f32[2,256,128]{2,1,0:T(8,128)S(1)}, f32[2,256,512]{2,1,0:T(8,128)S(1)}) custom-call(s32[10]{0:T(128)S(1)} %stack.58.info, bf16[2,256,592]{2,1,0:T(8,128)(2,1)S(1)} %bitcast.41, bf16[2,592,128]{2,1,0:T(8,128)(2,1)S(1)} %collective-permute-done.2.p1, bf16[2,592,128]{2,1,0:T(8,128)(2,1)S(1)} %collective-permute-done.3.p2, ...), custom_call_target="tpu_custom_call" | custom-call | tf_op jit(solution)/shard_map/pallas_call | solution.py:367
  44.6 3.7 %shard_map.122 = (bf16[128,2560]{1,0:T(8,128)(2,1)S(1)}, f32[128,2560]{1,0:T(8,128)S(1)}) custom-call(s32[10]{0:T(128)S(1)} %stack.58.info, bf16[2,256,592]{2,1,0:T(8,128)(2,1)S(1)} %bitcast.42, bf16[6,592,128]{2,1,0:T(8,128)(2,1)S(1)} %collective-permute-done.6.others, f32[2,256,128]{2,1,0:T(8,128)S(1)} %get-tuple-element.40.old_peak, ...), custom_call_target="tpu_custom_call" | custom-call | tf_op jit(solution)/shard_map/pallas_call | solution.py:370
  53.4 13.3 %all-to-all-start = ((bf16[16,8,2560]{2,1,0:T(8,128)(2,1)}), bf16[16,8,2560]{2,1,0:T(8,128)(2,1)S(1)}, u32[]{:S(2)}, u32[]{:S(2)}) async-start(bf16[16,8,2560]{2,1,0:T(8,128)(2,1)} %shard_map.123), calls=%async_computation | async-start | bytes 1310720 | tf_op jit(solution)/shard_map/all_to_all | solution.py:387
  66.7 2.7 %collective-permute-start.8 = (bf16[3,160,1152]{2,1,0:T(8,128)(2,1)}, bf16[3,160,1152]{2,1,0:T(8,128)(2,1)S(1)}, u32[]{:S(2)}, u32[]{:S(2)}) collective-permute-start(bf16[3,160,1152]{2,1,0:T(8,128)(2,1)} %copy-done.15), channel_id=1, source_target_pairs={{0,32},{32,0},{1,33},{33,1},{2,34},{34,2},{3,35},{35,3},{4,36},{36... | collective-permute-start | bytes 3317768 | tf_op jit(solution)/shard_map/ppermute | solution.py:385
  70.0 16.1 %all-to-all-done.spread = bf16[16,8,2560]{2,1,0:T(8,128)(2,1)S(1)} async-done(((bf16[16,8,2560]{2,1,0:T(8,128)(2,1)}), bf16[16,8,2560]{2,1,0:T(8,128)(2,1)S(1)}, u32[]{:S(2)}, u32[]{:S(2)}) %all-to-all-start) | async-done | bytes 655392 | tf_op jit(solution)/shard_map/all_to_all | solution.py:387
  87.1 8.6 %all-to-all-start.1 = ((bf16[16,8,512]{2,1,0:T(8,128)(2,1)}), bf16[16,8,512]{2,1,0:T(8,128)(2,1)S(1)}, u32[]{:S(2)}, u32[]{:S(2)}) async-start(bf16[16,8,512]{2,1,0:T(8,128)(2,1)} %shard_map.125), calls=%async_computation.1 | async-start | bytes 262144 | tf_op jit(solution)/shard_map/all_to_all | solution.py:391
  96.3 5.7 %collective-permute-done.8.got = bf16[3,160,1152]{2,1,0:T(8,128)(2,1)S(1)} collective-permute-done((bf16[3,160,1152]{2,1,0:T(8,128)(2,1)}, bf16[3,160,1152]{2,1,0:T(8,128)(2,1)S(1)}, u32[]{:S(2)}, u32[]{:S(2)}) %collective-permute-start.8) | collective-permute-done | bytes 1105952 | tf_op jit(solution)/shard_map/ppermute | solution.py:385
  106.0 7.8 %all-to-all-start.2 = ((bf16[32,80,128]{2,1,0:T(8,128)(2,1)}), bf16[32,80,128]{2,1,0:T(8,128)(2,1)S(1)}, u32[]{:S(2)}, u32[]{:S(2)}) async-start(bf16[32,80,128]{2,1,0:T(8,128)(2,1)} %shard_map.126), calls=%async_computation.2 | async-start | bytes 1310720 | tf_op jit(solution)/shard_map/all_to_all | solution.py:422
  116.2 18.1 %all-to-all-done.2.received = bf16[32,80,128]{2,1,0:T(8,128)(2,1)S(1)} async-done(((bf16[32,80,128]{2,1,0:T(8,128)(2,1)}), bf16[32,80,128]{2,1,0:T(8,128)(2,1)S(1)}, u32[]{:S(2)}, u32[]{:S(2)}) %all-to-all-start.2) | async-done | bytes 655392 | tf_op jit(solution)/shard_map/all_to_all | solution.py:422
  136.6 46.7 %all_to_all.30.parts = bf16[8,128,768]{2,1,0:T(8,128)(2,1)S(1)} all-to-all(bf16[8,128,768]{2,1,0:T(8,128)(2,1)S(1)} %bitcast.43), channel_id=1, replica_groups=mesh['y'=8,'xl'=2,'z'=8,'xh'=2,'core'=2] {'y'}, dimensions={0} | all-to-all | bytes 3145728 | tf_op jit(solution)/shard_map/all_to_all | solution.py:424
  183.5 24.1 %all_to_all.31 = bf16[8,128,384]{2,1,0:T(8,128)(2,1)S(1)} all-to-all(bf16[8,128,384]{2,1,0:T(8,128)(2,1)S(1)} %shard_map.129), channel_id=1, replica_groups=mesh['y'=8,'xl'=2,'z'=8,'xh'=2,'core'=2] {'y'}, dimensions={0} | all-to-all | bytes 1572864 | tf_op jit(solution)/shard_map/all_to_all | solution.py:428
  207.6 2.4 shard_map.130
  210.0 7.1 %all-to-all-start.5 = ((bf16[32,80,128]{2,1,0:T(8,128)(2,1)}), bf16[32,80,128]{2,1,0:T(8,128)(2,1)S(1)}, u32[]{:S(2)}, u32[]{:S(2)}) async-start(bf16[32,80,128]{2,1,0:T(8,128)(2,1)} %shard_map.130), calls=%async_computation.5 | async-start | bytes 1310720 | tf_op jit(solution)/shard_map/all_to_all | solution.py:432
  217.9 19.7 %all-to-all-done.5.returned = bf16[32,80,128]{2,1,0:T(8,128)(2,1)S(1)} async-done(((bf16[32,80,128]{2,1,0:T(8,128)(2,1)}), bf16[32,80,128]{2,1,0:T(8,128)(2,1)S(1)}, u32[]{:S(2)}, u32[]{:S(2)}) %all-to-all-start.5) | async-done | bytes 655392 | tf_op jit(solution)/shard_map/all_to_all | solution.py:432
  238.1 2.8 %collective-permute-start.9 = (bf16[128,160]{1,0:T(8,128)(2,1)S(1)}, bf16[128,160]{1,0:T(8,128)(2,1)S(1)}, u32[]{:S(2)}, u32[]{:S(2)}) collective-permute-start(bf16[128,160]{1,0:T(8,128)(2,1)S(1)} %get-tuple-element.54), channel_id=1, source_target_pairs={{0,32},{32,0},{1,33},{33,1},{2,34},{34,2},{3,35},{35,3},{4,36},{36... | collective-permute-start | bytes 122888 | tf_op jit(solution)/shard_map/ppermute | solution.py:436
  241.0 3.3 %collective-permute-done.9 = bf16[128,160]{1,0:T(8,128)(2,1)S(1)} collective-permute-done((bf16[128,160]{1,0:T(8,128)(2,1)S(1)}, bf16[128,160]{1,0:T(8,128)(2,1)S(1)}, u32[]{:S(2)}, u32[]{:S(2)}) %collective-permute-start.9) | collective-permute-done | bytes 40992 | tf_op jit(solution)/shard_map/ppermute | solution.py:436
  (93 shorter events, 25.2 us)
Async XLA Ops:
  0.0 36.6 %copy-start.14 = (s32[256]{0:T(256)S(1)}, s32[256]{0:T(256)}, u32[]{:S(2)}) copy-start(s32[256]{0:T(256)} %param.14) | copy-start | bytes 3076
  1.7 35.1 %copy-start.16 = (bf16[256,2,576]{0,2,1:T(8,128)(2,1)S(1)}, bf16[256,2,576]{0,2,1:T(8,128)(2,1)}, u32[]{:S(2)}) copy-start(bf16[256,2,576]{0,2,1:T(8,128)(2,1)} %param.12) | copy-start | bytes 1769476
  1.7 11.2 %collective-permute-start = (bf16[592,128]{1,0:T(8,128)(2,1)S(1)}, bf16[592,128]{1,0:T(8,128)(2,1)S(1)}, u32[]{:S(2)}, u32[]{:S(2)}) collective-permute-start(bf16[592,128]{1,0:T(8,128)(2,1)S(1)} %constant_dynamic-slice_fusion), channel_id=1, source_target_pairs={{0,64},{2,130},{64,128},{66,194},{128,192},{130,258},{192,256},{19... | collective-permute-start | bytes 454664 | tf_op jit(solution)/shard_map/ppermute | solution.py:312
  6.4 14.7 %collective-permute-start.1 = (bf16[592,128]{1,0:T(8,128)(2,1)S(1)}, bf16[592,128]{1,0:T(8,128)(2,1)S(1)}, u32[]{:S(2)}, u32[]{:S(2)}) collective-permute-start(bf16[592,128]{1,0:T(8,128)(2,1)S(1)} %constant_dynamic-slice_fusion), channel_id=1, source_target_pairs={{0,192},{2,258},{64,256},{66,322},{128,320},{130,386},{192,384},{1... | collective-permute-start | bytes 454664 | tf_op jit(solution)/shard_map/ppermute | solution.py:312
  21.1 13.5 %collective-permute-start.2 = (bf16[2,592,128]{2,1,0:T(8,128)(2,1)S(1)}, bf16[2,592,128]{2,1,0:T(8,128)(2,1)S(1)}, u32[]{:S(2)}, u32[]{:S(2)}) collective-permute-start(bf16[2,592,128]{2,1,0:T(8,128)(2,1)S(1)} %get-tuple-element.31.p0), channel_id=1, source_target_pairs={{0,2},{2,0},{1,3},{3,1},{4,6},{6,4},{5,7},{7,5},{8,10},{10,8},{9,1... | collective-permute-start | bytes 909320 | tf_op jit(solution)/shard_map/ppermute | solution.py:321
  23.9 15.5 %collective-permute-start.3 = (bf16[2,592,128]{2,1,0:T(8,128)(2,1)S(1)}, bf16[2,592,128]{2,1,0:T(8,128)(2,1)S(1)}, u32[]{:S(2)}, u32[]{:S(2)}) collective-permute-start(bf16[2,592,128]{2,1,0:T(8,128)(2,1)S(1)} %get-tuple-element.55), channel_id=1, source_target_pairs={{0,32},{32,0},{1,33},{33,1},{2,34},{34,2},{3,35},{35,3},{4,36},{36... | collective-permute-start | bytes 909320 | tf_op jit(solution)/shard_map/ppermute | solution.py:322
  27.5 12.0 %collective-permute-start.4 = (bf16[2,592,128]{2,1,0:T(8,128)(2,1)S(1)}, bf16[2,592,128]{2,1,0:T(8,128)(2,1)S(1)}, u32[]{:S(2)}, u32[]{:S(2)}) collective-permute-start(bf16[2,592,128]{2,1,0:T(8,128)(2,1)S(1)} %get-tuple-element.55), channel_id=1, source_target_pairs={{0,34},{2,32},{32,2},{34,0},{1,35},{3,33},{33,3},{35,1},{4,38},{6,... | collective-permute-start | bytes 909320 | tf_op jit(solution)/shard_map/ppermute | solution.py:323
  34.6 4.8 %collective-permute-start.5 = (bf16[2,592,128]{2,1,0:T(8,128)(2,1)S(1)}, bf16[2,592,128]{2,1,0:T(8,128)(2,1)S(1)}, u32[]{:S(2)}, u32[]{:S(2)}) collective-permute-start(bf16[2,592,128]{2,1,0:T(8,128)(2,1)S(1)} %get-tuple-element.31.p0), channel_id=1, source_target_pairs={{0,1},{1,0},{2,3},{3,2},{4,5},{5,4},{6,7},{7,6},{8,9},{9,8},{10,11... | collective-permute-start | bytes 909320 | tf_op jit(solution)/shard_map/ppermute | solution.py:362
  39.6 5.0 %collective-permute-start.6 = (bf16[6,592,128]{2,1,0:T(8,128)(2,1)S(1)}, bf16[6,592,128]{2,1,0:T(8,128)(2,1)S(1)}, u32[]{:S(2)}, u32[]{:S(2)}) collective-permute-start(bf16[6,592,128]{2,1,0:T(8,128)(2,1)S(1)} %shard_map.120), channel_id=1, source_target_pairs={{0,1},{1,0},{2,3},{3,2},{4,5},{5,4},{6,7},{7,6},{8,9},{9,8},{10,11... | collective-permute-start | bytes 2727944 | tf_op jit(solution)/shard_map/ppermute | solution.py:366
  48.4 4.0 %collective-permute-start.7 = (bf16[128,2560]{1,0:T(8,128)(2,1)S(1)}, bf16[128,2560]{1,0:T(8,128)(2,1)S(1)}, u32[]{:S(2)}, u32[]{:S(2)}) collective-permute-start(bf16[128,2560]{1,0:T(8,128)(2,1)S(1)} %get-tuple-element.44), channel_id=1, source_target_pairs={{0,1},{1,0},{2,3},{3,2},{4,5},{5,4},{6,7},{7,6},{8,9},{9,8},{10,11... | collective-permute-start | bytes 1966088 | tf_op jit(solution)/shard_map/ppermute | solution.py:377
  52.4 17.1 %copy-start.21 = (f32[2560]{0:T(1024)S(1)}, f32[2560]{0:T(1024)}, u32[]{:S(2)}) copy-start(f32[2560]{0:T(1024)} %param.18) | copy-start | bytes 30724
  52.4 17.1 %copy-start.20 = (s32[8,16,6]{1,0,2:T(8,128)S(1)}, s32[8,16,6]{1,0,2:T(8,128)}, u32[]{:S(2)}) copy-start(s32[8,16,6]{1,0,2:T(8,128)} %param.19) | copy-start | bytes 9220
  52.4 33.7 %copy-start.12 = (bf16[8,2560]{1,0:T(8,128)(2,1)S(1)}, bf16[8,2560]{1,0:T(8,128)(2,1)}, u32[]{:S(2)}) copy-start(bf16[8,2560]{1,0:T(8,128)(2,1)} %residual.1) | copy-start | bytes 122884
  53.4 32.7 %all-to-all-start = ((bf16[16,8,2560]{2,1,0:T(8,128)(2,1)}), bf16[16,8,2560]{2,1,0:T(8,128)(2,1)S(1)}, u32[]{:S(2)}, u32[]{:S(2)}) async-start(bf16[16,8,2560]{2,1,0:T(8,128)(2,1)} %shard_map.123), calls=%async_computation | async-start | bytes 1310720 | tf_op jit(solution)/shard_map/all_to_all | solution.py:387
  66.7 35.2 %collective-permute-start.8 = (bf16[3,160,1152]{2,1,0:T(8,128)(2,1)}, bf16[3,160,1152]{2,1,0:T(8,128)(2,1)S(1)}, u32[]{:S(2)}, u32[]{:S(2)}) collective-permute-start(bf16[3,160,1152]{2,1,0:T(8,128)(2,1)} %copy-done.15), channel_id=1, source_target_pairs={{0,32},{32,0},{1,33},{33,1},{2,34},{34,2},{3,35},{35,3},{4,36},{36... | collective-permute-start | bytes 3317768 | tf_op jit(solution)/shard_map/ppermute | solution.py:385
  69.5 36.5 %copy-start.17 = (s32[8,16,6]{0,1,2:T(8,128)}, s32[8,16,6]{0,1,2:T(8,128)S(1)}, u32[]{:S(2)}) copy-start(s32[8,16,6]{0,1,2:T(8,128)S(1)} %copy.37) | copy-start | bytes 9220
  87.1 17.0 %all-to-all-start.1 = ((bf16[16,8,512]{2,1,0:T(8,128)(2,1)}), bf16[16,8,512]{2,1,0:T(8,128)(2,1)S(1)}, u32[]{:S(2)}, u32[]{:S(2)}) async-start(bf16[16,8,512]{2,1,0:T(8,128)(2,1)} %shard_map.125), calls=%async_computation.1 | async-start | bytes 262144 | tf_op jit(solution)/shard_map/all_to_all | solution.py:391
  102.0 11.9 %copy-start.1 = (bf16[3,160,1152]{2,1,0:T(8,128)(2,1)}, bf16[3,160,1152]{2,1,0:T(8,128)(2,1)S(1)}, u32[]{:S(2)}) copy-start(bf16[3,160,1152]{2,1,0:T(8,128)(2,1)S(1)} %collective-permute-done.8.got) | copy-start | bytes 3317764
  106.0 28.3 %all-to-all-start.2 = ((bf16[32,80,128]{2,1,0:T(8,128)(2,1)}), bf16[32,80,128]{2,1,0:T(8,128)(2,1)S(1)}, u32[]{:S(2)}, u32[]{:S(2)}) async-start(bf16[32,80,128]{2,1,0:T(8,128)(2,1)} %shard_map.126), calls=%async_computation.2 | async-start | bytes 1310720 | tf_op jit(solution)/shard_map/all_to_all | solution.py:422
  183.3 24.3 %copy-start.4 = (bf16[384,1152]{1,0:T(8,128)(2,1)S(1)}, bf16[384,1152]{1,0:T(8,128)(2,1)}, u32[]{:S(2)}) copy-start(bf16[384,1152]{1,0:T(8,128)(2,1)} %copy-done.3) | copy-start | bytes 2654212
  207.6 9.8 %copy-start.19 = (f32[8,16,6]{1,0,2:T(8,128)S(1)}, f32[8,16,6]{1,0,2:T(8,128)}, u32[]{:S(2)}) copy-start(f32[8,16,6]{1,0,2:T(8,128)} %param.20) | copy-start | bytes 9220
  210.0 34.3 %copy-start.6 = (bf16[16,8,512]{2,1,0:T(8,128)(2,1)S(1)}, bf16[16,8,512]{2,1,0:T(8,128)(2,1)}, u32[]{:S(2)}) copy-start(bf16[16,8,512]{2,1,0:T(8,128)(2,1)} %copy-done.5) | copy-start | bytes 393220
  210.0 27.6 %all-to-all-start.5 = ((bf16[32,80,128]{2,1,0:T(8,128)(2,1)}), bf16[32,80,128]{2,1,0:T(8,128)(2,1)S(1)}, u32[]{:S(2)}, u32[]{:S(2)}) async-start(bf16[32,80,128]{2,1,0:T(8,128)(2,1)} %shard_map.130), calls=%async_computation.5 | async-start | bytes 1310720 | tf_op jit(solution)/shard_map/all_to_all | solution.py:432
  238.1 6.2 %collective-permute-start.9 = (bf16[128,160]{1,0:T(8,128)(2,1)S(1)}, bf16[128,160]{1,0:T(8,128)(2,1)S(1)}, u32[]{:S(2)}, u32[]{:S(2)}) collective-permute-start(bf16[128,160]{1,0:T(8,128)(2,1)S(1)} %get-tuple-element.54), channel_id=1, source_target_pairs={{0,32},{32,0},{1,33},{33,1},{2,34},{34,2},{3,35},{35,3},{4,36},{36... | collective-permute-start | bytes 122888 | tf_op jit(solution)/shard_map/ppermute | solution.py:436
  (12 other events, 39.0 us)

commit v8 on v7

--- a/solution.py
+++ b/solution.py
@@ -182,37 +182,41 @@
     return jnp.concatenate([rows * mask for mask in masks], axis=1)
 
 
-def split_weights_kernel(info, gate, up, down, send, keep):
+def split_weights_kernel(info, gate, up, down, in_send, in_keep, down_send, down_keep):
     half = gate.shape[2] // 2
 
-    def move(out, start):
-        for n, weights in enumerate((gate, up, down)):
-            out[:, :, n * half : (n + 1) * half] = weights[:, :, start : start + half]
+    def move(into, onto, start):
+        into[:, :, :half] = gate[:, :, start : start + half]
+        into[:, :, half:] = up[:, :, start : start + half]
+        onto[...] = down[:, :, start : start + half]
 
     @pl.when(info[9] == 0)
     def _():
-        move(keep, 0)
-        move(send, half)
+        move(in_keep, down_keep, 0)
+        move(in_send, down_send, half)
 
     @pl.when(info[9] != 0)
     def _():
-        move(keep, half)
-        move(send, 0)
-
-
-def join_weights_kernel(keep, got, into, down):
+        move(in_keep, down_keep, half)
+        move(in_send, down_send, 0)
+
+
+def join_in_kernel(keep, got, out):
     rows = keep.shape[1]
-    wide = into.shape[1]
-    narrow = keep.shape[2] - wide
     for j in range(3):
         base = j * 384
-        into[base : base + rows, :] = keep[j, :, :wide]
-        into[base + rows : base + 2 * rows, :] = got[j, :, :wide]
-        into[base + 2 * rows : base + 384, :] = got[j, 256 - rows :, :wide]
-        lanes = slice(j * narrow, (j + 1) * narrow)
-        down[:rows, lanes] = keep[j, :, wide:]
-        down[rows : 2 * rows, lanes] = got[j, :, wide:]
-        down[2 * rows :, lanes] = got[j, 256 - rows :, wide:]
+        out[base : base + rows, :] = keep[j]
+        out[base + rows : base + 2 * rows, :] = got[j]
+        out[base + 2 * rows : base + 384, :] = got[j, 256 - rows :]
+
+
+def join_down_kernel(keep, got, out):
+    rows, width = keep.shape[1:]
+    for j in range(3):
+        lanes = slice(j * width, (j + 1) * width)
+        out[:rows, lanes] = keep[j]
+        out[rows : 2 * rows, lanes] = got[j]
+        out[2 * rows :, lanes] = got[j, 256 - rows :]
 
 
 def gate_up_kernel(received, weights, pre):
@@ -358,10 +362,10 @@
     state = call(
         first_attention_kernel, state_out, [pltpu.VMEM((256, 2 * 256), f32)], True, 4
     )(info, query_rows, keys_own, column)
-    pieces[1], column_late = lax.optimization_barrier((pieces[1], column))
+    pieces[1], column_late, peak = lax.optimization_barrier((pieces[1], column, state[0]))
+    state = [peak] + list(state[1:])
     first_other = lax.ppermute(column_late, "core", SWAP)
-    *pieces, first_other, peak = lax.optimization_barrier((*pieces, first_other, state[0]))
-    state = [peak] + list(state[1:])
+    *pieces, first_other = lax.optimization_barrier((*pieces, first_other))
     three = call(gather_kernel, [sds((6, KEYW, half), bf16)], count=3)(*pieces[1:])
     others = lax.ppermute(three, "core", SWAP)
     state = call(
@@ -377,25 +381,24 @@
     got = lax.ppermute(send, "core", SWAP)
     pair_sum = call(add_kernel, [sds((16, 8, width_model), bf16)], count=2)(keep, got)
 
-    weights_out = sds((3, width_out, 3 * ff_half), bf16)
-    w_send, w_keep = call(split_weights_kernel, [weights_out, weights_out], (), True, 4)(
-        info, expert_gate, expert_up, jnp.transpose(expert_down, (0, 2, 1))
-    )
-    pair_sum, w_send = lax.optimization_barrier((pair_sum, w_send))
-    w_got = lax.ppermute(w_send, "xl", SWAP)
+    in_out = sds((3, width_out, 2 * ff_half), bf16)
+    down_out = sds((3, width_out, ff_half), bf16)
+    in_send, in_keep, down_send, down_keep = call(
+        split_weights_kernel, [in_out, in_out, down_out, down_out], (), True, 4
+    )(info, expert_gate, expert_up, jnp.transpose(expert_down, (0, 2, 1)))
+    pair_sum, in_send = lax.optimization_barrier((pair_sum, in_send))
+    in_got = lax.ppermute(in_send, "xl", SWAP)
 
     spread = lax.all_to_all(pair_sum, ("z", "xh"), split_axis=0, concat_axis=0, tiled=True)
     packed = call(norm_kernel, [sds((16, 8, 512), bf16)], count=3)(
         spread, residual, norm_gain[None, :]
     )
     split = lax.all_to_all(packed, CTX, split_axis=0, concat_axis=0, tiled=True)
-    split, w_got = lax.optimization_barrier((split, w_got))
+    split, in_got, down_send = lax.optimization_barrier((split, in_got, down_send))
+    down_got = lax.ppermute(down_send, "xl", SWAP)
     split = split.reshape(128, 512)
-    w_in, w_down = call(
-        join_weights_kernel,
-        [sds((3 * 384, 2 * ff_half), bf16), sds((384, 3 * ff_half), bf16)],
-        count=2,
-    )(w_keep, w_got)
+    w_in = call(join_in_kernel, [sds((3 * 384, 2 * ff_half), bf16)], count=2)(in_keep, in_got)
+    w_down = call(join_down_kernel, [sds((384, 3 * ff_half), bf16)], count=2)(down_keep, down_got)
 
     routes = jnp.transpose(route_ids, (1, 0, 2)).reshape(128, TOPK)
     expert_axis = jnp.arange(EXPERTS, dtype=i32)
@@ -420,6 +423,7 @@
     travel = sds((32, 80, 128), bf16)
     outgoing = call(pick_kernel, [travel], count=2)(picker, split)
     received = lax.all_to_all(outgoing, EXP, split_axis=0, concat_axis=0, tiled=True)
+    received, w_in, w_down = lax.optimization_barrier((received, w_in, w_down))
     pre = call(gate_up_kernel, [sds((32 * SLOTS, 2 * ff_half), bf16)], count=2)(received, w_in)
     pre_parts = lax.all_to_all(
         pre.reshape(8, 128, 2 * ff_half), "y", split_axis=0, concat_axis=0, tiled=True

time: 246 us -> 241 us (0.980)
  blocking collectives: 70.8 us -> 67 us
  waiting for transfers between devices: 78.9 us -> 75.7 us
    all_to_all x1, waiting for transfers between devices: 18.1 us -> 1.89 us  [on_device(): lax.all_to_all(outgoing, EXP, split_axis=0, concat_axis=0, tiled=True)]
    ppermute x1 -> x2, waiting for transfers between devices: 5.7 us -> 14.8 us  [the longest x1 14.8 us: on_device(): down_got = lax.ppermute(down_send, 'xl', SWAP)]
    all_to_all x1, waiting for transfers between devices: 2.15 us -> 7.82 us  [on_device(): split = lax.all_to_all(packed, CTX, split_axis=0, concat_axis=0, tiled=True)]
    all_to_all x1, blocking collectives: 46.7 us -> 42.6 us  [on_device(): lax.all_to_all(pre.reshape(8, 128, 2 * ff_half), 'y', split_axis=0, conca...]
    ppermute x1, waiting for transfers between devices: 3.67 us -> 0.89 us  [on_device(): lax.ppermute(column, 'xh', SWAP)]
    ppermute x1 -> x2, starting transfers between devices: 2.72 us -> 5.33 us  [the longest x1 2.74 us: on_device(): in_got = lax.ppermute(in_send, 'xl', SWAP)]
  transfers between devices with their start and end apart: 14 -> 15, of which waited for: 11 -> 12; matrix products, arithmetic and copies ran while one was open for 1% -> 1% of each run, Pallas kernels for 3% -> 3%
where the time goes in v8:
time: 241 us; the launch traced here: 239 us
  waiting for transfers between devices  75.7 us (31%)
  starting transfers between devices  70.8 us (29%)
  blocking collectives  67 us (28%)
  Pallas kernels  18.6 us (8%)
  local copies, waits for them, and re-layouts  3.88 us (2%)
    all_to_all x1, blocking collectives, on_device(): lax.all_to_all(pre.reshape(8, 128, 2 * ff_half), 'y', split_axis=0, conca...  42.6 us
    all_to_all x1, blocking collectives, on_device(): lax.all_to_all(hidden, 'y', split_axis=0, concat_axis=0, tiled=True)  24.4 us
    all_to_all x1, waiting for transfers between devices, on_device(): lax.all_to_all(expert_out, EXP, split_axis=0, concat_axis=0, tiled=True)  19.7 us
    all_to_all x1, waiting for transfers between devices, on_device(): lax.all_to_all(pair_sum, ('z', 'xh'), split_axis=0, concat_axis=0, tiled=...  16.4 us
    ppermute x1, waiting for transfers between devices, on_device(): down_got = lax.ppermute(down_send, 'xl', SWAP)  14.8 us
    all_to_all x1, starting transfers between devices, on_device(): lax.all_to_all(pair_sum, ('z', 'xh'), split_axis=0, concat_axis=0, tiled=...  13.3 us
    ppermute x2, starting transfers between devices, along_y(): return lax.ppermute(mine, ('y', 'xh'), pairs)  10.6 us
    ppermute x2, waiting for transfers between devices, along_y(): return lax.ppermute(mine, ('y', 'xh'), pairs)  8.73 us
  transfers between devices with their start and end apart: 15, of which 12 were waited for; matrix products, arithmetic and copies ran while one was open for 1% of the time, Pallas kernels for 3%

profile of v8, /device:TPU:6, one launch (start us, length us, event | category | flops | bytes accessed | tf_op | source)
XLA Modules:
  0.0 239.1 jit_solution(1759092830716890609)
XLA Ops:
  1.7 4.6 %collective-permute-start = (bf16[592,128]{1,0:T(8,128)(2,1)S(1)}, bf16[592,128]{1,0:T(8,128)(2,1)S(1)}, u32[]{:S(2)}, u32[]{:S(2)}) collective-permute-start(bf16[592,128]{1,0:T(8,128)(2,1)S(1)} %constant_dynamic-slice_fusion), channel_id=1, source_target_pairs={{0,64},{2,130},{64,128},{66,194},{128,192},{130,258},{192,256},{19... | collective-permute-start | bytes 454664 | tf_op jit(solution)/shard_map/ppermute | solution.py:316
  6.4 5.9 %collective-permute-start.1 = (bf16[592,128]{1,0:T(8,128)(2,1)S(1)}, bf16[592,128]{1,0:T(8,128)(2,1)S(1)}, u32[]{:S(2)}, u32[]{:S(2)}) collective-permute-start(bf16[592,128]{1,0:T(8,128)(2,1)S(1)} %constant_dynamic-slice_fusion), channel_id=1, source_target_pairs={{0,192},{2,258},{64,256},{66,322},{128,320},{130,386},{192,384},{1... | collective-permute-start | bytes 454664 | tf_op jit(solution)/shard_map/ppermute | solution.py:316
  12.9 8.2 %collective-permute-done.1 = bf16[592,128]{1,0:T(8,128)(2,1)S(1)} collective-permute-done((bf16[592,128]{1,0:T(8,128)(2,1)S(1)}, bf16[592,128]{1,0:T(8,128)(2,1)S(1)}, u32[]{:S(2)}, u32[]{:S(2)}) %collective-permute-start.1) | collective-permute-done | bytes 151584 | tf_op jit(solution)/shard_map/ppermute | solution.py:316
  21.1 2.7 %collective-permute-start.2 = (bf16[2,592,128]{2,1,0:T(8,128)(2,1)S(1)}, bf16[2,592,128]{2,1,0:T(8,128)(2,1)S(1)}, u32[]{:S(2)}, u32[]{:S(2)}) collective-permute-start(bf16[2,592,128]{2,1,0:T(8,128)(2,1)S(1)} %get-tuple-element.36.p0), channel_id=1, source_target_pairs={{0,2},{2,0},{1,3},{3,1},{4,6},{6,4},{5,7},{7,5},{8,10},{10,8},{9,1... | collective-permute-start | bytes 909320 | tf_op jit(solution)/shard_map/ppermute | solution.py:325
  24.8 3.6 %collective-permute-start.3 = (bf16[2,592,128]{2,1,0:T(8,128)(2,1)S(1)}, bf16[2,592,128]{2,1,0:T(8,128)(2,1)S(1)}, u32[]{:S(2)}, u32[]{:S(2)}) collective-permute-start(bf16[2,592,128]{2,1,0:T(8,128)(2,1)S(1)} %get-tuple-element.63), channel_id=1, source_target_pairs={{0,32},{32,0},{1,33},{33,1},{2,34},{34,2},{3,35},{35,3},{4,36},{36... | collective-permute-start | bytes 909320 | tf_op jit(solution)/shard_map/ppermute | solution.py:326
  28.3 3.5 %collective-permute-start.4 = (bf16[2,592,128]{2,1,0:T(8,128)(2,1)S(1)}, bf16[2,592,128]{2,1,0:T(8,128)(2,1)S(1)}, u32[]{:S(2)}, u32[]{:S(2)}) collective-permute-start(bf16[2,592,128]{2,1,0:T(8,128)(2,1)S(1)} %get-tuple-element.63), channel_id=1, source_target_pairs={{0,34},{2,32},{32,2},{34,0},{1,35},{3,33},{33,3},{35,1},{4,38},{6,... | collective-permute-start | bytes 909320 | tf_op jit(solution)/shard_map/ppermute | solution.py:327
  37.1 2.5 %collective-permute-done.4.p3 = bf16[2,592,128]{2,1,0:T(8,128)(2,1)S(1)} collective-permute-done((bf16[2,592,128]{2,1,0:T(8,128)(2,1)S(1)}, bf16[2,592,128]{2,1,0:T(8,128)(2,1)S(1)}, u32[]{:S(2)}, u32[]{:S(2)}) %collective-permute-start.4) | collective-permute-done | bytes 303136 | tf_op jit(solution)/shard_map/ppermute | solution.py:327
  41.6 2.7 %shard_map.121 = (f32[2,256,128]{2,1,0:T(8,128)S(1)}, f32[2,256,128]{2,1,0:T(8,128)S(1)}, f32[2,256,512]{2,1,0:T(8,128)S(1)}) custom-call(s32[10]{0:T(128)S(1)} %stack.58.info, bf16[2,256,592]{2,1,0:T(8,128)(2,1)S(1)} %bitcast.41, bf16[2,592,128]{2,1,0:T(8,128)(2,1)S(1)} %collective-permute-done.2.p1, bf16[2,592,128]{2,1,0:T(8,128)(2,1)S(1)} %collective-permute-done.3.p2, ...), custom_call_target="tpu_custom_call" | custom-call | tf_op jit(solution)/shard_map/pallas_call | solution.py:371
  44.3 3.8 %shard_map.122 = (bf16[128,2560]{1,0:T(8,128)(2,1)S(1)}, f32[128,2560]{1,0:T(8,128)S(1)}) custom-call(s32[10]{0:T(128)S(1)} %stack.58.info, bf16[2,256,592]{2,1,0:T(8,128)(2,1)S(1)} %bitcast.42, bf16[6,592,128]{2,1,0:T(8,128)(2,1)S(1)} %collective-permute-done.6.others, f32[2,256,128]{2,1,0:T(8,128)S(1)} %get-tuple-element.44.old_peak, ...), custom_call_target="tpu_custom_call" | custom-call | tf_op jit(solution)/shard_map/pallas_call | solution.py:374
  48.1 2.4 %collective-permute-start.7 = (bf16[128,2560]{1,0:T(8,128)(2,1)S(1)}, bf16[128,2560]{1,0:T(8,128)(2,1)S(1)}, u32[]{:S(2)}, u32[]{:S(2)}) collective-permute-start(bf16[128,2560]{1,0:T(8,128)(2,1)S(1)} %get-tuple-element.48), channel_id=1, source_target_pairs={{0,1},{1,0},{2,3},{3,2},{4,5},{5,4},{6,7},{7,6},{8,9},{9,8},{10,11... | collective-permute-start | bytes 1966088 | tf_op jit(solution)/shard_map/ppermute | solution.py:381
  53.2 13.3 %all-to-all-start = ((bf16[16,8,2560]{2,1,0:T(8,128)(2,1)}), bf16[16,8,2560]{2,1,0:T(8,128)(2,1)S(1)}, u32[]{:S(2)}, u32[]{:S(2)}) async-start(bf16[16,8,2560]{2,1,0:T(8,128)(2,1)} %shard_map.123), calls=%async_computation | async-start | bytes 1310720 | tf_op jit(solution)/shard_map/all_to_all | solution.py:392
  66.7 2.7 %collective-permute-start.8 = (bf16[3,160,768]{2,1,0:T(8,128)(2,1)S(1)}, bf16[3,160,768]{2,1,0:T(8,128)(2,1)S(1)}, u32[]{:S(2)}, u32[]{:S(2)}) collective-permute-start(bf16[3,160,768]{2,1,0:T(8,128)(2,1)S(1)} %get-tuple-element.51), channel_id=1, source_target_pairs={{0,32},{32,0},{1,33},{33,1},{2,34},{34,2},{3,35},{35,3},{4,36},{36... | collective-permute-start | bytes 2211848 | tf_op jit(solution)/shard_map/ppermute | solution.py:390
  69.8 16.4 %all-to-all-done.spread = bf16[16,8,2560]{2,1,0:T(8,128)(2,1)S(1)} async-done(((bf16[16,8,2560]{2,1,0:T(8,128)(2,1)}), bf16[16,8,2560]{2,1,0:T(8,128)(2,1)S(1)}, u32[]{:S(2)}, u32[]{:S(2)}) %all-to-all-start) | async-done | bytes 655392 | tf_op jit(solution)/shard_map/all_to_all | solution.py:392
  87.2 8.5 %all-to-all-start.1 = ((bf16[16,8,512]{2,1,0:T(8,128)(2,1)}), bf16[16,8,512]{2,1,0:T(8,128)(2,1)S(1)}, u32[]{:S(2)}, u32[]{:S(2)}) async-start(bf16[16,8,512]{2,1,0:T(8,128)(2,1)} %shard_map.125), calls=%async_computation.1 | async-start | bytes 262144 | tf_op jit(solution)/shard_map/all_to_all | solution.py:396
  96.2 7.8 %all-to-all-done.1 = bf16[16,8,512]{2,1,0:T(8,128)(2,1)S(1)} async-done(((bf16[16,8,512]{2,1,0:T(8,128)(2,1)}), bf16[16,8,512]{2,1,0:T(8,128)(2,1)S(1)}, u32[]{:S(2)}, u32[]{:S(2)}) %all-to-all-start.1) | async-done | bytes 131104 | tf_op jit(solution)/shard_map/all_to_all | solution.py:396
  105.3 6.6 %all-to-all-start.2 = ((bf16[32,80,128]{2,1,0:T(8,128)(2,1)}), bf16[32,80,128]{2,1,0:T(8,128)(2,1)S(1)}, u32[]{:S(2)}, u32[]{:S(2)}) async-start(bf16[32,80,128]{2,1,0:T(8,128)(2,1)} %shard_map.126), calls=%async_computation.2 | async-start | bytes 1310720 | tf_op jit(solution)/shard_map/all_to_all | solution.py:425
  111.9 2.6 %collective-permute-start.9 = (bf16[3,160,384]{2,1,0:T(8,128)(2,1)}, bf16[3,160,384]{2,1,0:T(8,128)(2,1)S(1)}, u32[]{:S(2)}, u32[]{:S(2)}) collective-permute-start(bf16[3,160,384]{2,1,0:T(8,128)(2,1)} %get-tuple-element.57), channel_id=1, source_target_pairs={{0,32},{32,0},{1,33},{33,1},{2,34},{34,2},{3,35},{35,3},{4,36},{36... | collective-permute-start | bytes 1105928 | tf_op jit(solution)/shard_map/ppermute | solution.py:398
  115.7 14.8 %collective-permute-done.9.got = bf16[3,160,384]{2,1,0:T(8,128)(2,1)S(1)} collective-permute-done((bf16[3,160,384]{2,1,0:T(8,128)(2,1)}, bf16[3,160,384]{2,1,0:T(8,128)(2,1)S(1)}, u32[]{:S(2)}, u32[]{:S(2)}) %collective-permute-start.9) | collective-permute-done | bytes 368672 | tf_op jit(solution)/shard_map/ppermute | solution.py:398
  134.7 42.6 %all_to_all.30.parts = bf16[8,128,768]{2,1,0:T(8,128)(2,1)S(1)} all-to-all(bf16[8,128,768]{2,1,0:T(8,128)(2,1)S(1)} %bitcast.43), channel_id=1, replica_groups=mesh['y'=8,'xl'=2,'z'=8,'xh'=2,'core'=2] {'y'}, dimensions={0} | all-to-all | bytes 3145728 | tf_op jit(solution)/shard_map/all_to_all | solution.py:428
  177.6 24.4 %all_to_all.31 = bf16[8,128,384]{2,1,0:T(8,128)(2,1)S(1)} all-to-all(bf16[8,128,384]{2,1,0:T(8,128)(2,1)S(1)} %shard_map.130), channel_id=1, replica_groups=mesh['y'=8,'xl'=2,'z'=8,'xh'=2,'core'=2] {'y'}, dimensions={0} | all-to-all | bytes 1572864 | tf_op jit(solution)/shard_map/all_to_all | solution.py:432
  202.0 2.4 shard_map.131
  204.3 6.7 %all-to-all-start.5 = ((bf16[32,80,128]{2,1,0:T(8,128)(2,1)}), bf16[32,80,128]{2,1,0:T(8,128)(2,1)S(1)}, u32[]{:S(2)}, u32[]{:S(2)}) async-start(bf16[32,80,128]{2,1,0:T(8,128)(2,1)} %shard_map.131), calls=%async_computation.5 | async-start | bytes 1310720 | tf_op jit(solution)/shard_map/all_to_all | solution.py:436
  211.8 19.7 %all-to-all-done.5.returned = bf16[32,80,128]{2,1,0:T(8,128)(2,1)S(1)} async-done(((bf16[32,80,128]{2,1,0:T(8,128)(2,1)}), bf16[32,80,128]{2,1,0:T(8,128)(2,1)S(1)}, u32[]{:S(2)}, u32[]{:S(2)}) %all-to-all-start.5) | async-done | bytes 655392 | tf_op jit(solution)/shard_map/all_to_all | solution.py:436
  232.1 3.9 %collective-permute-start.10 = (bf16[128,160]{1,0:T(8,128)(2,1)S(1)}, bf16[128,160]{1,0:T(8,128)(2,1)S(1)}, u32[]{:S(2)}, u32[]{:S(2)}) collective-permute-start(bf16[128,160]{1,0:T(8,128)(2,1)S(1)} %get-tuple-element.62), channel_id=1, source_target_pairs={{0,32},{32,0},{1,33},{33,1},{2,34},{34,2},{3,35},{35,3},{4,36},{36... | collective-permute-start | bytes 122888 | tf_op jit(solution)/shard_map/ppermute | solution.py:440
  (86 shorter events, 26.4 us)
Async XLA Ops:
  0.0 23.9 %copy-start.12 = (s32[256]{0:T(256)S(1)}, s32[256]{0:T(256)}, u32[]{:S(2)}) copy-start(s32[256]{0:T(256)} %param.14) | copy-start | bytes 3076
  1.7 22.4 %copy-start.13 = (bf16[256,2,576]{0,2,1:T(8,128)(2,1)S(1)}, bf16[256,2,576]{0,2,1:T(8,128)(2,1)}, u32[]{:S(2)}) copy-start(bf16[256,2,576]{0,2,1:T(8,128)(2,1)} %param.12) | copy-start | bytes 1769476
  1.7 11.2 %collective-permute-start = (bf16[592,128]{1,0:T(8,128)(2,1)S(1)}, bf16[592,128]{1,0:T(8,128)(2,1)S(1)}, u32[]{:S(2)}, u32[]{:S(2)}) collective-permute-start(bf16[592,128]{1,0:T(8,128)(2,1)S(1)} %constant_dynamic-slice_fusion), channel_id=1, source_target_pairs={{0,64},{2,130},{64,128},{66,194},{128,192},{130,258},{192,256},{19... | collective-permute-start | bytes 454664 | tf_op jit(solution)/shard_map/ppermute | solution.py:316
  6.4 14.7 %collective-permute-start.1 = (bf16[592,128]{1,0:T(8,128)(2,1)S(1)}, bf16[592,128]{1,0:T(8,128)(2,1)S(1)}, u32[]{:S(2)}, u32[]{:S(2)}) collective-permute-start(bf16[592,128]{1,0:T(8,128)(2,1)S(1)} %constant_dynamic-slice_fusion), channel_id=1, source_target_pairs={{0,192},{2,258},{64,256},{66,322},{128,320},{130,386},{192,384},{1... | collective-permute-start | bytes 454664 | tf_op jit(solution)/shard_map/ppermute | solution.py:316
  21.1 13.5 %collective-permute-start.2 = (bf16[2,592,128]{2,1,0:T(8,128)(2,1)S(1)}, bf16[2,592,128]{2,1,0:T(8,128)(2,1)S(1)}, u32[]{:S(2)}, u32[]{:S(2)}) collective-permute-start(bf16[2,592,128]{2,1,0:T(8,128)(2,1)S(1)} %get-tuple-element.36.p0), channel_id=1, source_target_pairs={{0,2},{2,0},{1,3},{3,1},{4,6},{6,4},{5,7},{7,5},{8,10},{10,8},{9,1... | collective-permute-start | bytes 909320 | tf_op jit(solution)/shard_map/ppermute | solution.py:325
  24.8 12.3 %collective-permute-start.3 = (bf16[2,592,128]{2,1,0:T(8,128)(2,1)S(1)}, bf16[2,592,128]{2,1,0:T(8,128)(2,1)S(1)}, u32[]{:S(2)}, u32[]{:S(2)}) collective-permute-start(bf16[2,592,128]{2,1,0:T(8,128)(2,1)S(1)} %get-tuple-element.63), channel_id=1, source_target_pairs={{0,32},{32,0},{1,33},{33,1},{2,34},{34,2},{3,35},{35,3},{4,36},{36... | collective-permute-start | bytes 909320 | tf_op jit(solution)/shard_map/ppermute | solution.py:326
  28.3 11.2 %collective-permute-start.4 = (bf16[2,592,128]{2,1,0:T(8,128)(2,1)S(1)}, bf16[2,592,128]{2,1,0:T(8,128)(2,1)S(1)}, u32[]{:S(2)}, u32[]{:S(2)}) collective-permute-start(bf16[2,592,128]{2,1,0:T(8,128)(2,1)S(1)} %get-tuple-element.63), channel_id=1, source_target_pairs={{0,34},{2,32},{32,2},{34,0},{1,35},{3,33},{33,3},{35,1},{4,38},{6,... | collective-permute-start | bytes 909320 | tf_op jit(solution)/shard_map/ppermute | solution.py:327
  34.6 4.9 %collective-permute-start.5 = (bf16[2,592,128]{2,1,0:T(8,128)(2,1)S(1)}, bf16[2,592,128]{2,1,0:T(8,128)(2,1)S(1)}, u32[]{:S(2)}, u32[]{:S(2)}) collective-permute-start(bf16[2,592,128]{2,1,0:T(8,128)(2,1)S(1)} %get-tuple-element.36.p0), channel_id=1, source_target_pairs={{0,1},{1,0},{2,3},{3,2},{4,5},{5,4},{6,7},{7,6},{8,9},{9,8},{10,11... | collective-permute-start | bytes 909320 | tf_op jit(solution)/shard_map/ppermute | solution.py:367
  39.6 4.6 %collective-permute-start.6 = (bf16[6,592,128]{2,1,0:T(8,128)(2,1)S(1)}, bf16[6,592,128]{2,1,0:T(8,128)(2,1)S(1)}, u32[]{:S(2)}, u32[]{:S(2)}) collective-permute-start(bf16[6,592,128]{2,1,0:T(8,128)(2,1)S(1)} %shard_map.120), channel_id=1, source_target_pairs={{0,1},{1,0},{2,3},{3,2},{4,5},{5,4},{6,7},{7,6},{8,9},{9,8},{10,11... | collective-permute-start | bytes 2727944 | tf_op jit(solution)/shard_map/ppermute | solution.py:370
  44.3 6.2 %copy-start.1 = (bf16[3,160,768]{2,1,0:T(8,128)(2,1)S(1)}, bf16[3,160,768]{2,1,0:T(8,128)(2,1)}, u32[]{:S(2)}) copy-start(bf16[3,160,768]{2,1,0:T(8,128)(2,1)} %gate.1) | copy-start | bytes 2211844
  48.1 4.1 %collective-permute-start.7 = (bf16[128,2560]{1,0:T(8,128)(2,1)S(1)}, bf16[128,2560]{1,0:T(8,128)(2,1)S(1)}, u32[]{:S(2)}, u32[]{:S(2)}) collective-permute-start(bf16[128,2560]{1,0:T(8,128)(2,1)S(1)} %get-tuple-element.48), channel_id=1, source_target_pairs={{0,1},{1,0},{2,3},{3,2},{4,5},{5,4},{6,7},{7,6},{8,9},{9,8},{10,11... | collective-permute-start | bytes 1966088 | tf_op jit(solution)/shard_map/ppermute | solution.py:381
  52.2 14.3 %copy-start.15 = (s32[8,16,6]{1,0,2:T(8,128)S(1)}, s32[8,16,6]{1,0,2:T(8,128)}, u32[]{:S(2)}) copy-start(s32[8,16,6]{1,0,2:T(8,128)} %param.19) | copy-start | bytes 9220
  52.2 17.3 %copy-start.16 = (f32[2560]{0:T(1024)S(1)}, f32[2560]{0:T(1024)}, u32[]{:S(2)}) copy-start(f32[2560]{0:T(1024)} %param.18) | copy-start | bytes 30724
  52.2 34.0 %copy-start.10 = (bf16[8,2560]{1,0:T(8,128)(2,1)S(1)}, bf16[8,2560]{1,0:T(8,128)(2,1)}, u32[]{:S(2)}) copy-start(bf16[8,2560]{1,0:T(8,128)(2,1)} %residual.1) | copy-start | bytes 122884
  53.2 33.0 %all-to-all-start = ((bf16[16,8,2560]{2,1,0:T(8,128)(2,1)}), bf16[16,8,2560]{2,1,0:T(8,128)(2,1)S(1)}, u32[]{:S(2)}, u32[]{:S(2)}) async-start(bf16[16,8,2560]{2,1,0:T(8,128)(2,1)} %shard_map.123), calls=%async_computation | async-start | bytes 1310720 | tf_op jit(solution)/shard_map/all_to_all | solution.py:392
  66.7 29.5 %collective-permute-start.8 = (bf16[3,160,768]{2,1,0:T(8,128)(2,1)S(1)}, bf16[3,160,768]{2,1,0:T(8,128)(2,1)S(1)}, u32[]{:S(2)}, u32[]{:S(2)}) collective-permute-start(bf16[3,160,768]{2,1,0:T(8,128)(2,1)S(1)} %get-tuple-element.51), channel_id=1, source_target_pairs={{0,32},{32,0},{1,33},{33,1},{2,34},{34,2},{3,35},{35,3},{4,36},{36... | collective-permute-start | bytes 2211848 | tf_op jit(solution)/shard_map/ppermute | solution.py:390
  87.2 16.9 %all-to-all-start.1 = ((bf16[16,8,512]{2,1,0:T(8,128)(2,1)}), bf16[16,8,512]{2,1,0:T(8,128)(2,1)S(1)}, u32[]{:S(2)}, u32[]{:S(2)}) async-start(bf16[16,8,512]{2,1,0:T(8,128)(2,1)} %shard_map.125), calls=%async_computation.1 | async-start | bytes 262144 | tf_op jit(solution)/shard_map/all_to_all | solution.py:396
  96.2 9.1 %copy-start.4 = (bf16[3,160,768]{2,1,0:T(8,128)(2,1)}, bf16[3,160,768]{2,1,0:T(8,128)(2,1)S(1)}, u32[]{:S(2)}) copy-start(bf16[3,160,768]{2,1,0:T(8,128)(2,1)S(1)} %collective-permute-done.8.got) | copy-start | bytes 2211844
  105.3 27.2 %all-to-all-start.2 = ((bf16[32,80,128]{2,1,0:T(8,128)(2,1)}), bf16[32,80,128]{2,1,0:T(8,128)(2,1)S(1)}, u32[]{:S(2)}, u32[]{:S(2)}) async-start(bf16[32,80,128]{2,1,0:T(8,128)(2,1)} %shard_map.126), calls=%async_computation.2 | async-start | bytes 1310720 | tf_op jit(solution)/shard_map/all_to_all | solution.py:425
  111.9 18.6 %collective-permute-start.9 = (bf16[3,160,384]{2,1,0:T(8,128)(2,1)}, bf16[3,160,384]{2,1,0:T(8,128)(2,1)S(1)}, u32[]{:S(2)}, u32[]{:S(2)}) collective-permute-start(bf16[3,160,384]{2,1,0:T(8,128)(2,1)} %get-tuple-element.57), channel_id=1, source_target_pairs={{0,32},{32,0},{1,33},{33,1},{2,34},{34,2},{3,35},{35,3},{4,36},{36... | collective-permute-start | bytes 1105928 | tf_op jit(solution)/shard_map/ppermute | solution.py:398
  115.6 14.9 %copy-start.7 = (bf16[3,160,384]{2,1,0:T(8,128)(2,1)S(1)}, bf16[3,160,384]{2,1,0:T(8,128)(2,1)}, u32[]{:S(2)}) copy-start(bf16[3,160,384]{2,1,0:T(8,128)(2,1)} %copy-done.6) | copy-start | bytes 1105924
  202.0 9.3 %copy-start.14 = (f32[8,16,6]{1,0,2:T(8,128)S(1)}, f32[8,16,6]{1,0,2:T(8,128)}, u32[]{:S(2)}) copy-start(f32[8,16,6]{1,0,2:T(8,128)} %param.20) | copy-start | bytes 9220
  204.3 27.2 %all-to-all-start.5 = ((bf16[32,80,128]{2,1,0:T(8,128)(2,1)}), bf16[32,80,128]{2,1,0:T(8,128)(2,1)S(1)}, u32[]{:S(2)}, u32[]{:S(2)}) async-start(bf16[32,80,128]{2,1,0:T(8,128)(2,1)} %shard_map.131), calls=%async_computation.5 | async-start | bytes 1310720 | tf_op jit(solution)/shard_map/all_to_all | solution.py:436
  232.1 6.2 %collective-permute-start.10 = (bf16[128,160]{1,0:T(8,128)(2,1)S(1)}, bf16[128,160]{1,0:T(8,128)(2,1)S(1)}, u32[]{:S(2)}, u32[]{:S(2)}) collective-permute-start(bf16[128,160]{1,0:T(8,128)(2,1)S(1)} %get-tuple-element.62), channel_id=1, source_target_pairs={{0,32},{32,0},{1,33},{33,1},{2,34},{34,2},{3,35},{35,3},{4,36},{36... | collective-permute-start | bytes 122888 | tf_op jit(solution)/shard_map/ppermute | solution.py:440
  (8 other events, 21.8 us)

commit v9 on v8

--- a/solution.py
+++ b/solution.py
@@ -16,7 +16,8 @@
 KEYW = 592
 FAR = float(2**20)
 
-CTX = ("y", "xl")
+CTX = ("yh", "yl", "xl")
+YS = ("yh", "yl")
 EXP = ("z", "xh", "core")
 SWAP = [(0, 1), (1, 0)]
 BIG_VMEM = pltpu.CompilerParams(vmem_limit_bytes=20 * 2**20)
@@ -136,18 +137,11 @@
     mean_sq = jnp.mean(stream * stream, axis=1, keepdims=True)
     normed = (stream * lax.rsqrt(mean_sq + 1e-06) * gain[...]).astype(bf16).astype(f32)
     width = stream.shape[1] // 16
-    fill = jnp.zeros((stream.shape[0], packed.shape[2] - 3 * width), f32)
+    fill = jnp.zeros((stream.shape[0], packed.shape[2] - 5 * width), f32)
     for c in range(16):
-        mine, other = c * width, (c ^ 1) * width
-        packed[c] = jnp.concatenate(
-            [
-                normed[:, mine : mine + width],
-                normed[:, other : other + width],
-                stream[:, mine : mine + width],
-                fill,
-            ],
-            axis=1,
-        ).astype(bf16)
+        parts = [normed[:, (c ^ k) * width : ((c ^ k) + 1) * width] for k in range(4)]
+        parts += [stream[:, c * width : (c + 1) * width], fill]
+        packed[c] = jnp.concatenate(parts, axis=1).astype(bf16)
 
 
 def store_packed(out, n, rows):
@@ -165,12 +159,10 @@
 
 
 def pick_kernel(picker, split, out):
-    values = split[:, :384]
-    doubled = jnp.concatenate([values[:, :320], values[:, 256:320]], axis=1)
+    width = out.shape[2]
     for r in range(0, picker.shape[0], 256):
-        rows = jnp.dot(picker[r : r + 256, :], doubled, preferred_element_type=f32)
-        for n in range(256 // SLOTS):
-            store_packed(out, r // SLOTS + n, rows[n * SLOTS : (n + 1) * SLOTS])
+        rows = jnp.dot(picker[r : r + 256, :], split[:, :width], preferred_element_type=f32)
+        out[r // SLOTS : (r + 256) // SLOTS] = rows.reshape(256 // SLOTS, SLOTS, width).astype(bf16)
 
 
 def row_mask(count, j):
@@ -182,32 +174,34 @@
     return jnp.concatenate([rows * mask for mask in masks], axis=1)
 
 
-def split_weights_kernel(info, gate, up, down, in_send, in_keep, down_send, down_keep):
-    half = gate.shape[2] // 2
-
-    def move(into, onto, start):
-        into[:, :, :half] = gate[:, :, start : start + half]
-        into[:, :, half:] = up[:, :, start : start + half]
-        onto[...] = down[:, :, start : start + half]
-
-    @pl.when(info[9] == 0)
-    def _():
-        move(in_keep, down_keep, 0)
-        move(in_send, down_send, half)
-
-    @pl.when(info[9] != 0)
-    def _():
-        move(in_keep, down_keep, half)
-        move(in_send, down_send, 0)
-
-
-def join_in_kernel(keep, got, out):
-    rows = keep.shape[1]
+def split_weights_kernel(info, gate, up, down, keep, send_x, send_y, send_d, down_keep, down_send):
+    part = gate.shape[2] // 4
+
+    def quarter(weights, q):
+        return weights[:, :, q * part : (q + 1) * part]
+
+    for own in range(4):
+
+        @pl.when(info[10] == own)
+        def _():
+            for k, out in enumerate((keep, send_x, send_y, send_d)):
+                q = own ^ k
+                out[...] = jnp.concatenate([quarter(gate, q), quarter(up, q)], axis=2)
+
+    for own in range(2):
+
+        @pl.when(info[9] == own)
+        def _():
+            for q, out in ((own, down_keep), (1 - own, down_send)):
+                out[...] = jnp.concatenate([quarter(down, q), quarter(down, q + 2)], axis=2)
+
+
+def join_in_kernel(own, from_x, from_y, from_d, out):
+    rows = own.shape[1]
     for j in range(3):
-        base = j * 384
-        out[base : base + rows, :] = keep[j]
-        out[base + rows : base + 2 * rows, :] = got[j]
-        out[base + 2 * rows : base + 384, :] = got[j, 256 - rows :]
+        for k, part in enumerate((own, from_x, from_y, from_d)):
+            base = (4 * j + k) * rows
+            out[base : base + rows, :] = part[j]
 
 
 def join_down_kernel(keep, got, out):
@@ -222,30 +216,39 @@
 def gate_up_kernel(received, weights, pre):
     masks = [row_mask(256, j) for j in range(3)]
     for r in range(0, received.shape[0], 8):
-        rows = jnp.concatenate([load_packed(received, r + n) for n in range(8)], axis=0)
+        rows = received[r : r + 8].reshape(256, received.shape[2])
         total = jnp.dot(spread_experts(rows, masks), weights[...], preferred_element_type=f32)
-        pre[r * SLOTS : (r + 8) * SLOTS, :] = total.astype(bf16)
+        pre[r * SLOTS // 256] = total.astype(bf16)
 
 
 def hidden_kernel(parts, out):
     total = jnp.sum(parts[...].astype(f32), axis=0)
     half = total.shape[1] // 2
     gate, up = total[:, :half], total[:, half:]
-    hidden = (gate / (1.0 + jnp.exp(-gate)) * up).astype(bf16)
+    hidden = gate / (1.0 + jnp.exp(-gate)) * up
+    hidden = jnp.concatenate([hidden[:128], hidden[128:]], axis=1).astype(bf16)
     for n in range(out.shape[0]):
         out[n] = hidden
 
 
 def down_kernel(hidden, weights, out):
     masks = [row_mask(256, j) for j in range(3)]
-    for r in range(0, hidden.shape[0], 256):
-        rows = spread_experts(hidden[r : r + 256, :], masks)
-        total = nt_dot(rows, weights[...])
+    half = hidden.shape[2] // 2
+    for r in range(0, hidden.shape[0], 2):
+        first, second = hidden[r], hidden[r + 1]
+        rows = jnp.concatenate(
+            [
+                jnp.concatenate([first[:, :half], second[:, :half]], axis=1),
+                jnp.concatenate([first[:, half:], second[:, half:]], axis=1),
+            ],
+            axis=0,
+        )
+        total = nt_dot(spread_experts(rows, masks), weights[...])
         for n in range(256 // SLOTS):
-            store_packed(out, r // SLOTS + n, total[n * SLOTS : (n + 1) * SLOTS])
-
-
-def combine_kernel(weighting, returned, keep, send):
+            store_packed(out, r * 128 // SLOTS + n, total[n * SLOTS : (n + 1) * SLOTS])
+
+
+def combine_kernel(weighting, returned, order, stream, keep, send):
     width = keep.shape[1]
     rows = jnp.concatenate([load_packed(returned, n) for n in range(returned.shape[0])], axis=0)
     top = weighting[...].astype(bf16)
@@ -254,7 +257,8 @@
         rest, rows, preferred_element_type=f32
     )
     tail = mixture[:, 256:320] + mixture[:, 320:384]
-    keep[...] = mixture[:, :width]
+    kept = jnp.dot(order[...], stream[:, 4 * width : 5 * width], preferred_element_type=f32)
+    keep[...] = kept + mixture[:, :width]
     send[...] = jnp.concatenate([mixture[:, width:256], tail], axis=1).astype(bf16)
 
 
@@ -298,7 +302,8 @@
     width_pair = 2 * width_out
     ff = expert_gate.shape[2]
     ff_half = ff // 2
-    y, xl, xh, core = (lax.axis_index(a) for a in ("y", "xl", "xh", "core"))
+    y = lax.axis_index(YS)
+    yl, xl, xh, core = (lax.axis_index(a) for a in ("yl", "xl", "xh", "core"))
     half = block_len // 2
 
     segment_axis = jnp.arange(SEGMENTS, dtype=i32)
@@ -313,7 +318,7 @@
         pairs = [
             (2 * i + h, 2 * ((i + (near, far)[h]) % 8) + h) for i in range(8) for h in range(2)
         ]
-        return lax.ppermute(mine, ("y", "xh"), pairs)
+        return lax.ppermute(mine, YS + ("xh",), pairs)
 
     column = jnp.stack([along_y(1, 2), along_y(3, 4)])
     to_other = jnp.where(
@@ -340,7 +345,7 @@
         + blocks_of(xl, 1 - xh)
         + blocks_sent(1 - xl, xh)
         + blocks_sent(1 - xl, 1 - xh)
-        + [core, xl]
+        + [core, xl, 2 * yl + xl]
     ).astype(i32)
 
     masks = jnp.where(own_segment, 0.0, -FAR).astype(bf16)
@@ -365,7 +370,13 @@
     pieces[1], column_late, peak = lax.optimization_barrier((pieces[1], column, state[0]))
     state = [peak] + list(state[1:])
     first_other = lax.ppermute(column_late, "core", SWAP)
-    *pieces, first_other = lax.optimization_barrier((*pieces, first_other))
+    quarter_out = sds((3, width_out, 2 * (ff // 4)), bf16)
+    in_keep, *in_sends, down_keep, down_send = call(
+        split_weights_kernel, [quarter_out] * 6, (), True, 4
+    )(info, expert_gate, expert_up, jnp.transpose(expert_down, (0, 2, 1)))
+    *pieces, first_other, in_sends[0] = lax.optimization_barrier(
+        (*pieces, first_other, in_sends[0])
+    )
     three = call(gather_kernel, [sds((6, KEYW, half), bf16)], count=3)(*pieces[1:])
     others = lax.ppermute(three, "core", SWAP)
     state = call(
@@ -381,23 +392,24 @@
     got = lax.ppermute(send, "core", SWAP)
     pair_sum = call(add_kernel, [sds((16, 8, width_model), bf16)], count=2)(keep, got)
 
-    in_out = sds((3, width_out, 2 * ff_half), bf16)
-    down_out = sds((3, width_out, ff_half), bf16)
-    in_send, in_keep, down_send, down_keep = call(
-        split_weights_kernel, [in_out, in_out, down_out, down_out], (), True, 4
-    )(info, expert_gate, expert_up, jnp.transpose(expert_down, (0, 2, 1)))
-    pair_sum, in_send = lax.optimization_barrier((pair_sum, in_send))
-    in_got = lax.ppermute(in_send, "xl", SWAP)
+    pair_sum, send_x, send_y, send_d = lax.optimization_barrier((pair_sum, *in_sends))
+    in_parts = [
+        in_keep,
+        lax.ppermute(send_x, "xl", SWAP),
+        lax.ppermute(send_y, "yl", SWAP),
+        lax.ppermute(send_d, ("yl", "xl"), diagonal),
+    ]
 
     spread = lax.all_to_all(pair_sum, ("z", "xh"), split_axis=0, concat_axis=0, tiled=True)
-    packed = call(norm_kernel, [sds((16, 8, 512), bf16)], count=3)(
+    spread, down_send, *in_parts = lax.optimization_barrier((spread, down_send, *in_parts))
+    down_got = lax.ppermute(down_send, "xl", SWAP)
+    packed = call(norm_kernel, [sds((16, 8, 896), bf16)], count=3)(
         spread, residual, norm_gain[None, :]
     )
     split = lax.all_to_all(packed, CTX, split_axis=0, concat_axis=0, tiled=True)
-    split, in_got, down_send = lax.optimization_barrier((split, in_got, down_send))
-    down_got = lax.ppermute(down_send, "xl", SWAP)
-    split = split.reshape(128, 512)
-    w_in = call(join_in_kernel, [sds((3 * 384, 2 * ff_half), bf16)], count=2)(in_keep, in_got)
+    split, down_got = lax.optimization_barrier((split, down_got))
+    split = split.reshape(128, 896)
+    w_in = call(join_in_kernel, [sds((12 * width_out, ff // 2), bf16)], count=4)(*in_parts)
     w_down = call(join_down_kernel, [sds((384, 3 * ff_half), bf16)], count=2)(down_keep, down_got)
 
     routes = jnp.transpose(route_ids, (1, 0, 2)).reshape(128, TOPK)
@@ -421,34 +433,27 @@
     )
 
     travel = sds((32, 80, 128), bf16)
-    outgoing = call(pick_kernel, [travel], count=2)(picker, split)
+    outgoing = call(pick_kernel, [sds((32, SLOTS, 4 * width_out), bf16)], count=2)(picker, split)
     received = lax.all_to_all(outgoing, EXP, split_axis=0, concat_axis=0, tiled=True)
     received, w_in, w_down = lax.optimization_barrier((received, w_in, w_down))
-    pre = call(gate_up_kernel, [sds((32 * SLOTS, 2 * ff_half), bf16)], count=2)(received, w_in)
-    pre_parts = lax.all_to_all(
-        pre.reshape(8, 128, 2 * ff_half), "y", split_axis=0, concat_axis=0, tiled=True
-    )
+    pre = call(gate_up_kernel, [sds((4, 256, ff // 2), bf16)], count=2)(received, w_in)
+    pre_parts = lax.all_to_all(pre, "yh", split_axis=0, concat_axis=0, tiled=True)
     hidden = call(hidden_kernel, [sds((8, 128, ff_half), bf16)], count=1)(pre_parts)
-    hidden_all = lax.all_to_all(hidden, "y", split_axis=0, concat_axis=0, tiled=True)
+    hidden_all = lax.all_to_all(hidden, YS, split_axis=0, concat_axis=0, tiled=True)
     expert_out = call(down_kernel, [travel], count=2)(
-        hidden_all.reshape(32 * SLOTS, ff_half), w_down
+        hidden_all, w_down
     )
     returned = lax.all_to_all(expert_out, EXP, split_axis=0, concat_axis=0, tiled=True)
     mix_keep, mix_send = call(
-        combine_kernel, [sds((128, width_out), f32), sds((128, width_out), bf16)], count=2
-    )(weighting, returned)
+        combine_kernel, [sds((128, width_out), f32), sds((128, width_out), bf16)], count=4
+    )(weighting, returned, back_order.astype(bf16), split)
     mix_got = lax.ppermute(mix_send, "xl", SWAP)
-    stream_rb = jnp.dot(
-        back_order.astype(bf16),
-        split[:, width_pair : width_pair + width_out],
-        preferred_element_type=f32,
-    )
-    result = (stream_rb + mix_keep + mix_got.astype(f32)).astype(bf16)
+    result = (mix_keep + mix_got.astype(f32)).astype(bf16)
     return result.reshape(8, 16, width_out)
 
 
 def solution(mesh):
-    grid = Mesh(mesh.devices.reshape(8, 2, 8, 2, 2), ("y", "xl", "z", "xh", "core"))
+    grid = Mesh(mesh.devices.reshape(4, 2, 2, 8, 2, 2), ("yh", "yl", "xl", "z", "xh", "core"))
     return jax.shard_map(
         on_device,
         mesh=grid,

time: 241 us -> 257 us (1.066)
  waiting for transfers between devices: 75.7 us -> 91.8 us
  blocking collectives: 67 us -> 54.2 us
  starting transfers between devices: 70.8 us -> 78.3 us
  local copies, waits for them, and re-layouts: 3.88 us -> 8.53 us
    all_to_all x1, waiting for transfers between devices: 1.89 us -> 27.8 us  [on_device(): lax.all_to_all(outgoing, EXP, split_axis=0, concat_axis=0, tiled=True)]
    ppermute x3 -> x5, waiting for transfers between devices: 8.73 us -> 26.3 us  [the longest x1 8.82 us: on_device(): lax.ppermute(send_x, 'xl', SWAP)]
    all_to_all x1, waiting for transfers between devices: 16.4 us -> 0.01 us  [on_device(): lax.all_to_all(pair_sum, ('z', 'xh'), split_axis=0, concat_axis=0, tiled=...]
    all_to_all x2, blocking collectives: 67 us -> 54.2 us  [the longest x1 28.2 us: on_device(): lax.all_to_all(pre, 'yh', split_axis=0, concat_axis=0, tiled=True)]
    all_to_all x1, waiting for transfers between devices: 7.82 us -> 0.01 us  [on_device(): split = lax.all_to_all(packed, CTX, split_axis=0, concat_axis=0, tiled=True)]
    ppermute x3 -> x5, starting transfers between devices: 13.3 us -> 19.8 us  [the longest x2 10.6 us: along_y(): return lax.ppermute(mine, YS + ('xh',), pairs)]
    unnamed x36 -> x64, local copies, waits for them, and re-layouts: 3.2 us -> 7.84 us
    ppermute x1, waiting for transfers between devices: 14.8 us -> 11 us  [on_device(): down_got = lax.ppermute(down_send, 'xl', SWAP)]
  transfers between devices with their start and end apart: 15 -> 17, of which waited for: 12 -> 11; matrix products, arithmetic and copies ran while one was open for 1% -> 1% of each run, Pallas kernels for 3% -> 3%
where the time goes in v9:
time: 257 us; the launch traced here: 256 us
  waiting for transfers between devices  91.8 us (36%)
  starting transfers between devices  78.3 us (30%)
  blocking collectives  54.2 us (21%)
  Pallas kernels  19.6 us (8%)
  local copies, waits for them, and re-layouts  8.53 us (3%)
  other arithmetic  2.9 us (1%)
    all_to_all x1, blocking collectives, on_device(): lax.all_to_all(pre, 'yh', split_axis=0, concat_axis=0, tiled=True)  28.2 us
    all_to_all x1, waiting for transfers between devices, on_device(): lax.all_to_all(outgoing, EXP, split_axis=0, concat_axis=0, tiled=True)  27.8 us
    all_to_all x1, blocking collectives, on_device(): lax.all_to_all(hidden, YS, split_axis=0, concat_axis=0, tiled=True)  26 us
    all_to_all x1, waiting for transfers between devices, on_device(): lax.all_to_all(expert_out, EXP, split_axis=0, concat_axis=0, tiled=True)  19.6 us
    all_to_all x1, starting transfers between devices, on_device(): lax.all_to_all(pair_sum, ('z', 'xh'), split_axis=0, concat_axis=0, tiled=...  13.5 us
    ppermute x1, waiting for transfers between devices, on_device(): down_got = lax.ppermute(down_send, 'xl', SWAP)  11 us
    ppermute x2, starting transfers between devices, along_y(): return lax.ppermute(mine, YS + ('xh',), pairs)  10.6 us
    all_to_all x1, starting transfers between devices, on_device(): lax.all_to_all(outgoing, EXP, split_axis=0, concat_axis=0, tiled=True)  9.68 us
  transfers between devices with their start and end apart: 17, of which 11 were waited for; matrix products, arithmetic and copies ran while one was open for 1% of the time, Pallas kernels for 3%

profile of v9, /device:TPU:6, one launch (start us, length us, event | category | flops | bytes accessed | tf_op | source)
XLA Modules:
  0.0 256.1 jit_solution(12414990014632535293)
XLA Ops:
  1.7 4.6 %collective-permute-start = (bf16[592,128]{1,0:T(8,128)(2,1)S(1)}, bf16[592,128]{1,0:T(8,128)(2,1)S(1)}, u32[]{:S(2)}, u32[]{:S(2)}) collective-permute-start(bf16[592,128]{1,0:T(8,128)(2,1)S(1)} %constant_dynamic-slice_fusion), channel_id=1, source_target_pairs={{0,64},{2,130},{64,128},{66,194},{128,192},{130,258},{192,256},{19... | collective-permute-start | bytes 454664 | tf_op jit(solution)/shard_map/ppermute | solution.py:321
  6.4 5.9 %collective-permute-start.1 = (bf16[592,128]{1,0:T(8,128)(2,1)S(1)}, bf16[592,128]{1,0:T(8,128)(2,1)S(1)}, u32[]{:S(2)}, u32[]{:S(2)}) collective-permute-start(bf16[592,128]{1,0:T(8,128)(2,1)S(1)} %constant_dynamic-slice_fusion), channel_id=1, source_target_pairs={{0,192},{2,258},{64,256},{66,322},{128,320},{130,386},{192,384},{1... | collective-permute-start | bytes 454664 | tf_op jit(solution)/shard_map/ppermute | solution.py:321
  12.9 8.2 %collective-permute-done.1 = bf16[592,128]{1,0:T(8,128)(2,1)S(1)} collective-permute-done((bf16[592,128]{1,0:T(8,128)(2,1)S(1)}, bf16[592,128]{1,0:T(8,128)(2,1)S(1)}, u32[]{:S(2)}, u32[]{:S(2)}) %collective-permute-start.1) | collective-permute-done | bytes 151584 | tf_op jit(solution)/shard_map/ppermute | solution.py:321
  21.8 2.7 %collective-permute-start.2 = (bf16[2,592,128]{2,1,0:T(8,128)(2,1)S(1)}, bf16[2,592,128]{2,1,0:T(8,128)(2,1)S(1)}, u32[]{:S(2)}, u32[]{:S(2)}) collective-permute-start(bf16[2,592,128]{2,1,0:T(8,128)(2,1)S(1)} %get-tuple-element.46.p0), channel_id=1, source_target_pairs={{0,2},{2,0},{1,3},{3,1},{4,6},{6,4},{5,7},{7,5},{8,10},{10,8},{9,1... | collective-permute-start | bytes 909320 | tf_op jit(solution)/shard_map/ppermute | solution.py:330
  25.5 3.7 %collective-permute-start.3 = (bf16[2,592,128]{2,1,0:T(8,128)(2,1)}, bf16[2,592,128]{2,1,0:T(8,128)(2,1)S(1)}, u32[]{:S(2)}, u32[]{:S(2)}) collective-permute-start(bf16[2,592,128]{2,1,0:T(8,128)(2,1)} %get-tuple-element.83), channel_id=1, source_target_pairs={{0,32},{32,0},{1,33},{33,1},{2,34},{34,2},{3,35},{35,3},{4,36},{36... | collective-permute-start | bytes 909320 | tf_op jit(solution)/shard_map/ppermute | solution.py:331
  29.2 3.5 %collective-permute-start.4 = (bf16[2,592,128]{2,1,0:T(8,128)(2,1)}, bf16[2,592,128]{2,1,0:T(8,128)(2,1)S(1)}, u32[]{:S(2)}, u32[]{:S(2)}) collective-permute-start(bf16[2,592,128]{2,1,0:T(8,128)(2,1)} %get-tuple-element.83), channel_id=1, source_target_pairs={{0,34},{2,32},{32,2},{34,0},{1,35},{3,33},{33,3},{35,1},{4,38},{6,... | collective-permute-start | bytes 909320 | tf_op jit(solution)/shard_map/ppermute | solution.py:332
  42.5 2.7 %shard_map.122 = (f32[2,256,128]{2,1,0:T(8,128)S(1)}, f32[2,256,128]{2,1,0:T(8,128)S(1)}, f32[2,256,512]{2,1,0:T(8,128)S(1)}) custom-call(s32[11]{0:T(128)S(1)} %stack.62.info, bf16[2,256,592]{2,1,0:T(8,128)(2,1)S(1)} %bitcast.40, bf16[2,592,128]{2,1,0:T(8,128)(2,1)S(1)} %collective-permute-done.2.p1, bf16[2,592,128]{2,1,0:T(8,128)(2,1)S(1)} %collective-permute-done.3.p2, ...), custom_call_target="tpu_custom_call" | custom-call | tf_op jit(solution)/shard_map/pallas_call | solution.py:382
  45.2 3.8 %shard_map.123 = (bf16[128,2560]{1,0:T(8,128)(2,1)S(1)}, f32[128,2560]{1,0:T(8,128)S(1)}) custom-call(s32[11]{0:T(128)S(1)} %stack.62.info, bf16[2,256,592]{2,1,0:T(8,128)(2,1)S(1)} %bitcast.41, bf16[6,592,128]{2,1,0:T(8,128)(2,1)S(1)} %collective-permute-done.6.others, f32[2,256,128]{2,1,0:T(8,128)S(1)} %get-tuple-element.55.old_peak, ...), custom_call_target="tpu_custom_call" | custom-call | tf_op jit(solution)/shard_map/pallas_call | solution.py:385
  49.0 2.4 collective-permute-start.7
  54.2 13.5 %all-to-all-start = ((bf16[16,8,2560]{2,1,0:T(8,128)(2,1)}), bf16[16,8,2560]{2,1,0:T(8,128)(2,1)S(1)}, u32[]{:S(2)}, u32[]{:S(2)}) async-start(bf16[16,8,2560]{2,1,0:T(8,128)(2,1)} %shard_map.124), calls=%async_computation | async-start | bytes 1310720 | tf_op jit(solution)/shard_map/all_to_all | solution.py:403
  67.6 4.0 %collective-permute-start.10 = (bf16[3,160,384]{2,1,0:T(8,128)(2,1)}, bf16[3,160,384]{2,1,0:T(8,128)(2,1)S(1)}, u32[]{:S(2)}, u32[]{:S(2)}) collective-permute-start(bf16[3,160,384]{2,1,0:T(8,128)(2,1)} %get-tuple-element.68), channel_id=1, source_target_pairs={{0,96},{32,64},{64,32},{96,0},{1,97},{33,65},{65,33},{97,1},{2,98}... | collective-permute-start | bytes 1105928 | tf_op jit(solution)/shard_map/ppermute | solution.py:400
  71.6 3.3 %collective-permute-start.8 = (bf16[3,160,384]{2,1,0:T(8,128)(2,1)S(1)}, bf16[3,160,384]{2,1,0:T(8,128)(2,1)S(1)}, u32[]{:S(2)}, u32[]{:S(2)}) collective-permute-start(bf16[3,160,384]{2,1,0:T(8,128)(2,1)S(1)} %copy-done.26), channel_id=1, source_target_pairs={{0,32},{32,0},{1,33},{33,1},{2,34},{34,2},{3,35},{35,3},{4,36},{36... | collective-permute-start | bytes 1105928 | tf_op jit(solution)/shard_map/ppermute | solution.py:398
  77.4 8.7 %collective-permute-done.10.from_d = bf16[3,160,384]{2,1,0:T(8,128)(2,1)S(1)} collective-permute-done((bf16[3,160,384]{2,1,0:T(8,128)(2,1)}, bf16[3,160,384]{2,1,0:T(8,128)(2,1)S(1)}, u32[]{:S(2)}, u32[]{:S(2)}) %collective-permute-start.10) | collective-permute-done | bytes 368672 | tf_op jit(solution)/shard_map/ppermute | solution.py:400
  86.1 8.8 %collective-permute-done.8.from_x = bf16[3,160,384]{2,1,0:T(8,128)(2,1)S(1)} collective-permute-done((bf16[3,160,384]{2,1,0:T(8,128)(2,1)S(1)}, bf16[3,160,384]{2,1,0:T(8,128)(2,1)S(1)}, u32[]{:S(2)}, u32[]{:S(2)}) %collective-permute-start.8) | collective-permute-done | bytes 368672 | tf_op jit(solution)/shard_map/ppermute | solution.py:398
  95.9 8.4 %all-to-all-start.1 = ((bf16[16,8,896]{2,1,0:T(8,128)(2,1)}), bf16[16,8,896]{2,1,0:T(8,128)(2,1)S(1)}, u32[]{:S(2)}, u32[]{:S(2)}) async-start(bf16[16,8,896]{2,1,0:T(8,128)(2,1)} %shard_map.125), calls=%async_computation.1 | async-start | bytes 458752 | tf_op jit(solution)/shard_map/all_to_all | solution.py:409
  107.0 11.0 %collective-permute-done.11.got = bf16[3,160,384]{2,1,0:T(8,128)(2,1)S(1)} collective-permute-done((bf16[3,160,384]{2,1,0:T(8,128)(2,1)S(1)}, bf16[3,160,384]{2,1,0:T(8,128)(2,1)S(1)}, u32[]{:S(2)}, u32[]{:S(2)}) %collective-permute-start.11) | collective-permute-done | bytes 368672 | tf_op jit(solution)/shard_map/ppermute | solution.py:405
  119.7 9.7 %all-to-all-start.2 = ((bf16[32,32,640]{2,1,0:T(8,128)(2,1)}), bf16[32,32,640]{2,1,0:T(8,128)(2,1)S(1)}, u32[]{:S(2)}, u32[]{:S(2)}) async-start(bf16[32,32,640]{2,1,0:T(8,128)(2,1)} %shard_map.126), calls=%async_computation.2 | async-start | bytes 2621440 | tf_op jit(solution)/shard_map/all_to_all | solution.py:437
  135.4 27.8 %all-to-all-done.2.received = bf16[32,32,640]{2,1,0:T(8,128)(2,1)S(1)} async-done(((bf16[32,32,640]{2,1,0:T(8,128)(2,1)}), bf16[32,32,640]{2,1,0:T(8,128)(2,1)S(1)}, u32[]{:S(2)}, u32[]{:S(2)}) %all-to-all-start.2) | async-done | bytes 1310752 | tf_op jit(solution)/shard_map/all_to_all | solution.py:437
  165.4 28.2 %all_to_all.30.parts = bf16[4,256,384]{2,1,0:T(8,128)(2,1)S(1)} all-to-all(bf16[4,256,384]{2,1,0:T(8,128)(2,1)S(1)} %shard_map.129), channel_id=1, replica_groups=mesh['yh'=4,'yl'=2,'xl'=2,'z'=8,'xh'=2,'core'=2] {'yh'}, dimensions={0} | all-to-all | bytes 1572864 | tf_op jit(solution)/shard_map/all_to_all | solution.py:440
  193.9 26.0 %all_to_all.31.hidden = bf16[8,128,384]{2,1,0:T(8,128)(2,1)S(1)} all-to-all(bf16[8,128,384]{2,1,0:T(8,128)(2,1)S(1)} %shard_map.130), channel_id=1, replica_groups=mesh['yh'=4,'yl'=2,'xl'=2,'z'=8,'xh'=2,'core'=2] {'yh','yl'}, dimensions={0} | all-to-all | bytes 1572864 | tf_op jit(solution)/shard_map/all_to_all | solution.py:442
  222.3 5.9 %all-to-all-start.5 = ((bf16[32,80,128]{2,1,0:T(8,128)(2,1)}), bf16[32,80,128]{2,1,0:T(8,128)(2,1)S(1)}, u32[]{:S(2)}, u32[]{:S(2)}) async-start(bf16[32,80,128]{2,1,0:T(8,128)(2,1)} %shard_map.131), calls=%async_computation.5 | async-start | bytes 1310720 | tf_op jit(solution)/shard_map/all_to_all | solution.py:446
  229.1 19.6 %all-to-all-done.5.returned = bf16[32,80,128]{2,1,0:T(8,128)(2,1)S(1)} async-done(((bf16[32,80,128]{2,1,0:T(8,128)(2,1)}), bf16[32,80,128]{2,1,0:T(8,128)(2,1)S(1)}, u32[]{:S(2)}, u32[]{:S(2)}) %all-to-all-start.5) | async-done | bytes 655392 | tf_op jit(solution)/shard_map/all_to_all | solution.py:446
  249.3 2.8 %collective-permute-start.12 = (bf16[128,160]{1,0:T(8,128)(2,1)S(1)}, bf16[128,160]{1,0:T(8,128)(2,1)S(1)}, u32[]{:S(2)}, u32[]{:S(2)}) collective-permute-start(bf16[128,160]{1,0:T(8,128)(2,1)S(1)} %get-tuple-element.82), channel_id=1, source_target_pairs={{0,32},{32,0},{1,33},{33,1},{2,34},{34,2},{3,35},{35,3},{4,36},{36... | collective-permute-start | bytes 122888 | tf_op jit(solution)/shard_map/ppermute | solution.py:450
  252.1 3.4 %collective-permute-done.12 = bf16[128,160]{1,0:T(8,128)(2,1)S(1)} collective-permute-done((bf16[128,160]{1,0:T(8,128)(2,1)S(1)}, bf16[128,160]{1,0:T(8,128)(2,1)S(1)}, u32[]{:S(2)}, u32[]{:S(2)}) %collective-permute-start.12) | collective-permute-done | bytes 40992 | tf_op jit(solution)/shard_map/ppermute | solution.py:450
  (119 shorter events, 36.9 us)
Async XLA Ops:
  0.0 24.6 %copy-start.20 = (s32[256]{0:T(256)S(1)}, s32[256]{0:T(256)}, u32[]{:S(2)}) copy-start(s32[256]{0:T(256)} %param.14) | copy-start | bytes 3076
  1.7 11.2 %collective-permute-start = (bf16[592,128]{1,0:T(8,128)(2,1)S(1)}, bf16[592,128]{1,0:T(8,128)(2,1)S(1)}, u32[]{:S(2)}, u32[]{:S(2)}) collective-permute-start(bf16[592,128]{1,0:T(8,128)(2,1)S(1)} %constant_dynamic-slice_fusion), channel_id=1, source_target_pairs={{0,64},{2,130},{64,128},{66,194},{128,192},{130,258},{192,256},{19... | collective-permute-start | bytes 454664 | tf_op jit(solution)/shard_map/ppermute | solution.py:321
  6.4 14.7 %collective-permute-start.1 = (bf16[592,128]{1,0:T(8,128)(2,1)S(1)}, bf16[592,128]{1,0:T(8,128)(2,1)S(1)}, u32[]{:S(2)}, u32[]{:S(2)}) collective-permute-start(bf16[592,128]{1,0:T(8,128)(2,1)S(1)} %constant_dynamic-slice_fusion), channel_id=1, source_target_pairs={{0,192},{2,258},{64,256},{66,322},{128,320},{130,386},{192,384},{1... | collective-permute-start | bytes 454664 | tf_op jit(solution)/shard_map/ppermute | solution.py:321
  21.8 13.5 %collective-permute-start.2 = (bf16[2,592,128]{2,1,0:T(8,128)(2,1)S(1)}, bf16[2,592,128]{2,1,0:T(8,128)(2,1)S(1)}, u32[]{:S(2)}, u32[]{:S(2)}) collective-permute-start(bf16[2,592,128]{2,1,0:T(8,128)(2,1)S(1)} %get-tuple-element.46.p0), channel_id=1, source_target_pairs={{0,2},{2,0},{1,3},{3,1},{4,6},{6,4},{5,7},{7,5},{8,10},{10,8},{9,1... | collective-permute-start | bytes 909320 | tf_op jit(solution)/shard_map/ppermute | solution.py:330
  25.5 13.6 %collective-permute-start.3 = (bf16[2,592,128]{2,1,0:T(8,128)(2,1)}, bf16[2,592,128]{2,1,0:T(8,128)(2,1)S(1)}, u32[]{:S(2)}, u32[]{:S(2)}) collective-permute-start(bf16[2,592,128]{2,1,0:T(8,128)(2,1)} %get-tuple-element.83), channel_id=1, source_target_pairs={{0,32},{32,0},{1,33},{33,1},{2,34},{34,2},{3,35},{35,3},{4,36},{36... | collective-permute-start | bytes 909320 | tf_op jit(solution)/shard_map/ppermute | solution.py:331
  29.2 11.3 %collective-permute-start.4 = (bf16[2,592,128]{2,1,0:T(8,128)(2,1)}, bf16[2,592,128]{2,1,0:T(8,128)(2,1)S(1)}, u32[]{:S(2)}, u32[]{:S(2)}) collective-permute-start(bf16[2,592,128]{2,1,0:T(8,128)(2,1)} %get-tuple-element.83), channel_id=1, source_target_pairs={{0,34},{2,32},{32,2},{34,0},{1,35},{3,33},{33,3},{35,1},{4,38},{6,... | collective-permute-start | bytes 909320 | tf_op jit(solution)/shard_map/ppermute | solution.py:332
  35.3 5.1 %collective-permute-start.5 = (bf16[2,592,128]{2,1,0:T(8,128)(2,1)S(1)}, bf16[2,592,128]{2,1,0:T(8,128)(2,1)S(1)}, u32[]{:S(2)}, u32[]{:S(2)}) collective-permute-start(bf16[2,592,128]{2,1,0:T(8,128)(2,1)S(1)} %get-tuple-element.46.p0), channel_id=1, source_target_pairs={{0,1},{1,0},{2,3},{3,2},{4,5},{5,4},{6,7},{7,6},{8,9},{9,8},{10,11... | collective-permute-start | bytes 909320 | tf_op jit(solution)/shard_map/ppermute | solution.py:372
  40.5 4.7 %collective-permute-start.6 = (bf16[6,592,128]{2,1,0:T(8,128)(2,1)S(1)}, bf16[6,592,128]{2,1,0:T(8,128)(2,1)S(1)}, u32[]{:S(2)}, u32[]{:S(2)}) collective-permute-start(bf16[6,592,128]{2,1,0:T(8,128)(2,1)S(1)} %shard_map.121), channel_id=1, source_target_pairs={{0,1},{1,0},{2,3},{3,2},{4,5},{5,4},{6,7},{7,6},{8,9},{9,8},{10,11... | collective-permute-start | bytes 2727944 | tf_op jit(solution)/shard_map/ppermute | solution.py:381
  49.0 4.1 %collective-permute-start.7 = (bf16[128,2560]{1,0:T(8,128)(2,1)S(1)}, bf16[128,2560]{1,0:T(8,128)(2,1)S(1)}, u32[]{:S(2)}, u32[]{:S(2)}) collective-permute-start(bf16[128,2560]{1,0:T(8,128)(2,1)S(1)} %get-tuple-element.59), channel_id=1, source_target_pairs={{0,1},{1,0},{2,3},{3,2},{4,5},{5,4},{6,7},{7,6},{8,9},{9,8},{10,11... | collective-permute-start | bytes 1966088 | tf_op jit(solution)/shard_map/ppermute | solution.py:392
  54.1 40.8 %copy-start.18 = (bf16[8,2560]{1,0:T(8,128)(2,1)S(1)}, bf16[8,2560]{1,0:T(8,128)(2,1)}, u32[]{:S(2)}) copy-start(bf16[8,2560]{1,0:T(8,128)(2,1)} %residual.1) | copy-start | bytes 122884
  54.2 50.3 %copy-start.22 = (bf16[3,160,384]{2,1,0:T(8,128)(2,1)S(1)}, bf16[3,160,384]{2,1,0:T(8,128)(2,1)}, u32[]{:S(2)}) copy-start(bf16[3,160,384]{2,1,0:T(8,128)(2,1)} %copy-done.21) | copy-start | bytes 1105924
  54.2 40.7 %all-to-all-start = ((bf16[16,8,2560]{2,1,0:T(8,128)(2,1)}), bf16[16,8,2560]{2,1,0:T(8,128)(2,1)S(1)}, u32[]{:S(2)}, u32[]{:S(2)}) async-start(bf16[16,8,2560]{2,1,0:T(8,128)(2,1)} %shard_map.124), calls=%async_computation | async-start | bytes 1310720 | tf_op jit(solution)/shard_map/all_to_all | solution.py:403
  67.6 18.4 %collective-permute-start.10 = (bf16[3,160,384]{2,1,0:T(8,128)(2,1)}, bf16[3,160,384]{2,1,0:T(8,128)(2,1)S(1)}, u32[]{:S(2)}, u32[]{:S(2)}) collective-permute-start(bf16[3,160,384]{2,1,0:T(8,128)(2,1)} %get-tuple-element.68), channel_id=1, source_target_pairs={{0,96},{32,64},{64,32},{96,0},{1,97},{33,65},{65,33},{97,1},{2,98}... | collective-permute-start | bytes 1105928 | tf_op jit(solution)/shard_map/ppermute | solution.py:400
  71.6 23.3 %collective-permute-start.8 = (bf16[3,160,384]{2,1,0:T(8,128)(2,1)S(1)}, bf16[3,160,384]{2,1,0:T(8,128)(2,1)S(1)}, u32[]{:S(2)}, u32[]{:S(2)}) collective-permute-start(bf16[3,160,384]{2,1,0:T(8,128)(2,1)S(1)} %copy-done.26), channel_id=1, source_target_pairs={{0,32},{32,0},{1,33},{33,1},{2,34},{34,2},{3,35},{35,3},{4,36},{36... | collective-permute-start | bytes 1105928 | tf_op jit(solution)/shard_map/ppermute | solution.py:398
  75.0 19.9 %collective-permute-start.9 = (bf16[3,160,384]{2,1,0:T(8,128)(2,1)S(1)}, bf16[3,160,384]{2,1,0:T(8,128)(2,1)S(1)}, u32[]{:S(2)}, u32[]{:S(2)}) collective-permute-start(bf16[3,160,384]{2,1,0:T(8,128)(2,1)S(1)} %copy-done.24), channel_id=1, source_target_pairs={{0,64},{64,0},{1,65},{65,1},{2,66},{66,2},{3,67},{67,3},{4,68},{68... | collective-permute-start | bytes 1105928 | tf_op jit(solution)/shard_map/ppermute | solution.py:399
  86.1 33.6 %copy-start.8 = (bf16[3,160,384]{2,1,0:T(8,128)(2,1)}, bf16[3,160,384]{2,1,0:T(8,128)(2,1)S(1)}, u32[]{:S(2)}) copy-start(bf16[3,160,384]{2,1,0:T(8,128)(2,1)S(1)} %collective-permute-done.10.from_d) | copy-start | bytes 1105924
  94.9 24.8 %copy-start.10 = (bf16[3,160,384]{2,1,0:T(8,128)(2,1)}, bf16[3,160,384]{2,1,0:T(8,128)(2,1)S(1)}, u32[]{:S(2)}) copy-start(bf16[3,160,384]{2,1,0:T(8,128)(2,1)S(1)} %collective-permute-done.8.from_x) | copy-start | bytes 1105924
  94.9 24.8 %copy-start.12 = (bf16[3,160,384]{2,1,0:T(8,128)(2,1)}, bf16[3,160,384]{2,1,0:T(8,128)(2,1)S(1)}, u32[]{:S(2)}) copy-start(bf16[3,160,384]{2,1,0:T(8,128)(2,1)S(1)} %collective-permute-done.9.from_y) | copy-start | bytes 1105924
  95.9 22.1 %all-to-all-start.1 = ((bf16[16,8,896]{2,1,0:T(8,128)(2,1)}), bf16[16,8,896]{2,1,0:T(8,128)(2,1)S(1)}, u32[]{:S(2)}, u32[]{:S(2)}) async-start(bf16[16,8,896]{2,1,0:T(8,128)(2,1)} %shard_map.125), calls=%async_computation.1 | async-start | bytes 458752 | tf_op jit(solution)/shard_map/all_to_all | solution.py:409
  104.4 13.6 %collective-permute-start.11 = (bf16[3,160,384]{2,1,0:T(8,128)(2,1)S(1)}, bf16[3,160,384]{2,1,0:T(8,128)(2,1)S(1)}, u32[]{:S(2)}, u32[]{:S(2)}) collective-permute-start(bf16[3,160,384]{2,1,0:T(8,128)(2,1)S(1)} %copy-done.22), channel_id=1, source_target_pairs={{0,32},{32,0},{1,33},{33,1},{2,34},{34,2},{3,35},{35,3},{4,36},{36... | collective-permute-start | bytes 1105928 | tf_op jit(solution)/shard_map/ppermute | solution.py:405
  119.7 43.4 %all-to-all-start.2 = ((bf16[32,32,640]{2,1,0:T(8,128)(2,1)}), bf16[32,32,640]{2,1,0:T(8,128)(2,1)S(1)}, u32[]{:S(2)}, u32[]{:S(2)}) async-start(bf16[32,32,640]{2,1,0:T(8,128)(2,1)} %shard_map.126), calls=%async_computation.2 | async-start | bytes 2621440 | tf_op jit(solution)/shard_map/all_to_all | solution.py:437
  193.6 26.3 %copy-start.1 = (bf16[384,1152]{1,0:T(8,128)(2,1)S(1)}, bf16[384,1152]{1,0:T(8,128)(2,1)}, u32[]{:S(2)}) copy-start(bf16[384,1152]{1,0:T(8,128)(2,1)} %copy-done) | copy-start | bytes 2654212
  222.3 26.5 %all-to-all-start.5 = ((bf16[32,80,128]{2,1,0:T(8,128)(2,1)}), bf16[32,80,128]{2,1,0:T(8,128)(2,1)S(1)}, u32[]{:S(2)}, u32[]{:S(2)}) async-start(bf16[32,80,128]{2,1,0:T(8,128)(2,1)} %shard_map.131), calls=%async_computation.5 | async-start | bytes 1310720 | tf_op jit(solution)/shard_map/all_to_all | solution.py:446
  249.3 6.2 %collective-permute-start.12 = (bf16[128,160]{1,0:T(8,128)(2,1)S(1)}, bf16[128,160]{1,0:T(8,128)(2,1)S(1)}, u32[]{:S(2)}, u32[]{:S(2)}) collective-permute-start(bf16[128,160]{1,0:T(8,128)(2,1)S(1)} %get-tuple-element.82), channel_id=1, source_target_pairs={{0,32},{32,0},{1,33},{33,1},{2,34},{34,2},{3,35},{35,3},{4,36},{36... | collective-permute-start | bytes 122888 | tf_op jit(solution)/shard_map/ppermute | solution.py:450
  (24 other events, 185.0 us)

commit v10 on v8

--- a/solution.py
+++ b/solution.py
@@ -40,14 +40,15 @@
 
 def attend_chunks(rows, chunks, biases, scores, old):
     scale = QKDIM ** (-0.5)
-    peak = jnp.full((256, 128), -FAR, f32) if old is None else old[0]
+    count = rows.shape[0]
+    peak = jnp.full((count, 128), -FAR, f32) if old is None else old[0]
     for n, (chunk, bias) in enumerate(zip(chunks, biases)):
         part = bias(jnp.dot(rows, keys_of(chunk), preferred_element_type=f32) * scale)
         scores[:, n * 256 : (n + 1) * 256] = part
         peak = jnp.maximum(peak, jnp.maximum(part[:, :128], part[:, 128:]))
     peak = jnp.max(peak, axis=1, keepdims=True)
     if old is None:
-        sums, mixed = jnp.zeros((256, 128), f32), jnp.zeros((256, LATENT), f32)
+        sums, mixed = jnp.zeros((count, 128), f32), jnp.zeros((count, LATENT), f32)
     else:
         factor = jnp.exp(old[0][:, :1] - peak)
         sums, mixed = old[1] * factor, old[2] * factor
@@ -55,12 +56,12 @@
         terms = jnp.exp(scores[:, n * 256 : (n + 1) * 256] - peak)
         sums = sums + terms[:, :128] + terms[:, 128:]
         mixed = mixed + nt_dot(terms.astype(bf16), keys_of(chunk)[:LATENT])
-    return jnp.broadcast_to(peak, (256, 128)), sums, mixed
+    return jnp.broadcast_to(peak, (count, 128)), sums, mixed
 
 
 def valid_bias(info, piece):
     def bias(part):
-        lane = lax.broadcasted_iota(i32, (256, 256), 1)
+        lane = lax.broadcasted_iota(i32, (1, 256), 1)
         first = jnp.where(info[2 * piece] >= 0, 0.0, -FAR)
         second = jnp.where(info[2 * piece + 1] >= 0, 0.0, -FAR)
         return part + jnp.where(lane < 128, first, second)
@@ -69,45 +70,40 @@
 
 
 def causal_bias(part):
-    lane = lax.broadcasted_iota(i32, (256, 256), 1)
-    row = lax.broadcasted_iota(i32, (256, 256), 0)
-    token = (row % 128) // 8 * 16 + row // 128 * 8 + row % 8
+    lane = lax.broadcasted_iota(i32, part.shape, 1)
+    row = lax.broadcasted_iota(i32, part.shape, 0)
+    token = (row % 128) // 8 * 16 + row // 128 % 2 * 8 + row % 8
     return jnp.where(lane <= token, part, -FAR)
 
 
-def first_attention_kernel(info, query, own, p0, peak, sums, mixed, scores):
-    @pl.loop(0, 2)
-    def _(head):
-        state = attend_chunks(
-            query[head], [own, p0], [causal_bias, valid_bias(info, 0)], scores, None
-        )
-        peak[head], sums[head], mixed[head] = state
+def first_attention_kernel(query, own, peak, sums, mixed, scores):
+    peak[...], sums[...], mixed[...] = attend_chunks(
+        query[...], [own], [causal_bias], scores, None
+    )
 
 
 def second_attention_kernel(
-    info, query, p1, p2, p3, o0, old_peak, old_sums, old_mixed, peak, sums, mixed, scores
+    info, query, p0, p1, p2, p3, o0, old_peak, old_sums, old_mixed, peak, sums, mixed, scores
 ):
-    @pl.loop(0, 2)
-    def _(head):
-        old = old_peak[head], old_sums[head], old_mixed[head]
-        biases = [valid_bias(info, n) for n in (1, 2, 3, 0)]
-        state = attend_chunks(query[head], [p1, p2, p3, o0], biases, scores, old)
-        peak[head], sums[head], mixed[head] = state
+    old = old_peak[...], old_sums[...], old_mixed[...]
+    biases = [valid_bias(info, n) for n in (0, 1, 2, 3, 0)]
+    peak[...], sums[...], mixed[...] = attend_chunks(
+        query[...], [p0, p1, p2, p3, o0], biases, scores, old
+    )
 
 
 def last_attention_kernel(
     info, query, others, old_peak, old_sums, old_mixed, value_up, out_proj, send, keep, scores, values
 ):
     core = info[8]
-
-    @pl.loop(0, 2)
-    def _(head):
-        old = old_peak[head], old_sums[head], old_mixed[head]
-        chunks = [others.at[2 * n : 2 * n + 2] for n in range(3)]
-        biases = [valid_bias(info, n) for n in (1, 2, 3)]
-        _, sums, mixed = attend_chunks(query[head], chunks, biases, scores, old)
-        mixed = (mixed / jnp.sum(sums, axis=1, keepdims=True)).astype(bf16)
-        values[head] = jnp.dot(mixed, value_up[head], preferred_element_type=f32).astype(bf16)
+    old = old_peak[...], old_sums[...], old_mixed[...]
+    chunks = [others.at[2 * n : 2 * n + 2] for n in range(3)]
+    biases = [valid_bias(info, n) for n in (1, 2, 3)]
+    _, sums, mixed = attend_chunks(query[...], chunks, biases, scores, old)
+    mixed = (mixed / jnp.sum(sums, axis=1, keepdims=True)).astype(bf16)
+    for head in range(2):
+        rows = mixed[head * 256 : (head + 1) * 256]
+        values[head] = jnp.dot(rows, value_up[head], preferred_element_type=f32).astype(bf16)
 
     def project(which, out):
         start = pl.multiple_of(which * 128, 128)
@@ -245,7 +241,7 @@
             store_packed(out, r // SLOTS + n, total[n * SLOTS : (n + 1) * SLOTS])
 
 
-def combine_kernel(weighting, returned, keep, send):
+def combine_kernel(weighting, returned, order, stream, keep, send):
     width = keep.shape[1]
     rows = jnp.concatenate([load_packed(returned, n) for n in range(returned.shape[0])], axis=0)
     top = weighting[...].astype(bf16)
@@ -254,7 +250,8 @@
         rest, rows, preferred_element_type=f32
     )
     tail = mixture[:, 256:320] + mixture[:, 320:384]
-    keep[...] = mixture[:, :width]
+    kept = jnp.dot(order[...], stream[:, 2 * width : 3 * width], preferred_element_type=f32)
+    keep[...] = kept + mixture[:, :width]
     send[...] = jnp.concatenate([mixture[:, width:256], tail], axis=1).astype(bf16)
 
 
@@ -315,17 +312,7 @@
         ]
         return lax.ppermute(mine, ("y", "xh"), pairs)
 
-    column = jnp.stack([along_y(1, 2), along_y(3, 4)])
-    to_other = jnp.where(
-        (xl == 0) & (xh == 1), jnp.stack([mine, column[0]]), column
-    )
-    diagonal = [(0, 3), (1, 2), (2, 1), (3, 0)]
-    pieces = [
-        column,
-        lax.ppermute(column, "xh", SWAP),
-        lax.ppermute(to_other, "xl", SWAP),
-        lax.ppermute(to_other, ("xl", "xh"), diagonal),
-    ]
+    near, far = along_y(1, 2), along_y(3, 4)
 
     def blocks_of(x, h):
         return [2 * (y - 1 - h) + x, 2 * (y - 3 - h) + x]
@@ -353,39 +340,55 @@
         axis=2,
     )
     query_rows = query_rows.reshape(16, 2, 8, local_heads, KEYW).transpose(3, 1, 0, 2, 4)
-    query_rows = query_rows.reshape(local_heads, block_len, KEYW)
+    query_rows = query_rows.reshape(local_heads * block_len, KEYW)
+    rows_all = local_heads * block_len
     state_out = [
-        sds((2, 256, 128), f32),
-        sds((2, 256, 128), f32),
-        sds((2, 256, LATENT), f32),
+        sds((rows_all, 128), f32),
+        sds((rows_all, 128), f32),
+        sds((rows_all, LATENT), f32),
     ]
     state = call(
-        first_attention_kernel, state_out, [pltpu.VMEM((256, 2 * 256), f32)], True, 4
-    )(info, query_rows, keys_own, column)
-    pieces[1], column_late, peak = lax.optimization_barrier((pieces[1], column, state[0]))
+        first_attention_kernel, state_out, [pltpu.VMEM((rows_all, 256), f32)], count=2
+    )(query_rows, keys_own)
+
+    in_out = sds((3, width_out, 2 * ff_half), bf16)
+    down_out = sds((3, width_out, ff_half), bf16)
+    in_send, in_keep, down_send, down_keep = call(
+        split_weights_kernel, [in_out, in_out, down_out, down_out], (), True, 4
+    )(info, expert_gate, expert_up, jnp.transpose(expert_down, (0, 2, 1)))
+    near, far, peak, in_send = lax.optimization_barrier((near, far, state[0], in_send))
     state = [peak] + list(state[1:])
+
+    column = jnp.stack([near, far])
+    to_other = jnp.where(
+        (xl == 0) & (xh == 1), jnp.stack([mine, column[0]]), column
+    )
+    diagonal = [(0, 3), (1, 2), (2, 1), (3, 0)]
+    pieces = [
+        column,
+        lax.ppermute(column, "xh", SWAP),
+        lax.ppermute(to_other, "xl", SWAP),
+        lax.ppermute(to_other, ("xl", "xh"), diagonal),
+    ]
+
+    pieces[1], column_late = lax.optimization_barrier((pieces[1], column))
     first_other = lax.ppermute(column_late, "core", SWAP)
     *pieces, first_other = lax.optimization_barrier((*pieces, first_other))
     three = call(gather_kernel, [sds((6, KEYW, half), bf16)], count=3)(*pieces[1:])
     others = lax.ppermute(three, "core", SWAP)
     state = call(
-        second_attention_kernel, state_out, [pltpu.VMEM((256, 4 * 256), f32)], True, 9
-    )(info, query_rows, pieces[1], pieces[2], pieces[3], first_other, *state)
+        second_attention_kernel, state_out, [pltpu.VMEM((rows_all, 5 * 256), f32)], True, 10
+    )(info, query_rows, *pieces, first_other, *state)
     send, keep = call(
         last_attention_kernel,
         [sds((half, width_model), bf16), sds((half, width_model), f32)],
-        [pltpu.VMEM((256, 3 * 256), f32), pltpu.VMEM((2, 256, VDIM), bf16)],
+        [pltpu.VMEM((rows_all, 3 * 256), f32), pltpu.VMEM((2, 256, VDIM), bf16)],
         True,
         8,
     )(info, query_rows, others, *state, value_up, out_proj)
     got = lax.ppermute(send, "core", SWAP)
     pair_sum = call(add_kernel, [sds((16, 8, width_model), bf16)], count=2)(keep, got)
 
-    in_out = sds((3, width_out, 2 * ff_half), bf16)
-    down_out = sds((3, width_out, ff_half), bf16)
-    in_send, in_keep, down_send, down_keep = call(
-        split_weights_kernel, [in_out, in_out, down_out, down_out], (), True, 4
-    )(info, expert_gate, expert_up, jnp.transpose(expert_down, (0, 2, 1)))
     pair_sum, in_send = lax.optimization_barrier((pair_sum, in_send))
     in_got = lax.ppermute(in_send, "xl", SWAP)
 
@@ -394,8 +397,9 @@
         spread, residual, norm_gain[None, :]
     )
     split = lax.all_to_all(packed, CTX, split_axis=0, concat_axis=0, tiled=True)
-    split, in_got, down_send = lax.optimization_barrier((split, in_got, down_send))
+    in_got, down_send = lax.optimization_barrier((in_got, down_send))
     down_got = lax.ppermute(down_send, "xl", SWAP)
+    split, in_got = lax.optimization_barrier((split, in_got))
     split = split.reshape(128, 512)
     w_in = call(join_in_kernel, [sds((3 * 384, 2 * ff_half), bf16)], count=2)(in_keep, in_got)
     w_down = call(join_down_kernel, [sds((384, 3 * ff_half), bf16)], count=2)(down_keep, down_got)
@@ -435,15 +439,10 @@
     )
     returned = lax.all_to_all(expert_out, EXP, split_axis=0, concat_axis=0, tiled=True)
     mix_keep, mix_send = call(
-        combine_kernel, [sds((128, width_out), f32), sds((128, width_out), bf16)], count=2
-    )(weighting, returned)
+        combine_kernel, [sds((128, width_out), f32), sds((128, width_out), bf16)], count=4
+    )(weighting, returned, back_order.astype(bf16), split)
     mix_got = lax.ppermute(mix_send, "xl", SWAP)
-    stream_rb = jnp.dot(
-        back_order.astype(bf16),
-        split[:, width_pair : width_pair + width_out],
-        preferred_element_type=f32,
-    )
-    result = (stream_rb + mix_keep + mix_got.astype(f32)).astype(bf16)
+    result = (mix_keep + mix_got.astype(f32)).astype(bf16)
     return result.reshape(8, 16, width_out)
 
 

time: 241 us -> 245 us (1.017)
  local copies, waits for them, and re-layouts: 3.88 us -> 9.73 us
  waiting for transfers between devices: 75.7 us -> 72 us
    ppermute x2, waiting for transfers between devices: 8.73 us -> 1.22 us  [along_y(): return lax.ppermute(mine, ('y', 'xh'), pairs)]
    unnamed x36 -> x52, local copies, waits for them, and re-layouts: 3.2 us -> 8.38 us
    ppermute x1, waiting for transfers between devices: 0.89 us -> 3.67 us  [on_device(): lax.ppermute(column, 'xh', SWAP)]
  transfers between devices with their start and end apart: 15 -> 15, of which waited for: 12 -> 11; matrix products, arithmetic and copies ran while one was open for 1% -> 2% of each run, Pallas kernels for 3% -> 3%
where the time goes in v10:
time: 245 us; the launch traced here: 243 us
  starting transfers between devices  72.2 us (29%)
  waiting for transfers between devices  72 us (29%)
  blocking collectives  67 us (27%)
  Pallas kernels  17.9 us (7%)
  local copies, waits for them, and re-layouts  9.73 us (4%)
  other arithmetic  3.27 us (1%)
    all_to_all x1, blocking collectives, on_device(): lax.all_to_all(pre.reshape(8, 128, 2 * ff_half), 'y', split_axis=0, conca...  42.6 us
    all_to_all x1, blocking collectives, on_device(): lax.all_to_all(hidden, 'y', split_axis=0, concat_axis=0, tiled=True)  24.4 us
    all_to_all x1, waiting for transfers between devices, on_device(): lax.all_to_all(expert_out, EXP, split_axis=0, concat_axis=0, tiled=True)  19.6 us
    all_to_all x1, waiting for transfers between devices, on_device(): lax.all_to_all(pair_sum, ('z', 'xh'), split_axis=0, concat_axis=0, tiled=...  16.4 us
    ppermute x1, waiting for transfers between devices, on_device(): down_got = lax.ppermute(down_send, 'xl', SWAP)  15.7 us
    all_to_all x1, starting transfers between devices, on_device(): lax.all_to_all(pair_sum, ('z', 'xh'), split_axis=0, concat_axis=0, tiled=...  13.3 us
    ppermute x2, starting transfers between devices, along_y(): return lax.ppermute(mine, ('y', 'xh'), pairs)  10.4 us
    all_to_all x1, starting transfers between devices, on_device(): split = lax.all_to_all(packed, CTX, split_axis=0, concat_axis=0, tiled=True)  8.45 us
  transfers between devices with their start and end apart: 15, of which 11 were waited for; matrix products, arithmetic and copies ran while one was open for 2% of the time, Pallas kernels for 3%

profile of v10, /device:TPU:6, one launch (start us, length us, event | category | flops | bytes accessed | tf_op | source)
XLA Modules:
  0.0 242.9 jit_solution(15854717789682415097)
XLA Ops:
  2.4 4.5 %collective-permute-start = (bf16[592,128]{1,0:T(8,128)(2,1)}, bf16[592,128]{1,0:T(8,128)(2,1)}, u32[]{:S(2)}, u32[]{:S(2)}) collective-permute-start(bf16[592,128]{1,0:T(8,128)(2,1)} %constant_dynamic-slice_fusion), channel_id=1, source_target_pairs={{0,64},{2,130},{64,128},{66,194},{128,192},{130,258},{192,256},{19... | collective-permute-start | bytes 454664 | tf_op jit(solution)/shard_map/ppermute | solution.py:313
  6.8 5.9 %collective-permute-start.1 = (bf16[592,128]{1,0:T(8,128)(2,1)}, bf16[592,128]{1,0:T(8,128)(2,1)}, u32[]{:S(2)}, u32[]{:S(2)}) collective-permute-start(bf16[592,128]{1,0:T(8,128)(2,1)} %constant_dynamic-slice_fusion), channel_id=1, source_target_pairs={{0,192},{2,258},{64,256},{66,322},{128,320},{130,386},{192,384},{1... | collective-permute-start | bytes 454664 | tf_op jit(solution)/shard_map/ppermute | solution.py:313
  23.0 2.7 %collective-permute-start.2 = (bf16[2,592,128]{2,1,0:T(8,128)(2,1)S(1)}, bf16[2,592,128]{2,1,0:T(8,128)(2,1)S(1)}, u32[]{:S(2)}, u32[]{:S(2)}) collective-permute-start(bf16[2,592,128]{2,1,0:T(8,128)(2,1)S(1)} %get-tuple-element.48.p0), channel_id=1, source_target_pairs={{0,2},{2,0},{1,3},{3,1},{4,6},{6,4},{5,7},{7,5},{8,10},{10,8},{9,1... | collective-permute-start | bytes 909320 | tf_op jit(solution)/shard_map/ppermute | solution.py:369
  25.7 3.6 %collective-permute-start.3 = (bf16[2,592,128]{2,1,0:T(8,128)(2,1)S(1)}, bf16[2,592,128]{2,1,0:T(8,128)(2,1)S(1)}, u32[]{:S(2)}, u32[]{:S(2)}) collective-permute-start(bf16[2,592,128]{2,1,0:T(8,128)(2,1)S(1)} %get-tuple-element.73), channel_id=1, source_target_pairs={{0,32},{32,0},{1,33},{33,1},{2,34},{34,2},{3,35},{35,3},{4,36},{36... | collective-permute-start | bytes 909320 | tf_op jit(solution)/shard_map/ppermute | solution.py:370
  29.3 3.5 %collective-permute-start.4 = (bf16[2,592,128]{2,1,0:T(8,128)(2,1)S(1)}, bf16[2,592,128]{2,1,0:T(8,128)(2,1)S(1)}, u32[]{:S(2)}, u32[]{:S(2)}) collective-permute-start(bf16[2,592,128]{2,1,0:T(8,128)(2,1)S(1)} %get-tuple-element.73), channel_id=1, source_target_pairs={{0,34},{2,32},{32,2},{34,0},{1,35},{3,33},{33,3},{35,1},{4,38},{6,... | collective-permute-start | bytes 909320 | tf_op jit(solution)/shard_map/ppermute | solution.py:371
  32.8 3.7 %collective-permute-done.2.p1 = bf16[2,592,128]{2,1,0:T(8,128)(2,1)S(1)} collective-permute-done((bf16[2,592,128]{2,1,0:T(8,128)(2,1)S(1)}, bf16[2,592,128]{2,1,0:T(8,128)(2,1)S(1)}, u32[]{:S(2)}, u32[]{:S(2)}) %collective-permute-start.2) | collective-permute-done | bytes 303136 | tf_op jit(solution)/shard_map/ppermute | solution.py:369
  39.0 2.4 collective-permute-done.4.p3
  43.4 4.0 %shard_map.122 = (f32[512,128]{1,0:T(8,128)S(1)}, f32[512,128]{1,0:T(8,128)S(1)}, f32[512,512]{1,0:T(8,128)S(1)}) custom-call(s32[10]{0:T(128)S(1)} %stack.58.info, bf16[512,592]{1,0:T(8,128)(2,1)S(1)} %bitcast.41, bf16[2,592,128]{2,1,0:T(8,128)(2,1)S(1)} %get-tuple-element.48.p0, bf16[2,592,128]{2,1,0:T(8,128)(2,1)S(1)} %collective-permute-done.2.p1, ...), custom_call_target="tpu_custom_call" | custom-call | tf_op jit(solution)/shard_map/pallas_call | solution.py:379
  47.4 3.3 %shard_map.123 = (bf16[128,2560]{1,0:T(8,128)(2,1)S(1)}, f32[128,2560]{1,0:T(8,128)S(1)}) custom-call(s32[10]{0:T(128)S(1)} %stack.58.info, bf16[512,592]{1,0:T(8,128)(2,1)S(1)} %bitcast.42, bf16[6,592,128]{2,1,0:T(8,128)(2,1)S(1)} %collective-permute-done.6.others, f32[512,128]{1,0:T(8,128)S(1)} %get-tuple-element.53.old_peak, ...), custom_call_target="tpu_custom_call" | custom-call | tf_op jit(solution)/shard_map/pallas_call | solution.py:382
  50.8 2.4 collective-permute-start.7
  55.9 13.3 %all-to-all-start = ((bf16[16,8,2560]{2,1,0:T(8,128)(2,1)}), bf16[16,8,2560]{2,1,0:T(8,128)(2,1)S(1)}, u32[]{:S(2)}, u32[]{:S(2)}) async-start(bf16[16,8,2560]{2,1,0:T(8,128)(2,1)} %shard_map.124), calls=%async_computation | async-start | bytes 1310720 | tf_op jit(solution)/shard_map/all_to_all | solution.py:395
  69.5 2.7 %collective-permute-start.8 = (bf16[3,160,768]{2,1,0:T(8,128)(2,1)S(1)}, bf16[3,160,768]{2,1,0:T(8,128)(2,1)S(1)}, u32[]{:S(2)}, u32[]{:S(2)}) collective-permute-start(bf16[3,160,768]{2,1,0:T(8,128)(2,1)S(1)} %copy-done.19), channel_id=1, source_target_pairs={{0,32},{32,0},{1,33},{33,1},{2,34},{34,2},{3,35},{35,3},{4,36},{36... | collective-permute-start | bytes 2211848 | tf_op jit(solution)/shard_map/ppermute | solution.py:393
  72.5 16.4 %all-to-all-done.spread = bf16[16,8,2560]{2,1,0:T(8,128)(2,1)S(1)} async-done(((bf16[16,8,2560]{2,1,0:T(8,128)(2,1)}), bf16[16,8,2560]{2,1,0:T(8,128)(2,1)S(1)}, u32[]{:S(2)}, u32[]{:S(2)}) %all-to-all-start) | async-done | bytes 655392 | tf_op jit(solution)/shard_map/all_to_all | solution.py:395
  89.9 8.4 %all-to-all-start.1 = ((bf16[16,8,512]{2,1,0:T(8,128)(2,1)}), bf16[16,8,512]{2,1,0:T(8,128)(2,1)S(1)}, u32[]{:S(2)}, u32[]{:S(2)}) async-start(bf16[16,8,512]{2,1,0:T(8,128)(2,1)} %shard_map.125), calls=%async_computation.1 | async-start | bytes 262144 | tf_op jit(solution)/shard_map/all_to_all | solution.py:399
  99.0 7.8 %all-to-all-done.1 = bf16[16,8,512]{2,1,0:T(8,128)(2,1)S(1)} async-done(((bf16[16,8,512]{2,1,0:T(8,128)(2,1)}), bf16[16,8,512]{2,1,0:T(8,128)(2,1)S(1)}, u32[]{:S(2)}, u32[]{:S(2)}) %all-to-all-start.1) | async-done | bytes 131104 | tf_op jit(solution)/shard_map/all_to_all | solution.py:399
  108.0 6.6 %all-to-all-start.2 = ((bf16[32,80,128]{2,1,0:T(8,128)(2,1)}), bf16[32,80,128]{2,1,0:T(8,128)(2,1)S(1)}, u32[]{:S(2)}, u32[]{:S(2)}) async-start(bf16[32,80,128]{2,1,0:T(8,128)(2,1)} %shard_map.126), calls=%async_computation.2 | async-start | bytes 1310720 | tf_op jit(solution)/shard_map/all_to_all | solution.py:429
  114.6 2.9 %collective-permute-start.9 = (bf16[3,160,384]{2,1,0:T(8,128)(2,1)S(1)}, bf16[3,160,384]{2,1,0:T(8,128)(2,1)S(1)}, u32[]{:S(2)}, u32[]{:S(2)}) collective-permute-start(bf16[3,160,384]{2,1,0:T(8,128)(2,1)S(1)} %copy-done.21), channel_id=1, source_target_pairs={{0,32},{32,0},{1,33},{33,1},{2,34},{34,2},{3,35},{35,3},{4,36},{36... | collective-permute-start | bytes 1105928 | tf_op jit(solution)/shard_map/ppermute | solution.py:401
  117.5 15.7 %collective-permute-done.9.got = bf16[3,160,384]{2,1,0:T(8,128)(2,1)S(1)} collective-permute-done((bf16[3,160,384]{2,1,0:T(8,128)(2,1)S(1)}, bf16[3,160,384]{2,1,0:T(8,128)(2,1)S(1)}, u32[]{:S(2)}, u32[]{:S(2)}) %collective-permute-start.9) | collective-permute-done | bytes 368672 | tf_op jit(solution)/shard_map/ppermute | solution.py:401
  137.4 42.6 %all_to_all.30.parts = bf16[8,128,768]{2,1,0:T(8,128)(2,1)S(1)} all-to-all(bf16[8,128,768]{2,1,0:T(8,128)(2,1)S(1)} %bitcast.43), channel_id=1, replica_groups=mesh['y'=8,'xl'=2,'z'=8,'xh'=2,'core'=2] {'y'}, dimensions={0} | all-to-all | bytes 3145728 | tf_op jit(solution)/shard_map/all_to_all | solution.py:432
  180.3 24.4 %all_to_all.31 = bf16[8,128,384]{2,1,0:T(8,128)(2,1)S(1)} all-to-all(bf16[8,128,384]{2,1,0:T(8,128)(2,1)S(1)} %shard_map.130), channel_id=1, replica_groups=mesh['y'=8,'xl'=2,'z'=8,'xh'=2,'core'=2] {'y'}, dimensions={0} | all-to-all | bytes 1572864 | tf_op jit(solution)/shard_map/all_to_all | solution.py:436
  204.7 2.4 shard_map.131
  207.1 7.9 %all-to-all-start.5 = ((bf16[32,80,128]{2,1,0:T(8,128)(2,1)}), bf16[32,80,128]{2,1,0:T(8,128)(2,1)S(1)}, u32[]{:S(2)}, u32[]{:S(2)}) async-start(bf16[32,80,128]{2,1,0:T(8,128)(2,1)} %shard_map.131), calls=%async_computation.5 | async-start | bytes 1310720 | tf_op jit(solution)/shard_map/all_to_all | solution.py:440
  215.9 19.6 %all-to-all-done.5.returned = bf16[32,80,128]{2,1,0:T(8,128)(2,1)S(1)} async-done(((bf16[32,80,128]{2,1,0:T(8,128)(2,1)}), bf16[32,80,128]{2,1,0:T(8,128)(2,1)S(1)}, u32[]{:S(2)}, u32[]{:S(2)}) %all-to-all-start.5) | async-done | bytes 655392 | tf_op jit(solution)/shard_map/all_to_all | solution.py:440
  236.1 3.9 %collective-permute-start.10 = (bf16[128,160]{1,0:T(8,128)(2,1)S(1)}, bf16[128,160]{1,0:T(8,128)(2,1)S(1)}, u32[]{:S(2)}, u32[]{:S(2)}) collective-permute-start(bf16[128,160]{1,0:T(8,128)(2,1)S(1)} %get-tuple-element.72), channel_id=1, source_target_pairs={{0,32},{32,0},{1,33},{33,1},{2,34},{34,2},{3,35},{35,3},{4,36},{36... | collective-permute-start | bytes 122888 | tf_op jit(solution)/shard_map/ppermute | solution.py:444
  (103 shorter events, 31.7 us)
Async XLA Ops:
  2.4 18.3 %collective-permute-start = (bf16[592,128]{1,0:T(8,128)(2,1)}, bf16[592,128]{1,0:T(8,128)(2,1)}, u32[]{:S(2)}, u32[]{:S(2)}) collective-permute-start(bf16[592,128]{1,0:T(8,128)(2,1)} %constant_dynamic-slice_fusion), channel_id=1, source_target_pairs={{0,64},{2,130},{64,128},{66,194},{128,192},{130,258},{192,256},{19... | collective-permute-start | bytes 454664 | tf_op jit(solution)/shard_map/ppermute | solution.py:313
  6.8 15.0 %collective-permute-start.1 = (bf16[592,128]{1,0:T(8,128)(2,1)}, bf16[592,128]{1,0:T(8,128)(2,1)}, u32[]{:S(2)}, u32[]{:S(2)}) collective-permute-start(bf16[592,128]{1,0:T(8,128)(2,1)} %constant_dynamic-slice_fusion), channel_id=1, source_target_pairs={{0,192},{2,258},{64,256},{66,322},{128,320},{130,386},{192,384},{1... | collective-permute-start | bytes 454664 | tf_op jit(solution)/shard_map/ppermute | solution.py:313
  20.6 20.8 %copy-start.4 = (bf16[3,160,768]{2,1,0:T(8,128)(2,1)}, bf16[3,160,768]{2,1,0:T(8,128)(2,1)S(1)}, u32[]{:S(2)}) copy-start(bf16[3,160,768]{2,1,0:T(8,128)(2,1)S(1)} %get-tuple-element.64.keep) | copy-start | bytes 2211844
  20.6 20.8 %copy-start.20 = (bf16[3,160,384]{2,1,0:T(8,128)(2,1)}, bf16[3,160,384]{2,1,0:T(8,128)(2,1)S(1)}, u32[]{:S(2)}) copy-start(bf16[3,160,384]{2,1,0:T(8,128)(2,1)S(1)} %get-tuple-element.67) | copy-start | bytes 1105924
  20.6 22.8 %copy-start.13 = (f32[512,128]{1,0:T(8,128)S(1)}, f32[512,128]{1,0:T(8,128)}, u32[]{:S(2)}) copy-start(f32[512,128]{1,0:T(8,128)} %copy-done.12) | copy-start | bytes 786436
  20.6 22.8 %copy-start.15 = (f32[512,128]{1,0:T(8,128)S(1)}, f32[512,128]{1,0:T(8,128)}, u32[]{:S(2)}) copy-start(f32[512,128]{1,0:T(8,128)} %copy-done.14) | copy-start | bytes 786436
  23.0 13.5 %collective-permute-start.2 = (bf16[2,592,128]{2,1,0:T(8,128)(2,1)S(1)}, bf16[2,592,128]{2,1,0:T(8,128)(2,1)S(1)}, u32[]{:S(2)}, u32[]{:S(2)}) collective-permute-start(bf16[2,592,128]{2,1,0:T(8,128)(2,1)S(1)} %get-tuple-element.48.p0), channel_id=1, source_target_pairs={{0,2},{2,0},{1,3},{3,1},{4,6},{6,4},{5,7},{7,5},{8,10},{10,8},{9,1... | collective-permute-start | bytes 909320 | tf_op jit(solution)/shard_map/ppermute | solution.py:369
  25.7 13.2 %collective-permute-start.3 = (bf16[2,592,128]{2,1,0:T(8,128)(2,1)S(1)}, bf16[2,592,128]{2,1,0:T(8,128)(2,1)S(1)}, u32[]{:S(2)}, u32[]{:S(2)}) collective-permute-start(bf16[2,592,128]{2,1,0:T(8,128)(2,1)S(1)} %get-tuple-element.73), channel_id=1, source_target_pairs={{0,32},{32,0},{1,33},{33,1},{2,34},{34,2},{3,35},{35,3},{4,36},{36... | collective-permute-start | bytes 909320 | tf_op jit(solution)/shard_map/ppermute | solution.py:370
  29.3 12.0 %collective-permute-start.4 = (bf16[2,592,128]{2,1,0:T(8,128)(2,1)S(1)}, bf16[2,592,128]{2,1,0:T(8,128)(2,1)S(1)}, u32[]{:S(2)}, u32[]{:S(2)}) collective-permute-start(bf16[2,592,128]{2,1,0:T(8,128)(2,1)S(1)} %get-tuple-element.73), channel_id=1, source_target_pairs={{0,34},{2,32},{32,2},{34,0},{1,35},{3,33},{33,3},{35,1},{4,38},{6,... | collective-permute-start | bytes 909320 | tf_op jit(solution)/shard_map/ppermute | solution.py:371
  36.5 4.9 %collective-permute-start.5 = (bf16[2,592,128]{2,1,0:T(8,128)(2,1)S(1)}, bf16[2,592,128]{2,1,0:T(8,128)(2,1)S(1)}, u32[]{:S(2)}, u32[]{:S(2)}) collective-permute-start(bf16[2,592,128]{2,1,0:T(8,128)(2,1)S(1)} %get-tuple-element.48.p0), channel_id=1, source_target_pairs={{0,1},{1,0},{2,3},{3,2},{4,5},{5,4},{6,7},{7,6},{8,9},{9,8},{10,11... | collective-permute-start | bytes 909320 | tf_op jit(solution)/shard_map/ppermute | solution.py:375
  41.4 6.0 %collective-permute-start.6 = (bf16[6,592,128]{2,1,0:T(8,128)(2,1)S(1)}, bf16[6,592,128]{2,1,0:T(8,128)(2,1)S(1)}, u32[]{:S(2)}, u32[]{:S(2)}) collective-permute-start(bf16[6,592,128]{2,1,0:T(8,128)(2,1)S(1)} %shard_map.121), channel_id=1, source_target_pairs={{0,1},{1,0},{2,3},{3,2},{4,5},{5,4},{6,7},{7,6},{8,9},{9,8},{10,11... | collective-permute-start | bytes 2727944 | tf_op jit(solution)/shard_map/ppermute | solution.py:378
  50.8 4.1 %collective-permute-start.7 = (bf16[128,2560]{1,0:T(8,128)(2,1)S(1)}, bf16[128,2560]{1,0:T(8,128)(2,1)S(1)}, u32[]{:S(2)}, u32[]{:S(2)}) collective-permute-start(bf16[128,2560]{1,0:T(8,128)(2,1)S(1)} %get-tuple-element.57), channel_id=1, source_target_pairs={{0,1},{1,0},{2,3},{3,2},{4,5},{5,4},{6,7},{7,6},{8,9},{9,8},{10,11... | collective-permute-start | bytes 1966088 | tf_op jit(solution)/shard_map/ppermute | solution.py:389
  54.9 34.0 %copy-start.16 = (bf16[8,2560]{1,0:T(8,128)(2,1)S(1)}, bf16[8,2560]{1,0:T(8,128)(2,1)}, u32[]{:S(2)}) copy-start(bf16[8,2560]{1,0:T(8,128)(2,1)} %residual.1) | copy-start | bytes 122884
  55.9 33.0 %all-to-all-start = ((bf16[16,8,2560]{2,1,0:T(8,128)(2,1)}), bf16[16,8,2560]{2,1,0:T(8,128)(2,1)S(1)}, u32[]{:S(2)}, u32[]{:S(2)}) async-start(bf16[16,8,2560]{2,1,0:T(8,128)(2,1)} %shard_map.124), calls=%async_computation | async-start | bytes 1310720 | tf_op jit(solution)/shard_map/all_to_all | solution.py:395
  69.5 29.5 %collective-permute-start.8 = (bf16[3,160,768]{2,1,0:T(8,128)(2,1)S(1)}, bf16[3,160,768]{2,1,0:T(8,128)(2,1)S(1)}, u32[]{:S(2)}, u32[]{:S(2)}) collective-permute-start(bf16[3,160,768]{2,1,0:T(8,128)(2,1)S(1)} %copy-done.19), channel_id=1, source_target_pairs={{0,32},{32,0},{1,33},{33,1},{2,34},{34,2},{3,35},{35,3},{4,36},{36... | collective-permute-start | bytes 2211848 | tf_op jit(solution)/shard_map/ppermute | solution.py:393
  89.9 24.7 %copy-start.21 = (bf16[3,160,384]{2,1,0:T(8,128)(2,1)S(1)}, bf16[3,160,384]{2,1,0:T(8,128)(2,1)}, u32[]{:S(2)}) copy-start(bf16[3,160,384]{2,1,0:T(8,128)(2,1)} %copy-done.20) | copy-start | bytes 1105924
  89.9 43.3 %copy-start.9 = (bf16[3,160,384]{2,1,0:T(8,128)(2,1)S(1)}, bf16[3,160,384]{2,1,0:T(8,128)(2,1)}, u32[]{:S(2)}) copy-start(bf16[3,160,384]{2,1,0:T(8,128)(2,1)} %copy-done.8) | copy-start | bytes 1105924
  89.9 16.9 %all-to-all-start.1 = ((bf16[16,8,512]{2,1,0:T(8,128)(2,1)}), bf16[16,8,512]{2,1,0:T(8,128)(2,1)S(1)}, u32[]{:S(2)}, u32[]{:S(2)}) async-start(bf16[16,8,512]{2,1,0:T(8,128)(2,1)} %shard_map.125), calls=%async_computation.1 | async-start | bytes 262144 | tf_op jit(solution)/shard_map/all_to_all | solution.py:399
  99.0 34.3 %copy-start.6 = (bf16[3,160,768]{2,1,0:T(8,128)(2,1)}, bf16[3,160,768]{2,1,0:T(8,128)(2,1)S(1)}, u32[]{:S(2)}) copy-start(bf16[3,160,768]{2,1,0:T(8,128)(2,1)S(1)} %collective-permute-done.8.got) | copy-start | bytes 2211844
  108.0 27.2 %all-to-all-start.2 = ((bf16[32,80,128]{2,1,0:T(8,128)(2,1)}), bf16[32,80,128]{2,1,0:T(8,128)(2,1)S(1)}, u32[]{:S(2)}, u32[]{:S(2)}) async-start(bf16[32,80,128]{2,1,0:T(8,128)(2,1)} %shard_map.126), calls=%async_computation.2 | async-start | bytes 1310720 | tf_op jit(solution)/shard_map/all_to_all | solution.py:429
  114.6 18.7 %copy-start.5 = (bf16[3,160,768]{2,1,0:T(8,128)(2,1)S(1)}, bf16[3,160,768]{2,1,0:T(8,128)(2,1)}, u32[]{:S(2)}) copy-start(bf16[3,160,768]{2,1,0:T(8,128)(2,1)} %copy-done.4) | copy-start | bytes 2211844
  114.6 18.6 %collective-permute-start.9 = (bf16[3,160,384]{2,1,0:T(8,128)(2,1)S(1)}, bf16[3,160,384]{2,1,0:T(8,128)(2,1)S(1)}, u32[]{:S(2)}, u32[]{:S(2)}) collective-permute-start(bf16[3,160,384]{2,1,0:T(8,128)(2,1)S(1)} %copy-done.21), channel_id=1, source_target_pairs={{0,32},{32,0},{1,33},{33,1},{2,34},{34,2},{3,35},{35,3},{4,36},{36... | collective-permute-start | bytes 1105928 | tf_op jit(solution)/shard_map/ppermute | solution.py:401
  207.1 28.4 %all-to-all-start.5 = ((bf16[32,80,128]{2,1,0:T(8,128)(2,1)}), bf16[32,80,128]{2,1,0:T(8,128)(2,1)S(1)}, u32[]{:S(2)}, u32[]{:S(2)}) async-start(bf16[32,80,128]{2,1,0:T(8,128)(2,1)} %shard_map.131), calls=%async_computation.5 | async-start | bytes 1310720 | tf_op jit(solution)/shard_map/all_to_all | solution.py:440
  236.1 6.2 %collective-permute-start.10 = (bf16[128,160]{1,0:T(8,128)(2,1)S(1)}, bf16[128,160]{1,0:T(8,128)(2,1)S(1)}, u32[]{:S(2)}, u32[]{:S(2)}) collective-permute-start(bf16[128,160]{1,0:T(8,128)(2,1)S(1)} %get-tuple-element.72), channel_id=1, source_target_pairs={{0,32},{32,0},{1,33},{33,1},{2,34},{34,2},{3,35},{35,3},{4,36},{36... | collective-permute-start | bytes 122888 | tf_op jit(solution)/shard_map/ppermute | solution.py:444
  (16 other events, 77.3 us)

commit v11 on v8

--- a/solution.py
+++ b/solution.py
@@ -245,7 +245,7 @@
             store_packed(out, r // SLOTS + n, total[n * SLOTS : (n + 1) * SLOTS])
 
 
-def combine_kernel(weighting, returned, keep, send):
+def combine_kernel(weighting, returned, order, stream, keep, send):
     width = keep.shape[1]
     rows = jnp.concatenate([load_packed(returned, n) for n in range(returned.shape[0])], axis=0)
     top = weighting[...].astype(bf16)
@@ -254,7 +254,8 @@
         rest, rows, preferred_element_type=f32
     )
     tail = mixture[:, 256:320] + mixture[:, 320:384]
-    keep[...] = mixture[:, :width]
+    kept = jnp.dot(order[...], stream[:, 2 * width : 3 * width], preferred_element_type=f32)
+    keep[...] = kept + mixture[:, :width]
     send[...] = jnp.concatenate([mixture[:, width:256], tail], axis=1).astype(bf16)
 
 
@@ -315,9 +316,11 @@
         ]
         return lax.ppermute(mine, ("y", "xh"), pairs)
 
-    column = jnp.stack([along_y(1, 2), along_y(3, 4)])
+    far = along_y(3, 4)
+    near = along_y(1, 2)
+    column = jnp.stack([far, near])
     to_other = jnp.where(
-        (xl == 0) & (xh == 1), jnp.stack([mine, column[0]]), column
+        (xl == 0) & (xh == 1), jnp.stack([mine, near]), column
     )
     diagonal = [(0, 3), (1, 2), (2, 1), (3, 0)]
     pieces = [
@@ -328,12 +331,12 @@
     ]
 
     def blocks_of(x, h):
-        return [2 * (y - 1 - h) + x, 2 * (y - 3 - h) + x]
+        return [2 * (y - 3 - h) + x, 2 * (y - 1 - h) + x]
 
     def blocks_sent(x, h):
-        near, far = blocks_of(x, h)
+        late, early = blocks_of(x, h)
         odd = (x == 0) & (h == 1)
-        return [jnp.where(odd, 2 * y, near), jnp.where(odd, near, far)]
+        return [jnp.where(odd, 2 * y, late), early]
 
     info = jnp.stack(
         blocks_of(xl, xh)
@@ -435,15 +438,10 @@
     )
     returned = lax.all_to_all(expert_out, EXP, split_axis=0, concat_axis=0, tiled=True)
     mix_keep, mix_send = call(
-        combine_kernel, [sds((128, width_out), f32), sds((128, width_out), bf16)], count=2
-    )(weighting, returned)
+        combine_kernel, [sds((128, width_out), f32), sds((128, width_out), bf16)], count=4
+    )(weighting, returned, back_order.astype(bf16), split)
     mix_got = lax.ppermute(mix_send, "xl", SWAP)
-    stream_rb = jnp.dot(
-        back_order.astype(bf16),
-        split[:, width_pair : width_pair + width_out],
-        preferred_element_type=f32,
-    )
-    result = (stream_rb + mix_keep + mix_got.astype(f32)).astype(bf16)
+    result = (mix_keep + mix_got.astype(f32)).astype(bf16)
     return result.reshape(8, 16, width_out)
 
 

time: 241 us -> 242 us (level)
    ppermute x1, waiting for transfers between devices: 0.51 us -> 3.3 us  [on_device(): lax.ppermute(to_other, 'xl', SWAP)]
where the time goes in v11:
time: 242 us; the launch traced here: 240 us
  waiting for transfers between devices  76.6 us (32%)
  starting transfers between devices  71 us (29%)
  blocking collectives  67 us (28%)
  Pallas kernels  18.7 us (8%)
  local copies, waits for them, and re-layouts  3.88 us (2%)
    all_to_all x1, blocking collectives, on_device(): lax.all_to_all(pre.reshape(8, 128, 2 * ff_half), 'y', split_axis=0, conca...  42.6 us
    all_to_all x1, blocking collectives, on_device(): lax.all_to_all(hidden, 'y', split_axis=0, concat_axis=0, tiled=True)  24.4 us
    all_to_all x1, waiting for transfers between devices, on_device(): lax.all_to_all(expert_out, EXP, split_axis=0, concat_axis=0, tiled=True)  19.6 us
    all_to_all x1, waiting for transfers between devices, on_device(): lax.all_to_all(pair_sum, ('z', 'xh'), split_axis=0, concat_axis=0, tiled=...  16.5 us
    ppermute x1, waiting for transfers between devices, on_device(): down_got = lax.ppermute(down_send, 'xl', SWAP)  14.8 us
    all_to_all x1, starting transfers between devices, on_device(): lax.all_to_all(pair_sum, ('z', 'xh'), split_axis=0, concat_axis=0, tiled=...  13.3 us
    ppermute x2, starting transfers between devices, along_y(): return lax.ppermute(mine, ('y', 'xh'), pairs)  10.6 us
    all_to_all x1, starting transfers between devices, on_device(): split = lax.all_to_all(packed, CTX, split_axis=0, concat_axis=0, tiled=True)  8.64 us
  transfers between devices with their start and end apart: 15, of which 12 were waited for; matrix products, arithmetic and copies ran while one was open for 1% of the time, Pallas kernels for 3%

profile of v11, /device:TPU:6, one launch (start us, length us, event | category | flops | bytes accessed | tf_op | source)
XLA Modules:
  0.0 240.0 jit_solution(15929372765486058386)
XLA Ops:
  1.7 7.9 %collective-permute-start = (bf16[592,128]{1,0:T(8,128)(2,1)S(1)}, bf16[592,128]{1,0:T(8,128)(2,1)S(1)}, u32[]{:S(2)}, u32[]{:S(2)}) collective-permute-start(bf16[592,128]{1,0:T(8,128)(2,1)S(1)} %constant_dynamic-slice_fusion), channel_id=1, source_target_pairs={{0,192},{2,258},{64,256},{66,322},{128,320},{130,386},{192,384},{1... | collective-permute-start | bytes 454664 | tf_op jit(solution)/shard_map/ppermute | solution.py:317
  9.6 2.7 %collective-permute-start.1 = (bf16[592,128]{1,0:T(8,128)(2,1)S(1)}, bf16[592,128]{1,0:T(8,128)(2,1)S(1)}, u32[]{:S(2)}, u32[]{:S(2)}) collective-permute-start(bf16[592,128]{1,0:T(8,128)(2,1)S(1)} %constant_dynamic-slice_fusion), channel_id=1, source_target_pairs={{0,64},{2,130},{64,128},{66,194},{128,192},{130,258},{192,256},{19... | collective-permute-start | bytes 454664 | tf_op jit(solution)/shard_map/ppermute | solution.py:317
  12.3 4.7 %collective-permute-done = bf16[592,128]{1,0:T(8,128)(2,1)S(1)} collective-permute-done((bf16[592,128]{1,0:T(8,128)(2,1)S(1)}, bf16[592,128]{1,0:T(8,128)(2,1)S(1)}, u32[]{:S(2)}, u32[]{:S(2)}) %collective-permute-start) | collective-permute-done | bytes 151584 | tf_op jit(solution)/shard_map/ppermute | solution.py:317
  17.0 3.5 %collective-permute-done.1 = bf16[592,128]{1,0:T(8,128)(2,1)S(1)} collective-permute-done((bf16[592,128]{1,0:T(8,128)(2,1)S(1)}, bf16[592,128]{1,0:T(8,128)(2,1)S(1)}, u32[]{:S(2)}, u32[]{:S(2)}) %collective-permute-start.1) | collective-permute-done | bytes 151584 | tf_op jit(solution)/shard_map/ppermute | solution.py:317
  20.6 5.1 %collective-permute-start.2 = (bf16[2,592,128]{2,1,0:T(8,128)(2,1)S(1)}, bf16[2,592,128]{2,1,0:T(8,128)(2,1)S(1)}, u32[]{:S(2)}, u32[]{:S(2)}) collective-permute-start(bf16[2,592,128]{2,1,0:T(8,128)(2,1)S(1)} %get-tuple-element.36.p0), channel_id=1, source_target_pairs={{0,2},{2,0},{1,3},{3,1},{4,6},{6,4},{5,7},{7,5},{8,10},{10,8},{9,1... | collective-permute-start | bytes 909320 | tf_op jit(solution)/shard_map/ppermute | solution.py:328
  28.5 2.8 %collective-permute-start.4 = (bf16[2,592,128]{2,1,0:T(8,128)(2,1)S(1)}, bf16[2,592,128]{2,1,0:T(8,128)(2,1)S(1)}, u32[]{:S(2)}, u32[]{:S(2)}) collective-permute-start(bf16[2,592,128]{2,1,0:T(8,128)(2,1)S(1)} %get-tuple-element.63), channel_id=1, source_target_pairs={{0,34},{2,32},{32,2},{34,0},{1,35},{3,33},{33,3},{35,1},{4,38},{6,... | collective-permute-start | bytes 909320 | tf_op jit(solution)/shard_map/ppermute | solution.py:330
  35.9 3.3 %collective-permute-done.3.p2 = bf16[2,592,128]{2,1,0:T(8,128)(2,1)S(1)} collective-permute-done((bf16[2,592,128]{2,1,0:T(8,128)(2,1)S(1)}, bf16[2,592,128]{2,1,0:T(8,128)(2,1)S(1)}, u32[]{:S(2)}, u32[]{:S(2)}) %collective-permute-start.3) | collective-permute-done | bytes 303136 | tf_op jit(solution)/shard_map/ppermute | solution.py:329
  42.5 2.7 %shard_map.121 = (f32[2,256,128]{2,1,0:T(8,128)S(1)}, f32[2,256,128]{2,1,0:T(8,128)S(1)}, f32[2,256,512]{2,1,0:T(8,128)S(1)}) custom-call(s32[10]{0:T(128)S(1)} %stack.59.info, bf16[2,256,592]{2,1,0:T(8,128)(2,1)S(1)} %bitcast.41, bf16[2,592,128]{2,1,0:T(8,128)(2,1)S(1)} %collective-permute-done.2.p1, bf16[2,592,128]{2,1,0:T(8,128)(2,1)S(1)} %collective-permute-done.3.p2, ...), custom_call_target="tpu_custom_call" | custom-call | tf_op jit(solution)/shard_map/pallas_call | solution.py:374
  45.2 3.8 %shard_map.122 = (bf16[128,2560]{1,0:T(8,128)(2,1)S(1)}, f32[128,2560]{1,0:T(8,128)S(1)}) custom-call(s32[10]{0:T(128)S(1)} %stack.59.info, bf16[2,256,592]{2,1,0:T(8,128)(2,1)S(1)} %bitcast.42, bf16[6,592,128]{2,1,0:T(8,128)(2,1)S(1)} %collective-permute-done.6.others, f32[2,256,128]{2,1,0:T(8,128)S(1)} %get-tuple-element.44.old_peak, ...), custom_call_target="tpu_custom_call" | custom-call | tf_op jit(solution)/shard_map/pallas_call | solution.py:377
  49.0 2.4 %collective-permute-start.7 = (bf16[128,2560]{1,0:T(8,128)(2,1)S(1)}, bf16[128,2560]{1,0:T(8,128)(2,1)S(1)}, u32[]{:S(2)}, u32[]{:S(2)}) collective-permute-start(bf16[128,2560]{1,0:T(8,128)(2,1)S(1)} %get-tuple-element.48), channel_id=1, source_target_pairs={{0,1},{1,0},{2,3},{3,2},{4,5},{5,4},{6,7},{7,6},{8,9},{9,8},{10,11... | collective-permute-start | bytes 1966088 | tf_op jit(solution)/shard_map/ppermute | solution.py:384
  54.1 13.3 %all-to-all-start = ((bf16[16,8,2560]{2,1,0:T(8,128)(2,1)}), bf16[16,8,2560]{2,1,0:T(8,128)(2,1)S(1)}, u32[]{:S(2)}, u32[]{:S(2)}) async-start(bf16[16,8,2560]{2,1,0:T(8,128)(2,1)} %shard_map.123), calls=%async_computation | async-start | bytes 1310720 | tf_op jit(solution)/shard_map/all_to_all | solution.py:395
  67.6 2.7 %collective-permute-start.8 = (bf16[3,160,768]{2,1,0:T(8,128)(2,1)S(1)}, bf16[3,160,768]{2,1,0:T(8,128)(2,1)S(1)}, u32[]{:S(2)}, u32[]{:S(2)}) collective-permute-start(bf16[3,160,768]{2,1,0:T(8,128)(2,1)S(1)} %get-tuple-element.51), channel_id=1, source_target_pairs={{0,32},{32,0},{1,33},{33,1},{2,34},{34,2},{3,35},{35,3},{4,36},{36... | collective-permute-start | bytes 2211848 | tf_op jit(solution)/shard_map/ppermute | solution.py:393
  70.7 16.5 %all-to-all-done.spread = bf16[16,8,2560]{2,1,0:T(8,128)(2,1)S(1)} async-done(((bf16[16,8,2560]{2,1,0:T(8,128)(2,1)}), bf16[16,8,2560]{2,1,0:T(8,128)(2,1)S(1)}, u32[]{:S(2)}, u32[]{:S(2)}) %all-to-all-start) | async-done | bytes 655392 | tf_op jit(solution)/shard_map/all_to_all | solution.py:395
  88.1 8.6 %all-to-all-start.1 = ((bf16[16,8,512]{2,1,0:T(8,128)(2,1)}), bf16[16,8,512]{2,1,0:T(8,128)(2,1)S(1)}, u32[]{:S(2)}, u32[]{:S(2)}) async-start(bf16[16,8,512]{2,1,0:T(8,128)(2,1)} %shard_map.125), calls=%async_computation.1 | async-start | bytes 262144 | tf_op jit(solution)/shard_map/all_to_all | solution.py:399
  97.3 7.8 %all-to-all-done.1 = bf16[16,8,512]{2,1,0:T(8,128)(2,1)S(1)} async-done(((bf16[16,8,512]{2,1,0:T(8,128)(2,1)}), bf16[16,8,512]{2,1,0:T(8,128)(2,1)S(1)}, u32[]{:S(2)}, u32[]{:S(2)}) %all-to-all-start.1) | async-done | bytes 131104 | tf_op jit(solution)/shard_map/all_to_all | solution.py:399
  106.4 6.6 %all-to-all-start.2 = ((bf16[32,80,128]{2,1,0:T(8,128)(2,1)}), bf16[32,80,128]{2,1,0:T(8,128)(2,1)S(1)}, u32[]{:S(2)}, u32[]{:S(2)}) async-start(bf16[32,80,128]{2,1,0:T(8,128)(2,1)} %shard_map.126), calls=%async_computation.2 | async-start | bytes 1310720 | tf_op jit(solution)/shard_map/all_to_all | solution.py:428
  113.0 2.6 %collective-permute-start.9 = (bf16[3,160,384]{2,1,0:T(8,128)(2,1)}, bf16[3,160,384]{2,1,0:T(8,128)(2,1)S(1)}, u32[]{:S(2)}, u32[]{:S(2)}) collective-permute-start(bf16[3,160,384]{2,1,0:T(8,128)(2,1)} %get-tuple-element.57), channel_id=1, source_target_pairs={{0,32},{32,0},{1,33},{33,1},{2,34},{34,2},{3,35},{35,3},{4,36},{36... | collective-permute-start | bytes 1105928 | tf_op jit(solution)/shard_map/ppermute | solution.py:401
  116.8 14.8 %collective-permute-done.9.got = bf16[3,160,384]{2,1,0:T(8,128)(2,1)S(1)} collective-permute-done((bf16[3,160,384]{2,1,0:T(8,128)(2,1)}, bf16[3,160,384]{2,1,0:T(8,128)(2,1)S(1)}, u32[]{:S(2)}, u32[]{:S(2)}) %collective-permute-start.9) | collective-permute-done | bytes 368672 | tf_op jit(solution)/shard_map/ppermute | solution.py:401
  135.8 42.6 %all_to_all.30.parts = bf16[8,128,768]{2,1,0:T(8,128)(2,1)S(1)} all-to-all(bf16[8,128,768]{2,1,0:T(8,128)(2,1)S(1)} %bitcast.43), channel_id=1, replica_groups=mesh['y'=8,'xl'=2,'z'=8,'xh'=2,'core'=2] {'y'}, dimensions={0} | all-to-all | bytes 3145728 | tf_op jit(solution)/shard_map/all_to_all | solution.py:431
  178.7 24.4 %all_to_all.31 = bf16[8,128,384]{2,1,0:T(8,128)(2,1)S(1)} all-to-all(bf16[8,128,384]{2,1,0:T(8,128)(2,1)S(1)} %shard_map.130), channel_id=1, replica_groups=mesh['y'=8,'xl'=2,'z'=8,'xh'=2,'core'=2] {'y'}, dimensions={0} | all-to-all | bytes 1572864 | tf_op jit(solution)/shard_map/all_to_all | solution.py:435
  203.1 2.4 shard_map.131
  205.4 6.7 %all-to-all-start.5 = ((bf16[32,80,128]{2,1,0:T(8,128)(2,1)}), bf16[32,80,128]{2,1,0:T(8,128)(2,1)S(1)}, u32[]{:S(2)}, u32[]{:S(2)}) async-start(bf16[32,80,128]{2,1,0:T(8,128)(2,1)} %shard_map.131), calls=%async_computation.5 | async-start | bytes 1310720 | tf_op jit(solution)/shard_map/all_to_all | solution.py:439
  213.0 19.6 %all-to-all-done.5.returned = bf16[32,80,128]{2,1,0:T(8,128)(2,1)S(1)} async-done(((bf16[32,80,128]{2,1,0:T(8,128)(2,1)}), bf16[32,80,128]{2,1,0:T(8,128)(2,1)S(1)}, u32[]{:S(2)}, u32[]{:S(2)}) %all-to-all-start.5) | async-done | bytes 655392 | tf_op jit(solution)/shard_map/all_to_all | solution.py:439
  233.2 3.9 %collective-permute-start.10 = (bf16[128,160]{1,0:T(8,128)(2,1)S(1)}, bf16[128,160]{1,0:T(8,128)(2,1)S(1)}, u32[]{:S(2)}, u32[]{:S(2)}) collective-permute-start(bf16[128,160]{1,0:T(8,128)(2,1)S(1)} %get-tuple-element.62), channel_id=1, source_target_pairs={{0,32},{32,0},{1,33},{33,1},{2,34},{34,2},{3,35},{35,3},{4,36},{36... | collective-permute-start | bytes 122888 | tf_op jit(solution)/shard_map/ppermute | solution.py:443
  (87 shorter events, 28.3 us)
Async XLA Ops:
  0.0 25.7 %copy-start.12 = (s32[256]{0:T(256)S(1)}, s32[256]{0:T(256)}, u32[]{:S(2)}) copy-start(s32[256]{0:T(256)} %param.14) | copy-start | bytes 3076
  1.7 24.2 %copy-start.13 = (bf16[256,2,576]{0,2,1:T(8,128)(2,1)S(1)}, bf16[256,2,576]{0,2,1:T(8,128)(2,1)}, u32[]{:S(2)}) copy-start(bf16[256,2,576]{0,2,1:T(8,128)(2,1)} %param.12) | copy-start | bytes 1769476
  1.7 15.3 %collective-permute-start = (bf16[592,128]{1,0:T(8,128)(2,1)S(1)}, bf16[592,128]{1,0:T(8,128)(2,1)S(1)}, u32[]{:S(2)}, u32[]{:S(2)}) collective-permute-start(bf16[592,128]{1,0:T(8,128)(2,1)S(1)} %constant_dynamic-slice_fusion), channel_id=1, source_target_pairs={{0,192},{2,258},{64,256},{66,322},{128,320},{130,386},{192,384},{1... | collective-permute-start | bytes 454664 | tf_op jit(solution)/shard_map/ppermute | solution.py:317
  9.6 10.9 %collective-permute-start.1 = (bf16[592,128]{1,0:T(8,128)(2,1)S(1)}, bf16[592,128]{1,0:T(8,128)(2,1)S(1)}, u32[]{:S(2)}, u32[]{:S(2)}) collective-permute-start(bf16[592,128]{1,0:T(8,128)(2,1)S(1)} %constant_dynamic-slice_fusion), channel_id=1, source_target_pairs={{0,64},{2,130},{64,128},{66,194},{128,192},{130,258},{192,256},{19... | collective-permute-start | bytes 454664 | tf_op jit(solution)/shard_map/ppermute | solution.py:317
  20.6 13.4 %collective-permute-start.2 = (bf16[2,592,128]{2,1,0:T(8,128)(2,1)S(1)}, bf16[2,592,128]{2,1,0:T(8,128)(2,1)S(1)}, u32[]{:S(2)}, u32[]{:S(2)}) collective-permute-start(bf16[2,592,128]{2,1,0:T(8,128)(2,1)S(1)} %get-tuple-element.36.p0), channel_id=1, source_target_pairs={{0,2},{2,0},{1,3},{3,1},{4,6},{6,4},{5,7},{7,5},{8,10},{10,8},{9,1... | collective-permute-start | bytes 909320 | tf_op jit(solution)/shard_map/ppermute | solution.py:328
  26.6 12.6 %collective-permute-start.3 = (bf16[2,592,128]{2,1,0:T(8,128)(2,1)S(1)}, bf16[2,592,128]{2,1,0:T(8,128)(2,1)S(1)}, u32[]{:S(2)}, u32[]{:S(2)}) collective-permute-start(bf16[2,592,128]{2,1,0:T(8,128)(2,1)S(1)} %get-tuple-element.63), channel_id=1, source_target_pairs={{0,32},{32,0},{1,33},{33,1},{2,34},{34,2},{3,35},{35,3},{4,36},{36... | collective-permute-start | bytes 909320 | tf_op jit(solution)/shard_map/ppermute | solution.py:329
  28.5 12.0 %collective-permute-start.4 = (bf16[2,592,128]{2,1,0:T(8,128)(2,1)S(1)}, bf16[2,592,128]{2,1,0:T(8,128)(2,1)S(1)}, u32[]{:S(2)}, u32[]{:S(2)}) collective-permute-start(bf16[2,592,128]{2,1,0:T(8,128)(2,1)S(1)} %get-tuple-element.63), channel_id=1, source_target_pairs={{0,34},{2,32},{32,2},{34,0},{1,35},{3,33},{33,3},{35,1},{4,38},{6,... | collective-permute-start | bytes 909320 | tf_op jit(solution)/shard_map/ppermute | solution.py:330
  34.0 6.5 %collective-permute-start.5 = (bf16[2,592,128]{2,1,0:T(8,128)(2,1)S(1)}, bf16[2,592,128]{2,1,0:T(8,128)(2,1)S(1)}, u32[]{:S(2)}, u32[]{:S(2)}) collective-permute-start(bf16[2,592,128]{2,1,0:T(8,128)(2,1)S(1)} %get-tuple-element.36.p0), channel_id=1, source_target_pairs={{0,1},{1,0},{2,3},{3,2},{4,5},{5,4},{6,7},{7,6},{8,9},{9,8},{10,11... | collective-permute-start | bytes 909320 | tf_op jit(solution)/shard_map/ppermute | solution.py:370
  40.5 4.6 %collective-permute-start.6 = (bf16[6,592,128]{2,1,0:T(8,128)(2,1)S(1)}, bf16[6,592,128]{2,1,0:T(8,128)(2,1)S(1)}, u32[]{:S(2)}, u32[]{:S(2)}) collective-permute-start(bf16[6,592,128]{2,1,0:T(8,128)(2,1)S(1)} %shard_map.120), channel_id=1, source_target_pairs={{0,1},{1,0},{2,3},{3,2},{4,5},{5,4},{6,7},{7,6},{8,9},{9,8},{10,11... | collective-permute-start | bytes 2727944 | tf_op jit(solution)/shard_map/ppermute | solution.py:373
  45.2 6.2 %copy-start.1 = (bf16[3,160,768]{2,1,0:T(8,128)(2,1)S(1)}, bf16[3,160,768]{2,1,0:T(8,128)(2,1)}, u32[]{:S(2)}) copy-start(bf16[3,160,768]{2,1,0:T(8,128)(2,1)} %gate.1) | copy-start | bytes 2211844
  49.0 4.1 %collective-permute-start.7 = (bf16[128,2560]{1,0:T(8,128)(2,1)S(1)}, bf16[128,2560]{1,0:T(8,128)(2,1)S(1)}, u32[]{:S(2)}, u32[]{:S(2)}) collective-permute-start(bf16[128,2560]{1,0:T(8,128)(2,1)S(1)} %get-tuple-element.48), channel_id=1, source_target_pairs={{0,1},{1,0},{2,3},{3,2},{4,5},{5,4},{6,7},{7,6},{8,9},{9,8},{10,11... | collective-permute-start | bytes 1966088 | tf_op jit(solution)/shard_map/ppermute | solution.py:384
  53.1 14.3 %copy-start.15 = (s32[8,16,6]{1,0,2:T(8,128)S(1)}, s32[8,16,6]{1,0,2:T(8,128)}, u32[]{:S(2)}) copy-start(s32[8,16,6]{1,0,2:T(8,128)} %param.19) | copy-start | bytes 9220
  53.1 17.3 %copy-start.16 = (f32[2560]{0:T(1024)S(1)}, f32[2560]{0:T(1024)}, u32[]{:S(2)}) copy-start(f32[2560]{0:T(1024)} %param.18) | copy-start | bytes 30724
  53.1 34.0 %copy-start.10 = (bf16[8,2560]{1,0:T(8,128)(2,1)S(1)}, bf16[8,2560]{1,0:T(8,128)(2,1)}, u32[]{:S(2)}) copy-start(bf16[8,2560]{1,0:T(8,128)(2,1)} %residual.1) | copy-start | bytes 122884
  54.1 33.0 %all-to-all-start = ((bf16[16,8,2560]{2,1,0:T(8,128)(2,1)}), bf16[16,8,2560]{2,1,0:T(8,128)(2,1)S(1)}, u32[]{:S(2)}, u32[]{:S(2)}) async-start(bf16[16,8,2560]{2,1,0:T(8,128)(2,1)} %shard_map.123), calls=%async_computation | async-start | bytes 1310720 | tf_op jit(solution)/shard_map/all_to_all | solution.py:395
  67.6 29.7 %collective-permute-start.8 = (bf16[3,160,768]{2,1,0:T(8,128)(2,1)S(1)}, bf16[3,160,768]{2,1,0:T(8,128)(2,1)S(1)}, u32[]{:S(2)}, u32[]{:S(2)}) collective-permute-start(bf16[3,160,768]{2,1,0:T(8,128)(2,1)S(1)} %get-tuple-element.51), channel_id=1, source_target_pairs={{0,32},{32,0},{1,33},{33,1},{2,34},{34,2},{3,35},{35,3},{4,36},{36... | collective-permute-start | bytes 2211848 | tf_op jit(solution)/shard_map/ppermute | solution.py:393
  88.1 17.1 %all-to-all-start.1 = ((bf16[16,8,512]{2,1,0:T(8,128)(2,1)}), bf16[16,8,512]{2,1,0:T(8,128)(2,1)S(1)}, u32[]{:S(2)}, u32[]{:S(2)}) async-start(bf16[16,8,512]{2,1,0:T(8,128)(2,1)} %shard_map.125), calls=%async_computation.1 | async-start | bytes 262144 | tf_op jit(solution)/shard_map/all_to_all | solution.py:399
  97.3 9.1 %copy-start.4 = (bf16[3,160,768]{2,1,0:T(8,128)(2,1)}, bf16[3,160,768]{2,1,0:T(8,128)(2,1)S(1)}, u32[]{:S(2)}) copy-start(bf16[3,160,768]{2,1,0:T(8,128)(2,1)S(1)} %collective-permute-done.8.got) | copy-start | bytes 2211844
  106.4 27.2 %all-to-all-start.2 = ((bf16[32,80,128]{2,1,0:T(8,128)(2,1)}), bf16[32,80,128]{2,1,0:T(8,128)(2,1)S(1)}, u32[]{:S(2)}, u32[]{:S(2)}) async-start(bf16[32,80,128]{2,1,0:T(8,128)(2,1)} %shard_map.126), calls=%async_computation.2 | async-start | bytes 1310720 | tf_op jit(solution)/shard_map/all_to_all | solution.py:428
  113.0 18.6 %collective-permute-start.9 = (bf16[3,160,384]{2,1,0:T(8,128)(2,1)}, bf16[3,160,384]{2,1,0:T(8,128)(2,1)S(1)}, u32[]{:S(2)}, u32[]{:S(2)}) collective-permute-start(bf16[3,160,384]{2,1,0:T(8,128)(2,1)} %get-tuple-element.57), channel_id=1, source_target_pairs={{0,32},{32,0},{1,33},{33,1},{2,34},{34,2},{3,35},{35,3},{4,36},{36... | collective-permute-start | bytes 1105928 | tf_op jit(solution)/shard_map/ppermute | solution.py:401
  116.7 14.9 %copy-start.7 = (bf16[3,160,384]{2,1,0:T(8,128)(2,1)S(1)}, bf16[3,160,384]{2,1,0:T(8,128)(2,1)}, u32[]{:S(2)}) copy-start(bf16[3,160,384]{2,1,0:T(8,128)(2,1)} %copy-done.6) | copy-start | bytes 1105924
  203.1 9.3 %copy-start.14 = (f32[8,16,6]{1,0,2:T(8,128)S(1)}, f32[8,16,6]{1,0,2:T(8,128)}, u32[]{:S(2)}) copy-start(f32[8,16,6]{1,0,2:T(8,128)} %param.20) | copy-start | bytes 9220
  205.4 27.2 %all-to-all-start.5 = ((bf16[32,80,128]{2,1,0:T(8,128)(2,1)}), bf16[32,80,128]{2,1,0:T(8,128)(2,1)S(1)}, u32[]{:S(2)}, u32[]{:S(2)}) async-start(bf16[32,80,128]{2,1,0:T(8,128)(2,1)} %shard_map.131), calls=%async_computation.5 | async-start | bytes 1310720 | tf_op jit(solution)/shard_map/all_to_all | solution.py:439
  233.2 6.2 %collective-permute-start.10 = (bf16[128,160]{1,0:T(8,128)(2,1)S(1)}, bf16[128,160]{1,0:T(8,128)(2,1)S(1)}, u32[]{:S(2)}, u32[]{:S(2)}) collective-permute-start(bf16[128,160]{1,0:T(8,128)(2,1)S(1)} %get-tuple-element.62), channel_id=1, source_target_pairs={{0,32},{32,0},{1,33},{33,1},{2,34},{34,2},{3,35},{35,3},{4,36},{36... | collective-permute-start | bytes 122888 | tf_op jit(solution)/shard_map/ppermute | solution.py:443
  (8 other events, 21.8 us)

commit v12 on v11

--- a/solution.py
+++ b/solution.py
@@ -76,10 +76,9 @@
 
 
 def first_attention_kernel(info, query, own, p0, peak, sums, mixed, scores):
-    @pl.loop(0, 2)
-    def _(head):
+    for head in range(2):
         state = attend_chunks(
-            query[head], [own, p0], [causal_bias, valid_bias(info, 0)], scores, None
+            query[head], [own, p0], [causal_bias, valid_bias(info, 0)], scores.at[head], None
         )
         peak[head], sums[head], mixed[head] = state
 
@@ -87,11 +86,10 @@
 def second_attention_kernel(
     info, query, p1, p2, p3, o0, old_peak, old_sums, old_mixed, peak, sums, mixed, scores
 ):
-    @pl.loop(0, 2)
-    def _(head):
+    for head in range(2):
         old = old_peak[head], old_sums[head], old_mixed[head]
         biases = [valid_bias(info, n) for n in (1, 2, 3, 0)]
-        state = attend_chunks(query[head], [p1, p2, p3, o0], biases, scores, old)
+        state = attend_chunks(query[head], [p1, p2, p3, o0], biases, scores.at[head], old)
         peak[head], sums[head], mixed[head] = state
 
 
@@ -100,12 +98,11 @@
 ):
     core = info[8]
 
-    @pl.loop(0, 2)
-    def _(head):
+    for head in range(2):
         old = old_peak[head], old_sums[head], old_mixed[head]
         chunks = [others.at[2 * n : 2 * n + 2] for n in range(3)]
         biases = [valid_bias(info, n) for n in (1, 2, 3)]
-        _, sums, mixed = attend_chunks(query[head], chunks, biases, scores, old)
+        _, sums, mixed = attend_chunks(query[head], chunks, biases, scores.at[head], old)
         mixed = (mixed / jnp.sum(sums, axis=1, keepdims=True)).astype(bf16)
         values[head] = jnp.dot(mixed, value_up[head], preferred_element_type=f32).astype(bf16)
 
@@ -316,27 +313,15 @@
         ]
         return lax.ppermute(mine, ("y", "xh"), pairs)
 
-    far = along_y(3, 4)
-    near = along_y(1, 2)
-    column = jnp.stack([far, near])
-    to_other = jnp.where(
-        (xl == 0) & (xh == 1), jnp.stack([mine, near]), column
-    )
-    diagonal = [(0, 3), (1, 2), (2, 1), (3, 0)]
-    pieces = [
-        column,
-        lax.ppermute(column, "xh", SWAP),
-        lax.ppermute(to_other, "xl", SWAP),
-        lax.ppermute(to_other, ("xl", "xh"), diagonal),
-    ]
+    near, far = along_y(1, 2), along_y(3, 4)
 
     def blocks_of(x, h):
-        return [2 * (y - 3 - h) + x, 2 * (y - 1 - h) + x]
+        return [2 * (y - 1 - h) + x, 2 * (y - 3 - h) + x]
 
     def blocks_sent(x, h):
-        late, early = blocks_of(x, h)
+        early, late = blocks_of(x, h)
         odd = (x == 0) & (h == 1)
-        return [jnp.where(odd, 2 * y, late), early]
+        return [jnp.where(odd, 2 * y, early), jnp.where(odd, early, late)]
 
     info = jnp.stack(
         blocks_of(xl, xh)
@@ -357,13 +342,27 @@
     )
     query_rows = query_rows.reshape(16, 2, 8, local_heads, KEYW).transpose(3, 1, 0, 2, 4)
     query_rows = query_rows.reshape(local_heads, block_len, KEYW)
+    near, far, query_rows = lax.optimization_barrier((near, far, query_rows))
+
+    column = jnp.stack([near, far])
+    to_other = jnp.where(
+        (xl == 0) & (xh == 1), jnp.stack([mine, column[0]]), column
+    )
+    diagonal = [(0, 3), (1, 2), (2, 1), (3, 0)]
+    pieces = [
+        column,
+        lax.ppermute(column, "xh", SWAP),
+        lax.ppermute(to_other, "xl", SWAP),
+        lax.ppermute(to_other, ("xl", "xh"), diagonal),
+    ]
+
     state_out = [
         sds((2, 256, 128), f32),
         sds((2, 256, 128), f32),
         sds((2, 256, LATENT), f32),
     ]
     state = call(
-        first_attention_kernel, state_out, [pltpu.VMEM((256, 2 * 256), f32)], True, 4
+        first_attention_kernel, state_out, [pltpu.VMEM((2, 256, 2 * 256), f32)], True, 4
     )(info, query_rows, keys_own, column)
     pieces[1], column_late, peak = lax.optimization_barrier((pieces[1], column, state[0]))
     state = [peak] + list(state[1:])
@@ -372,12 +371,12 @@
     three = call(gather_kernel, [sds((6, KEYW, half), bf16)], count=3)(*pieces[1:])
     others = lax.ppermute(three, "core", SWAP)
     state = call(
-        second_attention_kernel, state_out, [pltpu.VMEM((256, 4 * 256), f32)], True, 9
+        second_attention_kernel, state_out, [pltpu.VMEM((2, 256, 4 * 256), f32)], True, 9
     )(info, query_rows, pieces[1], pieces[2], pieces[3], first_other, *state)
     send, keep = call(
         last_attention_kernel,
         [sds((half, width_model), bf16), sds((half, width_model), f32)],
-        [pltpu.VMEM((256, 3 * 256), f32), pltpu.VMEM((2, 256, VDIM), bf16)],
+        [pltpu.VMEM((2, 256, 3 * 256), f32), pltpu.VMEM((2, 256, VDIM), bf16)],
         True,
         8,
     )(info, query_rows, others, *state, value_up, out_proj)

time: 242 us -> 241 us (level)
    ppermute x1, waiting for transfers between devices: 3.3 us -> 0.52 us  [on_device(): lax.ppermute(to_other, 'xl', SWAP)]
  transfers between devices with their start and end apart: 15 -> 15, of which waited for: 12 -> 11; matrix products, arithmetic and copies ran while one was open for 1% -> 2% of each run, Pallas kernels for 3% -> 3%
where the time goes in v12:
time: 241 us; the launch traced here: 238 us
  waiting for transfers between devices  74.6 us (31%)
  starting transfers between devices  70.5 us (29%)
  blocking collectives  67 us (28%)
  Pallas kernels  18.4 us (8%)
  local copies, waits for them, and re-layouts  4.92 us (2%)
    all_to_all x1, blocking collectives, on_device(): lax.all_to_all(pre.reshape(8, 128, 2 * ff_half), 'y', split_axis=0, conca...  42.6 us
    all_to_all x1, blocking collectives, on_device(): lax.all_to_all(hidden, 'y', split_axis=0, concat_axis=0, tiled=True)  24.4 us
    all_to_all x1, waiting for transfers between devices, on_device(): lax.all_to_all(expert_out, EXP, split_axis=0, concat_axis=0, tiled=True)  19.6 us
    all_to_all x1, waiting for transfers between devices, on_device(): lax.all_to_all(pair_sum, ('z', 'xh'), split_axis=0, concat_axis=0, tiled=...  16.4 us
    ppermute x1, waiting for transfers between devices, on_device(): down_got = lax.ppermute(down_send, 'xl', SWAP)  14.8 us
    all_to_all x1, starting transfers between devices, on_device(): lax.all_to_all(pair_sum, ('z', 'xh'), split_axis=0, concat_axis=0, tiled=...  13.3 us
    ppermute x2, starting transfers between devices, along_y(): return lax.ppermute(mine, ('y', 'xh'), pairs)  10.4 us
    all_to_all x1, starting transfers between devices, on_device(): split = lax.all_to_all(packed, CTX, split_axis=0, concat_axis=0, tiled=True)  8.32 us
  transfers between devices with their start and end apart: 15, of which 11 were waited for; matrix products, arithmetic and copies ran while one was open for 2% of the time, Pallas kernels for 3%

profile of v12, /device:TPU:6, one launch (start us, length us, event | category | flops | bytes accessed | tf_op | source)
XLA Modules:
  0.0 238.4 jit_solution(16797422026137733652)
XLA Ops:
  1.7 4.5 %collective-permute-start = (bf16[592,128]{1,0:T(8,128)(2,1)S(1)}, bf16[592,128]{1,0:T(8,128)(2,1)S(1)}, u32[]{:S(2)}, u32[]{:S(2)}) collective-permute-start(bf16[592,128]{1,0:T(8,128)(2,1)S(1)} %constant_dynamic-slice_fusion), channel_id=1, source_target_pairs={{0,64},{2,130},{64,128},{66,194},{128,192},{130,258},{192,256},{19... | collective-permute-start | bytes 454664 | tf_op jit(solution)/shard_map/ppermute | solution.py:314
  6.2 5.9 %collective-permute-start.1 = (bf16[592,128]{1,0:T(8,128)(2,1)S(1)}, bf16[592,128]{1,0:T(8,128)(2,1)S(1)}, u32[]{:S(2)}, u32[]{:S(2)}) collective-permute-start(bf16[592,128]{1,0:T(8,128)(2,1)S(1)} %constant_dynamic-slice_fusion), channel_id=1, source_target_pairs={{0,192},{2,258},{64,256},{66,322},{128,320},{130,386},{192,384},{1... | collective-permute-start | bytes 454664 | tf_op jit(solution)/shard_map/ppermute | solution.py:314
  14.0 6.9 %collective-permute-done.1 = bf16[592,128]{1,0:T(8,128)(2,1)S(1)} collective-permute-done((bf16[592,128]{1,0:T(8,128)(2,1)S(1)}, bf16[592,128]{1,0:T(8,128)(2,1)S(1)}, u32[]{:S(2)}, u32[]{:S(2)}) %collective-permute-start.1) | collective-permute-done | bytes 151584 | tf_op jit(solution)/shard_map/ppermute | solution.py:314
  21.0 2.7 %collective-permute-start.2 = (bf16[2,592,128]{2,1,0:T(8,128)(2,1)S(1)}, bf16[2,592,128]{2,1,0:T(8,128)(2,1)S(1)}, u32[]{:S(2)}, u32[]{:S(2)}) collective-permute-start(bf16[2,592,128]{2,1,0:T(8,128)(2,1)S(1)} %get-tuple-element.42.p0), channel_id=1, source_target_pairs={{0,2},{2,0},{1,3},{3,1},{4,6},{6,4},{5,7},{7,5},{8,10},{10,8},{9,1... | collective-permute-start | bytes 909320 | tf_op jit(solution)/shard_map/ppermute | solution.py:354
  23.8 3.6 %collective-permute-start.3 = (bf16[2,592,128]{2,1,0:T(8,128)(2,1)S(1)}, bf16[2,592,128]{2,1,0:T(8,128)(2,1)S(1)}, u32[]{:S(2)}, u32[]{:S(2)}) collective-permute-start(bf16[2,592,128]{2,1,0:T(8,128)(2,1)S(1)} %get-tuple-element.69), channel_id=1, source_target_pairs={{0,32},{32,0},{1,33},{33,1},{2,34},{34,2},{3,35},{35,3},{4,36},{36... | collective-permute-start | bytes 909320 | tf_op jit(solution)/shard_map/ppermute | solution.py:355
  27.4 3.5 %collective-permute-start.4 = (bf16[2,592,128]{2,1,0:T(8,128)(2,1)S(1)}, bf16[2,592,128]{2,1,0:T(8,128)(2,1)S(1)}, u32[]{:S(2)}, u32[]{:S(2)}) collective-permute-start(bf16[2,592,128]{2,1,0:T(8,128)(2,1)S(1)} %get-tuple-element.69), channel_id=1, source_target_pairs={{0,34},{2,32},{32,2},{34,0},{1,35},{3,33},{33,3},{35,1},{4,38},{6,... | collective-permute-start | bytes 909320 | tf_op jit(solution)/shard_map/ppermute | solution.py:356
  36.9 2.4 %collective-permute-done.4.p3 = bf16[2,592,128]{2,1,0:T(8,128)(2,1)S(1)} collective-permute-done((bf16[2,592,128]{2,1,0:T(8,128)(2,1)S(1)}, bf16[2,592,128]{2,1,0:T(8,128)(2,1)S(1)}, u32[]{:S(2)}, u32[]{:S(2)}) %collective-permute-start.4) | collective-permute-done | bytes 303136 | tf_op jit(solution)/shard_map/ppermute | solution.py:356
  41.4 2.6 %shard_map.121 = (f32[2,256,128]{2,1,0:T(8,128)S(1)}, f32[2,256,128]{2,1,0:T(8,128)S(1)}, f32[2,256,512]{2,1,0:T(8,128)S(1)}) custom-call(s32[10]{0:T(128)S(1)} %stack.58.info, bf16[2,256,592]{2,1,0:T(8,128)(2,1)S(1)} %bitcast.41, bf16[2,592,128]{2,1,0:T(8,128)(2,1)S(1)} %collective-permute-done.2.p1, bf16[2,592,128]{2,1,0:T(8,128)(2,1)S(1)} %collective-permute-done.3.p2, ...), custom_call_target="tpu_custom_call" | custom-call | tf_op jit(solution)/shard_map/pallas_call | solution.py:373
  44.1 3.6 %shard_map.122 = (bf16[128,2560]{1,0:T(8,128)(2,1)S(1)}, f32[128,2560]{1,0:T(8,128)S(1)}) custom-call(s32[10]{0:T(128)S(1)} %stack.58.info, bf16[2,256,592]{2,1,0:T(8,128)(2,1)S(1)} %bitcast.42, bf16[6,592,128]{2,1,0:T(8,128)(2,1)S(1)} %collective-permute-done.6.others, f32[2,256,128]{2,1,0:T(8,128)S(1)} %get-tuple-element.50.old_peak, ...), custom_call_target="tpu_custom_call" | custom-call | tf_op jit(solution)/shard_map/pallas_call | solution.py:376
  47.7 2.4 %collective-permute-start.7 = (bf16[128,2560]{1,0:T(8,128)(2,1)S(1)}, bf16[128,2560]{1,0:T(8,128)(2,1)S(1)}, u32[]{:S(2)}, u32[]{:S(2)}) collective-permute-start(bf16[128,2560]{1,0:T(8,128)(2,1)S(1)} %get-tuple-element.54), channel_id=1, source_target_pairs={{0,1},{1,0},{2,3},{3,2},{4,5},{5,4},{6,7},{7,6},{8,9},{9,8},{10,11... | collective-permute-start | bytes 1966088 | tf_op jit(solution)/shard_map/ppermute | solution.py:383
  52.8 13.3 %all-to-all-start = ((bf16[16,8,2560]{2,1,0:T(8,128)(2,1)}), bf16[16,8,2560]{2,1,0:T(8,128)(2,1)S(1)}, u32[]{:S(2)}, u32[]{:S(2)}) async-start(bf16[16,8,2560]{2,1,0:T(8,128)(2,1)} %shard_map.123), calls=%async_computation | async-start | bytes 1310720 | tf_op jit(solution)/shard_map/all_to_all | solution.py:394
  66.3 2.7 %collective-permute-start.8 = (bf16[3,160,768]{2,1,0:T(8,128)(2,1)S(1)}, bf16[3,160,768]{2,1,0:T(8,128)(2,1)S(1)}, u32[]{:S(2)}, u32[]{:S(2)}) collective-permute-start(bf16[3,160,768]{2,1,0:T(8,128)(2,1)S(1)} %get-tuple-element.57), channel_id=1, source_target_pairs={{0,32},{32,0},{1,33},{33,1},{2,34},{34,2},{3,35},{35,3},{4,36},{36... | collective-permute-start | bytes 2211848 | tf_op jit(solution)/shard_map/ppermute | solution.py:392
  69.4 16.4 %all-to-all-done.spread = bf16[16,8,2560]{2,1,0:T(8,128)(2,1)S(1)} async-done(((bf16[16,8,2560]{2,1,0:T(8,128)(2,1)}), bf16[16,8,2560]{2,1,0:T(8,128)(2,1)S(1)}, u32[]{:S(2)}, u32[]{:S(2)}) %all-to-all-start) | async-done | bytes 655392 | tf_op jit(solution)/shard_map/all_to_all | solution.py:394
  86.8 8.3 %all-to-all-start.1 = ((bf16[16,8,512]{2,1,0:T(8,128)(2,1)}), bf16[16,8,512]{2,1,0:T(8,128)(2,1)S(1)}, u32[]{:S(2)}, u32[]{:S(2)}) async-start(bf16[16,8,512]{2,1,0:T(8,128)(2,1)} %shard_map.125), calls=%async_computation.1 | async-start | bytes 262144 | tf_op jit(solution)/shard_map/all_to_all | solution.py:398
  95.7 7.8 %all-to-all-done.1 = bf16[16,8,512]{2,1,0:T(8,128)(2,1)S(1)} async-done(((bf16[16,8,512]{2,1,0:T(8,128)(2,1)}), bf16[16,8,512]{2,1,0:T(8,128)(2,1)S(1)}, u32[]{:S(2)}, u32[]{:S(2)}) %all-to-all-start.1) | async-done | bytes 131104 | tf_op jit(solution)/shard_map/all_to_all | solution.py:398
  104.8 6.6 %all-to-all-start.2 = ((bf16[32,80,128]{2,1,0:T(8,128)(2,1)}), bf16[32,80,128]{2,1,0:T(8,128)(2,1)S(1)}, u32[]{:S(2)}, u32[]{:S(2)}) async-start(bf16[32,80,128]{2,1,0:T(8,128)(2,1)} %shard_map.126), calls=%async_computation.2 | async-start | bytes 1310720 | tf_op jit(solution)/shard_map/all_to_all | solution.py:427
  111.4 2.6 %collective-permute-start.9 = (bf16[3,160,384]{2,1,0:T(8,128)(2,1)}, bf16[3,160,384]{2,1,0:T(8,128)(2,1)S(1)}, u32[]{:S(2)}, u32[]{:S(2)}) collective-permute-start(bf16[3,160,384]{2,1,0:T(8,128)(2,1)} %get-tuple-element.63), channel_id=1, source_target_pairs={{0,32},{32,0},{1,33},{33,1},{2,34},{34,2},{3,35},{35,3},{4,36},{36... | collective-permute-start | bytes 1105928 | tf_op jit(solution)/shard_map/ppermute | solution.py:400
  115.2 14.8 %collective-permute-done.9.got = bf16[3,160,384]{2,1,0:T(8,128)(2,1)S(1)} collective-permute-done((bf16[3,160,384]{2,1,0:T(8,128)(2,1)}, bf16[3,160,384]{2,1,0:T(8,128)(2,1)S(1)}, u32[]{:S(2)}, u32[]{:S(2)}) %collective-permute-start.9) | collective-permute-done | bytes 368672 | tf_op jit(solution)/shard_map/ppermute | solution.py:400
  134.2 42.6 %all_to_all.30.parts = bf16[8,128,768]{2,1,0:T(8,128)(2,1)S(1)} all-to-all(bf16[8,128,768]{2,1,0:T(8,128)(2,1)S(1)} %bitcast.43), channel_id=1, replica_groups=mesh['y'=8,'xl'=2,'z'=8,'xh'=2,'core'=2] {'y'}, dimensions={0} | all-to-all | bytes 3145728 | tf_op jit(solution)/shard_map/all_to_all | solution.py:430
  177.1 24.4 %all_to_all.31 = bf16[8,128,384]{2,1,0:T(8,128)(2,1)S(1)} all-to-all(bf16[8,128,384]{2,1,0:T(8,128)(2,1)S(1)} %shard_map.130), channel_id=1, replica_groups=mesh['y'=8,'xl'=2,'z'=8,'xh'=2,'core'=2] {'y'}, dimensions={0} | all-to-all | bytes 1572864 | tf_op jit(solution)/shard_map/all_to_all | solution.py:434
  201.5 2.4 shard_map.131
  203.8 6.7 %all-to-all-start.5 = ((bf16[32,80,128]{2,1,0:T(8,128)(2,1)}), bf16[32,80,128]{2,1,0:T(8,128)(2,1)S(1)}, u32[]{:S(2)}, u32[]{:S(2)}) async-start(bf16[32,80,128]{2,1,0:T(8,128)(2,1)} %shard_map.131), calls=%async_computation.5 | async-start | bytes 1310720 | tf_op jit(solution)/shard_map/all_to_all | solution.py:438
  211.4 19.6 %all-to-all-done.5.returned = bf16[32,80,128]{2,1,0:T(8,128)(2,1)S(1)} async-done(((bf16[32,80,128]{2,1,0:T(8,128)(2,1)}), bf16[32,80,128]{2,1,0:T(8,128)(2,1)S(1)}, u32[]{:S(2)}, u32[]{:S(2)}) %all-to-all-start.5) | async-done | bytes 655392 | tf_op jit(solution)/shard_map/all_to_all | solution.py:438
  231.6 3.9 %collective-permute-start.10 = (bf16[128,160]{1,0:T(8,128)(2,1)S(1)}, bf16[128,160]{1,0:T(8,128)(2,1)S(1)}, u32[]{:S(2)}, u32[]{:S(2)}) collective-permute-start(bf16[128,160]{1,0:T(8,128)(2,1)S(1)} %get-tuple-element.68), channel_id=1, source_target_pairs={{0,32},{32,0},{1,33},{33,1},{2,34},{34,2},{3,35},{35,3},{4,36},{36... | collective-permute-start | bytes 122888 | tf_op jit(solution)/shard_map/ppermute | solution.py:442
  (83 shorter events, 27.6 us)
Async XLA Ops:
  1.7 12.3 %collective-permute-start = (bf16[592,128]{1,0:T(8,128)(2,1)S(1)}, bf16[592,128]{1,0:T(8,128)(2,1)S(1)}, u32[]{:S(2)}, u32[]{:S(2)}) collective-permute-start(bf16[592,128]{1,0:T(8,128)(2,1)S(1)} %constant_dynamic-slice_fusion), channel_id=1, source_target_pairs={{0,64},{2,130},{64,128},{66,194},{128,192},{130,258},{192,256},{19... | collective-permute-start | bytes 454664 | tf_op jit(solution)/shard_map/ppermute | solution.py:314
  6.2 14.7 %collective-permute-start.1 = (bf16[592,128]{1,0:T(8,128)(2,1)S(1)}, bf16[592,128]{1,0:T(8,128)(2,1)S(1)}, u32[]{:S(2)}, u32[]{:S(2)}) collective-permute-start(bf16[592,128]{1,0:T(8,128)(2,1)S(1)} %constant_dynamic-slice_fusion), channel_id=1, source_target_pairs={{0,192},{2,258},{64,256},{66,322},{128,320},{130,386},{192,384},{1... | collective-permute-start | bytes 454664 | tf_op jit(solution)/shard_map/ppermute | solution.py:314
  21.0 13.5 %collective-permute-start.2 = (bf16[2,592,128]{2,1,0:T(8,128)(2,1)S(1)}, bf16[2,592,128]{2,1,0:T(8,128)(2,1)S(1)}, u32[]{:S(2)}, u32[]{:S(2)}) collective-permute-start(bf16[2,592,128]{2,1,0:T(8,128)(2,1)S(1)} %get-tuple-element.42.p0), channel_id=1, source_target_pairs={{0,2},{2,0},{1,3},{3,1},{4,6},{6,4},{5,7},{7,5},{8,10},{10,8},{9,1... | collective-permute-start | bytes 909320 | tf_op jit(solution)/shard_map/ppermute | solution.py:354
  23.8 13.1 %collective-permute-start.3 = (bf16[2,592,128]{2,1,0:T(8,128)(2,1)S(1)}, bf16[2,592,128]{2,1,0:T(8,128)(2,1)S(1)}, u32[]{:S(2)}, u32[]{:S(2)}) collective-permute-start(bf16[2,592,128]{2,1,0:T(8,128)(2,1)S(1)} %get-tuple-element.69), channel_id=1, source_target_pairs={{0,32},{32,0},{1,33},{33,1},{2,34},{34,2},{3,35},{35,3},{4,36},{36... | collective-permute-start | bytes 909320 | tf_op jit(solution)/shard_map/ppermute | solution.py:355
  27.4 11.9 %collective-permute-start.4 = (bf16[2,592,128]{2,1,0:T(8,128)(2,1)S(1)}, bf16[2,592,128]{2,1,0:T(8,128)(2,1)S(1)}, u32[]{:S(2)}, u32[]{:S(2)}) collective-permute-start(bf16[2,592,128]{2,1,0:T(8,128)(2,1)S(1)} %get-tuple-element.69), channel_id=1, source_target_pairs={{0,34},{2,32},{32,2},{34,0},{1,35},{3,33},{33,3},{35,1},{4,38},{6,... | collective-permute-start | bytes 909320 | tf_op jit(solution)/shard_map/ppermute | solution.py:356
  34.5 4.8 %collective-permute-start.5 = (bf16[2,592,128]{2,1,0:T(8,128)(2,1)S(1)}, bf16[2,592,128]{2,1,0:T(8,128)(2,1)S(1)}, u32[]{:S(2)}, u32[]{:S(2)}) collective-permute-start(bf16[2,592,128]{2,1,0:T(8,128)(2,1)S(1)} %get-tuple-element.42.p0), channel_id=1, source_target_pairs={{0,1},{1,0},{2,3},{3,2},{4,5},{5,4},{6,7},{7,6},{8,9},{9,8},{10,11... | collective-permute-start | bytes 909320 | tf_op jit(solution)/shard_map/ppermute | solution.py:369
  39.4 4.6 %collective-permute-start.6 = (bf16[6,592,128]{2,1,0:T(8,128)(2,1)S(1)}, bf16[6,592,128]{2,1,0:T(8,128)(2,1)S(1)}, u32[]{:S(2)}, u32[]{:S(2)}) collective-permute-start(bf16[6,592,128]{2,1,0:T(8,128)(2,1)S(1)} %shard_map.120), channel_id=1, source_target_pairs={{0,1},{1,0},{2,3},{3,2},{4,5},{5,4},{6,7},{7,6},{8,9},{9,8},{10,11... | collective-permute-start | bytes 2727944 | tf_op jit(solution)/shard_map/ppermute | solution.py:372
  44.0 6.0 %copy-start.1 = (bf16[3,160,768]{2,1,0:T(8,128)(2,1)S(1)}, bf16[3,160,768]{2,1,0:T(8,128)(2,1)}, u32[]{:S(2)}) copy-start(bf16[3,160,768]{2,1,0:T(8,128)(2,1)} %gate.1) | copy-start | bytes 2211844
  44.0 6.0 %copy-start.2 = (bf16[3,160,768]{2,1,0:T(8,128)(2,1)S(1)}, bf16[3,160,768]{2,1,0:T(8,128)(2,1)}, u32[]{:S(2)}) copy-start(bf16[3,160,768]{2,1,0:T(8,128)(2,1)} %up.1) | copy-start | bytes 2211844
  44.1 6.0 %copy-start.3 = (bf16[3,768,160]{1,2,0:T(8,128)(2,1)S(1)}, bf16[3,768,160]{1,2,0:T(8,128)(2,1)}, u32[]{:S(2)}) copy-start(bf16[3,768,160]{1,2,0:T(8,128)(2,1)} %param.23) | copy-start | bytes 2211844
  47.7 4.1 %collective-permute-start.7 = (bf16[128,2560]{1,0:T(8,128)(2,1)S(1)}, bf16[128,2560]{1,0:T(8,128)(2,1)S(1)}, u32[]{:S(2)}, u32[]{:S(2)}) collective-permute-start(bf16[128,2560]{1,0:T(8,128)(2,1)S(1)} %get-tuple-element.54), channel_id=1, source_target_pairs={{0,1},{1,0},{2,3},{3,2},{4,5},{5,4},{6,7},{7,6},{8,9},{9,8},{10,11... | collective-permute-start | bytes 1966088 | tf_op jit(solution)/shard_map/ppermute | solution.py:383
  51.8 14.3 %copy-start.13 = (s32[8,16,6]{1,0,2:T(8,128)S(1)}, s32[8,16,6]{1,0,2:T(8,128)}, u32[]{:S(2)}) copy-start(s32[8,16,6]{1,0,2:T(8,128)} %param.19) | copy-start | bytes 9220
  51.8 17.3 %copy-start.14 = (f32[2560]{0:T(1024)S(1)}, f32[2560]{0:T(1024)}, u32[]{:S(2)}) copy-start(f32[2560]{0:T(1024)} %param.18) | copy-start | bytes 30724
  51.8 34.0 %copy-start.10 = (bf16[8,2560]{1,0:T(8,128)(2,1)S(1)}, bf16[8,2560]{1,0:T(8,128)(2,1)}, u32[]{:S(2)}) copy-start(bf16[8,2560]{1,0:T(8,128)(2,1)} %residual.1) | copy-start | bytes 122884
  52.8 33.0 %all-to-all-start = ((bf16[16,8,2560]{2,1,0:T(8,128)(2,1)}), bf16[16,8,2560]{2,1,0:T(8,128)(2,1)S(1)}, u32[]{:S(2)}, u32[]{:S(2)}) async-start(bf16[16,8,2560]{2,1,0:T(8,128)(2,1)} %shard_map.123), calls=%async_computation | async-start | bytes 1310720 | tf_op jit(solution)/shard_map/all_to_all | solution.py:394
  66.3 29.4 %collective-permute-start.8 = (bf16[3,160,768]{2,1,0:T(8,128)(2,1)S(1)}, bf16[3,160,768]{2,1,0:T(8,128)(2,1)S(1)}, u32[]{:S(2)}, u32[]{:S(2)}) collective-permute-start(bf16[3,160,768]{2,1,0:T(8,128)(2,1)S(1)} %get-tuple-element.57), channel_id=1, source_target_pairs={{0,32},{32,0},{1,33},{33,1},{2,34},{34,2},{3,35},{35,3},{4,36},{36... | collective-permute-start | bytes 2211848 | tf_op jit(solution)/shard_map/ppermute | solution.py:392
  86.8 16.7 %all-to-all-start.1 = ((bf16[16,8,512]{2,1,0:T(8,128)(2,1)}), bf16[16,8,512]{2,1,0:T(8,128)(2,1)S(1)}, u32[]{:S(2)}, u32[]{:S(2)}) async-start(bf16[16,8,512]{2,1,0:T(8,128)(2,1)} %shard_map.125), calls=%async_computation.1 | async-start | bytes 262144 | tf_op jit(solution)/shard_map/all_to_all | solution.py:398
  95.7 9.1 %copy-start.4 = (bf16[3,160,768]{2,1,0:T(8,128)(2,1)}, bf16[3,160,768]{2,1,0:T(8,128)(2,1)S(1)}, u32[]{:S(2)}) copy-start(bf16[3,160,768]{2,1,0:T(8,128)(2,1)S(1)} %collective-permute-done.8.got) | copy-start | bytes 2211844
  104.8 27.2 %all-to-all-start.2 = ((bf16[32,80,128]{2,1,0:T(8,128)(2,1)}), bf16[32,80,128]{2,1,0:T(8,128)(2,1)S(1)}, u32[]{:S(2)}, u32[]{:S(2)}) async-start(bf16[32,80,128]{2,1,0:T(8,128)(2,1)} %shard_map.126), calls=%async_computation.2 | async-start | bytes 1310720 | tf_op jit(solution)/shard_map/all_to_all | solution.py:427
  111.4 18.6 %collective-permute-start.9 = (bf16[3,160,384]{2,1,0:T(8,128)(2,1)}, bf16[3,160,384]{2,1,0:T(8,128)(2,1)S(1)}, u32[]{:S(2)}, u32[]{:S(2)}) collective-permute-start(bf16[3,160,384]{2,1,0:T(8,128)(2,1)} %get-tuple-element.63), channel_id=1, source_target_pairs={{0,32},{32,0},{1,33},{33,1},{2,34},{34,2},{3,35},{35,3},{4,36},{36... | collective-permute-start | bytes 1105928 | tf_op jit(solution)/shard_map/ppermute | solution.py:400
  115.1 14.9 %copy-start.7 = (bf16[3,160,384]{2,1,0:T(8,128)(2,1)S(1)}, bf16[3,160,384]{2,1,0:T(8,128)(2,1)}, u32[]{:S(2)}) copy-start(bf16[3,160,384]{2,1,0:T(8,128)(2,1)} %copy-done.6) | copy-start | bytes 1105924
  201.5 9.3 %copy-start.12 = (f32[8,16,6]{1,0,2:T(8,128)S(1)}, f32[8,16,6]{1,0,2:T(8,128)}, u32[]{:S(2)}) copy-start(f32[8,16,6]{1,0,2:T(8,128)} %param.20) | copy-start | bytes 9220
  203.8 27.2 %all-to-all-start.5 = ((bf16[32,80,128]{2,1,0:T(8,128)(2,1)}), bf16[32,80,128]{2,1,0:T(8,128)(2,1)S(1)}, u32[]{:S(2)}, u32[]{:S(2)}) async-start(bf16[32,80,128]{2,1,0:T(8,128)(2,1)} %shard_map.131), calls=%async_computation.5 | async-start | bytes 1310720 | tf_op jit(solution)/shard_map/all_to_all | solution.py:438
  231.6 6.2 %collective-permute-start.10 = (bf16[128,160]{1,0:T(8,128)(2,1)S(1)}, bf16[128,160]{1,0:T(8,128)(2,1)S(1)}, u32[]{:S(2)}, u32[]{:S(2)}) collective-permute-start(bf16[128,160]{1,0:T(8,128)(2,1)S(1)} %get-tuple-element.68), channel_id=1, source_target_pairs={{0,32},{32,0},{1,33},{33,1},{2,34},{34,2},{3,35},{35,3},{4,36},{36... | collective-permute-start | bytes 122888 | tf_op jit(solution)/shard_map/ppermute | solution.py:442
  (6 other events, 9.3 us)

commit v13 on v12

--- a/solution.py
+++ b/solution.py
@@ -30,10 +30,6 @@
     own[width:, :] = jnp.where(segments[...] == mark, 1.0, 0.0).astype(bf16)
 
 
-def keys_of(chunk):
-    return chunk[...] if len(chunk.shape) == 2 else jnp.concatenate([chunk[0], chunk[1]], axis=1)
-
-
 def nt_dot(a, b):
     return lax.dot_general(a, b, (((1,), (1,)), ((), ())), preferred_element_type=f32)
 
@@ -42,7 +38,7 @@
     scale = QKDIM ** (-0.5)
     peak = jnp.full((256, 128), -FAR, f32) if old is None else old[0]
     for n, (chunk, bias) in enumerate(zip(chunks, biases)):
-        part = bias(jnp.dot(rows, keys_of(chunk), preferred_element_type=f32) * scale)
+        part = bias(jnp.dot(rows, chunk[...], preferred_element_type=f32) * scale)
         scores[:, n * 256 : (n + 1) * 256] = part
         peak = jnp.maximum(peak, jnp.maximum(part[:, :128], part[:, 128:]))
     peak = jnp.max(peak, axis=1, keepdims=True)
@@ -54,18 +50,12 @@
     for n, chunk in enumerate(chunks):
         terms = jnp.exp(scores[:, n * 256 : (n + 1) * 256] - peak)
         sums = sums + terms[:, :128] + terms[:, 128:]
-        mixed = mixed + nt_dot(terms.astype(bf16), keys_of(chunk)[:LATENT])
+        mixed = mixed + nt_dot(terms.astype(bf16), chunk[:LATENT, :])
     return jnp.broadcast_to(peak, (256, 128)), sums, mixed
 
 
-def valid_bias(info, piece):
-    def bias(part):
-        lane = lax.broadcasted_iota(i32, (256, 256), 1)
-        first = jnp.where(info[2 * piece] >= 0, 0.0, -FAR)
-        second = jnp.where(info[2 * piece + 1] >= 0, 0.0, -FAR)
-        return part + jnp.where(lane < 128, first, second)
-
-    return bias
+def valid_bias(info, n):
+    return lambda part: part + jnp.where(info[n] >= 0, 0.0, -FAR)
 
 
 def causal_bias(part):
@@ -88,7 +78,7 @@
 ):
     for head in range(2):
         old = old_peak[head], old_sums[head], old_mixed[head]
-        biases = [valid_bias(info, n) for n in (1, 2, 3, 0)]
+        biases = [valid_bias(info, n) for n in (1, 2, 3, 4)]
         state = attend_chunks(query[head], [p1, p2, p3, o0], biases, scores.at[head], old)
         peak[head], sums[head], mixed[head] = state
 
@@ -100,8 +90,8 @@
 
     for head in range(2):
         old = old_peak[head], old_sums[head], old_mixed[head]
-        chunks = [others.at[2 * n : 2 * n + 2] for n in range(3)]
-        biases = [valid_bias(info, n) for n in (1, 2, 3)]
+        chunks = [others.at[n] for n in range(3)]
+        biases = [valid_bias(info, n) for n in (5, 6, 7)]
         _, sums, mixed = attend_chunks(query[head], chunks, biases, scores.at[head], old)
         mixed = (mixed / jnp.sum(sums, axis=1, keepdims=True)).astype(bf16)
         values[head] = jnp.dot(mixed, value_up[head], preferred_element_type=f32).astype(bf16)
@@ -124,7 +114,7 @@
 
 def gather_kernel(p1, p2, p3, out):
     for n, piece in enumerate((p1, p2, p3)):
-        out[2 * n : 2 * n + 2] = piece[...]
+        out[n] = piece[...]
 
 
 def norm_kernel(spread, residual, gain, packed):
@@ -305,31 +295,22 @@
     keys_own = call(keys_kernel, [sds((KEYW, block_len), bf16)], count=2)(
         latent.T, segment_ids[None, :]
     )
-    mine = lax.dynamic_slice_in_dim(keys_own, core * half, half, 1)
-
-    def along_y(near, far):
-        pairs = [
-            (2 * i + h, 2 * ((i + (near, far)[h]) % 8) + h) for i in range(8) for h in range(2)
-        ]
-        return lax.ppermute(mine, ("y", "xh"), pairs)
-
-    near, far = along_y(1, 2), along_y(3, 4)
-
-    def blocks_of(x, h):
-        return [2 * (y - 1 - h) + x, 2 * (y - 3 - h) + x]
-
-    def blocks_sent(x, h):
-        early, late = blocks_of(x, h)
-        odd = (x == 0) & (h == 1)
-        return [jnp.where(odd, 2 * y, early), jnp.where(odd, early, late)]
-
-    info = jnp.stack(
-        blocks_of(xl, xh)
-        + blocks_of(xl, 1 - xh)
-        + blocks_sent(1 - xl, xh)
-        + blocks_sent(1 - xl, 1 - xh)
-        + [core, xl]
-    ).astype(i32)
+    pairs = [
+        (4 * i + j, 4 * ((i + 1 + j // 2 + 2 * (j % 2)) % 8) + j) for i in range(8) for j in range(4)
+    ]
+    fetched = lax.ppermute(keys_own, ("y", "xh", "core"), pairs)
+
+    def block_of(x, h, c):
+        return 2 * (y - 1 - h - 2 * c) + x
+
+    def block_sent(x, h, c):
+        return jnp.where((x == 0) & (h == 1) & (c == 1), 2 * y, block_of(x, h, c))
+
+    def blocks_held(c):
+        own = [block_of(xl, xh, c), block_of(xl, 1 - xh, c)]
+        return own + [block_sent(1 - xl, xh, c), block_sent(1 - xl, 1 - xh, c)]
+
+    info = jnp.stack(blocks_held(core) + blocks_held(1 - core) + [core, xl]).astype(i32)
 
     masks = jnp.where(own_segment, 0.0, -FAR).astype(bf16)
     query_rows = jnp.concatenate(
@@ -342,16 +323,13 @@
     )
     query_rows = query_rows.reshape(16, 2, 8, local_heads, KEYW).transpose(3, 1, 0, 2, 4)
     query_rows = query_rows.reshape(local_heads, block_len, KEYW)
-    near, far, query_rows = lax.optimization_barrier((near, far, query_rows))
-
-    column = jnp.stack([near, far])
-    to_other = jnp.where(
-        (xl == 0) & (xh == 1), jnp.stack([mine, column[0]]), column
-    )
+    fetched, query_rows = lax.optimization_barrier((fetched, query_rows))
+
+    to_other = jnp.where((xl == 0) & (xh == 1) & (core == 1), keys_own, fetched)
     diagonal = [(0, 3), (1, 2), (2, 1), (3, 0)]
     pieces = [
-        column,
-        lax.ppermute(column, "xh", SWAP),
+        fetched,
+        lax.ppermute(fetched, "xh", SWAP),
         lax.ppermute(to_other, "xl", SWAP),
         lax.ppermute(to_other, ("xl", "xh"), diagonal),
     ]
@@ -363,12 +341,12 @@
     ]
     state = call(
         first_attention_kernel, state_out, [pltpu.VMEM((2, 256, 2 * 256), f32)], True, 4
-    )(info, query_rows, keys_own, column)
-    pieces[1], column_late, peak = lax.optimization_barrier((pieces[1], column, state[0]))
+    )(info, query_rows, keys_own, fetched)
+    pieces[1], fetched_late, peak = lax.optimization_barrier((pieces[1], fetched, state[0]))
     state = [peak] + list(state[1:])
-    first_other = lax.ppermute(column_late, "core", SWAP)
+    first_other = lax.ppermute(fetched_late, "core", SWAP)
     *pieces, first_other = lax.optimization_barrier((*pieces, first_other))
-    three = call(gather_kernel, [sds((6, KEYW, half), bf16)], count=3)(*pieces[1:])
+    three = call(gather_kernel, [sds((3, KEYW, block_len), bf16)], count=3)(*pieces[1:])
     others = lax.ppermute(three, "core", SWAP)
     state = call(
         second_attention_kernel, state_out, [pltpu.VMEM((2, 256, 4 * 256), f32)], True, 9

time: 241 us -> 241 us (level)
  waiting for transfers between devices: 74.6 us -> 78.4 us
  starting transfers between devices: 70.5 us -> 67 us
    ppermute x4 -> x3, starting transfers between devices: 15.1 us -> 11.4 us  [the longest x1 5.01 us: on_device(): lax.ppermute(fetched, 'xh', SWAP)]
    ppermute x4 -> x3, waiting for transfers between devices: 8.71 us -> 11.6 us  [the longest x1 10.6 us: on_device(): fetched = lax.ppermute(keys_own, ('y', 'xh', 'core'), pairs)]
  transfers between devices with their start and end apart: 15 -> 14, of which waited for: 11 -> 11; matrix products, arithmetic and copies ran while one was open for 2% -> 2% of each run, Pallas kernels for 3% -> 3%
where the time goes in v13:
time: 241 us; the launch traced here: 239 us
  waiting for transfers between devices  78.4 us (33%)
  starting transfers between devices  67 us (28%)
  blocking collectives  67 us (28%)
  Pallas kernels  18.4 us (8%)
  local copies, waits for them, and re-layouts  4.88 us (2%)
    all_to_all x1, blocking collectives, on_device(): lax.all_to_all(pre.reshape(8, 128, 2 * ff_half), 'y', split_axis=0, conca...  42.6 us
    all_to_all x1, blocking collectives, on_device(): lax.all_to_all(hidden, 'y', split_axis=0, concat_axis=0, tiled=True)  24.4 us
    all_to_all x1, waiting for transfers between devices, on_device(): lax.all_to_all(expert_out, EXP, split_axis=0, concat_axis=0, tiled=True)  19.6 us
    all_to_all x1, waiting for transfers between devices, on_device(): lax.all_to_all(pair_sum, ('z', 'xh'), split_axis=0, concat_axis=0, tiled=...  16.5 us
    ppermute x1, waiting for transfers between devices, on_device(): down_got = lax.ppermute(down_send, 'xl', SWAP)  14.8 us
    all_to_all x1, starting transfers between devices, on_device(): lax.all_to_all(pair_sum, ('z', 'xh'), split_axis=0, concat_axis=0, tiled=...  13.3 us
    ppermute x1, waiting for transfers between devices, on_device(): fetched = lax.ppermute(keys_own, ('y', 'xh', 'core'), pairs)  10.6 us
    all_to_all x1, starting transfers between devices, on_device(): split = lax.all_to_all(packed, CTX, split_axis=0, concat_axis=0, tiled=True)  10 us
  transfers between devices with their start and end apart: 14, of which 11 were waited for; matrix products, arithmetic and copies ran while one was open for 2% of the time, Pallas kernels for 3%

profile of v13, /device:TPU:6, one launch (start us, length us, event | category | flops | bytes accessed | tf_op | source)
XLA Modules:
  0.0 238.6 jit_solution(12870976096920671614)
XLA Ops:
  1.7 4.5 %collective-permute-start = (bf16[592,256]{1,0:T(8,128)(2,1)S(1)}, bf16[592,256]{1,0:T(8,128)(2,1)S(1)}, u32[]{:S(2)}, u32[]{:S(2)}) collective-permute-start(bf16[592,256]{1,0:T(8,128)(2,1)S(1)} %shard_map.118.own), channel_id=1, source_target_pairs={{0,64},{1,193},{2,130},{3,259},{64,128},{65,257},{66,194},{67,323}... | collective-permute-start | bytes 909320 | tf_op jit(solution)/shard_map/ppermute | solution.py:301
  8.0 10.6 %collective-permute-done.p0 = bf16[592,256]{1,0:T(8,128)(2,1)S(1)} collective-permute-done((bf16[592,256]{1,0:T(8,128)(2,1)S(1)}, bf16[592,256]{1,0:T(8,128)(2,1)S(1)}, u32[]{:S(2)}, u32[]{:S(2)}) %collective-permute-start) | collective-permute-done | bytes 303136 | tf_op jit(solution)/shard_map/ppermute | solution.py:301
  18.6 5.0 %collective-permute-start.1 = (bf16[592,256]{1,0:T(8,128)(2,1)S(1)}, bf16[592,256]{1,0:T(8,128)(2,1)S(1)}, u32[]{:S(2)}, u32[]{:S(2)}) collective-permute-start(bf16[592,256]{1,0:T(8,128)(2,1)S(1)} %collective-permute-done.p0), channel_id=1, source_target_pairs={{0,2},{2,0},{1,3},{3,1},{4,6},{6,4},{5,7},{7,5},{8,10},{10,8},{9,1... | collective-permute-start | bytes 909320 | tf_op jit(solution)/shard_map/ppermute | solution.py:332
  23.8 3.6 %collective-permute-start.2 = (bf16[592,256]{1,0:T(8,128)(2,1)S(1)}, bf16[592,256]{1,0:T(8,128)(2,1)S(1)}, u32[]{:S(2)}, u32[]{:S(2)}) collective-permute-start(bf16[592,256]{1,0:T(8,128)(2,1)S(1)} %broadcast_select_fusion), channel_id=1, source_target_pairs={{0,32},{32,0},{1,33},{33,1},{2,34},{34,2},{3,35},{35,3},{4,36},{36... | collective-permute-start | bytes 909320 | tf_op jit(solution)/shard_map/ppermute | solution.py:333
  34.0 2.7 %collective-permute-done.2.p2 = bf16[592,256]{1,0:T(8,128)(2,1)S(1)} collective-permute-done((bf16[592,256]{1,0:T(8,128)(2,1)S(1)}, bf16[592,256]{1,0:T(8,128)(2,1)S(1)}, u32[]{:S(2)}, u32[]{:S(2)}) %collective-permute-start.2) | collective-permute-done | bytes 303136 | tf_op jit(solution)/shard_map/ppermute | solution.py:333
  39.9 2.6 %shard_map.121 = (f32[2,256,128]{2,1,0:T(8,128)S(1)}, f32[2,256,128]{2,1,0:T(8,128)S(1)}, f32[2,256,512]{2,1,0:T(8,128)S(1)}) custom-call(s32[10]{0:T(128)S(1)} %stack.43.info, bf16[2,256,592]{2,1,0:T(8,128)(2,1)S(1)} %bitcast.37, bf16[592,256]{1,0:T(8,128)(2,1)S(1)} %collective-permute-done.1.p1, bf16[592,256]{1,0:T(8,128)(2,1)S(1)} %collective-permute-done.2.p2, ...), custom_call_target="tpu_custom_call" | custom-call | tf_op jit(solution)/shard_map/pallas_call | solution.py:351
  42.6 3.6 %shard_map.122 = (bf16[128,2560]{1,0:T(8,128)(2,1)S(1)}, f32[128,2560]{1,0:T(8,128)S(1)}) custom-call(s32[10]{0:T(128)S(1)} %stack.43.info, bf16[2,256,592]{2,1,0:T(8,128)(2,1)S(1)} %bitcast.38, bf16[3,592,256]{2,1,0:T(8,128)(2,1)S(1)} %collective-permute-done.5.others, f32[2,256,128]{2,1,0:T(8,128)S(1)} %get-tuple-element.48.old_peak, ...), custom_call_target="tpu_custom_call" | custom-call | tf_op jit(solution)/shard_map/pallas_call | solution.py:354
  46.2 2.4 %collective-permute-start.6 = (bf16[128,2560]{1,0:T(8,128)(2,1)S(1)}, bf16[128,2560]{1,0:T(8,128)(2,1)S(1)}, u32[]{:S(2)}, u32[]{:S(2)}) collective-permute-start(bf16[128,2560]{1,0:T(8,128)(2,1)S(1)} %get-tuple-element.52), channel_id=1, source_target_pairs={{0,1},{1,0},{2,3},{3,2},{4,5},{5,4},{6,7},{7,6},{8,9},{9,8},{10,11... | collective-permute-start | bytes 1966088 | tf_op jit(solution)/shard_map/ppermute | solution.py:361
  51.3 13.3 %all-to-all-start = ((bf16[16,8,2560]{2,1,0:T(8,128)(2,1)}), bf16[16,8,2560]{2,1,0:T(8,128)(2,1)S(1)}, u32[]{:S(2)}, u32[]{:S(2)}) async-start(bf16[16,8,2560]{2,1,0:T(8,128)(2,1)} %shard_map.123), calls=%async_computation | async-start | bytes 1310720 | tf_op jit(solution)/shard_map/all_to_all | solution.py:372
  64.8 2.7 %collective-permute-start.7 = (bf16[3,160,768]{2,1,0:T(8,128)(2,1)S(1)}, bf16[3,160,768]{2,1,0:T(8,128)(2,1)S(1)}, u32[]{:S(2)}, u32[]{:S(2)}) collective-permute-start(bf16[3,160,768]{2,1,0:T(8,128)(2,1)S(1)} %get-tuple-element.55), channel_id=1, source_target_pairs={{0,32},{32,0},{1,33},{33,1},{2,34},{34,2},{3,35},{35,3},{4,36},{36... | collective-permute-start | bytes 2211848 | tf_op jit(solution)/shard_map/ppermute | solution.py:370
  67.8 16.5 %all-to-all-done.spread = bf16[16,8,2560]{2,1,0:T(8,128)(2,1)S(1)} async-done(((bf16[16,8,2560]{2,1,0:T(8,128)(2,1)}), bf16[16,8,2560]{2,1,0:T(8,128)(2,1)S(1)}, u32[]{:S(2)}, u32[]{:S(2)}) %all-to-all-start) | async-done | bytes 655392 | tf_op jit(solution)/shard_map/all_to_all | solution.py:372
  85.3 10.0 %all-to-all-start.1 = ((bf16[16,8,512]{2,1,0:T(8,128)(2,1)}), bf16[16,8,512]{2,1,0:T(8,128)(2,1)S(1)}, u32[]{:S(2)}, u32[]{:S(2)}) async-start(bf16[16,8,512]{2,1,0:T(8,128)(2,1)} %shard_map.125), calls=%async_computation.1 | async-start | bytes 262144 | tf_op jit(solution)/shard_map/all_to_all | solution.py:376
  95.9 7.8 %all-to-all-done.1 = bf16[16,8,512]{2,1,0:T(8,128)(2,1)S(1)} async-done(((bf16[16,8,512]{2,1,0:T(8,128)(2,1)}), bf16[16,8,512]{2,1,0:T(8,128)(2,1)S(1)}, u32[]{:S(2)}, u32[]{:S(2)}) %all-to-all-start.1) | async-done | bytes 131104 | tf_op jit(solution)/shard_map/all_to_all | solution.py:376
  105.0 6.6 %all-to-all-start.2 = ((bf16[32,80,128]{2,1,0:T(8,128)(2,1)}), bf16[32,80,128]{2,1,0:T(8,128)(2,1)S(1)}, u32[]{:S(2)}, u32[]{:S(2)}) async-start(bf16[32,80,128]{2,1,0:T(8,128)(2,1)} %shard_map.126), calls=%async_computation.2 | async-start | bytes 1310720 | tf_op jit(solution)/shard_map/all_to_all | solution.py:405
  111.6 2.6 %collective-permute-start.8 = (bf16[3,160,384]{2,1,0:T(8,128)(2,1)}, bf16[3,160,384]{2,1,0:T(8,128)(2,1)S(1)}, u32[]{:S(2)}, u32[]{:S(2)}) collective-permute-start(bf16[3,160,384]{2,1,0:T(8,128)(2,1)} %get-tuple-element.61), channel_id=1, source_target_pairs={{0,32},{32,0},{1,33},{33,1},{2,34},{34,2},{3,35},{35,3},{4,36},{36... | collective-permute-start | bytes 1105928 | tf_op jit(solution)/shard_map/ppermute | solution.py:378
  115.4 14.8 %collective-permute-done.8.got = bf16[3,160,384]{2,1,0:T(8,128)(2,1)S(1)} collective-permute-done((bf16[3,160,384]{2,1,0:T(8,128)(2,1)}, bf16[3,160,384]{2,1,0:T(8,128)(2,1)S(1)}, u32[]{:S(2)}, u32[]{:S(2)}) %collective-permute-start.8) | collective-permute-done | bytes 368672 | tf_op jit(solution)/shard_map/ppermute | solution.py:378
  132.2 2.2 shard_map.129
  134.4 42.6 %all_to_all.30.parts = bf16[8,128,768]{2,1,0:T(8,128)(2,1)S(1)} all-to-all(bf16[8,128,768]{2,1,0:T(8,128)(2,1)S(1)} %bitcast.39), channel_id=1, replica_groups=mesh['y'=8,'xl'=2,'z'=8,'xh'=2,'core'=2] {'y'}, dimensions={0} | all-to-all | bytes 3145728 | tf_op jit(solution)/shard_map/all_to_all | solution.py:408
  177.2 24.4 %all_to_all.31 = bf16[8,128,384]{2,1,0:T(8,128)(2,1)S(1)} all-to-all(bf16[8,128,384]{2,1,0:T(8,128)(2,1)S(1)} %shard_map.130), channel_id=1, replica_groups=mesh['y'=8,'xl'=2,'z'=8,'xh'=2,'core'=2] {'y'}, dimensions={0} | all-to-all | bytes 1572864 | tf_op jit(solution)/shard_map/all_to_all | solution.py:412
  201.7 2.4 shard_map.131
  204.0 6.6 %all-to-all-start.5 = ((bf16[32,80,128]{2,1,0:T(8,128)(2,1)}), bf16[32,80,128]{2,1,0:T(8,128)(2,1)S(1)}, u32[]{:S(2)}, u32[]{:S(2)}) async-start(bf16[32,80,128]{2,1,0:T(8,128)(2,1)} %shard_map.131), calls=%async_computation.5 | async-start | bytes 1310720 | tf_op jit(solution)/shard_map/all_to_all | solution.py:416
  211.6 19.6 %all-to-all-done.5.returned = bf16[32,80,128]{2,1,0:T(8,128)(2,1)S(1)} async-done(((bf16[32,80,128]{2,1,0:T(8,128)(2,1)}), bf16[32,80,128]{2,1,0:T(8,128)(2,1)S(1)}, u32[]{:S(2)}, u32[]{:S(2)}) %all-to-all-start.5) | async-done | bytes 655392 | tf_op jit(solution)/shard_map/all_to_all | solution.py:416
  231.8 3.9 %collective-permute-start.9 = (bf16[128,160]{1,0:T(8,128)(2,1)S(1)}, bf16[128,160]{1,0:T(8,128)(2,1)S(1)}, u32[]{:S(2)}, u32[]{:S(2)}) collective-permute-start(bf16[128,160]{1,0:T(8,128)(2,1)S(1)} %get-tuple-element.66), channel_id=1, source_target_pairs={{0,32},{32,0},{1,33},{33,1},{2,34},{34,2},{3,35},{35,3},{4,36},{36... | collective-permute-start | bytes 122888 | tf_op jit(solution)/shard_map/ppermute | solution.py:420
  235.7 2.3 collective-permute-done.9
  (79 shorter events, 24.8 us)
Async XLA Ops:
  1.7 16.9 %collective-permute-start = (bf16[592,256]{1,0:T(8,128)(2,1)S(1)}, bf16[592,256]{1,0:T(8,128)(2,1)S(1)}, u32[]{:S(2)}, u32[]{:S(2)}) collective-permute-start(bf16[592,256]{1,0:T(8,128)(2,1)S(1)} %shard_map.118.own), channel_id=1, source_target_pairs={{0,64},{1,193},{2,130},{3,259},{64,128},{65,257},{66,194},{67,323}... | collective-permute-start | bytes 909320 | tf_op jit(solution)/shard_map/ppermute | solution.py:301
  18.6 13.5 %collective-permute-start.1 = (bf16[592,256]{1,0:T(8,128)(2,1)S(1)}, bf16[592,256]{1,0:T(8,128)(2,1)S(1)}, u32[]{:S(2)}, u32[]{:S(2)}) collective-permute-start(bf16[592,256]{1,0:T(8,128)(2,1)S(1)} %collective-permute-done.p0), channel_id=1, source_target_pairs={{0,2},{2,0},{1,3},{3,1},{4,6},{6,4},{5,7},{7,5},{8,10},{10,8},{9,1... | collective-permute-start | bytes 909320 | tf_op jit(solution)/shard_map/ppermute | solution.py:332
  23.8 12.9 %collective-permute-start.2 = (bf16[592,256]{1,0:T(8,128)(2,1)S(1)}, bf16[592,256]{1,0:T(8,128)(2,1)S(1)}, u32[]{:S(2)}, u32[]{:S(2)}) collective-permute-start(bf16[592,256]{1,0:T(8,128)(2,1)S(1)} %broadcast_select_fusion), channel_id=1, source_target_pairs={{0,32},{32,0},{1,33},{33,1},{2,34},{34,2},{3,35},{35,3},{4,36},{36... | collective-permute-start | bytes 909320 | tf_op jit(solution)/shard_map/ppermute | solution.py:333
  27.4 10.4 %collective-permute-start.3 = (bf16[592,256]{1,0:T(8,128)(2,1)S(1)}, bf16[592,256]{1,0:T(8,128)(2,1)S(1)}, u32[]{:S(2)}, u32[]{:S(2)}) collective-permute-start(bf16[592,256]{1,0:T(8,128)(2,1)S(1)} %broadcast_select_fusion), channel_id=1, source_target_pairs={{0,34},{2,32},{32,2},{34,0},{1,35},{3,33},{33,3},{35,1},{4,38},{6,... | collective-permute-start | bytes 909320 | tf_op jit(solution)/shard_map/ppermute | solution.py:334
  32.1 5.7 %collective-permute-start.4 = (bf16[592,256]{1,0:T(8,128)(2,1)S(1)}, bf16[592,256]{1,0:T(8,128)(2,1)S(1)}, u32[]{:S(2)}, u32[]{:S(2)}) collective-permute-start(bf16[592,256]{1,0:T(8,128)(2,1)S(1)} %collective-permute-done.p0), channel_id=1, source_target_pairs={{0,1},{1,0},{2,3},{3,2},{4,5},{5,4},{6,7},{7,6},{8,9},{9,8},{10,11... | collective-permute-start | bytes 909320 | tf_op jit(solution)/shard_map/ppermute | solution.py:347
  37.9 4.6 %collective-permute-start.5 = (bf16[3,592,256]{2,1,0:T(8,128)(2,1)S(1)}, bf16[3,592,256]{2,1,0:T(8,128)(2,1)S(1)}, u32[]{:S(2)}, u32[]{:S(2)}) collective-permute-start(bf16[3,592,256]{2,1,0:T(8,128)(2,1)S(1)} %shard_map.120), channel_id=1, source_target_pairs={{0,1},{1,0},{2,3},{3,2},{4,5},{5,4},{6,7},{7,6},{8,9},{9,8},{10,11... | collective-permute-start | bytes 2727944 | tf_op jit(solution)/shard_map/ppermute | solution.py:350
  39.8 2.7 %copy-start = (bf16[256,2560]{1,0:T(8,128)(2,1)S(1)}, bf16[256,2560]{1,0:T(8,128)(2,1)}, u32[]{:S(2)}) copy-start(bf16[256,2560]{1,0:T(8,128)(2,1)} %out_proj.1) | copy-start | bytes 3932164
  42.5 6.0 %copy-start.1 = (bf16[3,160,768]{2,1,0:T(8,128)(2,1)S(1)}, bf16[3,160,768]{2,1,0:T(8,128)(2,1)}, u32[]{:S(2)}) copy-start(bf16[3,160,768]{2,1,0:T(8,128)(2,1)} %gate.1) | copy-start | bytes 2211844
  42.6 6.0 %copy-start.2 = (bf16[3,160,768]{2,1,0:T(8,128)(2,1)S(1)}, bf16[3,160,768]{2,1,0:T(8,128)(2,1)}, u32[]{:S(2)}) copy-start(bf16[3,160,768]{2,1,0:T(8,128)(2,1)} %up.1) | copy-start | bytes 2211844
  42.6 6.0 %copy-start.3 = (bf16[3,768,160]{1,2,0:T(8,128)(2,1)S(1)}, bf16[3,768,160]{1,2,0:T(8,128)(2,1)}, u32[]{:S(2)}) copy-start(bf16[3,768,160]{1,2,0:T(8,128)(2,1)} %param.23) | copy-start | bytes 2211844
  46.2 4.1 %collective-permute-start.6 = (bf16[128,2560]{1,0:T(8,128)(2,1)S(1)}, bf16[128,2560]{1,0:T(8,128)(2,1)S(1)}, u32[]{:S(2)}, u32[]{:S(2)}) collective-permute-start(bf16[128,2560]{1,0:T(8,128)(2,1)S(1)} %get-tuple-element.52), channel_id=1, source_target_pairs={{0,1},{1,0},{2,3},{3,2},{4,5},{5,4},{6,7},{7,6},{8,9},{9,8},{10,11... | collective-permute-start | bytes 1966088 | tf_op jit(solution)/shard_map/ppermute | solution.py:361
  50.3 14.3 %copy-start.13 = (s32[8,16,6]{1,0,2:T(8,128)S(1)}, s32[8,16,6]{1,0,2:T(8,128)}, u32[]{:S(2)}) copy-start(s32[8,16,6]{1,0,2:T(8,128)} %param.19) | copy-start | bytes 9220
  50.3 17.3 %copy-start.14 = (f32[2560]{0:T(1024)S(1)}, f32[2560]{0:T(1024)}, u32[]{:S(2)}) copy-start(f32[2560]{0:T(1024)} %param.18) | copy-start | bytes 30724
  50.3 34.0 %copy-start.10 = (bf16[8,2560]{1,0:T(8,128)(2,1)S(1)}, bf16[8,2560]{1,0:T(8,128)(2,1)}, u32[]{:S(2)}) copy-start(bf16[8,2560]{1,0:T(8,128)(2,1)} %residual.1) | copy-start | bytes 122884
  51.3 33.0 %all-to-all-start = ((bf16[16,8,2560]{2,1,0:T(8,128)(2,1)}), bf16[16,8,2560]{2,1,0:T(8,128)(2,1)S(1)}, u32[]{:S(2)}, u32[]{:S(2)}) async-start(bf16[16,8,2560]{2,1,0:T(8,128)(2,1)} %shard_map.123), calls=%async_computation | async-start | bytes 1310720 | tf_op jit(solution)/shard_map/all_to_all | solution.py:372
  64.8 31.0 %collective-permute-start.7 = (bf16[3,160,768]{2,1,0:T(8,128)(2,1)S(1)}, bf16[3,160,768]{2,1,0:T(8,128)(2,1)S(1)}, u32[]{:S(2)}, u32[]{:S(2)}) collective-permute-start(bf16[3,160,768]{2,1,0:T(8,128)(2,1)S(1)} %get-tuple-element.55), channel_id=1, source_target_pairs={{0,32},{32,0},{1,33},{33,1},{2,34},{34,2},{3,35},{35,3},{4,36},{36... | collective-permute-start | bytes 2211848 | tf_op jit(solution)/shard_map/ppermute | solution.py:370
  85.3 18.4 %all-to-all-start.1 = ((bf16[16,8,512]{2,1,0:T(8,128)(2,1)}), bf16[16,8,512]{2,1,0:T(8,128)(2,1)S(1)}, u32[]{:S(2)}, u32[]{:S(2)}) async-start(bf16[16,8,512]{2,1,0:T(8,128)(2,1)} %shard_map.125), calls=%async_computation.1 | async-start | bytes 262144 | tf_op jit(solution)/shard_map/all_to_all | solution.py:376
  95.9 9.1 %copy-start.4 = (bf16[3,160,768]{2,1,0:T(8,128)(2,1)}, bf16[3,160,768]{2,1,0:T(8,128)(2,1)S(1)}, u32[]{:S(2)}) copy-start(bf16[3,160,768]{2,1,0:T(8,128)(2,1)S(1)} %collective-permute-done.7.got) | copy-start | bytes 2211844
  105.0 27.2 %all-to-all-start.2 = ((bf16[32,80,128]{2,1,0:T(8,128)(2,1)}), bf16[32,80,128]{2,1,0:T(8,128)(2,1)S(1)}, u32[]{:S(2)}, u32[]{:S(2)}) async-start(bf16[32,80,128]{2,1,0:T(8,128)(2,1)} %shard_map.126), calls=%async_computation.2 | async-start | bytes 1310720 | tf_op jit(solution)/shard_map/all_to_all | solution.py:405
  111.6 18.6 %collective-permute-start.8 = (bf16[3,160,384]{2,1,0:T(8,128)(2,1)}, bf16[3,160,384]{2,1,0:T(8,128)(2,1)S(1)}, u32[]{:S(2)}, u32[]{:S(2)}) collective-permute-start(bf16[3,160,384]{2,1,0:T(8,128)(2,1)} %get-tuple-element.61), channel_id=1, source_target_pairs={{0,32},{32,0},{1,33},{33,1},{2,34},{34,2},{3,35},{35,3},{4,36},{36... | collective-permute-start | bytes 1105928 | tf_op jit(solution)/shard_map/ppermute | solution.py:378
  115.3 14.9 %copy-start.7 = (bf16[3,160,384]{2,1,0:T(8,128)(2,1)S(1)}, bf16[3,160,384]{2,1,0:T(8,128)(2,1)}, u32[]{:S(2)}) copy-start(bf16[3,160,384]{2,1,0:T(8,128)(2,1)} %copy-done.6) | copy-start | bytes 1105924
  201.7 9.3 %copy-start.12 = (f32[8,16,6]{1,0,2:T(8,128)S(1)}, f32[8,16,6]{1,0,2:T(8,128)}, u32[]{:S(2)}) copy-start(f32[8,16,6]{1,0,2:T(8,128)} %param.20) | copy-start | bytes 9220
  204.0 27.2 %all-to-all-start.5 = ((bf16[32,80,128]{2,1,0:T(8,128)(2,1)}), bf16[32,80,128]{2,1,0:T(8,128)(2,1)S(1)}, u32[]{:S(2)}, u32[]{:S(2)}) async-start(bf16[32,80,128]{2,1,0:T(8,128)(2,1)} %shard_map.131), calls=%async_computation.5 | async-start | bytes 1310720 | tf_op jit(solution)/shard_map/all_to_all | solution.py:416
  231.8 6.2 %collective-permute-start.9 = (bf16[128,160]{1,0:T(8,128)(2,1)S(1)}, bf16[128,160]{1,0:T(8,128)(2,1)S(1)}, u32[]{:S(2)}, u32[]{:S(2)}) collective-permute-start(bf16[128,160]{1,0:T(8,128)(2,1)S(1)} %get-tuple-element.66), channel_id=1, source_target_pairs={{0,32},{32,0},{1,33},{33,1},{2,34},{34,2},{3,35},{35,3},{4,36},{36... | collective-permute-start | bytes 122888 | tf_op jit(solution)/shard_map/ppermute | solution.py:420
  (5 other events, 6.6 us)

commit v14 on v13

--- a/solution.py
+++ b/solution.py
@@ -323,7 +323,12 @@
     )
     query_rows = query_rows.reshape(16, 2, 8, local_heads, KEYW).transpose(3, 1, 0, 2, 4)
     query_rows = query_rows.reshape(local_heads, block_len, KEYW)
-    fetched, query_rows = lax.optimization_barrier((fetched, query_rows))
+    in_out = sds((3, width_out, 2 * ff_half), bf16)
+    down_out = sds((3, width_out, ff_half), bf16)
+    in_send, in_keep, down_send, down_keep = call(
+        split_weights_kernel, [in_out, in_out, down_out, down_out], (), True, 4
+    )(info, expert_gate, expert_up, jnp.transpose(expert_down, (0, 2, 1)))
+    fetched, query_rows, in_send = lax.optimization_barrier((fetched, query_rows, in_send))
 
     to_other = jnp.where((xl == 0) & (xh == 1) & (core == 1), keys_own, fetched)
     diagonal = [(0, 3), (1, 2), (2, 1), (3, 0)]
@@ -342,7 +347,7 @@
     state = call(
         first_attention_kernel, state_out, [pltpu.VMEM((2, 256, 2 * 256), f32)], True, 4
     )(info, query_rows, keys_own, fetched)
-    pieces[1], fetched_late, peak = lax.optimization_barrier((pieces[1], fetched, state[0]))
+    pieces[2], fetched_late, peak = lax.optimization_barrier((pieces[2], fetched, state[0]))
     state = [peak] + list(state[1:])
     first_other = lax.ppermute(fetched_late, "core", SWAP)
     *pieces, first_other = lax.optimization_barrier((*pieces, first_other))
@@ -361,11 +366,6 @@
     got = lax.ppermute(send, "core", SWAP)
     pair_sum = call(add_kernel, [sds((16, 8, width_model), bf16)], count=2)(keep, got)
 
-    in_out = sds((3, width_out, 2 * ff_half), bf16)
-    down_out = sds((3, width_out, ff_half), bf16)
-    in_send, in_keep, down_send, down_keep = call(
-        split_weights_kernel, [in_out, in_out, down_out, down_out], (), True, 4
-    )(info, expert_gate, expert_up, jnp.transpose(expert_down, (0, 2, 1)))
     pair_sum, in_send = lax.optimization_barrier((pair_sum, in_send))
     in_got = lax.ppermute(in_send, "xl", SWAP)
 

time: 241 us -> 242 us (level)
  local copies, waits for them, and re-layouts: 4.88 us -> 7.59 us
    ppermute x1, waiting for transfers between devices: 1.12 us -> 5.6 us  [on_device(): lax.ppermute(to_other, ('xl', 'xh'), diagonal)]
    ppermute x1, waiting for transfers between devices: 10.6 us -> 6.2 us  [on_device(): fetched = lax.ppermute(keys_own, ('y', 'xh', 'core'), pairs)]
    ppermute x1, starting transfers between devices: 1.92 us -> 5.07 us  [on_device(): lax.ppermute(to_other, ('xl', 'xh'), diagonal)]
    unnamed x32 -> x40, local copies, waits for them, and re-layouts: 4.24 us -> 6.95 us
    ppermute x1, waiting for transfers between devices: 2.7 us -> 0.01 us  [on_device(): lax.ppermute(to_other, 'xl', SWAP)]
  transfers between devices with their start and end apart: 14 -> 14, of which waited for: 11 -> 9; matrix products, arithmetic and copies ran while one was open for 2% -> 2% of each run, Pallas kernels for 3% -> 3%
where the time goes in v14:
time: 242 us; the launch traced here: 240 us
  waiting for transfers between devices  76.3 us (32%)
  starting transfers between devices  67.7 us (28%)
  blocking collectives  67.2 us (28%)
  Pallas kernels  18.4 us (8%)
  local copies, waits for them, and re-layouts  7.59 us (3%)
    all_to_all x1, blocking collectives, on_device(): lax.all_to_all(pre.reshape(8, 128, 2 * ff_half), 'y', split_axis=0, conca...  42.6 us
    all_to_all x1, blocking collectives, on_device(): lax.all_to_all(hidden, 'y', split_axis=0, concat_axis=0, tiled=True)  24.6 us
    all_to_all x1, waiting for transfers between devices, on_device(): lax.all_to_all(expert_out, EXP, split_axis=0, concat_axis=0, tiled=True)  19.6 us
    all_to_all x1, waiting for transfers between devices, on_device(): lax.all_to_all(pair_sum, ('z', 'xh'), split_axis=0, concat_axis=0, tiled=...  16.4 us
    ppermute x1, waiting for transfers between devices, on_device(): down_got = lax.ppermute(down_send, 'xl', SWAP)  14.8 us
    all_to_all x1, starting transfers between devices, on_device(): lax.all_to_all(pair_sum, ('z', 'xh'), split_axis=0, concat_axis=0, tiled=...  13.3 us
    all_to_all x1, starting transfers between devices, on_device(): split = lax.all_to_all(packed, CTX, split_axis=0, concat_axis=0, tiled=True)  10.1 us
    all_to_all x1, waiting for transfers between devices, on_device(): split = lax.all_to_all(packed, CTX, split_axis=0, concat_axis=0, tiled=True)  7.82 us
  transfers between devices with their start and end apart: 14, of which 9 were waited for; matrix products, arithmetic and copies ran while one was open for 2% of the time, Pallas kernels for 3%

profile of v14, /device:TPU:6, one launch (start us, length us, event | category | flops | bytes accessed | tf_op | source)
XLA Modules:
  0.0 240.1 jit_solution(3218166609627561769)
XLA Ops:
  1.7 4.5 %collective-permute-start = (bf16[592,256]{1,0:T(8,128)(2,1)S(1)}, bf16[592,256]{1,0:T(8,128)(2,1)S(1)}, u32[]{:S(2)}, u32[]{:S(2)}) collective-permute-start(bf16[592,256]{1,0:T(8,128)(2,1)S(1)} %shard_map.118.own), channel_id=1, source_target_pairs={{0,64},{1,193},{2,130},{3,259},{64,128},{65,257},{66,194},{67,323}... | collective-permute-start | bytes 909320 | tf_op jit(solution)/shard_map/ppermute | solution.py:301
  12.4 6.2 %collective-permute-done.p0 = bf16[592,256]{1,0:T(8,128)(2,1)S(1)} collective-permute-done((bf16[592,256]{1,0:T(8,128)(2,1)S(1)}, bf16[592,256]{1,0:T(8,128)(2,1)S(1)}, u32[]{:S(2)}, u32[]{:S(2)}) %collective-permute-start) | collective-permute-done | bytes 303136 | tf_op jit(solution)/shard_map/ppermute | solution.py:301
  18.6 2.7 %collective-permute-start.2 = (bf16[592,256]{1,0:T(8,128)(2,1)S(1)}, bf16[592,256]{1,0:T(8,128)(2,1)S(1)}, u32[]{:S(2)}, u32[]{:S(2)}) collective-permute-start(bf16[592,256]{1,0:T(8,128)(2,1)S(1)} %broadcast_select_fusion), channel_id=1, source_target_pairs={{0,32},{32,0},{1,33},{33,1},{2,34},{34,2},{3,35},{35,3},{4,36},{36... | collective-permute-start | bytes 909320 | tf_op jit(solution)/shard_map/ppermute | solution.py:338
  21.4 5.1 %collective-permute-start.3 = (bf16[592,256]{1,0:T(8,128)(2,1)S(1)}, bf16[592,256]{1,0:T(8,128)(2,1)S(1)}, u32[]{:S(2)}, u32[]{:S(2)}) collective-permute-start(bf16[592,256]{1,0:T(8,128)(2,1)S(1)} %broadcast_select_fusion), channel_id=1, source_target_pairs={{0,34},{2,32},{32,2},{34,0},{1,35},{3,33},{33,3},{35,1},{4,38},{6,... | collective-permute-start | bytes 909320 | tf_op jit(solution)/shard_map/ppermute | solution.py:339
  26.5 3.4 %collective-permute-start.1 = (bf16[592,256]{1,0:T(8,128)(2,1)S(1)}, bf16[592,256]{1,0:T(8,128)(2,1)S(1)}, u32[]{:S(2)}, u32[]{:S(2)}) collective-permute-start(bf16[592,256]{1,0:T(8,128)(2,1)S(1)} %collective-permute-done.p0), channel_id=1, source_target_pairs={{0,2},{2,0},{1,3},{3,1},{4,6},{6,4},{5,7},{7,5},{8,10},{10,8},{9,1... | collective-permute-start | bytes 909320 | tf_op jit(solution)/shard_map/ppermute | solution.py:337
  33.6 5.6 %collective-permute-done.3.p3 = bf16[592,256]{1,0:T(8,128)(2,1)S(1)} collective-permute-done((bf16[592,256]{1,0:T(8,128)(2,1)S(1)}, bf16[592,256]{1,0:T(8,128)(2,1)S(1)}, u32[]{:S(2)}, u32[]{:S(2)}) %collective-permute-start.3) | collective-permute-done | bytes 303136 | tf_op jit(solution)/shard_map/ppermute | solution.py:339
  41.2 2.6 %shard_map.122 = (f32[2,256,128]{2,1,0:T(8,128)S(1)}, f32[2,256,128]{2,1,0:T(8,128)S(1)}, f32[2,256,512]{2,1,0:T(8,128)S(1)}) custom-call(s32[10]{0:T(128)S(1)} %stack.43.info, bf16[2,256,592]{2,1,0:T(8,128)(2,1)S(1)} %bitcast.37, bf16[592,256]{1,0:T(8,128)(2,1)S(1)} %collective-permute-done.1.p1, bf16[592,256]{1,0:T(8,128)(2,1)S(1)} %collective-permute-done.2.p2, ...), custom_call_target="tpu_custom_call" | custom-call | tf_op jit(solution)/shard_map/pallas_call | solution.py:356
  43.9 3.6 %shard_map.123 = (bf16[128,2560]{1,0:T(8,128)(2,1)S(1)}, f32[128,2560]{1,0:T(8,128)S(1)}) custom-call(s32[10]{0:T(128)S(1)} %stack.43.info, bf16[2,256,592]{2,1,0:T(8,128)(2,1)S(1)} %bitcast.38, bf16[3,592,256]{2,1,0:T(8,128)(2,1)S(1)} %collective-permute-done.5.others, f32[2,256,128]{2,1,0:T(8,128)S(1)} %get-tuple-element.50.old_peak, ...), custom_call_target="tpu_custom_call" | custom-call | tf_op jit(solution)/shard_map/pallas_call | solution.py:359
  47.5 2.4 %collective-permute-start.6 = (bf16[128,2560]{1,0:T(8,128)(2,1)S(1)}, bf16[128,2560]{1,0:T(8,128)(2,1)S(1)}, u32[]{:S(2)}, u32[]{:S(2)}) collective-permute-start(bf16[128,2560]{1,0:T(8,128)(2,1)S(1)} %get-tuple-element.54), channel_id=1, source_target_pairs={{0,1},{1,0},{2,3},{3,2},{4,5},{5,4},{6,7},{7,6},{8,9},{9,8},{10,11... | collective-permute-start | bytes 1966088 | tf_op jit(solution)/shard_map/ppermute | solution.py:366
  52.6 13.3 %all-to-all-start = ((bf16[16,8,2560]{2,1,0:T(8,128)(2,1)}), bf16[16,8,2560]{2,1,0:T(8,128)(2,1)S(1)}, u32[]{:S(2)}, u32[]{:S(2)}) async-start(bf16[16,8,2560]{2,1,0:T(8,128)(2,1)} %shard_map.124), calls=%async_computation | async-start | bytes 1310720 | tf_op jit(solution)/shard_map/all_to_all | solution.py:372
  66.1 2.7 %collective-permute-start.7 = (bf16[3,160,768]{2,1,0:T(8,128)(2,1)S(1)}, bf16[3,160,768]{2,1,0:T(8,128)(2,1)S(1)}, u32[]{:S(2)}, u32[]{:S(2)}) collective-permute-start(bf16[3,160,768]{2,1,0:T(8,128)(2,1)S(1)} %copy-done.15), channel_id=1, source_target_pairs={{0,32},{32,0},{1,33},{33,1},{2,34},{34,2},{3,35},{35,3},{4,36},{36... | collective-permute-start | bytes 2211848 | tf_op jit(solution)/shard_map/ppermute | solution.py:370
  69.2 16.4 %all-to-all-done.spread = bf16[16,8,2560]{2,1,0:T(8,128)(2,1)S(1)} async-done(((bf16[16,8,2560]{2,1,0:T(8,128)(2,1)}), bf16[16,8,2560]{2,1,0:T(8,128)(2,1)S(1)}, u32[]{:S(2)}, u32[]{:S(2)}) %all-to-all-start) | async-done | bytes 655392 | tf_op jit(solution)/shard_map/all_to_all | solution.py:372
  86.6 10.1 %all-to-all-start.1 = ((bf16[16,8,512]{2,1,0:T(8,128)(2,1)}), bf16[16,8,512]{2,1,0:T(8,128)(2,1)S(1)}, u32[]{:S(2)}, u32[]{:S(2)}) async-start(bf16[16,8,512]{2,1,0:T(8,128)(2,1)} %shard_map.125), calls=%async_computation.1 | async-start | bytes 262144 | tf_op jit(solution)/shard_map/all_to_all | solution.py:376
  97.3 7.8 %all-to-all-done.1 = bf16[16,8,512]{2,1,0:T(8,128)(2,1)S(1)} async-done(((bf16[16,8,512]{2,1,0:T(8,128)(2,1)}), bf16[16,8,512]{2,1,0:T(8,128)(2,1)S(1)}, u32[]{:S(2)}, u32[]{:S(2)}) %all-to-all-start.1) | async-done | bytes 131104 | tf_op jit(solution)/shard_map/all_to_all | solution.py:376
  106.3 6.6 %all-to-all-start.2 = ((bf16[32,80,128]{2,1,0:T(8,128)(2,1)}), bf16[32,80,128]{2,1,0:T(8,128)(2,1)S(1)}, u32[]{:S(2)}, u32[]{:S(2)}) async-start(bf16[32,80,128]{2,1,0:T(8,128)(2,1)} %shard_map.126), calls=%async_computation.2 | async-start | bytes 1310720 | tf_op jit(solution)/shard_map/all_to_all | solution.py:405
  112.9 2.6 %collective-permute-start.8 = (bf16[3,160,384]{2,1,0:T(8,128)(2,1)}, bf16[3,160,384]{2,1,0:T(8,128)(2,1)S(1)}, u32[]{:S(2)}, u32[]{:S(2)}) collective-permute-start(bf16[3,160,384]{2,1,0:T(8,128)(2,1)} %get-tuple-element.63), channel_id=1, source_target_pairs={{0,32},{32,0},{1,33},{33,1},{2,34},{34,2},{3,35},{35,3},{4,36},{36... | collective-permute-start | bytes 1105928 | tf_op jit(solution)/shard_map/ppermute | solution.py:378
  116.8 14.8 %collective-permute-done.8.got = bf16[3,160,384]{2,1,0:T(8,128)(2,1)S(1)} collective-permute-done((bf16[3,160,384]{2,1,0:T(8,128)(2,1)}, bf16[3,160,384]{2,1,0:T(8,128)(2,1)S(1)}, u32[]{:S(2)}, u32[]{:S(2)}) %collective-permute-start.8) | collective-permute-done | bytes 368672 | tf_op jit(solution)/shard_map/ppermute | solution.py:378
  135.7 42.6 %all_to_all.30.parts = bf16[8,128,768]{2,1,0:T(8,128)(2,1)S(1)} all-to-all(bf16[8,128,768]{2,1,0:T(8,128)(2,1)S(1)} %bitcast.39), channel_id=1, replica_groups=mesh['y'=8,'xl'=2,'z'=8,'xh'=2,'core'=2] {'y'}, dimensions={0} | all-to-all | bytes 3145728 | tf_op jit(solution)/shard_map/all_to_all | solution.py:408
  178.6 24.6 %all_to_all.31 = bf16[8,128,384]{2,1,0:T(8,128)(2,1)S(1)} all-to-all(bf16[8,128,384]{2,1,0:T(8,128)(2,1)S(1)} %shard_map.130), channel_id=1, replica_groups=mesh['y'=8,'xl'=2,'z'=8,'xh'=2,'core'=2] {'y'}, dimensions={0} | all-to-all | bytes 1572864 | tf_op jit(solution)/shard_map/all_to_all | solution.py:412
  203.2 2.4 shard_map.131
  205.5 6.6 %all-to-all-start.5 = ((bf16[32,80,128]{2,1,0:T(8,128)(2,1)}), bf16[32,80,128]{2,1,0:T(8,128)(2,1)S(1)}, u32[]{:S(2)}, u32[]{:S(2)}) async-start(bf16[32,80,128]{2,1,0:T(8,128)(2,1)} %shard_map.131), calls=%async_computation.5 | async-start | bytes 1310720 | tf_op jit(solution)/shard_map/all_to_all | solution.py:416
  213.1 19.6 %all-to-all-done.5.returned = bf16[32,80,128]{2,1,0:T(8,128)(2,1)S(1)} async-done(((bf16[32,80,128]{2,1,0:T(8,128)(2,1)}), bf16[32,80,128]{2,1,0:T(8,128)(2,1)S(1)}, u32[]{:S(2)}, u32[]{:S(2)}) %all-to-all-start.5) | async-done | bytes 655392 | tf_op jit(solution)/shard_map/all_to_all | solution.py:416
  233.3 3.9 %collective-permute-start.9 = (bf16[128,160]{1,0:T(8,128)(2,1)S(1)}, bf16[128,160]{1,0:T(8,128)(2,1)S(1)}, u32[]{:S(2)}, u32[]{:S(2)}) collective-permute-start(bf16[128,160]{1,0:T(8,128)(2,1)S(1)} %get-tuple-element.68), channel_id=1, source_target_pairs={{0,32},{32,0},{1,33},{33,1},{2,34},{34,2},{3,35},{35,3},{4,36},{36... | collective-permute-start | bytes 122888 | tf_op jit(solution)/shard_map/ppermute | solution.py:420
  237.2 2.3 collective-permute-done.9
  (87 shorter events, 27.2 us)
Async XLA Ops:
  1.7 16.9 %collective-permute-start = (bf16[592,256]{1,0:T(8,128)(2,1)S(1)}, bf16[592,256]{1,0:T(8,128)(2,1)S(1)}, u32[]{:S(2)}, u32[]{:S(2)}) collective-permute-start(bf16[592,256]{1,0:T(8,128)(2,1)S(1)} %shard_map.118.own), channel_id=1, source_target_pairs={{0,64},{1,193},{2,130},{3,259},{64,128},{65,257},{66,194},{67,323}... | collective-permute-start | bytes 909320 | tf_op jit(solution)/shard_map/ppermute | solution.py:301
  12.4 14.1 %copy-start.4 = (bf16[3,160,768]{2,1,0:T(8,128)(2,1)}, bf16[3,160,768]{2,1,0:T(8,128)(2,1)S(1)}, u32[]{:S(2)}) copy-start(bf16[3,160,768]{2,1,0:T(8,128)(2,1)S(1)} %get-tuple-element.60.keep) | copy-start | bytes 2211844
  18.6 13.0 %collective-permute-start.2 = (bf16[592,256]{1,0:T(8,128)(2,1)S(1)}, bf16[592,256]{1,0:T(8,128)(2,1)S(1)}, u32[]{:S(2)}, u32[]{:S(2)}) collective-permute-start(bf16[592,256]{1,0:T(8,128)(2,1)S(1)} %broadcast_select_fusion), channel_id=1, source_target_pairs={{0,32},{32,0},{1,33},{33,1},{2,34},{34,2},{3,35},{35,3},{4,36},{36... | collective-permute-start | bytes 909320 | tf_op jit(solution)/shard_map/ppermute | solution.py:338
  21.4 17.8 %collective-permute-start.3 = (bf16[592,256]{1,0:T(8,128)(2,1)S(1)}, bf16[592,256]{1,0:T(8,128)(2,1)S(1)}, u32[]{:S(2)}, u32[]{:S(2)}) collective-permute-start(bf16[592,256]{1,0:T(8,128)(2,1)S(1)} %broadcast_select_fusion), channel_id=1, source_target_pairs={{0,34},{2,32},{32,2},{34,0},{1,35},{3,33},{33,3},{35,1},{4,38},{6,... | collective-permute-start | bytes 909320 | tf_op jit(solution)/shard_map/ppermute | solution.py:339
  26.5 12.7 %collective-permute-start.1 = (bf16[592,256]{1,0:T(8,128)(2,1)S(1)}, bf16[592,256]{1,0:T(8,128)(2,1)S(1)}, u32[]{:S(2)}, u32[]{:S(2)}) collective-permute-start(bf16[592,256]{1,0:T(8,128)(2,1)S(1)} %collective-permute-done.p0), channel_id=1, source_target_pairs={{0,2},{2,0},{1,3},{3,1},{4,6},{6,4},{5,7},{7,5},{8,10},{10,8},{9,1... | collective-permute-start | bytes 909320 | tf_op jit(solution)/shard_map/ppermute | solution.py:337
  31.6 7.5 %collective-permute-start.4 = (bf16[592,256]{1,0:T(8,128)(2,1)S(1)}, bf16[592,256]{1,0:T(8,128)(2,1)S(1)}, u32[]{:S(2)}, u32[]{:S(2)}) collective-permute-start(bf16[592,256]{1,0:T(8,128)(2,1)S(1)} %collective-permute-done.p0), channel_id=1, source_target_pairs={{0,1},{1,0},{2,3},{3,2},{4,5},{5,4},{6,7},{7,6},{8,9},{9,8},{10,11... | collective-permute-start | bytes 909320 | tf_op jit(solution)/shard_map/ppermute | solution.py:352
  39.2 4.6 %collective-permute-start.5 = (bf16[3,592,256]{2,1,0:T(8,128)(2,1)S(1)}, bf16[3,592,256]{2,1,0:T(8,128)(2,1)S(1)}, u32[]{:S(2)}, u32[]{:S(2)}) collective-permute-start(bf16[3,592,256]{2,1,0:T(8,128)(2,1)S(1)} %shard_map.121), channel_id=1, source_target_pairs={{0,1},{1,0},{2,3},{3,2},{4,5},{5,4},{6,7},{7,6},{8,9},{9,8},{10,11... | collective-permute-start | bytes 2727944 | tf_op jit(solution)/shard_map/ppermute | solution.py:355
  41.2 2.7 %copy-start = (bf16[256,2560]{1,0:T(8,128)(2,1)S(1)}, bf16[256,2560]{1,0:T(8,128)(2,1)}, u32[]{:S(2)}) copy-start(bf16[256,2560]{1,0:T(8,128)(2,1)} %out_proj.1) | copy-start | bytes 3932164
  47.5 4.1 %collective-permute-start.6 = (bf16[128,2560]{1,0:T(8,128)(2,1)S(1)}, bf16[128,2560]{1,0:T(8,128)(2,1)S(1)}, u32[]{:S(2)}, u32[]{:S(2)}) collective-permute-start(bf16[128,2560]{1,0:T(8,128)(2,1)S(1)} %get-tuple-element.54), channel_id=1, source_target_pairs={{0,1},{1,0},{2,3},{3,2},{4,5},{5,4},{6,7},{7,6},{8,9},{9,8},{10,11... | collective-permute-start | bytes 1966088 | tf_op jit(solution)/shard_map/ppermute | solution.py:366
  51.6 14.3 %copy-start.17 = (s32[8,16,6]{1,0,2:T(8,128)S(1)}, s32[8,16,6]{1,0,2:T(8,128)}, u32[]{:S(2)}) copy-start(s32[8,16,6]{1,0,2:T(8,128)} %param.19) | copy-start | bytes 9220
  51.6 14.6 %copy-start.15 = (bf16[3,160,768]{2,1,0:T(8,128)(2,1)S(1)}, bf16[3,160,768]{2,1,0:T(8,128)(2,1)}, u32[]{:S(2)}) copy-start(bf16[3,160,768]{2,1,0:T(8,128)(2,1)} %copy-done.14) | copy-start | bytes 2211844
  51.6 17.3 %copy-start.18 = (f32[2560]{0:T(1024)S(1)}, f32[2560]{0:T(1024)}, u32[]{:S(2)}) copy-start(f32[2560]{0:T(1024)} %param.18) | copy-start | bytes 30724
  51.6 34.0 %copy-start.12 = (bf16[8,2560]{1,0:T(8,128)(2,1)S(1)}, bf16[8,2560]{1,0:T(8,128)(2,1)}, u32[]{:S(2)}) copy-start(bf16[8,2560]{1,0:T(8,128)(2,1)} %residual.1) | copy-start | bytes 122884
  52.6 33.0 %all-to-all-start = ((bf16[16,8,2560]{2,1,0:T(8,128)(2,1)}), bf16[16,8,2560]{2,1,0:T(8,128)(2,1)S(1)}, u32[]{:S(2)}, u32[]{:S(2)}) async-start(bf16[16,8,2560]{2,1,0:T(8,128)(2,1)} %shard_map.124), calls=%async_computation | async-start | bytes 1310720 | tf_op jit(solution)/shard_map/all_to_all | solution.py:372
  66.1 31.1 %collective-permute-start.7 = (bf16[3,160,768]{2,1,0:T(8,128)(2,1)S(1)}, bf16[3,160,768]{2,1,0:T(8,128)(2,1)S(1)}, u32[]{:S(2)}, u32[]{:S(2)}) collective-permute-start(bf16[3,160,768]{2,1,0:T(8,128)(2,1)S(1)} %copy-done.15), channel_id=1, source_target_pairs={{0,32},{32,0},{1,33},{33,1},{2,34},{34,2},{3,35},{35,3},{4,36},{36... | collective-permute-start | bytes 2211848 | tf_op jit(solution)/shard_map/ppermute | solution.py:370
  86.6 28.9 %copy-start.5 = (bf16[3,160,768]{2,1,0:T(8,128)(2,1)S(1)}, bf16[3,160,768]{2,1,0:T(8,128)(2,1)}, u32[]{:S(2)}) copy-start(bf16[3,160,768]{2,1,0:T(8,128)(2,1)} %copy-done.4) | copy-start | bytes 2211844
  86.6 18.5 %all-to-all-start.1 = ((bf16[16,8,512]{2,1,0:T(8,128)(2,1)}), bf16[16,8,512]{2,1,0:T(8,128)(2,1)S(1)}, u32[]{:S(2)}, u32[]{:S(2)}) async-start(bf16[16,8,512]{2,1,0:T(8,128)(2,1)} %shard_map.125), calls=%async_computation.1 | async-start | bytes 262144 | tf_op jit(solution)/shard_map/all_to_all | solution.py:376
  97.3 9.1 %copy-start.6 = (bf16[3,160,768]{2,1,0:T(8,128)(2,1)}, bf16[3,160,768]{2,1,0:T(8,128)(2,1)S(1)}, u32[]{:S(2)}) copy-start(bf16[3,160,768]{2,1,0:T(8,128)(2,1)S(1)} %collective-permute-done.7.got) | copy-start | bytes 2211844
  106.3 27.2 %all-to-all-start.2 = ((bf16[32,80,128]{2,1,0:T(8,128)(2,1)}), bf16[32,80,128]{2,1,0:T(8,128)(2,1)S(1)}, u32[]{:S(2)}, u32[]{:S(2)}) async-start(bf16[32,80,128]{2,1,0:T(8,128)(2,1)} %shard_map.126), calls=%async_computation.2 | async-start | bytes 1310720 | tf_op jit(solution)/shard_map/all_to_all | solution.py:405
  112.9 18.6 %collective-permute-start.8 = (bf16[3,160,384]{2,1,0:T(8,128)(2,1)}, bf16[3,160,384]{2,1,0:T(8,128)(2,1)S(1)}, u32[]{:S(2)}, u32[]{:S(2)}) collective-permute-start(bf16[3,160,384]{2,1,0:T(8,128)(2,1)} %get-tuple-element.63), channel_id=1, source_target_pairs={{0,32},{32,0},{1,33},{33,1},{2,34},{34,2},{3,35},{35,3},{4,36},{36... | collective-permute-start | bytes 1105928 | tf_op jit(solution)/shard_map/ppermute | solution.py:378
  116.6 14.9 %copy-start.9 = (bf16[3,160,384]{2,1,0:T(8,128)(2,1)S(1)}, bf16[3,160,384]{2,1,0:T(8,128)(2,1)}, u32[]{:S(2)}) copy-start(bf16[3,160,384]{2,1,0:T(8,128)(2,1)} %copy-done.8) | copy-start | bytes 1105924
  203.2 9.3 %copy-start.16 = (f32[8,16,6]{1,0,2:T(8,128)S(1)}, f32[8,16,6]{1,0,2:T(8,128)}, u32[]{:S(2)}) copy-start(f32[8,16,6]{1,0,2:T(8,128)} %param.20) | copy-start | bytes 9220
  205.5 27.2 %all-to-all-start.5 = ((bf16[32,80,128]{2,1,0:T(8,128)(2,1)}), bf16[32,80,128]{2,1,0:T(8,128)(2,1)S(1)}, u32[]{:S(2)}, u32[]{:S(2)}) async-start(bf16[32,80,128]{2,1,0:T(8,128)(2,1)} %shard_map.131), calls=%async_computation.5 | async-start | bytes 1310720 | tf_op jit(solution)/shard_map/all_to_all | solution.py:416
  233.3 6.2 %collective-permute-start.9 = (bf16[128,160]{1,0:T(8,128)(2,1)S(1)}, bf16[128,160]{1,0:T(8,128)(2,1)S(1)}, u32[]{:S(2)}, u32[]{:S(2)}) collective-permute-start(bf16[128,160]{1,0:T(8,128)(2,1)S(1)} %get-tuple-element.68), channel_id=1, source_target_pairs={{0,32},{32,0},{1,33},{33,1},{2,34},{34,2},{3,35},{35,3},{4,36},{36... | collective-permute-start | bytes 122888 | tf_op jit(solution)/shard_map/ppermute | solution.py:420
  (9 other events, 11.1 us)

commit v15 on v13

--- a/solution.py
+++ b/solution.py
@@ -154,9 +154,10 @@
 def pick_kernel(picker, split, out):
     values = split[:, :384]
     doubled = jnp.concatenate([values[:, :320], values[:, 256:320]], axis=1)
-    for r in range(0, picker.shape[0], 256):
-        rows = jnp.dot(picker[r : r + 256, :], doubled, preferred_element_type=f32)
-        for n in range(256 // SLOTS):
+    step = 512
+    for r in range(0, picker.shape[0], step):
+        rows = jnp.dot(picker[r : r + step, :], doubled, preferred_element_type=f32)
+        for n in range(step // SLOTS):
             store_packed(out, r // SLOTS + n, rows[n * SLOTS : (n + 1) * SLOTS])
 
 
@@ -224,11 +225,12 @@
 
 
 def down_kernel(hidden, weights, out):
-    masks = [row_mask(256, j) for j in range(3)]
-    for r in range(0, hidden.shape[0], 256):
-        rows = spread_experts(hidden[r : r + 256, :], masks)
+    step = 512
+    masks = [row_mask(step, j) for j in range(3)]
+    for r in range(0, hidden.shape[0], step):
+        rows = spread_experts(hidden[r : r + step, :], masks)
         total = nt_dot(rows, weights[...])
-        for n in range(256 // SLOTS):
+        for n in range(step // SLOTS):
             store_packed(out, r // SLOTS + n, total[n * SLOTS : (n + 1) * SLOTS])
 
 

time: 241 us -> 241 us (level)
  no operation moved by 1% of the time
where the time goes in v15:
time: 241 us; the launch traced here: 239 us
  waiting for transfers between devices  78.5 us (33%)
  starting transfers between devices  67 us (28%)
  blocking collectives  67 us (28%)
  Pallas kernels  18.4 us (8%)
  local copies, waits for them, and re-layouts  4.88 us (2%)
    all_to_all x1, blocking collectives, on_device(): lax.all_to_all(pre.reshape(8, 128, 2 * ff_half), 'y', split_axis=0, conca...  42.6 us
    all_to_all x1, blocking collectives, on_device(): lax.all_to_all(hidden, 'y', split_axis=0, concat_axis=0, tiled=True)  24.4 us
    all_to_all x1, waiting for transfers between devices, on_device(): lax.all_to_all(expert_out, EXP, split_axis=0, concat_axis=0, tiled=True)  19.6 us
    all_to_all x1, waiting for transfers between devices, on_device(): lax.all_to_all(pair_sum, ('z', 'xh'), split_axis=0, concat_axis=0, tiled=...  16.5 us
    ppermute x1, waiting for transfers between devices, on_device(): down_got = lax.ppermute(down_send, 'xl', SWAP)  14.8 us
    all_to_all x1, starting transfers between devices, on_device(): lax.all_to_all(pair_sum, ('z', 'xh'), split_axis=0, concat_axis=0, tiled=...  13.3 us
    ppermute x1, waiting for transfers between devices, on_device(): fetched = lax.ppermute(keys_own, ('y', 'xh', 'core'), pairs)  10.6 us
    all_to_all x1, starting transfers between devices, on_device(): split = lax.all_to_all(packed, CTX, split_axis=0, concat_axis=0, tiled=True)  10 us
  transfers between devices with their start and end apart: 14, of which 11 were waited for; matrix products, arithmetic and copies ran while one was open for 2% of the time, Pallas kernels for 3%

profile of v15, /device:TPU:6, one launch (start us, length us, event | category | flops | bytes accessed | tf_op | source)
XLA Modules:
  0.0 238.5 jit_solution(9125551226228272931)
XLA Ops:
  1.7 4.5 %collective-permute-start = (bf16[592,256]{1,0:T(8,128)(2,1)S(1)}, bf16[592,256]{1,0:T(8,128)(2,1)S(1)}, u32[]{:S(2)}, u32[]{:S(2)}) collective-permute-start(bf16[592,256]{1,0:T(8,128)(2,1)S(1)} %shard_map.118.own), channel_id=1, source_target_pairs={{0,64},{1,193},{2,130},{3,259},{64,128},{65,257},{66,194},{67,323}... | collective-permute-start | bytes 909320 | tf_op jit(solution)/shard_map/ppermute | solution.py:303
  8.0 10.6 %collective-permute-done.p0 = bf16[592,256]{1,0:T(8,128)(2,1)S(1)} collective-permute-done((bf16[592,256]{1,0:T(8,128)(2,1)S(1)}, bf16[592,256]{1,0:T(8,128)(2,1)S(1)}, u32[]{:S(2)}, u32[]{:S(2)}) %collective-permute-start) | collective-permute-done | bytes 303136 | tf_op jit(solution)/shard_map/ppermute | solution.py:303
  18.6 5.0 %collective-permute-start.1 = (bf16[592,256]{1,0:T(8,128)(2,1)S(1)}, bf16[592,256]{1,0:T(8,128)(2,1)S(1)}, u32[]{:S(2)}, u32[]{:S(2)}) collective-permute-start(bf16[592,256]{1,0:T(8,128)(2,1)S(1)} %collective-permute-done.p0), channel_id=1, source_target_pairs={{0,2},{2,0},{1,3},{3,1},{4,6},{6,4},{5,7},{7,5},{8,10},{10,8},{9,1... | collective-permute-start | bytes 909320 | tf_op jit(solution)/shard_map/ppermute | solution.py:334
  23.8 3.6 %collective-permute-start.2 = (bf16[592,256]{1,0:T(8,128)(2,1)S(1)}, bf16[592,256]{1,0:T(8,128)(2,1)S(1)}, u32[]{:S(2)}, u32[]{:S(2)}) collective-permute-start(bf16[592,256]{1,0:T(8,128)(2,1)S(1)} %broadcast_select_fusion), channel_id=1, source_target_pairs={{0,32},{32,0},{1,33},{33,1},{2,34},{34,2},{3,35},{35,3},{4,36},{36... | collective-permute-start | bytes 909320 | tf_op jit(solution)/shard_map/ppermute | solution.py:335
  34.0 2.7 %collective-permute-done.2.p2 = bf16[592,256]{1,0:T(8,128)(2,1)S(1)} collective-permute-done((bf16[592,256]{1,0:T(8,128)(2,1)S(1)}, bf16[592,256]{1,0:T(8,128)(2,1)S(1)}, u32[]{:S(2)}, u32[]{:S(2)}) %collective-permute-start.2) | collective-permute-done | bytes 303136 | tf_op jit(solution)/shard_map/ppermute | solution.py:335
  39.9 2.6 %shard_map.121 = (f32[2,256,128]{2,1,0:T(8,128)S(1)}, f32[2,256,128]{2,1,0:T(8,128)S(1)}, f32[2,256,512]{2,1,0:T(8,128)S(1)}) custom-call(s32[10]{0:T(128)S(1)} %stack.43.info, bf16[2,256,592]{2,1,0:T(8,128)(2,1)S(1)} %bitcast.37, bf16[592,256]{1,0:T(8,128)(2,1)S(1)} %collective-permute-done.1.p1, bf16[592,256]{1,0:T(8,128)(2,1)S(1)} %collective-permute-done.2.p2, ...), custom_call_target="tpu_custom_call" | custom-call | tf_op jit(solution)/shard_map/pallas_call | solution.py:353
  42.6 3.6 %shard_map.122 = (bf16[128,2560]{1,0:T(8,128)(2,1)S(1)}, f32[128,2560]{1,0:T(8,128)S(1)}) custom-call(s32[10]{0:T(128)S(1)} %stack.43.info, bf16[2,256,592]{2,1,0:T(8,128)(2,1)S(1)} %bitcast.38, bf16[3,592,256]{2,1,0:T(8,128)(2,1)S(1)} %collective-permute-done.5.others, f32[2,256,128]{2,1,0:T(8,128)S(1)} %get-tuple-element.48.old_peak, ...), custom_call_target="tpu_custom_call" | custom-call | tf_op jit(solution)/shard_map/pallas_call | solution.py:356
  46.2 2.4 %collective-permute-start.6 = (bf16[128,2560]{1,0:T(8,128)(2,1)S(1)}, bf16[128,2560]{1,0:T(8,128)(2,1)S(1)}, u32[]{:S(2)}, u32[]{:S(2)}) collective-permute-start(bf16[128,2560]{1,0:T(8,128)(2,1)S(1)} %get-tuple-element.52), channel_id=1, source_target_pairs={{0,1},{1,0},{2,3},{3,2},{4,5},{5,4},{6,7},{7,6},{8,9},{9,8},{10,11... | collective-permute-start | bytes 1966088 | tf_op jit(solution)/shard_map/ppermute | solution.py:363
  51.3 13.3 %all-to-all-start = ((bf16[16,8,2560]{2,1,0:T(8,128)(2,1)}), bf16[16,8,2560]{2,1,0:T(8,128)(2,1)S(1)}, u32[]{:S(2)}, u32[]{:S(2)}) async-start(bf16[16,8,2560]{2,1,0:T(8,128)(2,1)} %shard_map.123), calls=%async_computation | async-start | bytes 1310720 | tf_op jit(solution)/shard_map/all_to_all | solution.py:374
  64.8 2.7 %collective-permute-start.7 = (bf16[3,160,768]{2,1,0:T(8,128)(2,1)S(1)}, bf16[3,160,768]{2,1,0:T(8,128)(2,1)S(1)}, u32[]{:S(2)}, u32[]{:S(2)}) collective-permute-start(bf16[3,160,768]{2,1,0:T(8,128)(2,1)S(1)} %get-tuple-element.55), channel_id=1, source_target_pairs={{0,32},{32,0},{1,33},{33,1},{2,34},{34,2},{3,35},{35,3},{4,36},{36... | collective-permute-start | bytes 2211848 | tf_op jit(solution)/shard_map/ppermute | solution.py:372
  67.8 16.5 %all-to-all-done.spread = bf16[16,8,2560]{2,1,0:T(8,128)(2,1)S(1)} async-done(((bf16[16,8,2560]{2,1,0:T(8,128)(2,1)}), bf16[16,8,2560]{2,1,0:T(8,128)(2,1)S(1)}, u32[]{:S(2)}, u32[]{:S(2)}) %all-to-all-start) | async-done | bytes 655392 | tf_op jit(solution)/shard_map/all_to_all | solution.py:374
  85.3 10.0 %all-to-all-start.1 = ((bf16[16,8,512]{2,1,0:T(8,128)(2,1)}), bf16[16,8,512]{2,1,0:T(8,128)(2,1)S(1)}, u32[]{:S(2)}, u32[]{:S(2)}) async-start(bf16[16,8,512]{2,1,0:T(8,128)(2,1)} %shard_map.125), calls=%async_computation.1 | async-start | bytes 262144 | tf_op jit(solution)/shard_map/all_to_all | solution.py:378
  95.9 7.8 %all-to-all-done.1 = bf16[16,8,512]{2,1,0:T(8,128)(2,1)S(1)} async-done(((bf16[16,8,512]{2,1,0:T(8,128)(2,1)}), bf16[16,8,512]{2,1,0:T(8,128)(2,1)S(1)}, u32[]{:S(2)}, u32[]{:S(2)}) %all-to-all-start.1) | async-done | bytes 131104 | tf_op jit(solution)/shard_map/all_to_all | solution.py:378
  105.0 6.6 %all-to-all-start.2 = ((bf16[32,80,128]{2,1,0:T(8,128)(2,1)}), bf16[32,80,128]{2,1,0:T(8,128)(2,1)S(1)}, u32[]{:S(2)}, u32[]{:S(2)}) async-start(bf16[32,80,128]{2,1,0:T(8,128)(2,1)} %shard_map.126), calls=%async_computation.2 | async-start | bytes 1310720 | tf_op jit(solution)/shard_map/all_to_all | solution.py:407
  111.6 2.6 %collective-permute-start.8 = (bf16[3,160,384]{2,1,0:T(8,128)(2,1)}, bf16[3,160,384]{2,1,0:T(8,128)(2,1)S(1)}, u32[]{:S(2)}, u32[]{:S(2)}) collective-permute-start(bf16[3,160,384]{2,1,0:T(8,128)(2,1)} %get-tuple-element.61), channel_id=1, source_target_pairs={{0,32},{32,0},{1,33},{33,1},{2,34},{34,2},{3,35},{35,3},{4,36},{36... | collective-permute-start | bytes 1105928 | tf_op jit(solution)/shard_map/ppermute | solution.py:380
  115.4 14.8 %collective-permute-done.8.got = bf16[3,160,384]{2,1,0:T(8,128)(2,1)S(1)} collective-permute-done((bf16[3,160,384]{2,1,0:T(8,128)(2,1)}, bf16[3,160,384]{2,1,0:T(8,128)(2,1)S(1)}, u32[]{:S(2)}, u32[]{:S(2)}) %collective-permute-start.8) | collective-permute-done | bytes 368672 | tf_op jit(solution)/shard_map/ppermute | solution.py:380
  132.2 2.2 shard_map.129
  134.4 42.6 %all_to_all.30.parts = bf16[8,128,768]{2,1,0:T(8,128)(2,1)S(1)} all-to-all(bf16[8,128,768]{2,1,0:T(8,128)(2,1)S(1)} %bitcast.39), channel_id=1, replica_groups=mesh['y'=8,'xl'=2,'z'=8,'xh'=2,'core'=2] {'y'}, dimensions={0} | all-to-all | bytes 3145728 | tf_op jit(solution)/shard_map/all_to_all | solution.py:410
  177.2 24.4 %all_to_all.31 = bf16[8,128,384]{2,1,0:T(8,128)(2,1)S(1)} all-to-all(bf16[8,128,384]{2,1,0:T(8,128)(2,1)S(1)} %shard_map.130), channel_id=1, replica_groups=mesh['y'=8,'xl'=2,'z'=8,'xh'=2,'core'=2] {'y'}, dimensions={0} | all-to-all | bytes 1572864 | tf_op jit(solution)/shard_map/all_to_all | solution.py:414
  201.7 2.3 shard_map.131
  204.0 6.6 %all-to-all-start.5 = ((bf16[32,80,128]{2,1,0:T(8,128)(2,1)}), bf16[32,80,128]{2,1,0:T(8,128)(2,1)S(1)}, u32[]{:S(2)}, u32[]{:S(2)}) async-start(bf16[32,80,128]{2,1,0:T(8,128)(2,1)} %shard_map.131), calls=%async_computation.5 | async-start | bytes 1310720 | tf_op jit(solution)/shard_map/all_to_all | solution.py:418
  211.5 19.6 %all-to-all-done.5.returned = bf16[32,80,128]{2,1,0:T(8,128)(2,1)S(1)} async-done(((bf16[32,80,128]{2,1,0:T(8,128)(2,1)}), bf16[32,80,128]{2,1,0:T(8,128)(2,1)S(1)}, u32[]{:S(2)}, u32[]{:S(2)}) %all-to-all-start.5) | async-done | bytes 655392 | tf_op jit(solution)/shard_map/all_to_all | solution.py:418
  231.7 3.9 %collective-permute-start.9 = (bf16[128,160]{1,0:T(8,128)(2,1)S(1)}, bf16[128,160]{1,0:T(8,128)(2,1)S(1)}, u32[]{:S(2)}, u32[]{:S(2)}) collective-permute-start(bf16[128,160]{1,0:T(8,128)(2,1)S(1)} %get-tuple-element.66), channel_id=1, source_target_pairs={{0,32},{32,0},{1,33},{33,1},{2,34},{34,2},{3,35},{35,3},{4,36},{36... | collective-permute-start | bytes 122888 | tf_op jit(solution)/shard_map/ppermute | solution.py:422
  235.6 2.3 collective-permute-done.9
  (79 shorter events, 24.8 us)
Async XLA Ops:
  1.7 16.9 %collective-permute-start = (bf16[592,256]{1,0:T(8,128)(2,1)S(1)}, bf16[592,256]{1,0:T(8,128)(2,1)S(1)}, u32[]{:S(2)}, u32[]{:S(2)}) collective-permute-start(bf16[592,256]{1,0:T(8,128)(2,1)S(1)} %shard_map.118.own), channel_id=1, source_target_pairs={{0,64},{1,193},{2,130},{3,259},{64,128},{65,257},{66,194},{67,323}... | collective-permute-start | bytes 909320 | tf_op jit(solution)/shard_map/ppermute | solution.py:303
  18.6 13.5 %collective-permute-start.1 = (bf16[592,256]{1,0:T(8,128)(2,1)S(1)}, bf16[592,256]{1,0:T(8,128)(2,1)S(1)}, u32[]{:S(2)}, u32[]{:S(2)}) collective-permute-start(bf16[592,256]{1,0:T(8,128)(2,1)S(1)} %collective-permute-done.p0), channel_id=1, source_target_pairs={{0,2},{2,0},{1,3},{3,1},{4,6},{6,4},{5,7},{7,5},{8,10},{10,8},{9,1... | collective-permute-start | bytes 909320 | tf_op jit(solution)/shard_map/ppermute | solution.py:334
  23.8 12.9 %collective-permute-start.2 = (bf16[592,256]{1,0:T(8,128)(2,1)S(1)}, bf16[592,256]{1,0:T(8,128)(2,1)S(1)}, u32[]{:S(2)}, u32[]{:S(2)}) collective-permute-start(bf16[592,256]{1,0:T(8,128)(2,1)S(1)} %broadcast_select_fusion), channel_id=1, source_target_pairs={{0,32},{32,0},{1,33},{33,1},{2,34},{34,2},{3,35},{35,3},{4,36},{36... | collective-permute-start | bytes 909320 | tf_op jit(solution)/shard_map/ppermute | solution.py:335
  27.4 10.4 %collective-permute-start.3 = (bf16[592,256]{1,0:T(8,128)(2,1)S(1)}, bf16[592,256]{1,0:T(8,128)(2,1)S(1)}, u32[]{:S(2)}, u32[]{:S(2)}) collective-permute-start(bf16[592,256]{1,0:T(8,128)(2,1)S(1)} %broadcast_select_fusion), channel_id=1, source_target_pairs={{0,34},{2,32},{32,2},{34,0},{1,35},{3,33},{33,3},{35,1},{4,38},{6,... | collective-permute-start | bytes 909320 | tf_op jit(solution)/shard_map/ppermute | solution.py:336
  32.1 5.7 %collective-permute-start.4 = (bf16[592,256]{1,0:T(8,128)(2,1)S(1)}, bf16[592,256]{1,0:T(8,128)(2,1)S(1)}, u32[]{:S(2)}, u32[]{:S(2)}) collective-permute-start(bf16[592,256]{1,0:T(8,128)(2,1)S(1)} %collective-permute-done.p0), channel_id=1, source_target_pairs={{0,1},{1,0},{2,3},{3,2},{4,5},{5,4},{6,7},{7,6},{8,9},{9,8},{10,11... | collective-permute-start | bytes 909320 | tf_op jit(solution)/shard_map/ppermute | solution.py:349
  37.9 4.6 %collective-permute-start.5 = (bf16[3,592,256]{2,1,0:T(8,128)(2,1)S(1)}, bf16[3,592,256]{2,1,0:T(8,128)(2,1)S(1)}, u32[]{:S(2)}, u32[]{:S(2)}) collective-permute-start(bf16[3,592,256]{2,1,0:T(8,128)(2,1)S(1)} %shard_map.120), channel_id=1, source_target_pairs={{0,1},{1,0},{2,3},{3,2},{4,5},{5,4},{6,7},{7,6},{8,9},{9,8},{10,11... | collective-permute-start | bytes 2727944 | tf_op jit(solution)/shard_map/ppermute | solution.py:352
  39.8 2.7 %copy-start = (bf16[256,2560]{1,0:T(8,128)(2,1)S(1)}, bf16[256,2560]{1,0:T(8,128)(2,1)}, u32[]{:S(2)}) copy-start(bf16[256,2560]{1,0:T(8,128)(2,1)} %out_proj.1) | copy-start | bytes 3932164
  42.5 6.0 %copy-start.1 = (bf16[3,160,768]{2,1,0:T(8,128)(2,1)S(1)}, bf16[3,160,768]{2,1,0:T(8,128)(2,1)}, u32[]{:S(2)}) copy-start(bf16[3,160,768]{2,1,0:T(8,128)(2,1)} %gate.1) | copy-start | bytes 2211844
  42.6 6.0 %copy-start.2 = (bf16[3,160,768]{2,1,0:T(8,128)(2,1)S(1)}, bf16[3,160,768]{2,1,0:T(8,128)(2,1)}, u32[]{:S(2)}) copy-start(bf16[3,160,768]{2,1,0:T(8,128)(2,1)} %up.1) | copy-start | bytes 2211844
  42.6 6.0 %copy-start.3 = (bf16[3,768,160]{1,2,0:T(8,128)(2,1)S(1)}, bf16[3,768,160]{1,2,0:T(8,128)(2,1)}, u32[]{:S(2)}) copy-start(bf16[3,768,160]{1,2,0:T(8,128)(2,1)} %param.23) | copy-start | bytes 2211844
  46.2 4.1 %collective-permute-start.6 = (bf16[128,2560]{1,0:T(8,128)(2,1)S(1)}, bf16[128,2560]{1,0:T(8,128)(2,1)S(1)}, u32[]{:S(2)}, u32[]{:S(2)}) collective-permute-start(bf16[128,2560]{1,0:T(8,128)(2,1)S(1)} %get-tuple-element.52), channel_id=1, source_target_pairs={{0,1},{1,0},{2,3},{3,2},{4,5},{5,4},{6,7},{7,6},{8,9},{9,8},{10,11... | collective-permute-start | bytes 1966088 | tf_op jit(solution)/shard_map/ppermute | solution.py:363
  50.3 14.3 %copy-start.13 = (s32[8,16,6]{1,0,2:T(8,128)S(1)}, s32[8,16,6]{1,0,2:T(8,128)}, u32[]{:S(2)}) copy-start(s32[8,16,6]{1,0,2:T(8,128)} %param.19) | copy-start | bytes 9220
  50.3 17.3 %copy-start.14 = (f32[2560]{0:T(1024)S(1)}, f32[2560]{0:T(1024)}, u32[]{:S(2)}) copy-start(f32[2560]{0:T(1024)} %param.18) | copy-start | bytes 30724
  50.3 34.0 %copy-start.10 = (bf16[8,2560]{1,0:T(8,128)(2,1)S(1)}, bf16[8,2560]{1,0:T(8,128)(2,1)}, u32[]{:S(2)}) copy-start(bf16[8,2560]{1,0:T(8,128)(2,1)} %residual.1) | copy-start | bytes 122884
  51.3 33.0 %all-to-all-start = ((bf16[16,8,2560]{2,1,0:T(8,128)(2,1)}), bf16[16,8,2560]{2,1,0:T(8,128)(2,1)S(1)}, u32[]{:S(2)}, u32[]{:S(2)}) async-start(bf16[16,8,2560]{2,1,0:T(8,128)(2,1)} %shard_map.123), calls=%async_computation | async-start | bytes 1310720 | tf_op jit(solution)/shard_map/all_to_all | solution.py:374
  64.8 31.0 %collective-permute-start.7 = (bf16[3,160,768]{2,1,0:T(8,128)(2,1)S(1)}, bf16[3,160,768]{2,1,0:T(8,128)(2,1)S(1)}, u32[]{:S(2)}, u32[]{:S(2)}) collective-permute-start(bf16[3,160,768]{2,1,0:T(8,128)(2,1)S(1)} %get-tuple-element.55), channel_id=1, source_target_pairs={{0,32},{32,0},{1,33},{33,1},{2,34},{34,2},{3,35},{35,3},{4,36},{36... | collective-permute-start | bytes 2211848 | tf_op jit(solution)/shard_map/ppermute | solution.py:372
  85.3 18.4 %all-to-all-start.1 = ((bf16[16,8,512]{2,1,0:T(8,128)(2,1)}), bf16[16,8,512]{2,1,0:T(8,128)(2,1)S(1)}, u32[]{:S(2)}, u32[]{:S(2)}) async-start(bf16[16,8,512]{2,1,0:T(8,128)(2,1)} %shard_map.125), calls=%async_computation.1 | async-start | bytes 262144 | tf_op jit(solution)/shard_map/all_to_all | solution.py:378
  95.9 9.1 %copy-start.4 = (bf16[3,160,768]{2,1,0:T(8,128)(2,1)}, bf16[3,160,768]{2,1,0:T(8,128)(2,1)S(1)}, u32[]{:S(2)}) copy-start(bf16[3,160,768]{2,1,0:T(8,128)(2,1)S(1)} %collective-permute-done.7.got) | copy-start | bytes 2211844
  105.0 27.2 %all-to-all-start.2 = ((bf16[32,80,128]{2,1,0:T(8,128)(2,1)}), bf16[32,80,128]{2,1,0:T(8,128)(2,1)S(1)}, u32[]{:S(2)}, u32[]{:S(2)}) async-start(bf16[32,80,128]{2,1,0:T(8,128)(2,1)} %shard_map.126), calls=%async_computation.2 | async-start | bytes 1310720 | tf_op jit(solution)/shard_map/all_to_all | solution.py:407
  111.6 18.6 %collective-permute-start.8 = (bf16[3,160,384]{2,1,0:T(8,128)(2,1)}, bf16[3,160,384]{2,1,0:T(8,128)(2,1)S(1)}, u32[]{:S(2)}, u32[]{:S(2)}) collective-permute-start(bf16[3,160,384]{2,1,0:T(8,128)(2,1)} %get-tuple-element.61), channel_id=1, source_target_pairs={{0,32},{32,0},{1,33},{33,1},{2,34},{34,2},{3,35},{35,3},{4,36},{36... | collective-permute-start | bytes 1105928 | tf_op jit(solution)/shard_map/ppermute | solution.py:380
  115.3 14.9 %copy-start.7 = (bf16[3,160,384]{2,1,0:T(8,128)(2,1)S(1)}, bf16[3,160,384]{2,1,0:T(8,128)(2,1)}, u32[]{:S(2)}) copy-start(bf16[3,160,384]{2,1,0:T(8,128)(2,1)} %copy-done.6) | copy-start | bytes 1105924
  201.7 9.3 %copy-start.12 = (f32[8,16,6]{1,0,2:T(8,128)S(1)}, f32[8,16,6]{1,0,2:T(8,128)}, u32[]{:S(2)}) copy-start(f32[8,16,6]{1,0,2:T(8,128)} %param.20) | copy-start | bytes 9220
  204.0 27.2 %all-to-all-start.5 = ((bf16[32,80,128]{2,1,0:T(8,128)(2,1)}), bf16[32,80,128]{2,1,0:T(8,128)(2,1)S(1)}, u32[]{:S(2)}, u32[]{:S(2)}) async-start(bf16[32,80,128]{2,1,0:T(8,128)(2,1)} %shard_map.131), calls=%async_computation.5 | async-start | bytes 1310720 | tf_op jit(solution)/shard_map/all_to_all | solution.py:418
  231.7 6.2 %collective-permute-start.9 = (bf16[128,160]{1,0:T(8,128)(2,1)S(1)}, bf16[128,160]{1,0:T(8,128)(2,1)S(1)}, u32[]{:S(2)}, u32[]{:S(2)}) collective-permute-start(bf16[128,160]{1,0:T(8,128)(2,1)S(1)} %get-tuple-element.66), channel_id=1, source_target_pairs={{0,32},{32,0},{1,33},{33,1},{2,34},{34,2},{3,35},{35,3},{4,36},{36... | collective-permute-start | bytes 122888 | tf_op jit(solution)/shard_map/ppermute | solution.py:422
  (5 other events, 6.6 us)

commit v16 on v15

--- a/solution.py
+++ b/solution.py
@@ -109,7 +109,7 @@
 
 
 def add_kernel(keep, got, out):
-    out[...] = (keep[...] + got[...].astype(f32)).reshape(out.shape).astype(bf16)
+    out[...] = (keep[...].astype(f32) + got[...].astype(f32)).reshape(out.shape).astype(bf16)
 
 
 def gather_kernel(p1, p2, p3, out):
@@ -201,10 +201,9 @@
 def join_down_kernel(keep, got, out):
     rows, width = keep.shape[1:]
     for j in range(3):
-        lanes = slice(j * width, (j + 1) * width)
-        out[:rows, lanes] = keep[j]
-        out[rows : 2 * rows, lanes] = got[j]
-        out[2 * rows :, lanes] = got[j, 256 - rows :]
+        parts = [keep[j], got[j], got[j, 256 - rows :]]
+        joined = jnp.concatenate([part.astype(f32) for part in parts], axis=0)
+        out[j * width : (j + 1) * width, :] = joined.T.astype(bf16)
 
 
 def gate_up_kernel(received, weights, pre):
@@ -229,7 +228,7 @@
     masks = [row_mask(step, j) for j in range(3)]
     for r in range(0, hidden.shape[0], step):
         rows = spread_experts(hidden[r : r + step, :], masks)
-        total = nt_dot(rows, weights[...])
+        total = jnp.dot(rows, weights[...], preferred_element_type=f32)
         for n in range(step // SLOTS):
             store_packed(out, r // SLOTS + n, total[n * SLOTS : (n + 1) * SLOTS])
 
@@ -355,7 +354,7 @@
     )(info, query_rows, pieces[1], pieces[2], pieces[3], first_other, *state)
     send, keep = call(
         last_attention_kernel,
-        [sds((half, width_model), bf16), sds((half, width_model), f32)],
+        [sds((half, width_model), bf16), sds((half, width_model), bf16)],
         [pltpu.VMEM((2, 256, 3 * 256), f32), pltpu.VMEM((2, 256, VDIM), bf16)],
         True,
         8,
@@ -380,7 +379,7 @@
     down_got = lax.ppermute(down_send, "xl", SWAP)
     split = split.reshape(128, 512)
     w_in = call(join_in_kernel, [sds((3 * 384, 2 * ff_half), bf16)], count=2)(in_keep, in_got)
-    w_down = call(join_down_kernel, [sds((384, 3 * ff_half), bf16)], count=2)(down_keep, down_got)
+    w_down = call(join_down_kernel, [sds((3 * ff_half, 384), bf16)], count=2)(down_keep, down_got)
 
     routes = jnp.transpose(route_ids, (1, 0, 2)).reshape(128, TOPK)
     expert_axis = jnp.arange(EXPERTS, dtype=i32)

time: 241 us -> 241 us (level)
  no operation moved by 1% of the time
where the time goes in v16:
time: 241 us; the launch traced here: 239 us
  waiting for transfers between devices  78.3 us (32%)
  starting transfers between devices  67.2 us (28%)
  blocking collectives  67.1 us (28%)
  Pallas kernels  18.6 us (8%)
  local copies, waits for them, and re-layouts  4.88 us (2%)
    all_to_all x1, blocking collectives, on_device(): lax.all_to_all(pre.reshape(8, 128, 2 * ff_half), 'y', split_axis=0, conca...  42.6 us
    all_to_all x1, blocking collectives, on_device(): lax.all_to_all(hidden, 'y', split_axis=0, concat_axis=0, tiled=True)  24.5 us
    all_to_all x1, waiting for transfers between devices, on_device(): lax.all_to_all(expert_out, EXP, split_axis=0, concat_axis=0, tiled=True)  19.6 us
    all_to_all x1, waiting for transfers between devices, on_device(): lax.all_to_all(pair_sum, ('z', 'xh'), split_axis=0, concat_axis=0, tiled=...  16.5 us
    ppermute x1, waiting for transfers between devices, on_device(): down_got = lax.ppermute(down_send, 'xl', SWAP)  14.8 us
    all_to_all x1, starting transfers between devices, on_device(): lax.all_to_all(pair_sum, ('z', 'xh'), split_axis=0, concat_axis=0, tiled=...  13.3 us
    ppermute x1, waiting for transfers between devices, on_device(): fetched = lax.ppermute(keys_own, ('y', 'xh', 'core'), pairs)  10.6 us
    all_to_all x1, starting transfers between devices, on_device(): split = lax.all_to_all(packed, CTX, split_axis=0, concat_axis=0, tiled=True)  10 us
  transfers between devices with their start and end apart: 14, of which 11 were waited for; matrix products, arithmetic and copies ran while one was open for 2% of the time, Pallas kernels for 3%

profile of v16, /device:TPU:6, one launch (start us, length us, event | category | flops | bytes accessed | tf_op | source)
XLA Modules:
  0.0 239.0 jit_solution(12828627413042905511)
XLA Ops:
  1.7 4.5 %collective-permute-start = (bf16[592,256]{1,0:T(8,128)(2,1)S(1)}, bf16[592,256]{1,0:T(8,128)(2,1)S(1)}, u32[]{:S(2)}, u32[]{:S(2)}) collective-permute-start(bf16[592,256]{1,0:T(8,128)(2,1)S(1)} %shard_map.118.own), channel_id=1, source_target_pairs={{0,64},{1,193},{2,130},{3,259},{64,128},{65,257},{66,194},{67,323}... | collective-permute-start | bytes 909320 | tf_op jit(solution)/shard_map/ppermute | solution.py:302
  8.0 10.6 %collective-permute-done.p0 = bf16[592,256]{1,0:T(8,128)(2,1)S(1)} collective-permute-done((bf16[592,256]{1,0:T(8,128)(2,1)S(1)}, bf16[592,256]{1,0:T(8,128)(2,1)S(1)}, u32[]{:S(2)}, u32[]{:S(2)}) %collective-permute-start) | collective-permute-done | bytes 303136 | tf_op jit(solution)/shard_map/ppermute | solution.py:302
  18.6 5.0 %collective-permute-start.1 = (bf16[592,256]{1,0:T(8,128)(2,1)S(1)}, bf16[592,256]{1,0:T(8,128)(2,1)S(1)}, u32[]{:S(2)}, u32[]{:S(2)}) collective-permute-start(bf16[592,256]{1,0:T(8,128)(2,1)S(1)} %collective-permute-done.p0), channel_id=1, source_target_pairs={{0,2},{2,0},{1,3},{3,1},{4,6},{6,4},{5,7},{7,5},{8,10},{10,8},{9,1... | collective-permute-start | bytes 909320 | tf_op jit(solution)/shard_map/ppermute | solution.py:333
  23.8 3.6 %collective-permute-start.2 = (bf16[592,256]{1,0:T(8,128)(2,1)S(1)}, bf16[592,256]{1,0:T(8,128)(2,1)S(1)}, u32[]{:S(2)}, u32[]{:S(2)}) collective-permute-start(bf16[592,256]{1,0:T(8,128)(2,1)S(1)} %broadcast_select_fusion), channel_id=1, source_target_pairs={{0,32},{32,0},{1,33},{33,1},{2,34},{34,2},{3,35},{35,3},{4,36},{36... | collective-permute-start | bytes 909320 | tf_op jit(solution)/shard_map/ppermute | solution.py:334
  34.0 2.7 %collective-permute-done.2.p2 = bf16[592,256]{1,0:T(8,128)(2,1)S(1)} collective-permute-done((bf16[592,256]{1,0:T(8,128)(2,1)S(1)}, bf16[592,256]{1,0:T(8,128)(2,1)S(1)}, u32[]{:S(2)}, u32[]{:S(2)}) %collective-permute-start.2) | collective-permute-done | bytes 303136 | tf_op jit(solution)/shard_map/ppermute | solution.py:334
  40.0 2.6 %shard_map.121 = (f32[2,256,128]{2,1,0:T(8,128)S(1)}, f32[2,256,128]{2,1,0:T(8,128)S(1)}, f32[2,256,512]{2,1,0:T(8,128)S(1)}) custom-call(s32[10]{0:T(128)S(1)} %stack.43.info, bf16[2,256,592]{2,1,0:T(8,128)(2,1)S(1)} %bitcast.37, bf16[592,256]{1,0:T(8,128)(2,1)S(1)} %collective-permute-done.1.p1, bf16[592,256]{1,0:T(8,128)(2,1)S(1)} %collective-permute-done.2.p2, ...), custom_call_target="tpu_custom_call" | custom-call | tf_op jit(solution)/shard_map/pallas_call | solution.py:352
  42.7 3.6 %shard_map.122 = (bf16[128,2560]{1,0:T(8,128)(2,1)S(1)}, bf16[128,2560]{1,0:T(8,128)(2,1)S(1)}) custom-call(s32[10]{0:T(128)S(1)} %stack.43.info, bf16[2,256,592]{2,1,0:T(8,128)(2,1)S(1)} %bitcast.38, bf16[3,592,256]{2,1,0:T(8,128)(2,1)S(1)} %collective-permute-done.5.others, f32[2,256,128]{2,1,0:T(8,128)S(1)} %get-tuple-element.48.old_peak, ...), custom_call_target="tpu_custom_call" | custom-call | tf_op jit(solution)/shard_map/pallas_call | solution.py:355
  46.3 2.4 %collective-permute-start.6 = (bf16[128,2560]{1,0:T(8,128)(2,1)S(1)}, bf16[128,2560]{1,0:T(8,128)(2,1)S(1)}, u32[]{:S(2)}, u32[]{:S(2)}) collective-permute-start(bf16[128,2560]{1,0:T(8,128)(2,1)S(1)} %get-tuple-element.52), channel_id=1, source_target_pairs={{0,1},{1,0},{2,3},{3,2},{4,5},{5,4},{6,7},{7,6},{8,9},{9,8},{10,11... | collective-permute-start | bytes 1966088 | tf_op jit(solution)/shard_map/ppermute | solution.py:362
  51.4 13.3 %all-to-all-start = ((bf16[16,8,2560]{2,1,0:T(8,128)(2,1)}), bf16[16,8,2560]{2,1,0:T(8,128)(2,1)S(1)}, u32[]{:S(2)}, u32[]{:S(2)}) async-start(bf16[16,8,2560]{2,1,0:T(8,128)(2,1)} %shard_map.123), calls=%async_computation | async-start | bytes 1310720 | tf_op jit(solution)/shard_map/all_to_all | solution.py:373
  65.0 2.7 %collective-permute-start.7 = (bf16[3,160,768]{2,1,0:T(8,128)(2,1)S(1)}, bf16[3,160,768]{2,1,0:T(8,128)(2,1)S(1)}, u32[]{:S(2)}, u32[]{:S(2)}) collective-permute-start(bf16[3,160,768]{2,1,0:T(8,128)(2,1)S(1)} %get-tuple-element.55), channel_id=1, source_target_pairs={{0,32},{32,0},{1,33},{33,1},{2,34},{34,2},{3,35},{35,3},{4,36},{36... | collective-permute-start | bytes 2211848 | tf_op jit(solution)/shard_map/ppermute | solution.py:371
  68.0 16.5 %all-to-all-done.spread = bf16[16,8,2560]{2,1,0:T(8,128)(2,1)S(1)} async-done(((bf16[16,8,2560]{2,1,0:T(8,128)(2,1)}), bf16[16,8,2560]{2,1,0:T(8,128)(2,1)S(1)}, u32[]{:S(2)}, u32[]{:S(2)}) %all-to-all-start) | async-done | bytes 655392 | tf_op jit(solution)/shard_map/all_to_all | solution.py:373
  85.4 10.0 %all-to-all-start.1 = ((bf16[16,8,512]{2,1,0:T(8,128)(2,1)}), bf16[16,8,512]{2,1,0:T(8,128)(2,1)S(1)}, u32[]{:S(2)}, u32[]{:S(2)}) async-start(bf16[16,8,512]{2,1,0:T(8,128)(2,1)} %shard_map.125), calls=%async_computation.1 | async-start | bytes 262144 | tf_op jit(solution)/shard_map/all_to_all | solution.py:377
  96.0 7.8 %all-to-all-done.1 = bf16[16,8,512]{2,1,0:T(8,128)(2,1)S(1)} async-done(((bf16[16,8,512]{2,1,0:T(8,128)(2,1)}), bf16[16,8,512]{2,1,0:T(8,128)(2,1)S(1)}, u32[]{:S(2)}, u32[]{:S(2)}) %all-to-all-start.1) | async-done | bytes 131104 | tf_op jit(solution)/shard_map/all_to_all | solution.py:377
  105.2 6.6 %all-to-all-start.2 = ((bf16[32,80,128]{2,1,0:T(8,128)(2,1)}), bf16[32,80,128]{2,1,0:T(8,128)(2,1)S(1)}, u32[]{:S(2)}, u32[]{:S(2)}) async-start(bf16[32,80,128]{2,1,0:T(8,128)(2,1)} %shard_map.126), calls=%async_computation.2 | async-start | bytes 1310720 | tf_op jit(solution)/shard_map/all_to_all | solution.py:406
  111.7 2.6 %collective-permute-start.8 = (bf16[3,160,384]{2,1,0:T(8,128)(2,1)}, bf16[3,160,384]{2,1,0:T(8,128)(2,1)S(1)}, u32[]{:S(2)}, u32[]{:S(2)}) collective-permute-start(bf16[3,160,384]{2,1,0:T(8,128)(2,1)} %get-tuple-element.61), channel_id=1, source_target_pairs={{0,32},{32,0},{1,33},{33,1},{2,34},{34,2},{3,35},{35,3},{4,36},{36... | collective-permute-start | bytes 1105928 | tf_op jit(solution)/shard_map/ppermute | solution.py:379
  115.6 14.8 %collective-permute-done.8.got = bf16[3,160,384]{2,1,0:T(8,128)(2,1)S(1)} collective-permute-done((bf16[3,160,384]{2,1,0:T(8,128)(2,1)}, bf16[3,160,384]{2,1,0:T(8,128)(2,1)S(1)}, u32[]{:S(2)}, u32[]{:S(2)}) %collective-permute-start.8) | collective-permute-done | bytes 368672 | tf_op jit(solution)/shard_map/ppermute | solution.py:379
  132.3 2.2 shard_map.129
  134.5 42.6 %all_to_all.30.parts = bf16[8,128,768]{2,1,0:T(8,128)(2,1)S(1)} all-to-all(bf16[8,128,768]{2,1,0:T(8,128)(2,1)S(1)} %bitcast.39), channel_id=1, replica_groups=mesh['y'=8,'xl'=2,'z'=8,'xh'=2,'core'=2] {'y'}, dimensions={0} | all-to-all | bytes 3145728 | tf_op jit(solution)/shard_map/all_to_all | solution.py:409
  177.4 24.5 %all_to_all.31 = bf16[8,128,384]{2,1,0:T(8,128)(2,1)S(1)} all-to-all(bf16[8,128,384]{2,1,0:T(8,128)(2,1)S(1)} %shard_map.130), channel_id=1, replica_groups=mesh['y'=8,'xl'=2,'z'=8,'xh'=2,'core'=2] {'y'}, dimensions={0} | all-to-all | bytes 1572864 | tf_op jit(solution)/shard_map/all_to_all | solution.py:413
  201.9 2.3 shard_map.131
  204.2 6.9 %all-to-all-start.5 = ((bf16[32,80,128]{2,1,0:T(8,128)(2,1)}), bf16[32,80,128]{2,1,0:T(8,128)(2,1)S(1)}, u32[]{:S(2)}, u32[]{:S(2)}) async-start(bf16[32,80,128]{2,1,0:T(8,128)(2,1)} %shard_map.131), calls=%async_computation.5 | async-start | bytes 1310720 | tf_op jit(solution)/shard_map/all_to_all | solution.py:417
  212.0 19.6 %all-to-all-done.5.returned = bf16[32,80,128]{2,1,0:T(8,128)(2,1)S(1)} async-done(((bf16[32,80,128]{2,1,0:T(8,128)(2,1)}), bf16[32,80,128]{2,1,0:T(8,128)(2,1)S(1)}, u32[]{:S(2)}, u32[]{:S(2)}) %all-to-all-start.5) | async-done | bytes 655392 | tf_op jit(solution)/shard_map/all_to_all | solution.py:417
  232.2 3.8 %collective-permute-start.9 = (bf16[128,160]{1,0:T(8,128)(2,1)S(1)}, bf16[128,160]{1,0:T(8,128)(2,1)S(1)}, u32[]{:S(2)}, u32[]{:S(2)}) collective-permute-start(bf16[128,160]{1,0:T(8,128)(2,1)S(1)} %get-tuple-element.66), channel_id=1, source_target_pairs={{0,32},{32,0},{1,33},{33,1},{2,34},{34,2},{3,35},{35,3},{4,36},{36... | collective-permute-start | bytes 122888 | tf_op jit(solution)/shard_map/ppermute | solution.py:421
  236.0 2.4 collective-permute-done.9
  (79 shorter events, 25.0 us)
Async XLA Ops:
  1.7 16.9 %collective-permute-start = (bf16[592,256]{1,0:T(8,128)(2,1)S(1)}, bf16[592,256]{1,0:T(8,128)(2,1)S(1)}, u32[]{:S(2)}, u32[]{:S(2)}) collective-permute-start(bf16[592,256]{1,0:T(8,128)(2,1)S(1)} %shard_map.118.own), channel_id=1, source_target_pairs={{0,64},{1,193},{2,130},{3,259},{64,128},{65,257},{66,194},{67,323}... | collective-permute-start | bytes 909320 | tf_op jit(solution)/shard_map/ppermute | solution.py:302
  18.6 13.5 %collective-permute-start.1 = (bf16[592,256]{1,0:T(8,128)(2,1)S(1)}, bf16[592,256]{1,0:T(8,128)(2,1)S(1)}, u32[]{:S(2)}, u32[]{:S(2)}) collective-permute-start(bf16[592,256]{1,0:T(8,128)(2,1)S(1)} %collective-permute-done.p0), channel_id=1, source_target_pairs={{0,2},{2,0},{1,3},{3,1},{4,6},{6,4},{5,7},{7,5},{8,10},{10,8},{9,1... | collective-permute-start | bytes 909320 | tf_op jit(solution)/shard_map/ppermute | solution.py:333
  23.8 12.9 %collective-permute-start.2 = (bf16[592,256]{1,0:T(8,128)(2,1)S(1)}, bf16[592,256]{1,0:T(8,128)(2,1)S(1)}, u32[]{:S(2)}, u32[]{:S(2)}) collective-permute-start(bf16[592,256]{1,0:T(8,128)(2,1)S(1)} %broadcast_select_fusion), channel_id=1, source_target_pairs={{0,32},{32,0},{1,33},{33,1},{2,34},{34,2},{3,35},{35,3},{4,36},{36... | collective-permute-start | bytes 909320 | tf_op jit(solution)/shard_map/ppermute | solution.py:334
  27.4 10.4 %collective-permute-start.3 = (bf16[592,256]{1,0:T(8,128)(2,1)S(1)}, bf16[592,256]{1,0:T(8,128)(2,1)S(1)}, u32[]{:S(2)}, u32[]{:S(2)}) collective-permute-start(bf16[592,256]{1,0:T(8,128)(2,1)S(1)} %broadcast_select_fusion), channel_id=1, source_target_pairs={{0,34},{2,32},{32,2},{34,0},{1,35},{3,33},{33,3},{35,1},{4,38},{6,... | collective-permute-start | bytes 909320 | tf_op jit(solution)/shard_map/ppermute | solution.py:335
  32.1 5.7 %collective-permute-start.4 = (bf16[592,256]{1,0:T(8,128)(2,1)S(1)}, bf16[592,256]{1,0:T(8,128)(2,1)S(1)}, u32[]{:S(2)}, u32[]{:S(2)}) collective-permute-start(bf16[592,256]{1,0:T(8,128)(2,1)S(1)} %collective-permute-done.p0), channel_id=1, source_target_pairs={{0,1},{1,0},{2,3},{3,2},{4,5},{5,4},{6,7},{7,6},{8,9},{9,8},{10,11... | collective-permute-start | bytes 909320 | tf_op jit(solution)/shard_map/ppermute | solution.py:348
  37.9 4.7 %copy-start = (bf16[256,2560]{1,0:T(8,128)(2,1)S(1)}, bf16[256,2560]{1,0:T(8,128)(2,1)}, u32[]{:S(2)}) copy-start(bf16[256,2560]{1,0:T(8,128)(2,1)} %out_proj.1) | copy-start | bytes 3932164
  37.9 4.7 %collective-permute-start.5 = (bf16[3,592,256]{2,1,0:T(8,128)(2,1)S(1)}, bf16[3,592,256]{2,1,0:T(8,128)(2,1)S(1)}, u32[]{:S(2)}, u32[]{:S(2)}) collective-permute-start(bf16[3,592,256]{2,1,0:T(8,128)(2,1)S(1)} %shard_map.120), channel_id=1, source_target_pairs={{0,1},{1,0},{2,3},{3,2},{4,5},{5,4},{6,7},{7,6},{8,9},{9,8},{10,11... | collective-permute-start | bytes 2727944 | tf_op jit(solution)/shard_map/ppermute | solution.py:351
  42.7 6.0 %copy-start.1 = (bf16[3,160,768]{2,1,0:T(8,128)(2,1)S(1)}, bf16[3,160,768]{2,1,0:T(8,128)(2,1)}, u32[]{:S(2)}) copy-start(bf16[3,160,768]{2,1,0:T(8,128)(2,1)} %gate.1) | copy-start | bytes 2211844
  42.7 6.0 %copy-start.2 = (bf16[3,160,768]{2,1,0:T(8,128)(2,1)S(1)}, bf16[3,160,768]{2,1,0:T(8,128)(2,1)}, u32[]{:S(2)}) copy-start(bf16[3,160,768]{2,1,0:T(8,128)(2,1)} %up.1) | copy-start | bytes 2211844
  42.7 6.0 %copy-start.3 = (bf16[3,768,160]{1,2,0:T(8,128)(2,1)S(1)}, bf16[3,768,160]{1,2,0:T(8,128)(2,1)}, u32[]{:S(2)}) copy-start(bf16[3,768,160]{1,2,0:T(8,128)(2,1)} %param.23) | copy-start | bytes 2211844
  46.3 4.1 %collective-permute-start.6 = (bf16[128,2560]{1,0:T(8,128)(2,1)S(1)}, bf16[128,2560]{1,0:T(8,128)(2,1)S(1)}, u32[]{:S(2)}, u32[]{:S(2)}) collective-permute-start(bf16[128,2560]{1,0:T(8,128)(2,1)S(1)} %get-tuple-element.52), channel_id=1, source_target_pairs={{0,1},{1,0},{2,3},{3,2},{4,5},{5,4},{6,7},{7,6},{8,9},{9,8},{10,11... | collective-permute-start | bytes 1966088 | tf_op jit(solution)/shard_map/ppermute | solution.py:362
  50.3 14.5 %copy-start.13 = (s32[8,16,6]{1,0,2:T(8,128)S(1)}, s32[8,16,6]{1,0,2:T(8,128)}, u32[]{:S(2)}) copy-start(s32[8,16,6]{1,0,2:T(8,128)} %param.19) | copy-start | bytes 9220
  50.3 17.4 %copy-start.14 = (f32[2560]{0:T(1024)S(1)}, f32[2560]{0:T(1024)}, u32[]{:S(2)}) copy-start(f32[2560]{0:T(1024)} %param.18) | copy-start | bytes 30724
  50.4 34.0 %copy-start.10 = (bf16[8,2560]{1,0:T(8,128)(2,1)S(1)}, bf16[8,2560]{1,0:T(8,128)(2,1)}, u32[]{:S(2)}) copy-start(bf16[8,2560]{1,0:T(8,128)(2,1)} %residual.1) | copy-start | bytes 122884
  51.4 33.0 %all-to-all-start = ((bf16[16,8,2560]{2,1,0:T(8,128)(2,1)}), bf16[16,8,2560]{2,1,0:T(8,128)(2,1)S(1)}, u32[]{:S(2)}, u32[]{:S(2)}) async-start(bf16[16,8,2560]{2,1,0:T(8,128)(2,1)} %shard_map.123), calls=%async_computation | async-start | bytes 1310720 | tf_op jit(solution)/shard_map/all_to_all | solution.py:373
  65.0 31.0 %collective-permute-start.7 = (bf16[3,160,768]{2,1,0:T(8,128)(2,1)S(1)}, bf16[3,160,768]{2,1,0:T(8,128)(2,1)S(1)}, u32[]{:S(2)}, u32[]{:S(2)}) collective-permute-start(bf16[3,160,768]{2,1,0:T(8,128)(2,1)S(1)} %get-tuple-element.55), channel_id=1, source_target_pairs={{0,32},{32,0},{1,33},{33,1},{2,34},{34,2},{3,35},{35,3},{4,36},{36... | collective-permute-start | bytes 2211848 | tf_op jit(solution)/shard_map/ppermute | solution.py:371
  85.4 18.4 %all-to-all-start.1 = ((bf16[16,8,512]{2,1,0:T(8,128)(2,1)}), bf16[16,8,512]{2,1,0:T(8,128)(2,1)S(1)}, u32[]{:S(2)}, u32[]{:S(2)}) async-start(bf16[16,8,512]{2,1,0:T(8,128)(2,1)} %shard_map.125), calls=%async_computation.1 | async-start | bytes 262144 | tf_op jit(solution)/shard_map/all_to_all | solution.py:377
  96.0 9.1 %copy-start.4 = (bf16[3,160,768]{2,1,0:T(8,128)(2,1)}, bf16[3,160,768]{2,1,0:T(8,128)(2,1)S(1)}, u32[]{:S(2)}) copy-start(bf16[3,160,768]{2,1,0:T(8,128)(2,1)S(1)} %collective-permute-done.7.got) | copy-start | bytes 2211844
  105.2 27.2 %all-to-all-start.2 = ((bf16[32,80,128]{2,1,0:T(8,128)(2,1)}), bf16[32,80,128]{2,1,0:T(8,128)(2,1)S(1)}, u32[]{:S(2)}, u32[]{:S(2)}) async-start(bf16[32,80,128]{2,1,0:T(8,128)(2,1)} %shard_map.126), calls=%async_computation.2 | async-start | bytes 1310720 | tf_op jit(solution)/shard_map/all_to_all | solution.py:406
  111.7 18.6 %collective-permute-start.8 = (bf16[3,160,384]{2,1,0:T(8,128)(2,1)}, bf16[3,160,384]{2,1,0:T(8,128)(2,1)S(1)}, u32[]{:S(2)}, u32[]{:S(2)}) collective-permute-start(bf16[3,160,384]{2,1,0:T(8,128)(2,1)} %get-tuple-element.61), channel_id=1, source_target_pairs={{0,32},{32,0},{1,33},{33,1},{2,34},{34,2},{3,35},{35,3},{4,36},{36... | collective-permute-start | bytes 1105928 | tf_op jit(solution)/shard_map/ppermute | solution.py:379
  115.4 14.9 %copy-start.7 = (bf16[3,160,384]{2,1,0:T(8,128)(2,1)S(1)}, bf16[3,160,384]{2,1,0:T(8,128)(2,1)}, u32[]{:S(2)}) copy-start(bf16[3,160,384]{2,1,0:T(8,128)(2,1)} %copy-done.6) | copy-start | bytes 1105924
  201.9 9.5 %copy-start.12 = (f32[8,16,6]{1,0,2:T(8,128)S(1)}, f32[8,16,6]{1,0,2:T(8,128)}, u32[]{:S(2)}) copy-start(f32[8,16,6]{1,0,2:T(8,128)} %param.20) | copy-start | bytes 9220
  204.2 27.4 %all-to-all-start.5 = ((bf16[32,80,128]{2,1,0:T(8,128)(2,1)}), bf16[32,80,128]{2,1,0:T(8,128)(2,1)S(1)}, u32[]{:S(2)}, u32[]{:S(2)}) async-start(bf16[32,80,128]{2,1,0:T(8,128)(2,1)} %shard_map.131), calls=%async_computation.5 | async-start | bytes 1310720 | tf_op jit(solution)/shard_map/all_to_all | solution.py:417
  232.2 6.2 %collective-permute-start.9 = (bf16[128,160]{1,0:T(8,128)(2,1)S(1)}, bf16[128,160]{1,0:T(8,128)(2,1)S(1)}, u32[]{:S(2)}, u32[]{:S(2)}) collective-permute-start(bf16[128,160]{1,0:T(8,128)(2,1)S(1)} %get-tuple-element.66), channel_id=1, source_target_pairs={{0,32},{32,0},{1,33},{33,1},{2,34},{34,2},{3,35},{35,3},{4,36},{36... | collective-permute-start | bytes 122888 | tf_op jit(solution)/shard_map/ppermute | solution.py:421
  (5 other events, 8.7 us)

commit v17 on v13

--- a/solution.py
+++ b/solution.py
@@ -374,11 +374,9 @@
         spread, residual, norm_gain[None, :]
     )
     split = lax.all_to_all(packed, CTX, split_axis=0, concat_axis=0, tiled=True)
-    split, in_got, down_send = lax.optimization_barrier((split, in_got, down_send))
-    down_got = lax.ppermute(down_send, "xl", SWAP)
+    split, in_got = lax.optimization_barrier((split, in_got))
     split = split.reshape(128, 512)
     w_in = call(join_in_kernel, [sds((3 * 384, 2 * ff_half), bf16)], count=2)(in_keep, in_got)
-    w_down = call(join_down_kernel, [sds((384, 3 * ff_half), bf16)], count=2)(down_keep, down_got)
 
     routes = jnp.transpose(route_ids, (1, 0, 2)).reshape(128, TOPK)
     expert_axis = jnp.arange(EXPERTS, dtype=i32)
@@ -403,11 +401,14 @@
     travel = sds((32, 80, 128), bf16)
     outgoing = call(pick_kernel, [travel], count=2)(picker, split)
     received = lax.all_to_all(outgoing, EXP, split_axis=0, concat_axis=0, tiled=True)
-    received, w_in, w_down = lax.optimization_barrier((received, w_in, w_down))
+    received, w_in, down_send = lax.optimization_barrier((received, w_in, down_send))
+    down_got = lax.ppermute(down_send, "xl", SWAP)
     pre = call(gate_up_kernel, [sds((32 * SLOTS, 2 * ff_half), bf16)], count=2)(received, w_in)
     pre_parts = lax.all_to_all(
         pre.reshape(8, 128, 2 * ff_half), "y", split_axis=0, concat_axis=0, tiled=True
     )
+    pre_parts, down_got = lax.optimization_barrier((pre_parts, down_got))
+    w_down = call(join_down_kernel, [sds((384, 3 * ff_half), bf16)], count=2)(down_keep, down_got)
     hidden = call(hidden_kernel, [sds((8, 128, ff_half), bf16)], count=1)(pre_parts)
     hidden_all = lax.all_to_all(hidden, "y", split_axis=0, concat_axis=0, tiled=True)
     expert_out = call(down_kernel, [travel], count=2)(

time: 241 us -> 242 us (level)
  blocking collectives: 67 us -> 0 us
  waiting for transfers between devices: 78.4 us -> 142 us
  starting transfers between devices: 67 us -> 71.7 us
    all_to_all x2 -> x0, blocking collectives: 67 us -> none  [the longest x1 42.6 us: on_device(): lax.all_to_all(pre.reshape(8, 128, 2 * ff_half), 'y', split_axis=0, conca...]
    all_to_all x0 -> x2, waiting for transfers between devices: none -> 49 us  [the longest x1 27.8 us: on_device(): lax.all_to_all(pre.reshape(8, 128, 2 * ff_half), 'y', split_axis=0, conca...]
    all_to_all x1, waiting for transfers between devices: 1.89 us -> 19.3 us  [on_device(): lax.all_to_all(outgoing, EXP, split_axis=0, concat_axis=0, tiled=True)]
    all_to_all x0 -> x2, starting transfers between devices: none -> 7.44 us  [the longest x1 3.73 us: on_device(): lax.all_to_all(hidden, 'y', split_axis=0, concat_axis=0, tiled=True)]
    ppermute x1, waiting for transfers between devices: 14.8 us -> 9.55 us  [on_device(): down_got = lax.ppermute(down_send, 'xl', SWAP)]
  transfers between devices with their start and end apart: 14 -> 16, of which waited for: 11 -> 13; matrix products, arithmetic and copies ran while one was open for 2% -> 2% of each run, Pallas kernels for 3% -> 3%
where the time goes in v17:
time: 242 us; the launch traced here: 241 us
  waiting for transfers between devices  142 us (59%)
  starting transfers between devices  71.7 us (30%)
  Pallas kernels  19.7 us (8%)
  local copies, waits for them, and re-layouts  4.89 us (2%)
    all_to_all x1, waiting for transfers between devices, on_device(): lax.all_to_all(pre.reshape(8, 128, 2 * ff_half), 'y', split_axis=0, conca...  27.8 us
    all_to_all x1, waiting for transfers between devices, on_device(): lax.all_to_all(hidden, 'y', split_axis=0, concat_axis=0, tiled=True)  21.2 us
    all_to_all x1, waiting for transfers between devices, on_device(): lax.all_to_all(expert_out, EXP, split_axis=0, concat_axis=0, tiled=True)  19.6 us
    all_to_all x1, waiting for transfers between devices, on_device(): lax.all_to_all(outgoing, EXP, split_axis=0, concat_axis=0, tiled=True)  19.3 us
    all_to_all x1, waiting for transfers between devices, on_device(): lax.all_to_all(pair_sum, ('z', 'xh'), split_axis=0, concat_axis=0, tiled=...  16.5 us
    all_to_all x1, starting transfers between devices, on_device(): lax.all_to_all(pair_sum, ('z', 'xh'), split_axis=0, concat_axis=0, tiled=...  13.3 us
    ppermute x1, waiting for transfers between devices, on_device(): fetched = lax.ppermute(keys_own, ('y', 'xh', 'core'), pairs)  10.6 us
    all_to_all x1, starting transfers between devices, on_device(): split = lax.all_to_all(packed, CTX, split_axis=0, concat_axis=0, tiled=True)  10 us
  transfers between devices with their start and end apart: 16, of which 13 were waited for; matrix products, arithmetic and copies ran while one was open for 2% of the time, Pallas kernels for 3%

profile of v17, /device:TPU:6, one launch (start us, length us, event | category | flops | bytes accessed | tf_op | source)
XLA Modules:
  0.0 240.9 jit_solution(6851754247890308998)
XLA Ops:
  1.7 4.5 %collective-permute-start = (bf16[592,256]{1,0:T(8,128)(2,1)S(1)}, bf16[592,256]{1,0:T(8,128)(2,1)S(1)}, u32[]{:S(2)}, u32[]{:S(2)}) collective-permute-start(bf16[592,256]{1,0:T(8,128)(2,1)S(1)} %shard_map.118.own), channel_id=1, source_target_pairs={{0,64},{1,193},{2,130},{3,259},{64,128},{65,257},{66,194},{67,323}... | collective-permute-start | bytes 909320 | tf_op jit(solution)/shard_map/ppermute | solution.py:301
  8.0 10.6 %collective-permute-done.p0 = bf16[592,256]{1,0:T(8,128)(2,1)S(1)} collective-permute-done((bf16[592,256]{1,0:T(8,128)(2,1)S(1)}, bf16[592,256]{1,0:T(8,128)(2,1)S(1)}, u32[]{:S(2)}, u32[]{:S(2)}) %collective-permute-start) | collective-permute-done | bytes 303136 | tf_op jit(solution)/shard_map/ppermute | solution.py:301
  18.6 5.0 %collective-permute-start.1 = (bf16[592,256]{1,0:T(8,128)(2,1)S(1)}, bf16[592,256]{1,0:T(8,128)(2,1)S(1)}, u32[]{:S(2)}, u32[]{:S(2)}) collective-permute-start(bf16[592,256]{1,0:T(8,128)(2,1)S(1)} %collective-permute-done.p0), channel_id=1, source_target_pairs={{0,2},{2,0},{1,3},{3,1},{4,6},{6,4},{5,7},{7,5},{8,10},{10,8},{9,1... | collective-permute-start | bytes 909320 | tf_op jit(solution)/shard_map/ppermute | solution.py:332
  23.8 3.6 %collective-permute-start.2 = (bf16[592,256]{1,0:T(8,128)(2,1)S(1)}, bf16[592,256]{1,0:T(8,128)(2,1)S(1)}, u32[]{:S(2)}, u32[]{:S(2)}) collective-permute-start(bf16[592,256]{1,0:T(8,128)(2,1)S(1)} %broadcast_select_fusion), channel_id=1, source_target_pairs={{0,32},{32,0},{1,33},{33,1},{2,34},{34,2},{3,35},{35,3},{4,36},{36... | collective-permute-start | bytes 909320 | tf_op jit(solution)/shard_map/ppermute | solution.py:333
  34.0 2.7 %collective-permute-done.2.p2 = bf16[592,256]{1,0:T(8,128)(2,1)S(1)} collective-permute-done((bf16[592,256]{1,0:T(8,128)(2,1)S(1)}, bf16[592,256]{1,0:T(8,128)(2,1)S(1)}, u32[]{:S(2)}, u32[]{:S(2)}) %collective-permute-start.2) | collective-permute-done | bytes 303136 | tf_op jit(solution)/shard_map/ppermute | solution.py:333
  39.9 2.6 %shard_map.121 = (f32[2,256,128]{2,1,0:T(8,128)S(1)}, f32[2,256,128]{2,1,0:T(8,128)S(1)}, f32[2,256,512]{2,1,0:T(8,128)S(1)}) custom-call(s32[10]{0:T(128)S(1)} %stack.43.info, bf16[2,256,592]{2,1,0:T(8,128)(2,1)S(1)} %bitcast.37, bf16[592,256]{1,0:T(8,128)(2,1)S(1)} %collective-permute-done.1.p1, bf16[592,256]{1,0:T(8,128)(2,1)S(1)} %collective-permute-done.2.p2, ...), custom_call_target="tpu_custom_call" | custom-call | tf_op jit(solution)/shard_map/pallas_call | solution.py:351
  42.6 3.6 %shard_map.122 = (bf16[128,2560]{1,0:T(8,128)(2,1)S(1)}, f32[128,2560]{1,0:T(8,128)S(1)}) custom-call(s32[10]{0:T(128)S(1)} %stack.43.info, bf16[2,256,592]{2,1,0:T(8,128)(2,1)S(1)} %bitcast.38, bf16[3,592,256]{2,1,0:T(8,128)(2,1)S(1)} %collective-permute-done.5.others, f32[2,256,128]{2,1,0:T(8,128)S(1)} %get-tuple-element.49.old_peak, ...), custom_call_target="tpu_custom_call" | custom-call | tf_op jit(solution)/shard_map/pallas_call | solution.py:354
  51.3 13.3 %all-to-all-start = ((bf16[16,8,2560]{2,1,0:T(8,128)(2,1)}), bf16[16,8,2560]{2,1,0:T(8,128)(2,1)S(1)}, u32[]{:S(2)}, u32[]{:S(2)}) async-start(bf16[16,8,2560]{2,1,0:T(8,128)(2,1)} %shard_map.123), calls=%async_computation | async-start | bytes 1310720 | tf_op jit(solution)/shard_map/all_to_all | solution.py:372
  64.8 2.7 %collective-permute-start.7 = (bf16[3,160,768]{2,1,0:T(8,128)(2,1)S(1)}, bf16[3,160,768]{2,1,0:T(8,128)(2,1)S(1)}, u32[]{:S(2)}, u32[]{:S(2)}) collective-permute-start(bf16[3,160,768]{2,1,0:T(8,128)(2,1)S(1)} %get-tuple-element.56), channel_id=1, source_target_pairs={{0,32},{32,0},{1,33},{33,1},{2,34},{34,2},{3,35},{35,3},{4,36},{36... | collective-permute-start | bytes 2211848 | tf_op jit(solution)/shard_map/ppermute | solution.py:370
  67.8 16.5 %all-to-all-done.spread = bf16[16,8,2560]{2,1,0:T(8,128)(2,1)S(1)} async-done(((bf16[16,8,2560]{2,1,0:T(8,128)(2,1)}), bf16[16,8,2560]{2,1,0:T(8,128)(2,1)S(1)}, u32[]{:S(2)}, u32[]{:S(2)}) %all-to-all-start) | async-done | bytes 655392 | tf_op jit(solution)/shard_map/all_to_all | solution.py:372
  85.3 10.0 %all-to-all-start.1 = ((bf16[16,8,512]{2,1,0:T(8,128)(2,1)}), bf16[16,8,512]{2,1,0:T(8,128)(2,1)S(1)}, u32[]{:S(2)}, u32[]{:S(2)}) async-start(bf16[16,8,512]{2,1,0:T(8,128)(2,1)} %shard_map.125), calls=%async_computation.1 | async-start | bytes 262144 | tf_op jit(solution)/shard_map/all_to_all | solution.py:376
  95.9 7.8 %all-to-all-done.1 = bf16[16,8,512]{2,1,0:T(8,128)(2,1)S(1)} async-done(((bf16[16,8,512]{2,1,0:T(8,128)(2,1)}), bf16[16,8,512]{2,1,0:T(8,128)(2,1)S(1)}, u32[]{:S(2)}, u32[]{:S(2)}) %all-to-all-start.1) | async-done | bytes 131104 | tf_op jit(solution)/shard_map/all_to_all | solution.py:376
  105.0 6.6 %all-to-all-start.2 = ((bf16[32,80,128]{2,1,0:T(8,128)(2,1)}), bf16[32,80,128]{2,1,0:T(8,128)(2,1)S(1)}, u32[]{:S(2)}, u32[]{:S(2)}) async-start(bf16[32,80,128]{2,1,0:T(8,128)(2,1)} %shard_map.126), calls=%async_computation.2 | async-start | bytes 1310720 | tf_op jit(solution)/shard_map/all_to_all | solution.py:403
  112.8 19.3 %all-to-all-done.2.received = bf16[32,80,128]{2,1,0:T(8,128)(2,1)S(1)} async-done(((bf16[32,80,128]{2,1,0:T(8,128)(2,1)}), bf16[32,80,128]{2,1,0:T(8,128)(2,1)S(1)}, u32[]{:S(2)}, u32[]{:S(2)}) %all-to-all-start.2) | async-done | bytes 655392 | tf_op jit(solution)/shard_map/all_to_all | solution.py:403
  132.2 3.4 %shard_map.128 = bf16[1024,768]{1,0:T(8,128)(2,1)} custom-call(bf16[32,80,128]{2,1,0:T(8,128)(2,1)S(1)} %all-to-all-done.2.received, bf16[1152,768]{1,0:T(8,128)(2,1)S(1)} %shard_map.127.weights), custom_call_target="tpu_custom_call" | custom-call | tf_op jit(solution)/shard_map/pallas_call | solution.py:406
  135.5 3.7 %all-to-all-start.3 = ((bf16[8,128,768]{2,1,0:T(8,128)(2,1)}), bf16[8,128,768]{2,1,0:T(8,128)(2,1)S(1)}, u32[]{:S(2)}, u32[]{:S(2)}) async-start(bf16[8,128,768]{2,1,0:T(8,128)(2,1)} %bitcast.20), calls=%async_computation.3 | async-start | bytes 3145728 | tf_op jit(solution)/shard_map/all_to_all | solution.py:407
  139.3 2.7 %collective-permute-start.8 = (bf16[3,160,384]{2,1,0:T(8,128)(2,1)S(1)}, bf16[3,160,384]{2,1,0:T(8,128)(2,1)S(1)}, u32[]{:S(2)}, u32[]{:S(2)}) collective-permute-start(bf16[3,160,384]{2,1,0:T(8,128)(2,1)S(1)} %copy-done.13), channel_id=1, source_target_pairs={{0,32},{32,0},{1,33},{33,1},{2,34},{34,2},{3,35},{35,3},{4,36},{36... | collective-permute-start | bytes 1105928 | tf_op jit(solution)/shard_map/ppermute | solution.py:405
  142.0 9.6 %collective-permute-done.8.got = bf16[3,160,384]{2,1,0:T(8,128)(2,1)S(1)} collective-permute-done((bf16[3,160,384]{2,1,0:T(8,128)(2,1)S(1)}, bf16[3,160,384]{2,1,0:T(8,128)(2,1)S(1)}, u32[]{:S(2)}, u32[]{:S(2)}) %collective-permute-start.8) | collective-permute-done | bytes 368672 | tf_op jit(solution)/shard_map/ppermute | solution.py:405
  151.6 27.8 %all-to-all-done.3.parts = bf16[8,128,768]{2,1,0:T(8,128)(2,1)S(1)} async-done(((bf16[8,128,768]{2,1,0:T(8,128)(2,1)}), bf16[8,128,768]{2,1,0:T(8,128)(2,1)S(1)}, u32[]{:S(2)}, u32[]{:S(2)}) %all-to-all-start.3) | async-done | bytes 1572896 | tf_op jit(solution)/shard_map/all_to_all | solution.py:407
  180.5 3.7 %all-to-all-start.4 = ((bf16[8,128,384]{2,1,0:T(8,128)(2,1)}), bf16[8,128,384]{2,1,0:T(8,128)(2,1)S(1)}, u32[]{:S(2)}, u32[]{:S(2)}) async-start(bf16[8,128,384]{2,1,0:T(8,128)(2,1)} %shard_map.129), calls=%async_computation.4 | async-start | bytes 1572864 | tf_op jit(solution)/shard_map/all_to_all | solution.py:413
  184.3 21.2 %all-to-all-done.4 = bf16[8,128,384]{2,1,0:T(8,128)(2,1)S(1)} async-done(((bf16[8,128,384]{2,1,0:T(8,128)(2,1)}), bf16[8,128,384]{2,1,0:T(8,128)(2,1)S(1)}, u32[]{:S(2)}, u32[]{:S(2)}) %all-to-all-start.4) | async-done | bytes 786464 | tf_op jit(solution)/shard_map/all_to_all | solution.py:413
  207.9 5.0 %all-to-all-start.5 = ((bf16[32,80,128]{2,1,0:T(8,128)(2,1)}), bf16[32,80,128]{2,1,0:T(8,128)(2,1)S(1)}, u32[]{:S(2)}, u32[]{:S(2)}) async-start(bf16[32,80,128]{2,1,0:T(8,128)(2,1)} %shard_map.131), calls=%async_computation.5 | async-start | bytes 1310720 | tf_op jit(solution)/shard_map/all_to_all | solution.py:417
  213.9 19.6 %all-to-all-done.5.returned = bf16[32,80,128]{2,1,0:T(8,128)(2,1)S(1)} async-done(((bf16[32,80,128]{2,1,0:T(8,128)(2,1)}), bf16[32,80,128]{2,1,0:T(8,128)(2,1)S(1)}, u32[]{:S(2)}, u32[]{:S(2)}) %all-to-all-start.5) | async-done | bytes 655392 | tf_op jit(solution)/shard_map/all_to_all | solution.py:417
  236.7 3.6 %collective-permute-done.9 = bf16[128,160]{1,0:T(8,128)(2,1)S(1)} collective-permute-done((bf16[128,160]{1,0:T(8,128)(2,1)S(1)}, bf16[128,160]{1,0:T(8,128)(2,1)S(1)}, u32[]{:S(2)}, u32[]{:S(2)}) %collective-permute-start.9) | collective-permute-done | bytes 40992 | tf_op jit(solution)/shard_map/ppermute | solution.py:421
  (85 shorter events, 31.1 us)
Async XLA Ops:
  1.7 16.9 %collective-permute-start = (bf16[592,256]{1,0:T(8,128)(2,1)S(1)}, bf16[592,256]{1,0:T(8,128)(2,1)S(1)}, u32[]{:S(2)}, u32[]{:S(2)}) collective-permute-start(bf16[592,256]{1,0:T(8,128)(2,1)S(1)} %shard_map.118.own), channel_id=1, source_target_pairs={{0,64},{1,193},{2,130},{3,259},{64,128},{65,257},{66,194},{67,323}... | collective-permute-start | bytes 909320 | tf_op jit(solution)/shard_map/ppermute | solution.py:301
  18.6 13.5 %collective-permute-start.1 = (bf16[592,256]{1,0:T(8,128)(2,1)S(1)}, bf16[592,256]{1,0:T(8,128)(2,1)S(1)}, u32[]{:S(2)}, u32[]{:S(2)}) collective-permute-start(bf16[592,256]{1,0:T(8,128)(2,1)S(1)} %collective-permute-done.p0), channel_id=1, source_target_pairs={{0,2},{2,0},{1,3},{3,1},{4,6},{6,4},{5,7},{7,5},{8,10},{10,8},{9,1... | collective-permute-start | bytes 909320 | tf_op jit(solution)/shard_map/ppermute | solution.py:332
  23.8 12.9 %collective-permute-start.2 = (bf16[592,256]{1,0:T(8,128)(2,1)S(1)}, bf16[592,256]{1,0:T(8,128)(2,1)S(1)}, u32[]{:S(2)}, u32[]{:S(2)}) collective-permute-start(bf16[592,256]{1,0:T(8,128)(2,1)S(1)} %broadcast_select_fusion), channel_id=1, source_target_pairs={{0,32},{32,0},{1,33},{33,1},{2,34},{34,2},{3,35},{35,3},{4,36},{36... | collective-permute-start | bytes 909320 | tf_op jit(solution)/shard_map/ppermute | solution.py:333
  27.4 10.4 %collective-permute-start.3 = (bf16[592,256]{1,0:T(8,128)(2,1)S(1)}, bf16[592,256]{1,0:T(8,128)(2,1)S(1)}, u32[]{:S(2)}, u32[]{:S(2)}) collective-permute-start(bf16[592,256]{1,0:T(8,128)(2,1)S(1)} %broadcast_select_fusion), channel_id=1, source_target_pairs={{0,34},{2,32},{32,2},{34,0},{1,35},{3,33},{33,3},{35,1},{4,38},{6,... | collective-permute-start | bytes 909320 | tf_op jit(solution)/shard_map/ppermute | solution.py:334
  32.1 5.7 %collective-permute-start.4 = (bf16[592,256]{1,0:T(8,128)(2,1)S(1)}, bf16[592,256]{1,0:T(8,128)(2,1)S(1)}, u32[]{:S(2)}, u32[]{:S(2)}) collective-permute-start(bf16[592,256]{1,0:T(8,128)(2,1)S(1)} %collective-permute-done.p0), channel_id=1, source_target_pairs={{0,1},{1,0},{2,3},{3,2},{4,5},{5,4},{6,7},{7,6},{8,9},{9,8},{10,11... | collective-permute-start | bytes 909320 | tf_op jit(solution)/shard_map/ppermute | solution.py:347
  37.9 4.6 %collective-permute-start.5 = (bf16[3,592,256]{2,1,0:T(8,128)(2,1)S(1)}, bf16[3,592,256]{2,1,0:T(8,128)(2,1)S(1)}, u32[]{:S(2)}, u32[]{:S(2)}) collective-permute-start(bf16[3,592,256]{2,1,0:T(8,128)(2,1)S(1)} %shard_map.120), channel_id=1, source_target_pairs={{0,1},{1,0},{2,3},{3,2},{4,5},{5,4},{6,7},{7,6},{8,9},{9,8},{10,11... | collective-permute-start | bytes 2727944 | tf_op jit(solution)/shard_map/ppermute | solution.py:350
  42.5 6.0 %copy-start.1 = (bf16[3,160,768]{2,1,0:T(8,128)(2,1)S(1)}, bf16[3,160,768]{2,1,0:T(8,128)(2,1)}, u32[]{:S(2)}) copy-start(bf16[3,160,768]{2,1,0:T(8,128)(2,1)} %gate.1) | copy-start | bytes 2211844
  42.6 6.0 %copy-start.2 = (bf16[3,160,768]{2,1,0:T(8,128)(2,1)S(1)}, bf16[3,160,768]{2,1,0:T(8,128)(2,1)}, u32[]{:S(2)}) copy-start(bf16[3,160,768]{2,1,0:T(8,128)(2,1)} %up.1) | copy-start | bytes 2211844
  46.2 4.1 %collective-permute-start.6 = (bf16[128,2560]{1,0:T(8,128)(2,1)S(1)}, bf16[128,2560]{1,0:T(8,128)(2,1)S(1)}, u32[]{:S(2)}, u32[]{:S(2)}) collective-permute-start(bf16[128,2560]{1,0:T(8,128)(2,1)S(1)} %get-tuple-element.53), channel_id=1, source_target_pairs={{0,1},{1,0},{2,3},{3,2},{4,5},{5,4},{6,7},{7,6},{8,9},{9,8},{10,11... | collective-permute-start | bytes 1966088 | tf_op jit(solution)/shard_map/ppermute | solution.py:361
  50.3 14.3 %copy-start.15 = (s32[8,16,6]{1,0,2:T(8,128)S(1)}, s32[8,16,6]{1,0,2:T(8,128)}, u32[]{:S(2)}) copy-start(s32[8,16,6]{1,0,2:T(8,128)} %param.19) | copy-start | bytes 9220
  50.3 17.2 %copy-start.16 = (f32[2560]{0:T(1024)S(1)}, f32[2560]{0:T(1024)}, u32[]{:S(2)}) copy-start(f32[2560]{0:T(1024)} %param.18) | copy-start | bytes 30724
  50.3 34.0 %copy-start.10 = (bf16[8,2560]{1,0:T(8,128)(2,1)S(1)}, bf16[8,2560]{1,0:T(8,128)(2,1)}, u32[]{:S(2)}) copy-start(bf16[8,2560]{1,0:T(8,128)(2,1)} %residual.1) | copy-start | bytes 122884
  51.3 33.0 %all-to-all-start = ((bf16[16,8,2560]{2,1,0:T(8,128)(2,1)}), bf16[16,8,2560]{2,1,0:T(8,128)(2,1)S(1)}, u32[]{:S(2)}, u32[]{:S(2)}) async-start(bf16[16,8,2560]{2,1,0:T(8,128)(2,1)} %shard_map.123), calls=%async_computation | async-start | bytes 1310720 | tf_op jit(solution)/shard_map/all_to_all | solution.py:372
  64.8 31.0 %collective-permute-start.7 = (bf16[3,160,768]{2,1,0:T(8,128)(2,1)S(1)}, bf16[3,160,768]{2,1,0:T(8,128)(2,1)S(1)}, u32[]{:S(2)}, u32[]{:S(2)}) collective-permute-start(bf16[3,160,768]{2,1,0:T(8,128)(2,1)S(1)} %get-tuple-element.56), channel_id=1, source_target_pairs={{0,32},{32,0},{1,33},{33,1},{2,34},{34,2},{3,35},{35,3},{4,36},{36... | collective-permute-start | bytes 2211848 | tf_op jit(solution)/shard_map/ppermute | solution.py:370
  85.3 18.4 %all-to-all-start.1 = ((bf16[16,8,512]{2,1,0:T(8,128)(2,1)}), bf16[16,8,512]{2,1,0:T(8,128)(2,1)S(1)}, u32[]{:S(2)}, u32[]{:S(2)}) async-start(bf16[16,8,512]{2,1,0:T(8,128)(2,1)} %shard_map.125), calls=%async_computation.1 | async-start | bytes 262144 | tf_op jit(solution)/shard_map/all_to_all | solution.py:376
  95.9 15.7 %copy-start.4 = (bf16[3,160,768]{2,1,0:T(8,128)(2,1)}, bf16[3,160,768]{2,1,0:T(8,128)(2,1)S(1)}, u32[]{:S(2)}) copy-start(bf16[3,160,768]{2,1,0:T(8,128)(2,1)S(1)} %collective-permute-done.7.got) | copy-start | bytes 2211844
  105.0 27.2 %all-to-all-start.2 = ((bf16[32,80,128]{2,1,0:T(8,128)(2,1)}), bf16[32,80,128]{2,1,0:T(8,128)(2,1)S(1)}, u32[]{:S(2)}, u32[]{:S(2)}) async-start(bf16[32,80,128]{2,1,0:T(8,128)(2,1)} %shard_map.126), calls=%async_computation.2 | async-start | bytes 1310720 | tf_op jit(solution)/shard_map/all_to_all | solution.py:403
  135.5 43.8 %all-to-all-start.3 = ((bf16[8,128,768]{2,1,0:T(8,128)(2,1)}), bf16[8,128,768]{2,1,0:T(8,128)(2,1)S(1)}, u32[]{:S(2)}, u32[]{:S(2)}) async-start(bf16[8,128,768]{2,1,0:T(8,128)(2,1)} %bitcast.20), calls=%async_computation.3 | async-start | bytes 3145728 | tf_op jit(solution)/shard_map/all_to_all | solution.py:407
  139.3 45.0 %copy-start.7 = (bf16[3,160,384]{2,1,0:T(8,128)(2,1)S(1)}, bf16[3,160,384]{2,1,0:T(8,128)(2,1)}, u32[]{:S(2)}) copy-start(bf16[3,160,384]{2,1,0:T(8,128)(2,1)} %copy-done.6) | copy-start | bytes 1105924
  139.3 12.3 %collective-permute-start.8 = (bf16[3,160,384]{2,1,0:T(8,128)(2,1)S(1)}, bf16[3,160,384]{2,1,0:T(8,128)(2,1)S(1)}, u32[]{:S(2)}, u32[]{:S(2)}) collective-permute-start(bf16[3,160,384]{2,1,0:T(8,128)(2,1)S(1)} %copy-done.13), channel_id=1, source_target_pairs={{0,32},{32,0},{1,33},{33,1},{2,34},{34,2},{3,35},{35,3},{4,36},{36... | collective-permute-start | bytes 1105928 | tf_op jit(solution)/shard_map/ppermute | solution.py:405
  180.5 25.1 %all-to-all-start.4 = ((bf16[8,128,384]{2,1,0:T(8,128)(2,1)}), bf16[8,128,384]{2,1,0:T(8,128)(2,1)S(1)}, u32[]{:S(2)}, u32[]{:S(2)}) async-start(bf16[8,128,384]{2,1,0:T(8,128)(2,1)} %shard_map.129), calls=%async_computation.4 | async-start | bytes 1572864 | tf_op jit(solution)/shard_map/all_to_all | solution.py:413
  205.6 7.7 %copy-start.14 = (f32[8,16,6]{1,0,2:T(8,128)S(1)}, f32[8,16,6]{1,0,2:T(8,128)}, u32[]{:S(2)}) copy-start(f32[8,16,6]{1,0,2:T(8,128)} %param.20) | copy-start | bytes 9220
  207.9 25.6 %all-to-all-start.5 = ((bf16[32,80,128]{2,1,0:T(8,128)(2,1)}), bf16[32,80,128]{2,1,0:T(8,128)(2,1)S(1)}, u32[]{:S(2)}, u32[]{:S(2)}) async-start(bf16[32,80,128]{2,1,0:T(8,128)(2,1)} %shard_map.131), calls=%async_computation.5 | async-start | bytes 1310720 | tf_op jit(solution)/shard_map/all_to_all | solution.py:417
  234.1 6.2 %collective-permute-start.9 = (bf16[128,160]{1,0:T(8,128)(2,1)S(1)}, bf16[128,160]{1,0:T(8,128)(2,1)S(1)}, u32[]{:S(2)}, u32[]{:S(2)}) collective-permute-start(bf16[128,160]{1,0:T(8,128)(2,1)S(1)} %get-tuple-element.68), channel_id=1, source_target_pairs={{0,32},{32,0},{1,33},{33,1},{2,34},{34,2},{3,35},{35,3},{4,36},{36... | collective-permute-start | bytes 122888 | tf_op jit(solution)/shard_map/ppermute | solution.py:421
  (9 other events, 21.7 us)
